TPU v7x, 32 devices: a whole 2x2x4 slice. The times are simulated.
32 devices in a mesh: seq: 2 (over core), blk: 16 (over z, y, x).
Axes of the slice: x: 2, y: 2, z: 4, core: 2. Of those that a mesh axis runs over, the one named last changes fastest.
Arguments:
- tokens: bfloat16 [4096, 1024], P(('seq', 'blk')), may hold values from -6 to 6
- cotangent: bfloat16 [4096, 1024], P(('seq', 'blk')), may hold values from -6 to 6
- routes: int32 [4096, 2], P(('seq', 'blk')), may hold values from 0 to 7, all different within a row; in each aligned block of 128 rows (0 to 127, 128 to 255, ...) at most 64 rows name the same one
- gate_codes: int32 [4096, 2], P(('seq', 'blk')), may hold values from 1 to 64
- dropout_key: int32 [2], replicated, may hold values from 0 to 1073741823
- w_gate: bfloat16 [16, 1024, 352], P('blk', 'seq'), may hold values from -0.1875 to 0.1875
- w_up: bfloat16 [16, 1024, 352], P('blk', 'seq'), may hold values from -0.1875 to 0.1875
- w_down: bfloat16 [16, 352, 1024], P('blk', None, 'seq'), may hold values from -0.21875 to 0.21875
Outputs:
- layer_out: bfloat16 [4096, 1024], P(('seq', 'blk'))
- tokens_grad: bfloat16 [4096, 1024], P(('seq', 'blk'))
- gate_grad: bfloat16 [16, 1024, 352], P('blk', 'seq')
- up_grad: bfloat16 [16, 1024, 352], P('blk', 'seq')
- down_grad: bfloat16 [16, 352, 1024], P('blk', None, 'seq')
Inputs may be any that keep to these rules, and one draw needn't show every extreme that they name: `routes`: each row names 2 different experts; in the 128 rows of one device no expert is named more than 64 times.
All inputs are finite; a program needn't handle non-finite values.
Results may differ from a plain program's by a relative error of at most 0.0095.
Values may be sent and summed in bfloat16 or wider, within the bound.
No kernel may reach another device: no remote copies, remote signals or barrier semaphores. Data moves between devices by JAX's collectives and lax.ppermute only.
A program may use at most 64 MiB of HBM per device.

v0:
```python
import jax
import jax.numpy as jnp
from jax import lax
from jax.sharding import PartitionSpec as P

mixing_factor = 73244475
contract_last = (((1,), (1,)), ((), ()))
contract_first = (((0,), (0,)), ((), ()))


def for_sending(shard):

    def short(part):
        return part.astype(jnp.bfloat16) if part.dtype == jnp.float32 else part

    return jax.tree.map(short, shard)


def swapped(shard, axis, stride):
    return lax.ppermute(shard, axis, [(i, i ^ 1 << stride) for i in range(lax.axis_size(axis))])


def scramble(values):
    values = values ^ values >> 16 & 65535
    values = values * mixing_factor
    values = values ^ values >> 16 & 65535
    values = values * mixing_factor
    return values ^ values >> 16 & 65535


def keep_scale(token_ids, columns, key_pair):
    base_hash = scramble(key_pair[0] ^ scramble(key_pair[1]))
    mixed_ids = scramble(token_ids ^ base_hash)
    hashed = scramble(mixed_ids[:, None] ^ columns[None, :] * 40503)
    return jnp.where(hashed & 1023 >= 128, jnp.float32(8.0 / 7.0), jnp.float32(0.0))


def expert_pass(inputs_flat, cot_flat, ids_flat, gate_mat, up_mat, down_mat, columns, key_pair):
    drop_scale = keep_scale(ids_flat, columns, key_pair)
    gate_pre = jnp.dot(inputs_flat, gate_mat, preferred_element_type=jnp.float32)
    up_pre = jnp.dot(inputs_flat, up_mat, preferred_element_type=jnp.float32)
    sigmoid_gate = jax.nn.sigmoid(gate_pre)
    silu_gate = gate_pre * sigmoid_gate
    hidden = (silu_gate * up_pre * drop_scale).astype(jnp.bfloat16)
    expert_out = jnp.dot(hidden, down_mat, preferred_element_type=jnp.float32)
    hidden_grad = (
        lax.dot_general(cot_flat, down_mat, contract_last, preferred_element_type=jnp.float32)
        * drop_scale
    )
    gate_pre_grad = (
        hidden_grad * up_pre * sigmoid_gate * (1.0 + gate_pre * (1.0 - sigmoid_gate))
    ).astype(jnp.bfloat16)
    up_pre_grad = (hidden_grad * silu_gate).astype(jnp.bfloat16)
    input_grad = lax.dot_general(
        gate_pre_grad, gate_mat, contract_last, preferred_element_type=jnp.float32
    ) + lax.dot_general(up_pre_grad, up_mat, contract_last, preferred_element_type=jnp.float32)
    partial_gate = lax.dot_general(
        inputs_flat, gate_pre_grad, contract_first, preferred_element_type=jnp.float32
    )
    partial_up = lax.dot_general(
        inputs_flat, up_pre_grad, contract_first, preferred_element_type=jnp.float32
    )
    partial_down = lax.dot_general(
        hidden, cot_flat, contract_first, preferred_element_type=jnp.float32
    )
    return (expert_out, input_grad, partial_gate, partial_up, partial_down)


def local(tokens, cotangent, routes, gate_codes, dropout_key, w_gate, w_up, w_down):
    block_count = lax.axis_size("blk")
    seq_index = lax.axis_index("seq")
    blk_index = lax.axis_index("blk")
    tok_rows, model_width = tokens.shape
    top_count = routes.shape[1]
    expert_count = block_count // 2
    capacity = 2 * tok_rows * top_count // expert_count
    half_cap = capacity // 2
    half_width = w_gate.shape[2]
    parity = blk_index % 2
    expert_here = blk_index // 2
    first_token = (seq_index * block_count + blk_index) * tok_rows
    token_ids = first_token + jnp.arange(tok_rows, dtype=jnp.int32)
    pair_expert = routes.reshape(-1)
    one_hot = (pair_expert[:, None] == jnp.arange(expert_count, dtype=jnp.int32)[None, :]).astype(
        jnp.int32
    )
    position = jnp.sum(jnp.cumsum(one_hot, axis=0) * one_hot, axis=1) - 1
    slot_index = pair_expert * capacity + position
    pair_gate = gate_codes.reshape(-1).astype(jnp.float32) / 64.0
    pair_inputs = jnp.repeat(tokens, top_count, axis=0)
    pair_cot = (
        pair_gate[:, None] * jnp.repeat(cotangent, top_count, axis=0).astype(jnp.float32)
    ).astype(jnp.bfloat16)
    slot_total = expert_count * capacity
    send_inputs = jnp.zeros((slot_total, model_width), jnp.bfloat16).at[slot_index].set(pair_inputs)
    send_cot = jnp.zeros((slot_total, model_width), jnp.bfloat16).at[slot_index].set(pair_cot)
    send_ids = (
        jnp.full((slot_total,), -1, jnp.int32).at[slot_index].set(jnp.repeat(token_ids, top_count))
    )
    gathered = (
        lax.all_gather(w_gate, "seq", axis=1, tiled=True),
        lax.all_gather(w_up, "seq", axis=1, tiled=True),
        lax.all_gather(w_down, "seq", axis=2, tiled=True),
    )
    gate_mat = gathered[0][0]
    up_mat = gathered[1][0]
    down_mat = gathered[2][0]

    def halved(values):
        return values.reshape((block_count, half_cap) + values.shape[1:])

    half_columns = (
        expert_here * (2 * half_width)
        + parity * half_width
        + jnp.arange(half_width, dtype=jnp.int32)
    )
    own_rows = (
        lax.all_to_all(halved(send_inputs), "blk", split_axis=0, concat_axis=0, tiled=True),
        lax.all_to_all(halved(send_cot), "blk", split_axis=0, concat_axis=0, tiled=True),
        lax.all_to_all(halved(send_ids), "blk", split_axis=0, concat_axis=0, tiled=True),
    )
    partner_rows = swapped((own_rows[0], own_rows[1], for_sending(own_rows[2])), "blk", 0)

    def joined(own_part, peer_part):
        lower_half = jnp.where(parity == 0, own_part, peer_part)
        upper_half = jnp.where(parity == 0, peer_part, own_part)
        return jnp.concatenate([lower_half, upper_half], axis=1)

    recv_inputs = joined(own_rows[0], partner_rows[0])
    recv_cot = joined(own_rows[1], partner_rows[1])
    recv_ids = joined(own_rows[2], partner_rows[2])
    slot_rows = block_count * capacity
    expert_out, input_grad, partial_gate, partial_up, partial_down = expert_pass(
        recv_inputs.reshape(slot_rows, model_width),
        recv_cot.reshape(slot_rows, model_width),
        recv_ids.reshape(slot_rows),
        gate_mat,
        up_mat,
        down_mat,
        half_columns,
        dropout_key,
    )
    out_blocks = expert_out.reshape(block_count, capacity, model_width)
    grad_blocks = input_grad.reshape(block_count, capacity, model_width)

    def split_owned(values):
        lower_half = values[:, :half_cap]
        upper_half = values[:, half_cap:]
        return (
            jnp.where(parity == 0, lower_half, upper_half),
            jnp.where(parity == 0, upper_half, lower_half),
        )

    keep_out, give_out = split_owned(out_blocks)
    keep_grad, give_grad = split_owned(grad_blocks)
    partner_sums = (
        swapped(give_out.astype(jnp.bfloat16), "blk", 0).astype(give_out.dtype),
        swapped(give_grad.astype(jnp.bfloat16), "blk", 0).astype(give_grad.dtype),
    )
    returned = (
        lax.all_to_all(keep_out + partner_sums[0], "blk", split_axis=0, concat_axis=0, tiled=True),
        lax.all_to_all(keep_grad + partner_sums[1], "blk", split_axis=0, concat_axis=0, tiled=True),
    )
    slot_out = returned[0].reshape(slot_total, model_width)
    slot_grad = returned[1].reshape(slot_total, model_width)
    summed = (
        lax.psum_scatter(
            partial_gate.astype(jnp.bfloat16), "seq", scatter_dimension=0, tiled=True
        ).astype(jnp.float32),
        lax.psum_scatter(
            partial_up.astype(jnp.bfloat16), "seq", scatter_dimension=0, tiled=True
        ).astype(jnp.float32),
        lax.psum_scatter(
            partial_down.astype(jnp.bfloat16), "seq", scatter_dimension=1, tiled=True
        ).astype(jnp.float32),
    )
    pair_out = slot_out[slot_index].reshape(tok_rows, top_count, model_width)
    layer_out = jnp.sum(pair_gate.reshape(tok_rows, top_count, 1) * pair_out, axis=1).astype(
        jnp.bfloat16
    )
    tokens_grad = jnp.sum(
        slot_grad[slot_index].reshape(tok_rows, top_count, model_width), axis=1
    ).astype(jnp.bfloat16)
    gate_grad = summed[0].astype(jnp.bfloat16)[None]
    up_grad = summed[1].astype(jnp.bfloat16)[None]
    down_grad = summed[2].astype(jnp.bfloat16)[None]
    return (layer_out, tokens_grad, gate_grad, up_grad, down_grad)


def solution(mesh):
    placed = (
        P(("seq", "blk"), None),
        P(("seq", "blk"), None),
        P(("seq", "blk"), None),
        P(("seq", "blk"), None),
        P(),
        P("blk", "seq", None),
        P("blk", "seq", None),
        P("blk", None, "seq"),
    )
    return jax.shard_map(
        local,
        mesh=mesh,
        in_specs=placed,
        out_specs=(
            P(("seq", "blk"), None),
            P(("seq", "blk"), None),
            P("blk", "seq", None),
            P("blk", "seq", None),
            P("blk", None, "seq"),
        ),
        check_vma=False,
    )
```

profile of v0, /device:TPU:0, one launch (start us, length us, event | category | flops | bytes accessed | tf_op | source)
XLA Modules:
  0.0 272.0 jit_solution(1820731432949583002)
XLA Ops:
  7.2 0.7 broadcast_multiply_fusion
  7.8 0.8 copy.23
  8.9 0.7 convert_multiply_fusion
  10.0 0.1 mul.120
  10.1 0.6 reduce-window.6
  10.7 0.2 slice_reduce_fusion
  11.1 1.2 broadcast_in_dim.43
  12.3 0.7 convert_element_type.74
  13.1 2.7 %scatter_custom_fusion.2 = bf16[512,1024]{1,0:T(8,128)(2,1)} fusion(s32[256]{0:T(256)S(1)} %bitcast.67, f32[256,1024]{1,0:T(8,128)S(1)} %convert_element_type.74, f32[256]{0:T(256)S(1)} %div.25, bf16[]{:T(256)} %constant.28.clone.1), kind=kCustom, calls=%fused_computation.47 | custom fusion | flops 524288 | bytes 2098178 | tf_op jit(solution)/shard_map/scatter | solution.py:96
  15.8 8.3 %all-to-all-start.3 = ((bf16[16,32,1024]{2,1,0:T(8,128)(2,1)}), bf16[16,32,1024]{2,1,0:T(8,128)(2,1)S(1)}, u32[]{:S(2)}, u32[]{:S(2)}) async-start(bf16[16,32,1024]{2,1,0:T(8,128)(2,1)} %bitcast.15), calls=%async_computation.3 | async-start | bytes 2097152 | tf_op jit(solution)/shard_map/all_to_all | solution.py:119
  24.1 0.3 broadcast_in_dim.38
  24.4 0.2 reshape.174
  24.6 2.7 scatter_custom_fusion
  27.3 21.3 %all-to-all-done.3 = bf16[16,32,1024]{2,1,0:T(8,128)(2,1)S(1)} async-done(((bf16[16,32,1024]{2,1,0:T(8,128)(2,1)}), bf16[16,32,1024]{2,1,0:T(8,128)(2,1)S(1)}, u32[]{:S(2)}, u32[]{:S(2)}) %all-to-all-start.3) | async-done | bytes 1048608 | tf_op jit(solution)/shard_map/all_to_all | solution.py:119
  48.6 5.8 %all-to-all-start = ((bf16[16,32,1024]{2,1,0:T(8,128)(2,1)}), bf16[16,32,1024]{2,1,0:T(8,128)(2,1)S(1)}, u32[]{:S(2)}, u32[]{:S(2)}) async-start(bf16[16,32,1024]{2,1,0:T(8,128)(2,1)} %bitcast.4), calls=%async_computation | async-start | bytes 2097152 | tf_op jit(solution)/shard_map/all_to_all | solution.py:118
  54.5 0.1 reshape.182
  54.7 1.4 scatter_custom_fusion.1
  56.1 0.7 all_to_all.21
  56.8 2.4 all_gather.9
  59.2 1.9 collective-permute-start.3
  61.1 16.2 %all-to-all-done = bf16[16,32,1024]{2,1,0:T(8,128)(2,1)S(1)} async-done(((bf16[16,32,1024]{2,1,0:T(8,128)(2,1)}), bf16[16,32,1024]{2,1,0:T(8,128)(2,1)S(1)}, u32[]{:S(2)}, u32[]{:S(2)}) %all-to-all-start) | async-done | bytes 1048608 | tf_op jit(solution)/shard_map/all_to_all | solution.py:118
  77.4 6.1 %all-to-all-start.1 = ((s32[16,1,32]{2,1,0:T(1,128)}), s32[16,1,32]{2,1,0:T(1,128)S(1)}, u32[]{:S(2)}, u32[]{:S(2)}) async-start(s32[16,1,32]{2,1,0:T(1,128)} %all_to_all.21), calls=%async_computation.1 | async-start | bytes 16384 | tf_op jit(solution)/shard_map/all_to_all | solution.py:120
  83.5 1.9 collective-permute-start
  85.4 2.3 all_gather.10
  87.7 2.7 all_gather.11
  90.4 0.6 fusion.27
  91.0 2.8 %all-to-all-done.1 = s32[16,1,32]{2,1,0:T(1,128)S(1)} async-done(((s32[16,1,32]{2,1,0:T(1,128)}), s32[16,1,32]{2,1,0:T(1,128)S(1)}, u32[]{:S(2)}, u32[]{:S(2)}) %all-to-all-start.1) | async-done | bytes 2080 | tf_op jit(solution)/shard_map/all_to_all | solution.py:120
  93.8 1.1 collective-permute-start.1
  94.9 0.6 add_multiply_fusion
  97.4 18.0 %collective-permute-done.1 = s32[16,32]{1,0:T(8,128)S(1)} collective-permute-done((s32[16,32]{1,0:T(8,128)S(1)}, s32[16,32]{1,0:T(8,128)S(1)}, u32[]{:S(2)}, u32[]{:S(2)}) %collective-permute-start.1) | collective-permute-done | bytes 2080 | tf_op jit(solution)/shard_map/ppermute | solution.py:20
  115.6 1.8 broadcast_select_fusion.1
  117.4 0.2 pad_maximum_fusion
  117.6 0.9 fusion.12
  118.6 0.7 copy-done.1
  119.3 0.9 fusion.16
  120.2 0.2 pad_maximum_fusion.1
  120.5 0.4 copy-done.18
  120.9 3.6 %multiply_convert_fusion = (bf16[1024,352]{0,1:T(8,128)(2,1)}, bf16[1024,352]{0,1:T(8,128)(2,1)}, bf16[1024,352]{0,1:T(8,128)(2,1)S(1)}) fusion(f32[1024,352]{0,1:T(8,128)S(1)} %fusion.16, f32[1024,352]{0,1:T(8,128)S(1)} %fusion.12, s32[352]{0:T(512)S(1)} %copy-done.18, s32[1024]{0:T(1024)S(1)} %and_xor_fusion, bf16[1024,1024]{1,0:T(8,128)(2,1)S(1)} %bitcast.63, ...), kind=kOutput, calls=%fused_computation.23 | convolution fusion | flops 749731840 | bytes 7869824 | tf_op jit(solution)/shard_map/dot_general | solution.py:47
  124.5 0.4 copy.25
  124.8 1.2 fusion.8
  126.1 0.2 select_convert_fusion.1
  126.3 1.7 collective-permute-start.2
  128.0 23.1 %collective-permute-done.2 = bf16[16,32,1024]{2,1,0:T(8,128)(2,1)S(1)} collective-permute-done((bf16[16,32,1024]{2,1,0:T(8,128)(2,1)S(1)}, bf16[16,32,1024]{2,1,0:T(8,128)(2,1)S(1)}, u32[]{:S(2)}, u32[]{:S(2)}) %collective-permute-start.2) | collective-permute-done | bytes 1048608 | tf_op jit(solution)/shard_map/ppermute | solution.py:20
  151.2 1.9 convert_add_fusion.1
  153.1 5.8 %all-to-all-start.2 = ((f32[16,32,1024]{2,1,0:T(8,128)}), f32[16,32,1024]{2,1,0:T(8,128)S(1)}, u32[]{:S(2)}, u32[]{:S(2)}) async-start(f32[16,32,1024]{2,1,0:T(8,128)} %convert_add_fusion.1), calls=%async_computation.2 | async-start | bytes 4194304 | tf_op jit(solution)/shard_map/all_to_all | solution.py:161
  159.0 2.5 fusion.14
  161.5 1.3 convolution_add_fusion
  162.8 2.1 copy-done
  164.9 0.2 select_convert_fusion
  165.1 2.0 collective-permute-start.4
  167.1 1.8 convolution_convert_fusion.2
  168.9 36.9 %collective-permute-done.4 = bf16[16,32,1024]{2,1,0:T(8,128)(2,1)} collective-permute-done((bf16[16,32,1024]{2,1,0:T(8,128)(2,1)S(1)}, bf16[16,32,1024]{2,1,0:T(8,128)(2,1)}, u32[]{:S(2)}, u32[]{:S(2)}) %collective-permute-start.4) | collective-permute-done | bytes 1048608 | tf_op jit(solution)/shard_map/ppermute | solution.py:20
  205.9 4.7 %convert_add_fusion = f32[16,32,1024]{2,1,0:T(8,128)} fusion(bf16[16,32,1024]{2,1,0:T(8,128)(2,1)} %collective-permute-done.4, f32[16,64,1024]{2,1,0:T(8,128)} %bitcast.57, pred[]{:T(512)S(6)} %eq.39), kind=kLoop, calls=%fused_computation.8 | loop fusion | flops 1572864 | bytes 7340033 | tf_op jit(solution)/shard_map/add | solution.py:162
  210.5 5.9 %all-to-all-start.4 = ((f32[16,32,1024]{2,1,0:T(8,128)}), f32[16,32,1024]{2,1,0:T(8,128)}, u32[]{:S(2)}, u32[]{:S(2)}) async-start(f32[16,32,1024]{2,1,0:T(8,128)} %convert_add_fusion), calls=%async_computation.4 | async-start | bytes 4194304 | tf_op jit(solution)/shard_map/all_to_all | solution.py:162
  216.5 3.5 %convolution_convert_fusion.1 = bf16[1024,352]{0,1:T(8,128)(2,1)} fusion(bf16[1024,352]{0,1:T(8,128)(2,1)S(1)} %copy-done.6, bf16[1024,1024]{1,0:T(8,128)(2,1)} %bitcast.61), kind=kOutput, calls=%fused_computation.29 | convolution fusion | flops 738557952 | bytes 3538944 | tf_op jit(solution)/shard_map/dot_general | solution.py:57
  220.0 0.3 reduce-scatter.6.cloned.1.call-start
  220.3 3.4 %convolution_convert_fusion = bf16[1024,352]{0,1:T(8,128)(2,1)} fusion(bf16[1024,352]{0,1:T(8,128)(2,1)S(1)} %copy-done.10, bf16[1024,1024]{1,0:T(8,128)(2,1)} %bitcast.62), kind=kOutput, calls=%fused_computation.28 | convolution fusion | flops 738557952 | bytes 3538944 | tf_op jit(solution)/shard_map/dot_general | solution.py:60
  223.7 1.1 gather_fusion
  224.8 0.6 reshape.148
  225.4 32.1 %all-to-all-done.4 = f32[16,32,1024]{2,1,0:T(8,128)} async-done(((f32[16,32,1024]{2,1,0:T(8,128)}), f32[16,32,1024]{2,1,0:T(8,128)}, u32[]{:S(2)}, u32[]{:S(2)}) %all-to-all-start.4) | async-done | bytes 2097184 | tf_op jit(solution)/shard_map/all_to_all | solution.py:162
  257.5 3.2 %gather_fusion.1 = f32[256,1024]{1,0:T(8,128)S(1)} fusion(f32[512,1024]{1,0:T(8,128)} %bitcast.18, s32[1024]{0:T(1024)S(1)} %pad_clamp_fusion), kind=kCustom, calls=%fused_computation.1 | custom fusion | bytes 2098176 | tf_op jit(solution)/shard_map/gather | solution.py:182
  260.7 0.6 reshape.153
  261.3 2.1 reduce_sum.29
  263.4 2.1 multiply_reduce_fusion
  (66 shorter events, 1.3 us)
Async XLA Ops:
  9.7 1.3 copy-start.11
  13.1 41.6 %copy-start.16 = (s32[256,1]{0,1:T(1,128)}, s32[256,1]{0,1:T(1,128)S(1)}, u32[]{:S(2)}) copy-start(s32[256,1]{0,1:T(1,128)S(1)} %compare_select_fusion) | copy-start | bytes 3076
  13.1 11.1 %copy-start.15 = (bf16[128,1024]{1,0:T(8,128)(2,1)S(1)}, bf16[128,1024]{1,0:T(8,128)(2,1)}, u32[]{:S(2)}) copy-start(bf16[128,1024]{1,0:T(8,128)(2,1)} %param.8) | copy-start | bytes 786436
  15.8 32.8 %all-to-all-start.3 = ((bf16[16,32,1024]{2,1,0:T(8,128)(2,1)}), bf16[16,32,1024]{2,1,0:T(8,128)(2,1)S(1)}, u32[]{:S(2)}, u32[]{:S(2)}) async-start(bf16[16,32,1024]{2,1,0:T(8,128)(2,1)} %bitcast.15), calls=%async_computation.3 | async-start | bytes 2097152 | tf_op jit(solution)/shard_map/all_to_all | solution.py:119
  24.4 32.3 %copy-start.13 = (bf16[1,512,352]{1,2,0:T(8,128)(2,1)S(1)}, bf16[1,512,352]{1,2,0:T(8,128)(2,1)}, u32[]{:S(2)}) copy-start(bf16[1,512,352]{1,2,0:T(8,128)(2,1)} %param.13) | copy-start | bytes 1081348
  24.6 60.8 %copy-start.14 = (bf16[1,512,352]{1,2,0:T(8,128)(2,1)S(1)}, bf16[1,512,352]{1,2,0:T(8,128)(2,1)}, u32[]{:S(2)}) copy-start(bf16[1,512,352]{1,2,0:T(8,128)(2,1)} %param.14) | copy-start | bytes 1081348
  48.6 28.8 %all-to-all-start = ((bf16[16,32,1024]{2,1,0:T(8,128)(2,1)}), bf16[16,32,1024]{2,1,0:T(8,128)(2,1)S(1)}, u32[]{:S(2)}, u32[]{:S(2)}) async-start(bf16[16,32,1024]{2,1,0:T(8,128)(2,1)} %bitcast.4), calls=%async_computation | async-start | bytes 2097152 | tf_op jit(solution)/shard_map/all_to_all | solution.py:118
  54.4 36.0 %copy-start.19 = (s32[2]{0:T(128)S(1)}, s32[2]{0:T(128)}, u32[]{:S(2)}) copy-start(s32[2]{0:T(128)} %param.12) | copy-start | bytes 28
  59.2 56.4 %collective-permute-start.3 = (bf16[16,32,1024]{2,1,0:T(8,128)(2,1)S(1)}, bf16[16,32,1024]{2,1,0:T(8,128)(2,1)}, u32[]{:S(2)}, u32[]{:S(2)}) collective-permute-start(bf16[16,32,1024]{2,1,0:T(8,128)(2,1)S(1)} %all-to-all-done.3), channel_id=1, source_target_pairs={{0,1},{1,0},{2,3},{3,2},{4,5},{5,4},{6,7},{7,6},{8,9},{9,8},{10,11... | collective-permute-start | bytes 3145736 | tf_op jit(solution)/shard_map/ppermute | solution.py:20
  77.4 16.4 %all-to-all-start.1 = ((s32[16,1,32]{2,1,0:T(1,128)}), s32[16,1,32]{2,1,0:T(1,128)S(1)}, u32[]{:S(2)}, u32[]{:S(2)}) async-start(s32[16,1,32]{2,1,0:T(1,128)} %all_to_all.21), calls=%async_computation.1 | async-start | bytes 16384 | tf_op jit(solution)/shard_map/all_to_all | solution.py:120
  83.5 32.1 %collective-permute-start = (bf16[16,32,1024]{2,1,0:T(8,128)(2,1)S(1)}, bf16[16,32,1024]{2,1,0:T(8,128)(2,1)}, u32[]{:S(2)}, u32[]{:S(2)}) collective-permute-start(bf16[16,32,1024]{2,1,0:T(8,128)(2,1)S(1)} %all-to-all-done), channel_id=1, source_target_pairs={{0,1},{1,0},{2,3},{3,2},{4,5},{5,4},{6,7},{7,6},{8,9},{9,8},{10,11... | collective-permute-start | bytes 3145736 | tf_op jit(solution)/shard_map/ppermute | solution.py:20
  93.8 21.6 %collective-permute-start.1 = (s32[16,32]{1,0:T(8,128)S(1)}, s32[16,32]{1,0:T(8,128)S(1)}, u32[]{:S(2)}, u32[]{:S(2)}) collective-permute-start(s32[16,32]{1,0:T(8,128)S(1)} %bitcast.65), channel_id=1, source_target_pairs={{0,1},{1,0},{2,3},{3,2},{4,5},{5,4},{6,7},{7,6},{8,9},{9,8},{10,11... | collective-permute-start | bytes 6152 | tf_op jit(solution)/shard_map/ppermute | solution.py:20
  117.6 2.6 copy-start.3
  117.6 1.6 copy-start.1
  120.2 0.7 copy-start.18
  120.5 4.0 %copy-start.4 = (bf16[16,64,1024]{2,1,0:T(8,128)(2,1)}, bf16[16,64,1024]{2,1,0:T(8,128)(2,1)S(1)}, u32[]{:S(2)}) copy-start(bf16[16,64,1024]{2,1,0:T(8,128)(2,1)S(1)} %pad_maximum_fusion.1) | copy-start | bytes 6291460
  124.5 1.6 copy-start.7
  126.3 24.9 %collective-permute-start.2 = (bf16[16,32,1024]{2,1,0:T(8,128)(2,1)S(1)}, bf16[16,32,1024]{2,1,0:T(8,128)(2,1)S(1)}, u32[]{:S(2)}, u32[]{:S(2)}) collective-permute-start(bf16[16,32,1024]{2,1,0:T(8,128)(2,1)S(1)} %select_convert_fusion.1), channel_id=1, source_target_pairs={{0,1},{1,0},{2,3},{3,2},{4,5},{5,4},{6,7},{7,6},{8,9},{9,8},{10,11... | collective-permute-start | bytes 3145736 | tf_op jit(solution)/shard_map/ppermute | solution.py:20
  153.1 5.9 %copy-start.2 = (bf16[1,1024,352]{1,2,0:T(8,128)(2,1)S(1)}, bf16[1,1024,352]{1,2,0:T(8,128)(2,1)}, u32[]{:S(2)}) copy-start(bf16[1,1024,352]{1,2,0:T(8,128)(2,1)} %all_gather.9) | copy-start | bytes 2162692
  153.1 57.4 %all-to-all-start.2 = ((f32[16,32,1024]{2,1,0:T(8,128)}), f32[16,32,1024]{2,1,0:T(8,128)S(1)}, u32[]{:S(2)}, u32[]{:S(2)}) async-start(f32[16,32,1024]{2,1,0:T(8,128)} %convert_add_fusion.1), calls=%async_computation.2 | async-start | bytes 4194304 | tf_op jit(solution)/shard_map/all_to_all | solution.py:161
  158.9 106.5 %reduce-scatter.8.cloned.1.call-start = ((), (), s32[]{:S(2)}) async-start(), calls=%async_computation.10 | async-start | bytes 1081344 | tf_op jit(solution)/shard_map/reduce_scatter | solution.py:173
  159.0 2.5 copy-start.9
  162.8 2.1 copy-start
  162.8 4.3 %copy-start.5 = (bf16[16,64,1024]{2,1,0:T(8,128)(2,1)S(1)}, bf16[16,64,1024]{2,1,0:T(8,128)(2,1)}, u32[]{:S(2)}) copy-start(bf16[16,64,1024]{2,1,0:T(8,128)(2,1)} %copy-done.4) | copy-start | bytes 6291460
  162.8 4.3 %copy-start.8 = (bf16[1024,352]{0,1:T(8,128)(2,1)S(1)}, bf16[1024,352]{0,1:T(8,128)(2,1)}, u32[]{:S(2)}) copy-start(bf16[1024,352]{0,1:T(8,128)(2,1)} %copy-done.7) | copy-start | bytes 2162692
  165.1 40.7 %collective-permute-start.4 = (bf16[16,32,1024]{2,1,0:T(8,128)(2,1)S(1)}, bf16[16,32,1024]{2,1,0:T(8,128)(2,1)}, u32[]{:S(2)}, u32[]{:S(2)}) collective-permute-start(bf16[16,32,1024]{2,1,0:T(8,128)(2,1)S(1)} %select_convert_fusion), channel_id=1, source_target_pairs={{0,1},{1,0},{2,3},{3,2},{4,5},{5,4},{6,7},{7,6},{8,9},{9,8},{10,11... | collective-permute-start | bytes 3145736 | tf_op jit(solution)/shard_map/ppermute | solution.py:20
  210.5 6.0 %copy-start.6 = (bf16[1024,352]{0,1:T(8,128)(2,1)S(1)}, bf16[1024,352]{0,1:T(8,128)(2,1)}, u32[]{:S(2)}) copy-start(bf16[1024,352]{0,1:T(8,128)(2,1)} %get-tuple-element.6) | copy-start | bytes 2162692
  210.5 47.0 %all-to-all-start.4 = ((f32[16,32,1024]{2,1,0:T(8,128)}), f32[16,32,1024]{2,1,0:T(8,128)}, u32[]{:S(2)}, u32[]{:S(2)}) async-start(f32[16,32,1024]{2,1,0:T(8,128)} %convert_add_fusion), calls=%async_computation.4 | async-start | bytes 4194304 | tf_op jit(solution)/shard_map/all_to_all | solution.py:162
  216.4 3.8 %copy-start.10 = (bf16[1024,352]{0,1:T(8,128)(2,1)S(1)}, bf16[1024,352]{0,1:T(8,128)(2,1)}, u32[]{:S(2)}) copy-start(bf16[1024,352]{0,1:T(8,128)(2,1)} %get-tuple-element.5) | copy-start | bytes 2162692
  216.5 49.0 %reduce-scatter.4.cloned.1.call-start = ((), (), s32[]{:S(2)}) async-start(), calls=%async_computation.8 | async-start | bytes 1081344 | tf_op jit(solution)/shard_map/reduce_scatter | solution.py:167
  220.0 3.7 %copy-start.17 = (s32[256,1]{0,1:T(1,128)S(1)}, s32[256,1]{0,1:T(1,128)}, u32[]{:S(2)}) copy-start(s32[256,1]{0,1:T(1,128)} %copy-done.16) | copy-start | bytes 3076
  220.0 45.5 %reduce-scatter.6.cloned.1.call-start = ((), (), s32[]{:S(2)}) async-start(), calls=%async_computation.9 | async-start | bytes 1081344 | tf_op jit(solution)/shard_map/reduce_scatter | solution.py:170
  260.7 2.7 copy-start.12
Sparse Core Ops, SparseCore 0:
  169.1 8.3 reduce-scatter.7
  220.2 9.4 reduce-scatter.3
  232.5 9.3 reduce-scatter.5
where the time goes:
time: 277 us; the launch traced here: 272 us
  waiting for transfers between devices  151 us (55%)
  starting transfers between devices  41 us (15%)
  matrix products  19.1 us (7%)
  other arithmetic  18.9 us (7%)
  local copies, waits for them, and re-layouts  18.9 us (7%)
  between operations  16.2 us (6%)
  blocking collectives  7.45 us (3%)
    ppermute x5, waiting for transfers between devices, swapped(): lax.ppermute(shard, axis, [(i, i ^ 1 << stride) for i in range(lax.axis_s...  78.1 us
    all_to_all x1, waiting for transfers between devices, local(): lax.all_to_all(keep_grad + partner_sums[1], 'blk', split_axis=0, concat_a...  32.1 us
    all_to_all x1, waiting for transfers between devices, local(): lax.all_to_all(halved(send_cot), 'blk', split_axis=0, concat_axis=0, tile...  21.3 us
    all_to_all x1, waiting for transfers between devices, local(): lax.all_to_all(halved(send_inputs), 'blk', split_axis=0, concat_axis=0, t...  16.2 us
    ppermute x5, starting transfers between devices, swapped(): lax.ppermute(shard, axis, [(i, i ^ 1 << stride) for i in range(lax.axis_s...  8.63 us
    all_to_all x1, starting transfers between devices, local(): lax.all_to_all(halved(send_cot), 'blk', split_axis=0, concat_axis=0, tile...  8.31 us
    all_to_all x1, starting transfers between devices, local(): lax.all_to_all(halved(send_ids), 'blk', split_axis=0, concat_axis=0, tile...  6.13 us
    all_to_all x1, starting transfers between devices, local(): lax.all_to_all(keep_grad + partner_sums[1], 'blk', split_axis=0, concat_a...  5.91 us
  transfers between devices with their start and end apart: 13, of which 7 were waited for; matrix products, arithmetic and copies ran while one was open for 12% of the time, Pallas kernels for 0%

commit v1 on v0

v1 whole, which is shorter than its diff:
```python
import jax
import jax.numpy as jnp
from jax import lax
from jax.sharding import PartitionSpec as P

mixing_factor = 73244475
contract_last = (((1,), (1,)), ((), ()))
contract_first = (((0,), (0,)), ((), ()))


def scramble(values):
    values = values ^ values >> 16 & 65535
    values = values * mixing_factor
    values = values ^ values >> 16 & 65535
    values = values * mixing_factor
    return values ^ values >> 16 & 65535


def keep_scale(token_ids, columns, key_pair):
    base_hash = scramble(key_pair[0] ^ scramble(key_pair[1]))
    mixed_ids = scramble(token_ids ^ base_hash)
    hashed = scramble(mixed_ids[:, None] ^ columns[None, :] * 40503)
    return jnp.where(hashed & 1023 >= 128, jnp.float32(8.0 / 7.0), jnp.float32(0.0))


def flipped(values, axis, mask):
    return lax.ppermute(values, axis, [(i, i ^ mask) for i in range(lax.axis_size(axis))])


def local(tokens, cotangent, routes, gate_codes, dropout_key, w_gate, w_up, w_down):
    seq_count = lax.axis_size("seq")
    block_count = lax.axis_size("blk")
    seq_index = lax.axis_index("seq")
    blk_index = lax.axis_index("blk")
    tok_rows, model_width = tokens.shape
    top_count = routes.shape[1]
    expert_count = block_count // 2
    capacity = 2 * tok_rows * top_count // expert_count
    half_width = w_gate.shape[2]
    part_width = w_gate.shape[1]
    planes = 1 << (block_count.bit_length() // 2)
    plane_experts = expert_count // planes
    plane_stride = 2 * plane_experts
    parity = blk_index % 2
    expert_here = blk_index // 2

    table = jnp.concatenate([routes.T, gate_codes.T], axis=0)
    tables = lax.all_gather(table, "blk")

    own_weights = jnp.stack([w_gate[0].T, w_up[0].T, w_down[0]])
    pair_weights = flipped(own_weights, "blk", 1)

    def spread(part):
        chunks = {0: part}
        step = planes // 2
        while step:
            for place in sorted(chunks):
                chunks[place ^ step] = flipped(chunks[place], "blk", step * plane_stride)
            step //= 2
        return [chunks[place] for place in range(planes)]

    token_chunks = spread(tokens)
    cot_chunks = spread(cotangent)

    def table_of(column, place):
        source = blk_index ^ (place * plane_stride + column * 2)
        return lax.dynamic_index_in_dim(tables, source, 0, keepdims=False), source

    earlier = (
        jnp.arange(tok_rows)[:, None] < jnp.arange(tok_rows)[None, :]
    ).astype(jnp.bfloat16)

    def placed(table_rows, expert):
        hits = [table_rows[:, k] == expert for k in range(top_count)]
        named = hits[0]
        for hit in hits[1:]:
            named = named | hit
        rank = jnp.dot(
            named.astype(jnp.bfloat16), earlier, preferred_element_type=jnp.float32
        ).astype(jnp.int32)
        slots = jnp.arange(capacity, dtype=jnp.int32)
        chosen = named[:, None, :] & (rank[:, None, :] == slots[None, :, None])
        gates = jnp.zeros(table_rows[:, 0].shape, jnp.float32)
        for k in range(top_count):
            gates = gates + jnp.where(hits[k], table_rows[:, top_count + k], 0).astype(jnp.float32)
        return chosen, gates / 64.0

    column_tables = []
    column_sources = []
    for column in range(plane_experts):
        picked = [table_of(column, place) for place in range(planes)]
        column_tables.append(jnp.stack([entry[0] for entry in picked]))
        column_sources.append(jnp.stack([entry[1] for entry in picked]))

    select = []
    weigh = []
    for column in range(plane_experts):
        chosen, gates = placed(column_tables[0], expert_here ^ column)
        select.append(chosen.astype(jnp.bfloat16))
        weigh.append(jnp.where(chosen, gates[:, None, :], 0.0).astype(jnp.bfloat16))

    token_ids = []
    for column in range(plane_experts):
        chosen, _ = placed(column_tables[column], expert_here)
        within = jnp.sum(
            jnp.where(chosen, jnp.arange(tok_rows, dtype=jnp.int32)[None, None, :], 0), axis=2
        )
        first = (seq_index * block_count + column_sources[column]) * tok_rows
        token_ids.append((within + first[:, None]).reshape(-1))
    token_ids = jnp.concatenate(token_ids)

    def compact(choice, chunks):
        return jnp.concatenate(
            [
                jnp.dot(choice[place], chunks[place], preferred_element_type=jnp.float32).astype(
                    jnp.bfloat16
                )
                for place in range(planes)
            ]
        )

    def gathered(choices, chunks):
        sent = [
            flipped(compact(choices[column], chunks), "blk", 2 * column)
            for column in range(1, plane_experts)
        ]
        return jnp.concatenate([compact(choices[0], chunks)] + sent)

    rows_in = gathered(select, token_chunks)
    rows_cot = gathered(weigh, cot_chunks)

    weights = lax.all_gather(
        jnp.stack([own_weights, pair_weights], axis=1), "seq", axis=3, tiled=True
    ).reshape(3, 2 * half_width, model_width)
    gate_mat, up_mat, down_mat = weights[0], weights[1], weights[2]

    unit = jnp.arange(half_width, dtype=jnp.int32)
    columns = expert_here * (2 * half_width) + jnp.concatenate(
        [parity * half_width + unit, (1 - parity) * half_width + unit]
    )
    drop_scale = keep_scale(token_ids, columns, dropout_key)
    gate_pre = lax.dot_general(rows_in, gate_mat, contract_last, preferred_element_type=jnp.float32)
    up_pre = lax.dot_general(rows_in, up_mat, contract_last, preferred_element_type=jnp.float32)
    sigmoid_gate = jax.nn.sigmoid(gate_pre)
    silu_gate = gate_pre * sigmoid_gate
    hidden = (silu_gate * up_pre * drop_scale).astype(jnp.bfloat16)
    expert_out = jnp.dot(hidden, down_mat, preferred_element_type=jnp.float32)
    hidden_grad = (
        lax.dot_general(rows_cot, down_mat, contract_last, preferred_element_type=jnp.float32)
        * drop_scale
    )
    gate_pre_grad = (
        hidden_grad * up_pre * sigmoid_gate * (1.0 + gate_pre * (1.0 - sigmoid_gate))
    ).astype(jnp.bfloat16)
    up_pre_grad = (hidden_grad * silu_gate).astype(jnp.bfloat16)
    input_grad = jnp.dot(gate_pre_grad, gate_mat, preferred_element_type=jnp.float32) + jnp.dot(
        up_pre_grad, up_mat, preferred_element_type=jnp.float32
    )

    def brought_back(slot_rows, choices):
        slot_rows = slot_rows.astype(jnp.bfloat16).reshape(
            plane_experts, planes, capacity, model_width
        )
        blocks = [slot_rows[0]] + [
            flipped(slot_rows[column], "blk", 2 * column) for column in range(1, plane_experts)
        ]
        sums = {}
        for place in range(planes):
            choice = jnp.concatenate([choices[column][place] for column in range(plane_experts)])
            block = jnp.concatenate([blocks[column][place] for column in range(plane_experts)])
            sums[place] = lax.dot_general(
                choice, block, contract_first, preferred_element_type=jnp.float32
            )
        step = 1
        while step < planes:
            for place in sorted(sums, reverse=True):
                if place & step:
                    sums[place ^ step] = sums[place ^ step] + flipped(
                        sums[place].astype(jnp.bfloat16), "blk", step * plane_stride
                    ).astype(jnp.float32)
                    del sums[place]
            step *= 2
        return sums[0].astype(jnp.bfloat16)

    layer_out = brought_back(expert_out, weigh)
    tokens_grad = brought_back(input_grad, select)

    def part_sums(target):
        width = part_width
        inputs_part = lax.dynamic_slice_in_dim(rows_in, target * width, width, 1)
        cot_part = lax.dynamic_slice_in_dim(rows_cot, target * width, width, 1)
        return jnp.stack(
            [
                lax.dot_general(left, right, contract_first, preferred_element_type=jnp.float32)
                for left, right in (
                    (gate_pre_grad, inputs_part),
                    (up_pre_grad, inputs_part),
                    (hidden, cot_part),
                )
            ]
        )

    arrived = [
        lax.ppermute(
            part_sums((seq_index + shift) % seq_count).astype(jnp.bfloat16),
            "seq",
            [(i, (i + shift) % seq_count) for i in range(seq_count)],
        ).astype(jnp.float32)
        for shift in range(1, seq_count)
    ]
    totals = part_sums(seq_index)
    for part in arrived:
        totals = totals + part
    totals = totals.reshape(3, 2, half_width, part_width)
    grads = totals[:, 0] + flipped(totals[:, 1].astype(jnp.bfloat16), "blk", 1).astype(jnp.float32)
    grads = grads.astype(jnp.bfloat16)
    return (layer_out, tokens_grad, grads[0].T[None], grads[1].T[None], grads[2][None])


def solution(mesh):
    placed = (
        P(("seq", "blk"), None),
        P(("seq", "blk"), None),
        P(("seq", "blk"), None),
        P(("seq", "blk"), None),
        P(),
        P("blk", "seq", None),
        P("blk", "seq", None),
        P("blk", None, "seq"),
    )
    return jax.shard_map(
        local,
        mesh=mesh,
        in_specs=placed,
        out_specs=(
            P(("seq", "blk"), None),
            P(("seq", "blk"), None),
            P("blk", "seq", None),
            P("blk", "seq", None),
            P("blk", None, "seq"),
        ),
        check_vma=False,
    )
```

time: 277 us -> 186 us (0.67); the launches traced: 272 us -> 186 us
  waiting for transfers between devices: 151 us -> 42.5 us
  blocking collectives: 7.45 us -> 56.4 us
  starting transfers between devices: 41 us -> 19 us
  matrix products: 19.1 us -> 32.4 us
  other arithmetic: 18.9 us -> 9.01 us
  local copies, waits for them, and re-layouts: 18.9 us -> 9.66 us
    all_to_all x5 -> x0, waiting for transfers between devices: 72.4 us -> none  [the longest x1 32.1 us: local(): lax.all_to_all(keep_grad + partner_sums[1], 'blk', split_axis=0, concat_a...]
    all_gather x3 -> x1, blocking collectives: 7.45 us -> 56.4 us  [local(): tables = lax.all_gather(table, 'blk')]
    ppermute x5 -> x19, waiting for transfers between devices: 78.1 us -> 42.5 us  [the longest x18 42.5 us: flipped(): lax.ppermute(values, axis, [(i, i ^ mask) for i in range(lax.axis_size(ax...]
    all_to_all x5 -> x0, starting transfers between devices: 32 us -> none  [the longest x1 8.31 us: local(): lax.all_to_all(halved(send_cot), 'blk', split_axis=0, concat_axis=0, tile...]
    dot_general x9 -> x39, matrix products: 19.1 us -> 32.4 us  [the longest x16 14.6 us: compact(): jnp.dot(choice[place], chunks[place], preferred_element_type=jnp.float32)]
    ppermute x5 -> x19, starting transfers between devices: 8.63 us -> 19 us  [the longest x18 18.9 us: flipped(): lax.ppermute(values, axis, [(i, i ^ mask) for i in range(lax.axis_size(ax...]
    add x3 -> x4, other arithmetic: 6.62 us -> 1.57 us  [the longest x1 0.83 us: local(): totals = totals + part]
    gather x2 -> x0, local copies, waits for them, and re-layouts: 4.23 us -> none  [the longest x1 3.16 us: local(): slot_grad[slot_index].reshape(tok_rows, top_count, model_width)]
  transfers between devices with their start and end apart: 13 -> 20, of which waited for: 7 -> 8; matrix products, arithmetic and copies ran while one was open for 12% -> 19% of each run, Pallas kernels for 0% -> 0%
where the time goes in v1:
time: 186 us
  blocking collectives  56.4 us (30%)
  waiting for transfers between devices  42.5 us (23%)
  matrix products  32.4 us (17%)
  starting transfers between devices  19 us (10%)
  between operations  16.7 us (9%)
  local copies, waits for them, and re-layouts  9.66 us (5%)
  other arithmetic  9.01 us (5%)
    all_gather x1, blocking collectives, local(): tables = lax.all_gather(table, 'blk')  56.4 us
    ppermute x18, waiting for transfers between devices, flipped(): lax.ppermute(values, axis, [(i, i ^ mask) for i in range(lax.axis_size(ax...  42.5 us
    ppermute x18, starting transfers between devices, flipped(): lax.ppermute(values, axis, [(i, i ^ mask) for i in range(lax.axis_size(ax...  18.9 us
    dot_general x16, matrix products, compact(): jnp.dot(choice[place], chunks[place], preferred_element_type=jnp.float32)  14.6 us
    dot_general x6, matrix products, part_sums(): lax.dot_general(left, right, contract_first, preferred_element_type=jnp.f...  5.37 us
    another operation x2, other arithmetic, local(): jnp.stack([own_weights, pair_weights], axis=1)  4.23 us
  transfers between devices with their start and end apart: 20, of which 8 were waited for; matrix products, arithmetic and copies ran while one was open for 19% of the time, Pallas kernels for 0%

profile of v1, /device:TPU:0, one launch (start us, length us, event | category | flops | bytes accessed | tf_op | source)
XLA Modules:
  0.0 185.7 jit_solution(2713325057993981442)
XLA Ops:
  7.2 3.1 %collective-permute-start = (bf16[128,1024]{1,0:T(8,128)(2,1)}, bf16[128,1024]{1,0:T(8,128)(2,1)}, u32[]{:S(2)}, u32[]{:S(2)}) collective-permute-start(bf16[128,1024]{1,0:T(8,128)(2,1)} %param.8), channel_id=1, source_target_pairs={{0,4},{1,5},{2,6},{3,7},{4,0},{5,1},{6,2},{7,3},{8,12},{9,13},{10,... | collective-permute-start | bytes 786440 | tf_op jit(solution)/shard_map/ppermute | solution.py:27
  10.3 2.6 %collective-permute-start.1 = (bf16[128,1024]{1,0:T(8,128)(2,1)}, bf16[128,1024]{1,0:T(8,128)(2,1)}, u32[]{:S(2)}, u32[]{:S(2)}) collective-permute-start(bf16[128,1024]{1,0:T(8,128)(2,1)} %param.8), channel_id=1, source_target_pairs={{0,8},{1,9},{2,10},{3,11},{4,12},{5,13},{6,14},{7,15},{8,0},{9,1},... | collective-permute-start | bytes 786440 | tf_op jit(solution)/shard_map/ppermute | solution.py:27
  12.9 0.4 collective-permute-start.9
  13.4 1.4 fusion.112
  14.8 1.9 %collective-permute-start.4 = (bf16[3,352,512]{2,1,0:T(8,128)(2,1)S(1)}, bf16[3,352,512]{2,1,0:T(8,128)(2,1)}, u32[]{:S(2)}, u32[]{:S(2)}) collective-permute-start(bf16[3,352,512]{2,1,0:T(8,128)(2,1)S(1)} %get-tuple-element.15), channel_id=1, source_target_pairs={{0,1},{1,0},{2,3},{3,2},{4,5},{5,4},{6,7},{7,6},{8,9},{9,8},{10,11... | collective-permute-start | bytes 3244040 | tf_op jit(solution)/shard_map/ppermute | solution.py:27
  16.7 56.4 %all-gather.1 = s32[16,4,128]{2,1,0:T(4,128)S(1)} all-gather(s32[1,4,128]{2,1,0:T(4,128)S(1)} %add_bitcast_fusion), channel_id=2, replica_groups=mesh['seq'=2,'blk'=16] {'blk'}, dimensions={0}, use_global_device_ids=true | all-gather | bytes 34816 | tf_op jit(solution)/shard_map/all_gather | solution.py:48
  73.5 0.7 fusion.110
  74.5 0.6 slice_bitcast_fusion.40
  75.2 0.6 slice_bitcast_fusion.41
  75.8 0.6 slice_bitcast_fusion.32
  76.4 0.7 fusion.100
  77.1 0.7 broadcast_add_fusion
  77.7 0.6 fusion.117
  78.4 0.7 select_reduce_fusion.1
  79.2 0.6 slice_bitcast_fusion.33
  80.0 1.6 convolution_convert_fusion.19
  81.6 2.8 %pad_maximum_fusion = bf16[3,2,352,512]{3,2,0,1:T(8,128)(2,1)} fusion(bf16[3,1,352,512]{3,2,0,1:T(8,128)(2,1)} %bitcast.22, bf16[3,1,352,512]{3,2,0,1:T(8,128)(2,1)S(1)} %get-tuple-element.14), kind=kLoop, calls=%fused_computation.5 | loop fusion | flops 1081344 | bytes 4325376 | tf_op jit(solution)/shard_map/stack | solution.py:133
  84.5 0.6 copy-done.24
  85.4 0.8 fusion.22
  88.7 1.2 convolution_convert_fusion.17
  89.9 1.1 convolution_convert_fusion.18
  91.0 1.2 fusion.25
  92.3 2.0 %collective-permute-start.11 = (bf16[128,1024]{1,0:T(8,128)(2,1)}, bf16[128,1024]{1,0:T(8,128)(2,1)S(1)}, u32[]{:S(2)}, u32[]{:S(2)}) collective-permute-start(bf16[128,1024]{1,0:T(8,128)(2,1)} %collective-permute-done.10), channel_id=1, source_target_pairs={{0,4},{1,5},{2,6},{3,7},{4,0},{5,1},{6,2},{7,3},{8,12},{9,13},{10,... | collective-permute-start | bytes 786440 | tf_op jit(solution)/shard_map/ppermute | solution.py:27
  94.3 1.2 convolution_convert_fusion.9
  95.5 1.1 convolution_convert_fusion.10
  96.6 1.8 fusion.21
  98.4 1.1 fusion.24
  99.5 1.8 fusion.20
  101.8 2.1 %collective-permute-start.12 = (bf16[256,1024]{1,0:T(8,128)(2,1)S(1)}, bf16[256,1024]{1,0:T(8,128)(2,1)S(1)}, u32[]{:S(2)}, u32[]{:S(2)}) collective-permute-start(bf16[256,1024]{1,0:T(8,128)(2,1)S(1)} %pad_maximum_fusion.4), channel_id=1, source_target_pairs={{0,2},{1,3},{2,0},{3,1},{4,6},{5,7},{6,4},{7,5},{8,10},{9,11},{10,... | collective-permute-start | bytes 1572872 | tf_op jit(solution)/shard_map/ppermute | solution.py:27
  104.1 0.8 fusion.19
  104.9 7.3 %collective-permute-done.3 = bf16[256,1024]{1,0:T(8,128)(2,1)S(1)} collective-permute-done((bf16[256,1024]{1,0:T(8,128)(2,1)S(1)}, bf16[256,1024]{1,0:T(8,128)(2,1)S(1)}, u32[]{:S(2)}, u32[]{:S(2)}) %collective-permute-start.3) | collective-permute-done | bytes 524320 | tf_op jit(solution)/shard_map/ppermute | solution.py:27
  112.2 5.6 %collective-permute-done.12 = bf16[256,1024]{1,0:T(8,128)(2,1)S(1)} collective-permute-done((bf16[256,1024]{1,0:T(8,128)(2,1)S(1)}, bf16[256,1024]{1,0:T(8,128)(2,1)S(1)}, u32[]{:S(2)}, u32[]{:S(2)}) %collective-permute-start.12) | collective-permute-done | bytes 524320 | tf_op jit(solution)/shard_map/ppermute | solution.py:27
  117.8 0.9 constant_dynamic-update-slice_fusion.1
  118.7 2.7 %fusion.113 = (bf16[1,2,352,1024]{3,2,0,1:T(8,128)(2,1)S(1)}, bf16[1,2,352,1024]{3,2,0,1:T(8,128)(2,1)S(1)}, bf16[1,2,352,1024]{3,2,0,1:T(8,128)(2,1)S(1)}) fusion(bf16[3,2,352,1024]{3,2,0,1:T(8,128)(2,1)} %all-gather.4.cloned.1.call-done), kind=kLoop, calls=%fused_computation.240 | loop fusion | bytes 8650752 | tf_op jit(solution)/shard_map/slice | solution.py:135
  121.4 1.0 fusion.118
  122.4 0.9 fusion.119
  123.3 3.7 %multiply_convert_fusion = (bf16[512,704]{0,1:T(8,128)(2,1)S(1)}, bf16[512,704]{0,1:T(8,128)(2,1)S(1)}, bf16[512,704]{0,1:T(8,128)(2,1)S(1)}) fusion(f32[512,704]{0,1:T(8,128)S(1)} %fusion.118, f32[512,704]{0,1:T(8,128)S(1)} %fusion.119, s32[704]{0:T(1024)S(1)} %fusion.85, s32[512]{0:T(512)S(1)} %and_xor_fusion, ...), kind=kOutput, calls=%fused_computation.23 | convolution fusion | flops 749731840 | bytes 7541504 | tf_op jit(solution)/shard_map/dot_general | solution.py:149
  127.0 1.0 convolution_convert_fusion
  128.0 1.0 fusion.120
  129.0 1.6 fusion.12
  130.6 0.6 fusion.10
  131.2 0.3 collective-permute-start.5
  131.5 0.5 fusion.11
  132.4 1.0 add_convert_fusion
  133.5 1.8 collective-permute-start.13
  135.3 1.6 convolution_bitcast_fusion
  136.9 0.6 convolution_bitcast_fusion.1
  137.5 0.6 convolution_bitcast_fusion.2
  138.1 6.1 %collective-permute-done.5 = bf16[4,64,1024]{2,1,0:T(8,128)(2,1)S(1)} collective-permute-done((bf16[4,64,1024]{2,1,0:T(8,128)(2,1)S(1)}, bf16[4,64,1024]{2,1,0:T(8,128)(2,1)S(1)}, u32[]{:S(2)}, u32[]{:S(2)}) %collective-permute-start.5) | collective-permute-done | bytes 524320 | tf_op jit(solution)/shard_map/ppermute | solution.py:27
  144.5 0.4 collective-permute-start.7
  145.1 1.8 collective-permute-start.6
  146.9 4.8 %collective-permute-done.13 = bf16[4,64,1024]{2,1,0:T(8,128)(2,1)S(1)} collective-permute-done((bf16[4,64,1024]{2,1,0:T(8,128)(2,1)S(1)}, bf16[4,64,1024]{2,1,0:T(8,128)(2,1)S(1)}, u32[]{:S(2)}, u32[]{:S(2)}) %collective-permute-start.13) | collective-permute-done | bytes 524320 | tf_op jit(solution)/shard_map/ppermute | solution.py:27
  152.0 0.4 collective-permute-start.15
  152.4 0.8 maximum_add_fusion
  153.5 0.4 copy-done.12
  154.5 1.8 collective-permute-start.14
  156.3 10.1 %collective-permute-done.15 = bf16[128,1024]{1,0:T(8,128)(2,1)S(1)} collective-permute-done((bf16[128,1024]{1,0:T(8,128)(2,1)S(1)}, bf16[128,1024]{1,0:T(8,128)(2,1)S(1)}, u32[]{:S(2)}, u32[]{:S(2)}) %collective-permute-start.15) | collective-permute-done | bytes 262176 | tf_op jit(solution)/shard_map/ppermute | solution.py:27
  166.8 2.8 %collective-permute-done.8 = bf16[128,1024]{1,0:T(8,128)(2,1)S(1)} collective-permute-done((bf16[128,1024]{1,0:T(8,128)(2,1)S(1)}, bf16[128,1024]{1,0:T(8,128)(2,1)S(1)}, u32[]{:S(2)}, u32[]{:S(2)}) %collective-permute-start.8) | collective-permute-done | bytes 262176 | tf_op jit(solution)/shard_map/ppermute | solution.py:27
  169.6 1.0 fusion.16
  170.6 1.8 collective-permute-done.14
  172.4 4.0 %collective-permute-done.16 = bf16[128,1024]{1,0:T(8,128)(2,1)S(1)} collective-permute-done((bf16[128,1024]{1,0:T(8,128)(2,1)S(1)}, bf16[128,1024]{1,0:T(8,128)(2,1)S(1)}, u32[]{:S(2)}, u32[]{:S(2)}) %collective-permute-start.16) | collective-permute-done | bytes 262176 | tf_op jit(solution)/shard_map/ppermute | solution.py:27
  176.4 1.0 fusion.15
  177.4 0.4 fusion.1
  177.9 1.0 fusion.114
  (120 shorter events, 5.0 us)
Async XLA Ops:
  7.2 111.5 %all-gather.4.cloned.1.call-start = ((), (), s32[]{:S(2)}) async-start(), calls=%async_computation | async-start | bytes 6488064 | tf_op jit(solution)/shard_map/all_gather | solution.py:132
  7.2 82.6 %collective-permute-start = (bf16[128,1024]{1,0:T(8,128)(2,1)}, bf16[128,1024]{1,0:T(8,128)(2,1)}, u32[]{:S(2)}, u32[]{:S(2)}) collective-permute-start(bf16[128,1024]{1,0:T(8,128)(2,1)} %param.8), channel_id=1, source_target_pairs={{0,4},{1,5},{2,6},{3,7},{4,0},{5,1},{6,2},{7,3},{8,12},{9,13},{10,... | collective-permute-start | bytes 786440 | tf_op jit(solution)/shard_map/ppermute | solution.py:27
  10.3 78.3 %collective-permute-start.1 = (bf16[128,1024]{1,0:T(8,128)(2,1)}, bf16[128,1024]{1,0:T(8,128)(2,1)}, u32[]{:S(2)}, u32[]{:S(2)}) collective-permute-start(bf16[128,1024]{1,0:T(8,128)(2,1)} %param.8), channel_id=1, source_target_pairs={{0,8},{1,9},{2,10},{3,11},{4,12},{5,13},{6,14},{7,15},{8,0},{9,1},... | collective-permute-start | bytes 786440 | tf_op jit(solution)/shard_map/ppermute | solution.py:27
  12.9 82.6 %collective-permute-start.9 = (bf16[128,1024]{1,0:T(8,128)(2,1)}, bf16[128,1024]{1,0:T(8,128)(2,1)}, u32[]{:S(2)}, u32[]{:S(2)}) collective-permute-start(bf16[128,1024]{1,0:T(8,128)(2,1)} %param.9), channel_id=1, source_target_pairs={{0,4},{1,5},{2,6},{3,7},{4,0},{5,1},{6,2},{7,3},{8,12},{9,13},{10,... | collective-permute-start | bytes 786440 | tf_op jit(solution)/shard_map/ppermute | solution.py:27
  13.3 79.0 %collective-permute-start.10 = (bf16[128,1024]{1,0:T(8,128)(2,1)}, bf16[128,1024]{1,0:T(8,128)(2,1)}, u32[]{:S(2)}, u32[]{:S(2)}) collective-permute-start(bf16[128,1024]{1,0:T(8,128)(2,1)} %param.9), channel_id=1, source_target_pairs={{0,8},{1,9},{2,10},{3,11},{4,12},{5,13},{6,14},{7,15},{8,0},{9,1},... | collective-permute-start | bytes 786440 | tf_op jit(solution)/shard_map/ppermute | solution.py:27
  13.3 3.3 %copy-start.27 = (s32[128,2]{0,1:T(2,128)S(1)}, s32[128,2]{0,1:T(2,128)}, u32[]{:S(2)}) copy-start(s32[128,2]{0,1:T(2,128)} %param.11) | copy-start | bytes 3076
  13.3 3.3 %copy-start.28 = (s32[128,2]{0,1:T(2,128)S(1)}, s32[128,2]{0,1:T(2,128)}, u32[]{:S(2)}) copy-start(s32[128,2]{0,1:T(2,128)} %param.10) | copy-start | bytes 3076
  13.3 64.4 %copy-start.25 = (s32[2]{0:T(128)S(1)}, s32[2]{0:T(128)}, u32[]{:S(2)}) copy-start(s32[2]{0:T(128)} %param.12) | copy-start | bytes 28
  13.4 66.5 %copy-start = (bf16[128,1024]{1,0:T(8,128)(2,1)S(1)}, bf16[128,1024]{1,0:T(8,128)(2,1)}, u32[]{:S(2)}) copy-start(bf16[128,1024]{1,0:T(8,128)(2,1)} %param.8) | copy-start | bytes 786436
  14.8 66.8 %collective-permute-start.4 = (bf16[3,352,512]{2,1,0:T(8,128)(2,1)S(1)}, bf16[3,352,512]{2,1,0:T(8,128)(2,1)}, u32[]{:S(2)}, u32[]{:S(2)}) collective-permute-start(bf16[3,352,512]{2,1,0:T(8,128)(2,1)S(1)} %get-tuple-element.15), channel_id=1, source_target_pairs={{0,1},{1,0},{2,3},{3,2},{4,5},{5,4},{6,7},{7,6},{8,9},{9,8},{10,11... | collective-permute-start | bytes 3244040 | tf_op jit(solution)/shard_map/ppermute | solution.py:27
  74.5 5.3 %copy-start.2 = (bf16[4,64,128]{2,1,0:T(8,128)(2,1)}, bf16[4,64,128]{2,1,0:T(8,128)(2,1)S(1)}, u32[]{:S(2)}) copy-start(bf16[4,64,128]{2,1,0:T(8,128)(2,1)S(1)} %select_convert_fusion) | copy-start | bytes 196612
  79.2 2.4 %copy-start.6 = (pred[4,64,128]{2,1,0:T(32,128)(4,1)}, pred[4,64,128]{2,1,0:T(32,128)(4,1)S(1)}, u32[]{:S(2)}) copy-start(pred[4,64,128]{2,1,0:T(32,128)(4,1)S(1)} %get-tuple-element.61) | copy-start | bytes 98308
  84.4 0.7 copy-start.24
  84.4 0.7 copy-start.26
  84.4 1.0 copy-start.1
  84.4 1.8 copy-start.3
  84.4 2.0 %copy-start.23 = (s32[4,64]{1,0:T(4,128)S(1)}, s32[4,64]{1,0:T(4,128)}, u32[]{:S(2)}) copy-start(s32[4,64]{1,0:T(4,128)} %broadcast_add_fusion) | copy-start | bytes 3076
  84.4 4.2 %copy-start.5 = (pred[4,64,128]{2,1,0:T(32,128)(4,1)S(1)}, pred[4,64,128]{2,1,0:T(32,128)(4,1)}, u32[]{:S(2)}) copy-start(pred[4,64,128]{2,1,0:T(32,128)(4,1)} %get-tuple-element.63) | copy-start | bytes 98308
  84.4 6.6 %copy-start.7 = (pred[4,64,128]{2,1,0:T(32,128)(4,1)S(1)}, pred[4,64,128]{2,1,0:T(32,128)(4,1)}, u32[]{:S(2)}) copy-start(pred[4,64,128]{2,1,0:T(32,128)(4,1)} %copy-done.6) | copy-start | bytes 98308
  88.6 12.7 %collective-permute-start.2 = (bf16[128,1024]{1,0:T(8,128)(2,1)}, bf16[128,1024]{1,0:T(8,128)(2,1)S(1)}, u32[]{:S(2)}, u32[]{:S(2)}) collective-permute-start(bf16[128,1024]{1,0:T(8,128)(2,1)} %collective-permute-done.1), channel_id=1, source_target_pairs={{0,4},{1,5},{2,6},{3,7},{4,0},{5,1},{6,2},{7,3},{8,12},{9,13},{10,... | collective-permute-start | bytes 786440 | tf_op jit(solution)/shard_map/ppermute | solution.py:27
  91.0 10.4 %copy-start.4 = (bf16[64,1024]{1,0:T(8,128)(2,1)S(1)}, bf16[64,1024]{1,0:T(8,128)(2,1)}, u32[]{:S(2)}) copy-start(bf16[64,1024]{1,0:T(8,128)(2,1)} %convolution_convert_fusion.19) | copy-start | bytes 393220
  92.3 9.3 %collective-permute-start.11 = (bf16[128,1024]{1,0:T(8,128)(2,1)}, bf16[128,1024]{1,0:T(8,128)(2,1)S(1)}, u32[]{:S(2)}, u32[]{:S(2)}) collective-permute-start(bf16[128,1024]{1,0:T(8,128)(2,1)} %collective-permute-done.10), channel_id=1, source_target_pairs={{0,4},{1,5},{2,6},{3,7},{4,0},{5,1},{6,2},{7,3},{8,12},{9,13},{10,... | collective-permute-start | bytes 786440 | tf_op jit(solution)/shard_map/ppermute | solution.py:27
  101.5 10.7 %collective-permute-start.3 = (bf16[256,1024]{1,0:T(8,128)(2,1)S(1)}, bf16[256,1024]{1,0:T(8,128)(2,1)S(1)}, u32[]{:S(2)}, u32[]{:S(2)}) collective-permute-start(bf16[256,1024]{1,0:T(8,128)(2,1)S(1)} %pad_maximum_fusion.3), channel_id=1, source_target_pairs={{0,2},{1,3},{2,0},{3,1},{4,6},{5,7},{6,4},{7,5},{8,10},{9,11},{10,... | collective-permute-start | bytes 1572872 | tf_op jit(solution)/shard_map/ppermute | solution.py:27
  101.8 16.0 %collective-permute-start.12 = (bf16[256,1024]{1,0:T(8,128)(2,1)S(1)}, bf16[256,1024]{1,0:T(8,128)(2,1)S(1)}, u32[]{:S(2)}, u32[]{:S(2)}) collective-permute-start(bf16[256,1024]{1,0:T(8,128)(2,1)S(1)} %pad_maximum_fusion.4), channel_id=1, source_target_pairs={{0,2},{1,3},{2,0},{3,1},{4,6},{5,7},{6,4},{7,5},{8,10},{9,11},{10,... | collective-permute-start | bytes 1572872 | tf_op jit(solution)/shard_map/ppermute | solution.py:27
  131.2 13.0 %collective-permute-start.5 = (bf16[4,64,1024]{2,1,0:T(8,128)(2,1)S(1)}, bf16[4,64,1024]{2,1,0:T(8,128)(2,1)S(1)}, u32[]{:S(2)}, u32[]{:S(2)}) collective-permute-start(bf16[4,64,1024]{2,1,0:T(8,128)(2,1)S(1)} %bitcast.200), channel_id=1, source_target_pairs={{0,2},{1,3},{2,0},{3,1},{4,6},{5,7},{6,4},{7,5},{8,10},{9,11},{10,... | collective-permute-start | bytes 1572872 | tf_op jit(solution)/shard_map/ppermute | solution.py:27
  132.3 20.0 %collective-permute-start.17 = (bf16[3,704,512]{2,1,0:T(8,128)(2,1)S(1)}, bf16[3,704,512]{2,1,0:T(8,128)(2,1)S(1)}, u32[]{:S(2)}, u32[]{:S(2)}) collective-permute-start(bf16[3,704,512]{2,1,0:T(8,128)(2,1)S(1)} %pad_maximum_fusion.1), channel_id=1, source_target_pairs={{0,16},{16,0},{1,17},{17,1},{2,18},{18,2},{3,19},{19,3},{4,20},{20... | collective-permute-start | bytes 6488072 | tf_op jit(solution)/shard_map/ppermute | solution.py:204
  133.5 18.2 %collective-permute-start.13 = (bf16[4,64,1024]{2,1,0:T(8,128)(2,1)S(1)}, bf16[4,64,1024]{2,1,0:T(8,128)(2,1)S(1)}, u32[]{:S(2)}, u32[]{:S(2)}) collective-permute-start(bf16[4,64,1024]{2,1,0:T(8,128)(2,1)S(1)} %bitcast.199), channel_id=1, source_target_pairs={{0,2},{1,3},{2,0},{3,1},{4,6},{5,7},{6,4},{7,5},{8,10},{9,11},{10,... | collective-permute-start | bytes 1572872 | tf_op jit(solution)/shard_map/ppermute | solution.py:27
  137.5 6.7 %copy-start.20 = (bf16[64,128]{1,0:T(8,128)(2,1)S(1)}, bf16[64,128]{1,0:T(8,128)(2,1)}, u32[]{:S(2)}) copy-start(bf16[64,128]{1,0:T(8,128)(2,1)} %get-tuple-element.45) | copy-start | bytes 49156
  137.5 6.7 %copy-start.21 = (bf16[64,128]{1,0:T(8,128)(2,1)S(1)}, bf16[64,128]{1,0:T(8,128)(2,1)}, u32[]{:S(2)}) copy-start(bf16[64,128]{1,0:T(8,128)(2,1)} %get-tuple-element.41) | copy-start | bytes 49156
  138.1 6.8 %copy-start.17 = (bf16[64,128]{1,0:T(8,128)(2,1)S(1)}, bf16[64,128]{1,0:T(8,128)(2,1)}, u32[]{:S(2)}) copy-start(bf16[64,128]{1,0:T(8,128)(2,1)} %get-tuple-element.47) | copy-start | bytes 49156
  138.1 6.8 %copy-start.19 = (bf16[64,128]{1,0:T(8,128)(2,1)S(1)}, bf16[64,128]{1,0:T(8,128)(2,1)}, u32[]{:S(2)}) copy-start(bf16[64,128]{1,0:T(8,128)(2,1)} %get-tuple-element.43) | copy-start | bytes 49156
  138.1 13.6 %copy-start.16 = (bf16[64,128]{1,0:T(8,128)(2,1)S(1)}, bf16[64,128]{1,0:T(8,128)(2,1)}, u32[]{:S(2)}) copy-start(bf16[64,128]{1,0:T(8,128)(2,1)} %get-tuple-element.37) | copy-start | bytes 49156
  138.1 13.6 %copy-start.22 = (bf16[64,128]{1,0:T(8,128)(2,1)S(1)}, bf16[64,128]{1,0:T(8,128)(2,1)}, u32[]{:S(2)}) copy-start(bf16[64,128]{1,0:T(8,128)(2,1)} %get-tuple-element.33) | copy-start | bytes 49156
  144.5 9.0 %collective-permute-start.7 = (bf16[128,1024]{1,0:T(8,128)(2,1)S(1)}, bf16[128,1024]{1,0:T(8,128)(2,1)S(1)}, u32[]{:S(2)}, u32[]{:S(2)}) collective-permute-start(bf16[128,1024]{1,0:T(8,128)(2,1)S(1)} %convolution_convert_fusion.6), channel_id=1, source_target_pairs={{0,4},{1,5},{2,6},{3,7},{4,0},{5,1},{6,2},{7,3},{8,12},{9,13},{10,... | collective-permute-start | bytes 786440 | tf_op jit(solution)/shard_map/ppermute | solution.py:27
  145.1 21.6 %collective-permute-start.6 = (bf16[128,1024]{1,0:T(8,128)(2,1)S(1)}, bf16[128,1024]{1,0:T(8,128)(2,1)S(1)}, u32[]{:S(2)}, u32[]{:S(2)}) collective-permute-start(bf16[128,1024]{1,0:T(8,128)(2,1)S(1)} %convolution_convert_fusion.7), channel_id=1, source_target_pairs={{0,4},{1,5},{2,6},{3,7},{4,0},{5,1},{6,2},{7,3},{8,12},{9,13},{10,... | collective-permute-start | bytes 786440 | tf_op jit(solution)/shard_map/ppermute | solution.py:27
  152.0 14.4 %collective-permute-start.15 = (bf16[128,1024]{1,0:T(8,128)(2,1)S(1)}, bf16[128,1024]{1,0:T(8,128)(2,1)S(1)}, u32[]{:S(2)}, u32[]{:S(2)}) collective-permute-start(bf16[128,1024]{1,0:T(8,128)(2,1)S(1)} %convolution_convert_fusion.4), channel_id=1, source_target_pairs={{0,4},{1,5},{2,6},{3,7},{4,0},{5,1},{6,2},{7,3},{8,12},{9,13},{10,... | collective-permute-start | bytes 786440 | tf_op jit(solution)/shard_map/ppermute | solution.py:27
  153.2 0.7 copy-start.12
  153.2 0.7 copy-start.14
  153.2 1.1 copy-start.13
  153.2 1.1 copy-start.18
  153.2 13.2 %copy-start.11 = (bf16[64,128]{1,0:T(8,128)(2,1)S(1)}, bf16[64,128]{1,0:T(8,128)(2,1)}, u32[]{:S(2)}) copy-start(bf16[64,128]{1,0:T(8,128)(2,1)} %get-tuple-element.38) | copy-start | bytes 49156
  153.2 13.2 %copy-start.15 = (bf16[64,128]{1,0:T(8,128)(2,1)S(1)}, bf16[64,128]{1,0:T(8,128)(2,1)}, u32[]{:S(2)}) copy-start(bf16[64,128]{1,0:T(8,128)(2,1)} %get-tuple-element.34) | copy-start | bytes 49156
  153.4 16.2 %copy-start.8 = (bf16[64,128]{1,0:T(8,128)(2,1)S(1)}, bf16[64,128]{1,0:T(8,128)(2,1)}, u32[]{:S(2)}) copy-start(bf16[64,128]{1,0:T(8,128)(2,1)} %get-tuple-element.44) | copy-start | bytes 49156
  153.4 16.2 %copy-start.9 = (bf16[64,128]{1,0:T(8,128)(2,1)S(1)}, bf16[64,128]{1,0:T(8,128)(2,1)}, u32[]{:S(2)}) copy-start(bf16[64,128]{1,0:T(8,128)(2,1)} %get-tuple-element.40) | copy-start | bytes 49156
  153.4 24.0 %collective-permute-start.18 = (bf16[3,352,512]{2,1,0:T(8,128)(2,1)S(1)}, bf16[3,352,512]{2,1,0:T(8,128)(2,1)S(1)}, u32[]{:S(2)}, u32[]{:S(2)}) collective-permute-start(bf16[3,352,512]{2,1,0:T(8,128)(2,1)S(1)} %fusion.27), channel_id=1, source_target_pairs={{0,1},{1,0},{2,3},{3,2},{4,5},{5,4},{6,7},{7,6},{8,9},{9,8},{10,11... | collective-permute-start | bytes 3244040 | tf_op jit(solution)/shard_map/ppermute | solution.py:27
  154.2 22.3 %copy-start.10 = (bf16[64,128]{1,0:T(8,128)(2,1)S(1)}, bf16[64,128]{1,0:T(8,128)(2,1)}, u32[]{:S(2)}) copy-start(bf16[64,128]{1,0:T(8,128)(2,1)} %get-tuple-element.32) | copy-start | bytes 49156
  154.2 15.4 %collective-permute-start.8 = (bf16[128,1024]{1,0:T(8,128)(2,1)S(1)}, bf16[128,1024]{1,0:T(8,128)(2,1)S(1)}, u32[]{:S(2)}, u32[]{:S(2)}) collective-permute-start(bf16[128,1024]{1,0:T(8,128)(2,1)S(1)} %fusion.17), channel_id=1, source_target_pairs={{0,8},{1,9},{2,10},{3,11},{4,12},{5,13},{6,14},{7,15},{8,0},{9,1},... | collective-permute-start | bytes 786440 | tf_op jit(solution)/shard_map/ppermute | solution.py:27
  154.5 17.9 %collective-permute-start.14 = (bf16[128,1024]{1,0:T(8,128)(2,1)S(1)}, bf16[128,1024]{1,0:T(8,128)(2,1)S(1)}, u32[]{:S(2)}, u32[]{:S(2)}) collective-permute-start(bf16[128,1024]{1,0:T(8,128)(2,1)S(1)} %convolution_convert_fusion.5), channel_id=1, source_target_pairs={{0,4},{1,5},{2,6},{3,7},{4,0},{5,1},{6,2},{7,3},{8,12},{9,13},{10,... | collective-permute-start | bytes 786440 | tf_op jit(solution)/shard_map/ppermute | solution.py:27
  166.7 9.8 %collective-permute-start.16 = (bf16[128,1024]{1,0:T(8,128)(2,1)S(1)}, bf16[128,1024]{1,0:T(8,128)(2,1)S(1)}, u32[]{:S(2)}, u32[]{:S(2)}) collective-permute-start(bf16[128,1024]{1,0:T(8,128)(2,1)S(1)} %fusion.18), channel_id=1, source_target_pairs={{0,8},{1,9},{2,10},{3,11},{4,12},{5,13},{6,14},{7,15},{8,0},{9,1},... | collective-permute-start | bytes 786440 | tf_op jit(solution)/shard_map/ppermute | solution.py:27
Sparse Core Ops, SparseCore 0:
  84.6 9.7 all-gather.3

commit v2 on v1

--- a/solution.py
+++ b/solution.py
@@ -44,11 +44,40 @@
     parity = blk_index % 2
     expert_here = blk_index // 2
 
-    table = jnp.concatenate([routes.T, gate_codes.T], axis=0)
-    tables = lax.all_gather(table, "blk")
+    tables = jnp.concatenate([routes.T, gate_codes.T], axis=0)[None]
+    step = planes // 2
+    while step:
+        tables = jnp.stack([tables, flipped(tables, "blk", step * plane_stride)], axis=1)
+        tables = tables.reshape((-1,) + tables.shape[2:])
+        step //= 2
+    tables = jnp.stack(
+        [tables]
+        + [flipped(tables, "blk", 2 * column) for column in range(1, plane_experts)]
+    )
 
     own_weights = jnp.stack([w_gate[0].T, w_up[0].T, w_down[0]])
     pair_weights = flipped(own_weights, "blk", 1)
+
+    def widened(part):
+        parts = [part] + [
+            lax.ppermute(
+                part, "seq", [(i, (i - shift) % seq_count) for i in range(seq_count)]
+            )
+            for shift in range(1, seq_count)
+        ]
+        return jnp.concatenate(
+            [
+                lax.select_n(
+                    (place - seq_index) % seq_count == 1, *parts
+                )
+                if seq_count == 2
+                else lax.switch(
+                    (place - seq_index) % seq_count, [lambda p=p: p for p in parts]
+                )
+                for place in range(seq_count)
+            ],
+            axis=2,
+        )
 
     def spread(part):
         chunks = {0: part}
@@ -61,10 +90,6 @@
 
     token_chunks = spread(tokens)
     cot_chunks = spread(cotangent)
-
-    def table_of(column, place):
-        source = blk_index ^ (place * plane_stride + column * 2)
-        return lax.dynamic_index_in_dim(tables, source, 0, keepdims=False), source
 
     earlier = (
         jnp.arange(tok_rows)[:, None] < jnp.arange(tok_rows)[None, :]
@@ -85,12 +110,9 @@
             gates = gates + jnp.where(hits[k], table_rows[:, top_count + k], 0).astype(jnp.float32)
         return chosen, gates / 64.0
 
-    column_tables = []
-    column_sources = []
-    for column in range(plane_experts):
-        picked = [table_of(column, place) for place in range(planes)]
-        column_tables.append(jnp.stack([entry[0] for entry in picked]))
-        column_sources.append(jnp.stack([entry[1] for entry in picked]))
+    places = jnp.arange(planes, dtype=jnp.int32) * plane_stride
+    column_tables = [tables[column] for column in range(plane_experts)]
+    column_sources = [blk_index ^ (places + 2 * column) for column in range(plane_experts)]
 
     select = []
     weigh = []
@@ -129,9 +151,7 @@
     rows_in = gathered(select, token_chunks)
     rows_cot = gathered(weigh, cot_chunks)
 
-    weights = lax.all_gather(
-        jnp.stack([own_weights, pair_weights], axis=1), "seq", axis=3, tiled=True
-    ).reshape(3, 2 * half_width, model_width)
+    weights = jnp.concatenate([widened(own_weights), widened(pair_weights)], axis=1)
     gate_mat, up_mat, down_mat = weights[0], weights[1], weights[2]
 
     unit = jnp.arange(half_width, dtype=jnp.int32)

time: 186 us -> 149 us (0.80)
  blocking collectives: 56.4 us -> 0 us
  waiting for transfers between devices: 42.5 us -> 66.1 us
  between operations: 16.7 us -> 3.44 us
  other arithmetic: 9.01 us -> 17.9 us
  starting transfers between devices: 19 us -> 24.3 us
  matrix products: 32.4 us -> 28.2 us
    all_gather x1 -> x0, blocking collectives: 56.4 us -> none  [local(): tables = lax.all_gather(table, 'blk')]
    ppermute x18 -> x21, waiting for transfers between devices: 42.5 us -> 66.1 us  [flipped(): lax.ppermute(values, axis, [(i, i ^ mask) for i in range(lax.axis_size(ax...]
    concatenate x0 -> x1, other arithmetic: none -> 6.5 us  [local(): jnp.concatenate([widened(own_weights), widened(pair_weights)], axis=1)]
    ppermute x18 -> x21, starting transfers between devices: 18.9 us -> 24.2 us  [flipped(): lax.ppermute(values, axis, [(i, i ^ mask) for i in range(lax.axis_size(ax...]
    another operation x3 -> x4, other arithmetic: 4.23 us -> 1.38 us  [the longest x1 1.36 us: local(): own_weights = jnp.stack([w_gate[0].T, w_up[0].T, w_down[0]])]
    slice x1 -> x0, local copies, waits for them, and re-layouts: 2.71 us -> none  [local(): gate_mat, up_mat, down_mat = (weights[0], weights[1], weights[2])]
    add x2, local copies, waits for them, and re-layouts: 0.16 us -> 2.67 us  [local(): token_ids.append((within + first[:, None]).reshape(-1))]
    dot_general x1, matrix products: 3.67 us -> 1.3 us  [local(): lax.dot_general(rows_cot, down_mat, contract_last, preferred_element_type...]
  transfers between devices with their start and end apart: 20 -> 24, of which waited for: 8 -> 11; matrix products, arithmetic and copies ran while one was open for 19% -> 26% of each run, Pallas kernels for 0% -> 0%
where the time goes in v2:
time: 149 us; the launch traced here: 148 us
  waiting for transfers between devices  66.1 us (44%)
  matrix products  28.2 us (19%)
  starting transfers between devices  24.3 us (16%)
  other arithmetic  17.9 us (12%)
  local copies, waits for them, and re-layouts  7.93 us (5%)
  between operations  3.44 us (2%)
    ppermute x21, waiting for transfers between devices, flipped(): lax.ppermute(values, axis, [(i, i ^ mask) for i in range(lax.axis_size(ax...  66.1 us
    ppermute x21, starting transfers between devices, flipped(): lax.ppermute(values, axis, [(i, i ^ mask) for i in range(lax.axis_size(ax...  24.2 us
    dot_general x16, matrix products, compact(): jnp.dot(choice[place], chunks[place], preferred_element_type=jnp.float32)  13.3 us
    concatenate x1, other arithmetic, local(): jnp.concatenate([widened(own_weights), widened(pair_weights)], axis=1)  6.5 us
    dot_general x8, matrix products, brought_back(): lax.dot_general(choice, block, contract_first, preferred_element_type=jnp...  3.4 us
    dot_general x6, matrix products, part_sums(): lax.dot_general(left, right, contract_first, preferred_element_type=jnp.f...  3.26 us
  transfers between devices with their start and end apart: 24, of which 11 were waited for; matrix products, arithmetic and copies ran while one was open for 26% of the time, Pallas kernels for 0%

profile of v2, /device:TPU:0, one launch (start us, length us, event | category | flops | bytes accessed | tf_op | source)
XLA Modules:
  0.0 147.9 jit_solution(625187096833859974)
XLA Ops:
  0.7 3.1 %collective-permute-start.14 = (bf16[128,1024]{1,0:T(8,128)(2,1)}, bf16[128,1024]{1,0:T(8,128)(2,1)}, u32[]{:S(2)}, u32[]{:S(2)}) collective-permute-start(bf16[128,1024]{1,0:T(8,128)(2,1)} %param.9), channel_id=1, source_target_pairs={{0,4},{1,5},{2,6},{3,7},{4,0},{5,1},{6,2},{7,3},{8,12},{9,13},{10,... | collective-permute-start | bytes 786440 | tf_op jit(solution)/shard_map/ppermute | solution.py:27
  3.8 2.6 %collective-permute-start.15 = (bf16[128,1024]{1,0:T(8,128)(2,1)}, bf16[128,1024]{1,0:T(8,128)(2,1)}, u32[]{:S(2)}, u32[]{:S(2)}) collective-permute-start(bf16[128,1024]{1,0:T(8,128)(2,1)} %param.9), channel_id=1, source_target_pairs={{0,8},{1,9},{2,10},{3,11},{4,12},{5,13},{6,14},{7,15},{8,0},{9,1},... | collective-permute-start | bytes 786440 | tf_op jit(solution)/shard_map/ppermute | solution.py:27
  6.4 1.4 pad_maximum_fusion.1
  7.7 1.6 %collective-permute-start.7 = (bf16[3,352,512]{2,1,0:T(8,128)(2,1)S(1)}, bf16[3,352,512]{2,1,0:T(8,128)(2,1)S(1)}, u32[]{:S(2)}, u32[]{:S(2)}) collective-permute-start(bf16[3,352,512]{2,1,0:T(8,128)(2,1)S(1)} %pad_maximum_fusion.1), channel_id=1, source_target_pairs={{0,1},{1,0},{2,3},{3,2},{4,5},{5,4},{6,7},{7,6},{8,9},{9,8},{10,11... | collective-permute-start | bytes 3244040 | tf_op jit(solution)/shard_map/ppermute | solution.py:27
  9.7 0.6 fusion.120
  10.3 0.7 fusion.88
  11.0 7.5 %collective-permute-done = s32[1,4,128]{2,1,0:T(4,128)S(1)} collective-permute-done((s32[1,4,128]{2,1,0:T(4,128)S(1)}, s32[1,4,128]{2,1,0:T(4,128)S(1)}, u32[]{:S(2)}, u32[]{:S(2)}) %collective-permute-start) | collective-permute-done | bytes 2080 | tf_op jit(solution)/shard_map/ppermute | solution.py:27
  18.9 0.6 add_multiply_fusion
  21.4 0.7 collective-permute-done.1
  22.1 0.6 copy.18
  22.7 0.9 fusion.98
  23.6 0.8 compare_or_fusion.1
  24.4 1.6 %collective-permute-start.9 = (s32[4,4,128]{2,1,0:T(4,128)}, s32[4,4,128]{2,1,0:T(4,128)}, u32[]{:S(2)}, u32[]{:S(2)}) collective-permute-start(s32[4,4,128]{2,1,0:T(4,128)} %bitcast.8), channel_id=1, source_target_pairs={{0,2},{1,3},{2,0},{3,1},{4,6},{5,7},{6,4},{7,5},{8,10},{9,11},{10,... | collective-permute-start | bytes 24584 | tf_op jit(solution)/shard_map/ppermute | solution.py:27
  26.5 0.8 convolution_convert_fusion.11
  27.4 0.6 slice_bitcast_fusion.49
  28.0 0.8 fusion.25
  28.9 0.6 slice_bitcast_fusion.50
  29.7 0.8 convolution_convert_fusion.19
  30.5 0.6 slice_bitcast_fusion.41
  31.1 0.6 slice_bitcast_fusion.42
  31.8 0.6 broadcast_add_fusion.1
  32.4 1.3 add.156
  33.8 1.0 collective-permute-start.2
  34.8 0.8 compare_or_fusion
  35.9 1.3 broadcast_add_fusion
  37.2 1.3 add.161
  38.5 0.7 and_xor_fusion
  39.2 2.1 %collective-permute-start.3 = (bf16[128,1024]{1,0:T(8,128)(2,1)S(1)}, bf16[128,1024]{1,0:T(8,128)(2,1)S(1)}, u32[]{:S(2)}, u32[]{:S(2)}) collective-permute-start(bf16[128,1024]{1,0:T(8,128)(2,1)S(1)} %copy-done.4), channel_id=1, source_target_pairs={{0,8},{1,9},{2,10},{3,11},{4,12},{5,13},{6,14},{7,15},{8,0},{9,1},... | collective-permute-start | bytes 786440 | tf_op jit(solution)/shard_map/ppermute | solution.py:27
  41.4 1.1 convolution_convert_fusion.9
  42.5 1.1 collective-permute-start.16
  43.6 1.1 convolution_convert_fusion.10
  44.8 6.3 %collective-permute-done.3 = bf16[128,1024]{1,0:T(8,128)(2,1)S(1)} collective-permute-done((bf16[128,1024]{1,0:T(8,128)(2,1)S(1)}, bf16[128,1024]{1,0:T(8,128)(2,1)S(1)}, u32[]{:S(2)}, u32[]{:S(2)}) %collective-permute-start.3) | collective-permute-done | bytes 262176 | tf_op jit(solution)/shard_map/ppermute | solution.py:27
  51.1 0.9 convolution_convert_fusion.17
  52.0 1.8 %fusion.24 = bf16[512,1024]{1,0:T(8,128)(2,1)} fusion(bf16[512,1024]{1,0:T(8,128)(2,1)} %fusion.25, bf16[128,1024]{1,0:T(8,128)(2,1)} %collective-permute-done.14, bf16[4,64,128]{2,1,0:T(8,128)(2,1)S(1)} %select_convert_fusion.1), kind=kOutput, calls=%fused_computation.63 | convolution fusion | flops 16842752 | bytes 409600 | tf_op jit(solution)/shard_map/dot_general | solution.py:137
  53.8 1.1 convolution_convert_fusion.18
  54.9 1.2 fusion.28
  56.3 1.8 %fusion.23 = bf16[512,1024]{1,0:T(8,128)(2,1)} fusion(bf16[512,1024]{1,0:T(8,128)(2,1)} %fusion.24, bf16[128,1024]{1,0:T(8,128)(2,1)} %collective-permute-done.15, bf16[4,64,128]{2,1,0:T(8,128)(2,1)S(1)} %select_convert_fusion.1), kind=kOutput, calls=%fused_computation.61 | convolution fusion | flops 16842752 | bytes 409600 | tf_op jit(solution)/shard_map/dot_general | solution.py:137
  58.0 0.9 convolution_convert_fusion.8
  60.0 1.6 %collective-permute-start.5 = (bf16[256,1024]{1,0:T(8,128)(2,1)S(1)}, bf16[256,1024]{1,0:T(8,128)(2,1)S(1)}, u32[]{:S(2)}, u32[]{:S(2)}) collective-permute-start(bf16[256,1024]{1,0:T(8,128)(2,1)S(1)} %pad_maximum_fusion.2), channel_id=1, source_target_pairs={{0,2},{1,3},{2,0},{3,1},{4,6},{5,7},{6,4},{7,5},{8,10},{9,11},{10,... | collective-permute-start | bytes 1572872 | tf_op jit(solution)/shard_map/ppermute | solution.py:27
  61.9 12.0 %collective-permute-done.17 = bf16[256,1024]{1,0:T(8,128)(2,1)S(1)} collective-permute-done((bf16[256,1024]{1,0:T(8,128)(2,1)S(1)}, bf16[256,1024]{1,0:T(8,128)(2,1)S(1)}, u32[]{:S(2)}, u32[]{:S(2)}) %collective-permute-start.17) | collective-permute-done | bytes 524320 | tf_op jit(solution)/shard_map/ppermute | solution.py:27
  74.0 7.1 %collective-permute-done.5 = bf16[256,1024]{1,0:T(8,128)(2,1)S(1)} collective-permute-done((bf16[256,1024]{1,0:T(8,128)(2,1)S(1)}, bf16[256,1024]{1,0:T(8,128)(2,1)S(1)}, u32[]{:S(2)}, u32[]{:S(2)}) %collective-permute-start.5) | collective-permute-done | bytes 524320 | tf_op jit(solution)/shard_map/ppermute | solution.py:27
  81.2 1.4 broadcast_select_fusion.3
  82.8 6.5 %maximum_maximum_fusion = bf16[3,704,1024]{2,1,0:T(8,128)(2,1)S(1)} fusion(bf16[3,352,512]{2,1,0:T(8,128)(2,1)S(1)} %get-tuple-element.11, bf16[3,352,512]{2,1,0:T(8,128)(2,1)S(1)} %get-tuple-element.10, bf16[3,352,512]{2,1,0:T(8,128)(2,1)S(1)} %get-tuple-element.9, bf16[3,352,512]{2,1,0:T(8,128)(2,1)S(1)} %get-tuple-element.8), kind=kLoop, calls=%fused_computation | loop fusion | flops 17301504 | bytes 8650752 | tf_op jit(solution)/shard_map/concatenate | solution.py:154
  89.3 1.0 fusion.15
  90.3 1.3 select_multiply_fusion
  91.6 2.5 %multiply_convert_fusion.1 = (bf16[512,704]{0,1:T(8,128)(2,1)S(1)}, bf16[512,704]{0,1:T(8,128)(2,1)S(1)}, bf16[512,704]{0,1:T(8,128)(2,1)S(1)}) fusion(f32[512,704]{0,1:T(8,128)S(1)} %select_multiply_fusion, f32[512,704]{0,1:T(8,128)S(1)} %fusion.15, s32[704]{0:T(1024)S(1)} %copy-done.28, s32[512]{0:T(512)S(1)} %and_xor_fusion, ...), kind=kOutput, calls=%fused_computation.27 | convolution fusion | flops 749371392 | bytes 7542784 | tf_op jit(solution)/shard_map/dot_general | solution.py:162
  94.1 1.0 convolution_convert_fusion
  95.1 1.0 fusion.14
  98.8 1.0 add_convert_fusion
  99.8 1.6 %collective-permute-start.18 = (bf16[4,64,1024]{2,1,0:T(8,128)(2,1)S(1)}, bf16[4,64,1024]{2,1,0:T(8,128)(2,1)S(1)}, u32[]{:S(2)}, u32[]{:S(2)}) collective-permute-start(bf16[4,64,1024]{2,1,0:T(8,128)(2,1)S(1)} %bitcast.200), channel_id=1, source_target_pairs={{0,2},{1,3},{2,0},{3,1},{4,6},{5,7},{6,4},{7,5},{8,10},{9,11},{10,... | collective-permute-start | bytes 1572872 | tf_op jit(solution)/shard_map/ppermute | solution.py:27
  103.2 8.3 %collective-permute-done.10 = bf16[4,64,1024]{2,1,0:T(8,128)(2,1)S(1)} collective-permute-done((bf16[4,64,1024]{2,1,0:T(8,128)(2,1)S(1)}, bf16[4,64,1024]{2,1,0:T(8,128)(2,1)S(1)}, u32[]{:S(2)}, u32[]{:S(2)}) %collective-permute-start.10) | collective-permute-done | bytes 524320 | tf_op jit(solution)/shard_map/ppermute | solution.py:27
  111.8 1.2 collective-permute-start.12
  113.3 0.9 collective-permute-start.11
  114.2 4.3 %collective-permute-done.18 = bf16[4,64,1024]{2,1,0:T(8,128)(2,1)S(1)} collective-permute-done((bf16[4,64,1024]{2,1,0:T(8,128)(2,1)S(1)}, bf16[4,64,1024]{2,1,0:T(8,128)(2,1)S(1)}, u32[]{:S(2)}, u32[]{:S(2)}) %collective-permute-start.18) | collective-permute-done | bytes 524320 | tf_op jit(solution)/shard_map/ppermute | solution.py:27
  118.8 1.5 %collective-permute-start.20 = (bf16[128,1024]{1,0:T(8,128)(2,1)S(1)}, bf16[128,1024]{1,0:T(8,128)(2,1)S(1)}, u32[]{:S(2)}, u32[]{:S(2)}) collective-permute-start(bf16[128,1024]{1,0:T(8,128)(2,1)S(1)} %convolution_convert_fusion.4), channel_id=1, source_target_pairs={{0,4},{1,5},{2,6},{3,7},{4,0},{5,1},{6,2},{7,3},{8,12},{9,13},{10,... | collective-permute-start | bytes 786440 | tf_op jit(solution)/shard_map/ppermute | solution.py:27
  120.3 0.8 maximum_add_fusion
  121.4 1.6 %collective-permute-start.23 = (bf16[3,352,512]{2,1,0:T(8,128)(2,1)S(1)}, bf16[3,352,512]{2,1,0:T(8,128)(2,1)S(1)}, u32[]{:S(2)}, u32[]{:S(2)}) collective-permute-start(bf16[3,352,512]{2,1,0:T(8,128)(2,1)S(1)} %fusion.30), channel_id=1, source_target_pairs={{0,1},{1,0},{2,3},{3,2},{4,5},{5,4},{6,7},{7,6},{8,9},{9,8},{10,11... | collective-permute-start | bytes 3244040 | tf_op jit(solution)/shard_map/ppermute | solution.py:27
  123.6 0.6 collective-permute-start.19
  124.3 11.9 %collective-permute-done.20 = bf16[128,1024]{1,0:T(8,128)(2,1)S(1)} collective-permute-done((bf16[128,1024]{1,0:T(8,128)(2,1)S(1)}, bf16[128,1024]{1,0:T(8,128)(2,1)S(1)}, u32[]{:S(2)}, u32[]{:S(2)}) %collective-permute-start.20) | collective-permute-done | bytes 262176 | tf_op jit(solution)/shard_map/ppermute | solution.py:27
  136.5 2.7 %collective-permute-done.13 = bf16[128,1024]{1,0:T(8,128)(2,1)S(1)} collective-permute-done((bf16[128,1024]{1,0:T(8,128)(2,1)S(1)}, bf16[128,1024]{1,0:T(8,128)(2,1)S(1)}, u32[]{:S(2)}, u32[]{:S(2)}) %collective-permute-start.13) | collective-permute-done | bytes 262176 | tf_op jit(solution)/shard_map/ppermute | solution.py:27
  139.3 1.0 fusion.19
  140.7 4.7 %collective-permute-done.21 = bf16[128,1024]{1,0:T(8,128)(2,1)S(1)} collective-permute-done((bf16[128,1024]{1,0:T(8,128)(2,1)S(1)}, bf16[128,1024]{1,0:T(8,128)(2,1)S(1)}, u32[]{:S(2)}, u32[]{:S(2)}) %collective-permute-start.21) | collective-permute-done | bytes 262176 | tf_op jit(solution)/shard_map/ppermute | solution.py:27
  145.4 1.0 fusion.18
  146.9 1.0 fusion.117
  (136 shorter events, 10.7 us)
Async XLA Ops:
  0.6 25.9 %copy-start.3 = (bf16[128,1024]{1,0:T(8,128)(2,1)S(1)}, bf16[128,1024]{1,0:T(8,128)(2,1)}, u32[]{:S(2)}) copy-start(bf16[128,1024]{1,0:T(8,128)(2,1)} %param.9) | copy-start | bytes 786436
  0.6 8.6 %copy-start.31 = (s32[128,2]{0,1:T(2,128)S(1)}, s32[128,2]{0,1:T(2,128)}, u32[]{:S(2)}) copy-start(s32[128,2]{0,1:T(2,128)} %param.11) | copy-start | bytes 3076
  0.7 8.6 %copy-start.32 = (s32[128,2]{0,1:T(2,128)S(1)}, s32[128,2]{0,1:T(2,128)}, u32[]{:S(2)}) copy-start(s32[128,2]{0,1:T(2,128)} %param.10) | copy-start | bytes 3076
  0.7 9.0 %copy-start.29 = (s32[2]{0:T(128)S(1)}, s32[2]{0:T(128)}, u32[]{:S(2)}) copy-start(s32[2]{0:T(128)} %param.12) | copy-start | bytes 28
  0.7 41.9 %collective-permute-start.14 = (bf16[128,1024]{1,0:T(8,128)(2,1)}, bf16[128,1024]{1,0:T(8,128)(2,1)}, u32[]{:S(2)}, u32[]{:S(2)}) collective-permute-start(bf16[128,1024]{1,0:T(8,128)(2,1)} %param.9), channel_id=1, source_target_pairs={{0,4},{1,5},{2,6},{3,7},{4,0},{5,1},{6,2},{7,3},{8,12},{9,13},{10,... | collective-permute-start | bytes 786440 | tf_op jit(solution)/shard_map/ppermute | solution.py:27
  3.8 35.5 %collective-permute-start.15 = (bf16[128,1024]{1,0:T(8,128)(2,1)}, bf16[128,1024]{1,0:T(8,128)(2,1)}, u32[]{:S(2)}, u32[]{:S(2)}) collective-permute-start(bf16[128,1024]{1,0:T(8,128)(2,1)} %param.9), channel_id=1, source_target_pairs={{0,8},{1,9},{2,10},{3,11},{4,12},{5,13},{6,14},{7,15},{8,0},{9,1},... | collective-permute-start | bytes 786440 | tf_op jit(solution)/shard_map/ppermute | solution.py:27
  6.4 23.1 %copy-start.4 = (bf16[128,1024]{1,0:T(8,128)(2,1)S(1)}, bf16[128,1024]{1,0:T(8,128)(2,1)}, u32[]{:S(2)}) copy-start(bf16[128,1024]{1,0:T(8,128)(2,1)} %param.8) | copy-start | bytes 786436
  7.7 52.1 %collective-permute-start.7 = (bf16[3,352,512]{2,1,0:T(8,128)(2,1)S(1)}, bf16[3,352,512]{2,1,0:T(8,128)(2,1)S(1)}, u32[]{:S(2)}, u32[]{:S(2)}) collective-permute-start(bf16[3,352,512]{2,1,0:T(8,128)(2,1)S(1)} %pad_maximum_fusion.1), channel_id=1, source_target_pairs={{0,1},{1,0},{2,3},{3,2},{4,5},{5,4},{6,7},{7,6},{8,9},{9,8},{10,11... | collective-permute-start | bytes 3244040 | tf_op jit(solution)/shard_map/ppermute | solution.py:27
  9.3 71.9 %collective-permute-start.6 = (bf16[3,352,512]{2,1,0:T(8,128)(2,1)S(1)}, bf16[3,352,512]{2,1,0:T(8,128)(2,1)}, u32[]{:S(2)}, u32[]{:S(2)}) collective-permute-start(bf16[3,352,512]{2,1,0:T(8,128)(2,1)S(1)} %pad_maximum_fusion.1), channel_id=1, source_target_pairs={{0,16},{16,0},{1,17},{17,1},{2,18},{18,2},{3,19},{19,3},{4,20},{20... | collective-permute-start | bytes 3244040 | tf_op jit(solution)/shard_map/ppermute | solution.py:63
  9.3 9.2 %collective-permute-start = (s32[1,4,128]{2,1,0:T(4,128)S(1)}, s32[1,4,128]{2,1,0:T(4,128)S(1)}, u32[]{:S(2)}, u32[]{:S(2)}) collective-permute-start(s32[1,4,128]{2,1,0:T(4,128)S(1)} %get-tuple-element.58), channel_id=1, source_target_pairs={{0,8},{1,9},{2,10},{3,11},{4,12},{5,13},{6,14},{7,15},{8,0},{9,1},... | collective-permute-start | bytes 6152 | tf_op jit(solution)/shard_map/ppermute | solution.py:27
  18.5 3.6 %collective-permute-start.1 = (s32[2,4,128]{2,1,0:T(4,128)S(1)}, s32[2,4,128]{2,1,0:T(4,128)S(1)}, u32[]{:S(2)}, u32[]{:S(2)}) collective-permute-start(s32[2,4,128]{2,1,0:T(4,128)S(1)} %get-tuple-element.52), channel_id=1, source_target_pairs={{0,4},{1,5},{2,6},{3,7},{4,0},{5,1},{6,2},{7,3},{8,12},{9,13},{10,... | collective-permute-start | bytes 12296 | tf_op jit(solution)/shard_map/ppermute | solution.py:27
  21.4 10.3 %copy-start.30 = (s32[4]{0:T(128)S(1)}, s32[4]{0:T(128)}, u32[]{:S(2)}) copy-start(s32[4]{0:T(128)} %get-tuple-element.62) | copy-start | bytes 52
  24.4 9.4 %collective-permute-start.9 = (s32[4,4,128]{2,1,0:T(4,128)}, s32[4,4,128]{2,1,0:T(4,128)}, u32[]{:S(2)}, u32[]{:S(2)}) collective-permute-start(s32[4,4,128]{2,1,0:T(4,128)} %bitcast.8), channel_id=1, source_target_pairs={{0,2},{1,3},{2,0},{3,1},{4,6},{5,7},{6,4},{7,5},{8,10},{9,11},{10,... | collective-permute-start | bytes 24584 | tf_op jit(solution)/shard_map/ppermute | solution.py:27
  26.3 5.5 %copy-start.9 = (pred[4,64,128]{2,1,0:T(32,128)(4,1)}, pred[4,64,128]{2,1,0:T(32,128)(4,1)S(1)}, u32[]{:S(2)}) copy-start(pred[4,64,128]{2,1,0:T(32,128)(4,1)S(1)} %get-tuple-element.54) | copy-start | bytes 98308
  26.5 5.3 %copy-start.11 = (pred[4,64,128]{2,1,0:T(32,128)(4,1)}, pred[4,64,128]{2,1,0:T(32,128)(4,1)S(1)}, u32[]{:S(2)}) copy-start(pred[4,64,128]{2,1,0:T(32,128)(4,1)S(1)} %get-tuple-element.56) | copy-start | bytes 98308
  26.5 3.0 %copy-start.5 = (bf16[4,64,128]{2,1,0:T(8,128)(2,1)}, bf16[4,64,128]{2,1,0:T(8,128)(2,1)S(1)}, u32[]{:S(2)}) copy-start(bf16[4,64,128]{2,1,0:T(8,128)(2,1)S(1)} %select_convert_fusion) | copy-start | bytes 196612
  33.8 20.0 %collective-permute-start.2 = (bf16[128,1024]{1,0:T(8,128)(2,1)S(1)}, bf16[128,1024]{1,0:T(8,128)(2,1)}, u32[]{:S(2)}, u32[]{:S(2)}) collective-permute-start(bf16[128,1024]{1,0:T(8,128)(2,1)S(1)} %copy-done.4), channel_id=1, source_target_pairs={{0,4},{1,5},{2,6},{3,7},{4,0},{5,1},{6,2},{7,3},{8,12},{9,13},{10,... | collective-permute-start | bytes 786440 | tf_op jit(solution)/shard_map/ppermute | solution.py:27
  38.5 15.3 %copy-start.12 = (pred[4,64,128]{2,1,0:T(32,128)(4,1)S(1)}, pred[4,64,128]{2,1,0:T(32,128)(4,1)}, u32[]{:S(2)}) copy-start(pred[4,64,128]{2,1,0:T(32,128)(4,1)} %copy-done.11) | copy-start | bytes 98308
  38.5 16.4 %copy-start.10 = (pred[4,64,128]{2,1,0:T(32,128)(4,1)S(1)}, pred[4,64,128]{2,1,0:T(32,128)(4,1)}, u32[]{:S(2)}) copy-start(pred[4,64,128]{2,1,0:T(32,128)(4,1)} %copy-done.9) | copy-start | bytes 98308
  39.2 11.8 %collective-permute-start.3 = (bf16[128,1024]{1,0:T(8,128)(2,1)S(1)}, bf16[128,1024]{1,0:T(8,128)(2,1)S(1)}, u32[]{:S(2)}, u32[]{:S(2)}) collective-permute-start(bf16[128,1024]{1,0:T(8,128)(2,1)S(1)} %copy-done.4), channel_id=1, source_target_pairs={{0,8},{1,9},{2,10},{3,11},{4,12},{5,13},{6,14},{7,15},{8,0},{9,1},... | collective-permute-start | bytes 786440 | tf_op jit(solution)/shard_map/ppermute | solution.py:27
  42.5 15.5 %collective-permute-start.16 = (bf16[128,1024]{1,0:T(8,128)(2,1)}, bf16[128,1024]{1,0:T(8,128)(2,1)S(1)}, u32[]{:S(2)}, u32[]{:S(2)}) collective-permute-start(bf16[128,1024]{1,0:T(8,128)(2,1)} %collective-permute-done.15), channel_id=1, source_target_pairs={{0,4},{1,5},{2,6},{3,7},{4,0},{5,1},{6,2},{7,3},{8,12},{9,13},{10,... | collective-permute-start | bytes 786440 | tf_op jit(solution)/shard_map/ppermute | solution.py:27
  44.7 14.2 %copy-start.7 = (bf16[64,1024]{1,0:T(8,128)(2,1)S(1)}, bf16[64,1024]{1,0:T(8,128)(2,1)}, u32[]{:S(2)}) copy-start(bf16[64,1024]{1,0:T(8,128)(2,1)} %convolution_convert_fusion.11) | copy-start | bytes 393220
  51.1 8.5 %collective-permute-start.4 = (bf16[128,1024]{1,0:T(8,128)(2,1)S(1)}, bf16[128,1024]{1,0:T(8,128)(2,1)S(1)}, u32[]{:S(2)}, u32[]{:S(2)}) collective-permute-start(bf16[128,1024]{1,0:T(8,128)(2,1)S(1)} %collective-permute-done.3), channel_id=1, source_target_pairs={{0,4},{1,5},{2,6},{3,7},{4,0},{5,1},{6,2},{7,3},{8,12},{9,13},{10,... | collective-permute-start | bytes 786440 | tf_op jit(solution)/shard_map/ppermute | solution.py:27
  54.9 5.0 %copy-start.6 = (bf16[64,1024]{1,0:T(8,128)(2,1)S(1)}, bf16[64,1024]{1,0:T(8,128)(2,1)}, u32[]{:S(2)}) copy-start(bf16[64,1024]{1,0:T(8,128)(2,1)} %convolution_convert_fusion.19) | copy-start | bytes 393220
  59.0 2.8 %copy-start.8 = (bf16[512,1024]{1,0:T(8,128)(2,1)S(1)}, bf16[512,1024]{1,0:T(8,128)(2,1)}, u32[]{:S(2)}) copy-start(bf16[512,1024]{1,0:T(8,128)(2,1)} %fusion.23) | copy-start | bytes 3145732
  59.0 14.9 %collective-permute-start.17 = (bf16[256,1024]{1,0:T(8,128)(2,1)S(1)}, bf16[256,1024]{1,0:T(8,128)(2,1)S(1)}, u32[]{:S(2)}, u32[]{:S(2)}) collective-permute-start(bf16[256,1024]{1,0:T(8,128)(2,1)S(1)} %pad_maximum_fusion.3), channel_id=1, source_target_pairs={{0,2},{1,3},{2,0},{3,1},{4,6},{5,7},{6,4},{7,5},{8,10},{9,11},{10,... | collective-permute-start | bytes 1572872 | tf_op jit(solution)/shard_map/ppermute | solution.py:27
  59.8 22.8 %collective-permute-start.8 = (bf16[3,352,512]{2,1,0:T(8,128)(2,1)S(1)}, bf16[3,352,512]{2,1,0:T(8,128)(2,1)S(1)}, u32[]{:S(2)}, u32[]{:S(2)}) collective-permute-start(bf16[3,352,512]{2,1,0:T(8,128)(2,1)S(1)} %collective-permute-done.7), channel_id=1, source_target_pairs={{0,16},{16,0},{1,17},{17,1},{2,18},{18,2},{3,19},{19,3},{4,20},{20... | collective-permute-start | bytes 3244040 | tf_op jit(solution)/shard_map/ppermute | solution.py:63
  59.9 21.3 %copy-start = (bf16[1,352,512]{2,1,0:T(8,128)(2,1)S(1)}, bf16[1,352,512]{2,1,0:T(8,128)(2,1)}, u32[]{:S(2)}) copy-start(bf16[1,352,512]{2,1,0:T(8,128)(2,1)} %param.15) | copy-start | bytes 1081348
  59.9 21.2 %copy-start.1 = (bf16[1,512,352]{1,2,0:T(8,128)(2,1)S(1)}, bf16[1,512,352]{1,2,0:T(8,128)(2,1)}, u32[]{:S(2)}) copy-start(bf16[1,512,352]{1,2,0:T(8,128)(2,1)} %param.14) | copy-start | bytes 1081348
  59.9 21.2 %copy-start.2 = (bf16[1,512,352]{1,2,0:T(8,128)(2,1)S(1)}, bf16[1,512,352]{1,2,0:T(8,128)(2,1)}, u32[]{:S(2)}) copy-start(bf16[1,512,352]{1,2,0:T(8,128)(2,1)} %param.13) | copy-start | bytes 1081348
  60.0 21.2 %collective-permute-start.5 = (bf16[256,1024]{1,0:T(8,128)(2,1)S(1)}, bf16[256,1024]{1,0:T(8,128)(2,1)S(1)}, u32[]{:S(2)}, u32[]{:S(2)}) collective-permute-start(bf16[256,1024]{1,0:T(8,128)(2,1)S(1)} %pad_maximum_fusion.2), channel_id=1, source_target_pairs={{0,2},{1,3},{2,0},{3,1},{4,6},{5,7},{6,4},{7,5},{8,10},{9,11},{10,... | collective-permute-start | bytes 1572872 | tf_op jit(solution)/shard_map/ppermute | solution.py:27
  89.3 1.0 copy-start.28
  97.3 14.2 %collective-permute-start.10 = (bf16[4,64,1024]{2,1,0:T(8,128)(2,1)S(1)}, bf16[4,64,1024]{2,1,0:T(8,128)(2,1)S(1)}, u32[]{:S(2)}, u32[]{:S(2)}) collective-permute-start(bf16[4,64,1024]{2,1,0:T(8,128)(2,1)S(1)} %bitcast.201), channel_id=1, source_target_pairs={{0,2},{1,3},{2,0},{3,1},{4,6},{5,7},{6,4},{7,5},{8,10},{9,11},{10,... | collective-permute-start | bytes 1572872 | tf_op jit(solution)/shard_map/ppermute | solution.py:27
  98.7 21.7 %collective-permute-start.22 = (bf16[3,704,512]{2,1,0:T(8,128)(2,1)S(1)}, bf16[3,704,512]{2,1,0:T(8,128)(2,1)S(1)}, u32[]{:S(2)}, u32[]{:S(2)}) collective-permute-start(bf16[3,704,512]{2,1,0:T(8,128)(2,1)S(1)} %pad_maximum_fusion), channel_id=1, source_target_pairs={{0,16},{16,0},{1,17},{17,1},{2,18},{18,2},{3,19},{19,3},{4,20},{20... | collective-permute-start | bytes 6488072 | tf_op jit(solution)/shard_map/ppermute | solution.py:224
  99.8 18.7 %collective-permute-start.18 = (bf16[4,64,1024]{2,1,0:T(8,128)(2,1)S(1)}, bf16[4,64,1024]{2,1,0:T(8,128)(2,1)S(1)}, u32[]{:S(2)}, u32[]{:S(2)}) collective-permute-start(bf16[4,64,1024]{2,1,0:T(8,128)(2,1)S(1)} %bitcast.200), channel_id=1, source_target_pairs={{0,2},{1,3},{2,0},{3,1},{4,6},{5,7},{6,4},{7,5},{8,10},{9,11},{10,... | collective-permute-start | bytes 1572872 | tf_op jit(solution)/shard_map/ppermute | solution.py:27
  102.6 8.9 %copy-start.25 = (bf16[64,128]{1,0:T(8,128)(2,1)S(1)}, bf16[64,128]{1,0:T(8,128)(2,1)}, u32[]{:S(2)}) copy-start(bf16[64,128]{1,0:T(8,128)(2,1)} %get-tuple-element.44) | copy-start | bytes 49156
  102.6 8.9 %copy-start.27 = (bf16[64,128]{1,0:T(8,128)(2,1)S(1)}, bf16[64,128]{1,0:T(8,128)(2,1)}, u32[]{:S(2)}) copy-start(bf16[64,128]{1,0:T(8,128)(2,1)} %get-tuple-element.40) | copy-start | bytes 49156
  103.2 9.9 %copy-start.23 = (bf16[64,128]{1,0:T(8,128)(2,1)S(1)}, bf16[64,128]{1,0:T(8,128)(2,1)}, u32[]{:S(2)}) copy-start(bf16[64,128]{1,0:T(8,128)(2,1)} %get-tuple-element.46) | copy-start | bytes 49156
  103.2 9.9 %copy-start.26 = (bf16[64,128]{1,0:T(8,128)(2,1)S(1)}, bf16[64,128]{1,0:T(8,128)(2,1)}, u32[]{:S(2)}) copy-start(bf16[64,128]{1,0:T(8,128)(2,1)} %get-tuple-element.42) | copy-start | bytes 49156
  103.2 15.4 %copy-start.22 = (bf16[64,128]{1,0:T(8,128)(2,1)S(1)}, bf16[64,128]{1,0:T(8,128)(2,1)}, u32[]{:S(2)}) copy-start(bf16[64,128]{1,0:T(8,128)(2,1)} %get-tuple-element.36) | copy-start | bytes 49156
  103.2 15.4 %copy-start.24 = (bf16[64,128]{1,0:T(8,128)(2,1)S(1)}, bf16[64,128]{1,0:T(8,128)(2,1)}, u32[]{:S(2)}) copy-start(bf16[64,128]{1,0:T(8,128)(2,1)} %get-tuple-element.32) | copy-start | bytes 49156
  111.8 11.2 %collective-permute-start.12 = (bf16[128,1024]{1,0:T(8,128)(2,1)S(1)}, bf16[128,1024]{1,0:T(8,128)(2,1)S(1)}, u32[]{:S(2)}, u32[]{:S(2)}) collective-permute-start(bf16[128,1024]{1,0:T(8,128)(2,1)S(1)} %convolution_convert_fusion.6), channel_id=1, source_target_pairs={{0,4},{1,5},{2,6},{3,7},{4,0},{5,1},{6,2},{7,3},{8,12},{9,13},{10,... | collective-permute-start | bytes 786440 | tf_op jit(solution)/shard_map/ppermute | solution.py:27
  113.3 23.2 %collective-permute-start.11 = (bf16[128,1024]{1,0:T(8,128)(2,1)S(1)}, bf16[128,1024]{1,0:T(8,128)(2,1)S(1)}, u32[]{:S(2)}, u32[]{:S(2)}) collective-permute-start(bf16[128,1024]{1,0:T(8,128)(2,1)S(1)} %convolution_convert_fusion.7), channel_id=1, source_target_pairs={{0,4},{1,5},{2,6},{3,7},{4,0},{5,1},{6,2},{7,3},{8,12},{9,13},{10,... | collective-permute-start | bytes 786440 | tf_op jit(solution)/shard_map/ppermute | solution.py:27
  118.8 17.4 %collective-permute-start.20 = (bf16[128,1024]{1,0:T(8,128)(2,1)S(1)}, bf16[128,1024]{1,0:T(8,128)(2,1)S(1)}, u32[]{:S(2)}, u32[]{:S(2)}) collective-permute-start(bf16[128,1024]{1,0:T(8,128)(2,1)S(1)} %convolution_convert_fusion.4), channel_id=1, source_target_pairs={{0,4},{1,5},{2,6},{3,7},{4,0},{5,1},{6,2},{7,3},{8,12},{9,13},{10,... | collective-permute-start | bytes 786440 | tf_op jit(solution)/shard_map/ppermute | solution.py:27
  121.2 1.8 %copy-start.17 = (bf16[64,128]{1,0:T(8,128)(2,1)S(1)}, bf16[64,128]{1,0:T(8,128)(2,1)}, u32[]{:S(2)}) copy-start(bf16[64,128]{1,0:T(8,128)(2,1)} %get-tuple-element.45) | copy-start | bytes 49156
  121.2 1.8 %copy-start.20 = (bf16[64,128]{1,0:T(8,128)(2,1)S(1)}, bf16[64,128]{1,0:T(8,128)(2,1)}, u32[]{:S(2)}) copy-start(bf16[64,128]{1,0:T(8,128)(2,1)} %get-tuple-element.41) | copy-start | bytes 49156
  121.2 2.2 %copy-start.19 = (bf16[64,128]{1,0:T(8,128)(2,1)S(1)}, bf16[64,128]{1,0:T(8,128)(2,1)}, u32[]{:S(2)}) copy-start(bf16[64,128]{1,0:T(8,128)(2,1)} %get-tuple-element.38) | copy-start | bytes 49156
  121.2 2.2 %copy-start.21 = (bf16[64,128]{1,0:T(8,128)(2,1)S(1)}, bf16[64,128]{1,0:T(8,128)(2,1)}, u32[]{:S(2)}) copy-start(bf16[64,128]{1,0:T(8,128)(2,1)} %get-tuple-element.34) | copy-start | bytes 49156
  121.2 15.0 %copy-start.16 = (bf16[64,128]{1,0:T(8,128)(2,1)S(1)}, bf16[64,128]{1,0:T(8,128)(2,1)}, u32[]{:S(2)}) copy-start(bf16[64,128]{1,0:T(8,128)(2,1)} %get-tuple-element.37) | copy-start | bytes 49156
  121.2 15.0 %copy-start.18 = (bf16[64,128]{1,0:T(8,128)(2,1)S(1)}, bf16[64,128]{1,0:T(8,128)(2,1)}, u32[]{:S(2)}) copy-start(bf16[64,128]{1,0:T(8,128)(2,1)} %get-tuple-element.33) | copy-start | bytes 49156
  121.4 17.9 %copy-start.15 = (bf16[64,128]{1,0:T(8,128)(2,1)S(1)}, bf16[64,128]{1,0:T(8,128)(2,1)}, u32[]{:S(2)}) copy-start(bf16[64,128]{1,0:T(8,128)(2,1)} %get-tuple-element.39) | copy-start | bytes 49156
  121.4 25.0 %collective-permute-start.23 = (bf16[3,352,512]{2,1,0:T(8,128)(2,1)S(1)}, bf16[3,352,512]{2,1,0:T(8,128)(2,1)S(1)}, u32[]{:S(2)}, u32[]{:S(2)}) collective-permute-start(bf16[3,352,512]{2,1,0:T(8,128)(2,1)S(1)} %fusion.30), channel_id=1, source_target_pairs={{0,1},{1,0},{2,3},{3,2},{4,5},{5,4},{6,7},{7,6},{8,9},{9,8},{10,11... | collective-permute-start | bytes 3244040 | tf_op jit(solution)/shard_map/ppermute | solution.py:27
  123.3 22.2 %copy-start.13 = (bf16[64,128]{1,0:T(8,128)(2,1)S(1)}, bf16[64,128]{1,0:T(8,128)(2,1)}, u32[]{:S(2)}) copy-start(bf16[64,128]{1,0:T(8,128)(2,1)} %get-tuple-element.35) | copy-start | bytes 49156
  123.3 22.2 %copy-start.14 = (bf16[64,128]{1,0:T(8,128)(2,1)S(1)}, bf16[64,128]{1,0:T(8,128)(2,1)}, u32[]{:S(2)}) copy-start(bf16[64,128]{1,0:T(8,128)(2,1)} %get-tuple-element.31) | copy-start | bytes 49156
  123.3 16.0 %collective-permute-start.13 = (bf16[128,1024]{1,0:T(8,128)(2,1)S(1)}, bf16[128,1024]{1,0:T(8,128)(2,1)S(1)}, u32[]{:S(2)}, u32[]{:S(2)}) collective-permute-start(bf16[128,1024]{1,0:T(8,128)(2,1)S(1)} %fusion.20), channel_id=1, source_target_pairs={{0,8},{1,9},{2,10},{3,11},{4,12},{5,13},{6,14},{7,15},{8,0},{9,1},... | collective-permute-start | bytes 786440 | tf_op jit(solution)/shard_map/ppermute | solution.py:27
  123.6 17.1 %collective-permute-start.19 = (bf16[128,1024]{1,0:T(8,128)(2,1)S(1)}, bf16[128,1024]{1,0:T(8,128)(2,1)S(1)}, u32[]{:S(2)}, u32[]{:S(2)}) collective-permute-start(bf16[128,1024]{1,0:T(8,128)(2,1)S(1)} %convolution_convert_fusion.5), channel_id=1, source_target_pairs={{0,4},{1,5},{2,6},{3,7},{4,0},{5,1},{6,2},{7,3},{8,12},{9,13},{10,... | collective-permute-start | bytes 786440 | tf_op jit(solution)/shard_map/ppermute | solution.py:27
  136.5 9.0 %collective-permute-start.21 = (bf16[128,1024]{1,0:T(8,128)(2,1)S(1)}, bf16[128,1024]{1,0:T(8,128)(2,1)S(1)}, u32[]{:S(2)}, u32[]{:S(2)}) collective-permute-start(bf16[128,1024]{1,0:T(8,128)(2,1)S(1)} %fusion.21), channel_id=1, source_target_pairs={{0,8},{1,9},{2,10},{3,11},{4,12},{5,13},{6,14},{7,15},{8,0},{9,1},... | collective-permute-start | bytes 786440 | tf_op jit(solution)/shard_map/ppermute | solution.py:27

commit v3 on v1

v3 whole, which is shorter than its diff:
```python
import functools

import jax
import jax.numpy as jnp
from jax import lax
from jax.experimental import pallas as pl
from jax.experimental.pallas import tpu as pltpu
from jax.sharding import PartitionSpec as P

mixing_factor = 73244475
contract_last = (((1,), (1,)), ((), ()))
contract_first = (((0,), (0,)), ((), ()))
f32 = jnp.float32
bf16 = jnp.bfloat16
vmem = pl.BlockSpec(memory_space=pltpu.VMEM)
smem = pl.BlockSpec(memory_space=pltpu.SMEM)
id_lanes = 128


def scramble(values):
    values = values ^ values >> 16 & 65535
    values = values * mixing_factor
    values = values ^ values >> 16 & 65535
    values = values * mixing_factor
    return values ^ values >> 16 & 65535


def flipped(values, axis, mask):
    return lax.ppermute(values, axis, [(i, i ^ mask) for i in range(lax.axis_size(axis))])


def after(values, *earlier):
    return lax.optimization_barrier((values,) + earlier)[0]


def called(kernel, out_shape, in_specs, flops, moved, scratch=()):
    return pl.pallas_call(
        kernel,
        out_shape=out_shape,
        in_specs=in_specs,
        out_specs=jax.tree.map(lambda _: vmem, out_shape),
        scratch_shapes=list(scratch),
        compiler_params=pltpu.CompilerParams(vmem_limit_bytes=40 * 1024 * 1024),
        cost_estimate=pl.CostEstimate(flops=flops, bytes_accessed=moved, transcendentals=0),
    )


def shape(dims, kind):
    return jax.ShapeDtypeStruct(dims, kind)


def prepare_kernel(top_count, plane_experts, capacity, place_ref, table_ref, slot_ref, gate_ref):
    planes, tok_rows = table_ref.shape[1:]
    token = lax.broadcasted_iota(jnp.int32, (tok_rows, tok_rows), 0)
    later = lax.broadcasted_iota(jnp.int32, (tok_rows, tok_rows), 1)
    earlier = jnp.where(token < later, 1.0, 0.0).astype(bf16)
    place = lax.broadcasted_iota(jnp.int32, (planes, tok_rows), 0)
    for column in range(plane_experts):
        expert = place_ref[0] ^ column
        named = jnp.zeros((planes, tok_rows), f32)
        gates = jnp.zeros((planes, tok_rows), f32)
        for k in range(top_count):
            hit = table_ref[k] == expert
            named = jnp.where(hit, 1.0, named)
            gates = jnp.where(hit, table_ref[top_count + k].astype(f32), gates)
        rank = jnp.dot(named.astype(bf16), earlier, preferred_element_type=f32).astype(jnp.int32)
        slot_ref[column] = jnp.where(named > 0.0, (place >> 1) * capacity + rank, -1)
        gate_ref[column] = gates * (1.0 / 64.0)


def choice_of(slot_ref, gate_ref, column, place, rows):
    row = lax.broadcasted_iota(jnp.int32, (rows, slot_ref.shape[2]), 0)
    hit = row == slot_ref[column, place : place + 1, :]
    if gate_ref is None:
        return jnp.where(hit, 1.0, 0.0).astype(bf16)
    return jnp.where(hit, gate_ref[column, place : place + 1, :], 0.0).astype(bf16)


def compact_kernel(half, with_ids, slot_ref, gate_ref, *refs):
    plane_experts, planes, tok_rows = slot_ref.shape
    count = planes // 2
    chunk_refs, out_refs = refs[:count], refs[count:]
    stacked = jnp.concatenate([chunk[...] for chunk in chunk_refs], axis=0)
    if with_ids:
        number = lax.broadcasted_iota(jnp.int32, (tok_rows, id_lanes), 0).astype(f32).astype(bf16)
        stacked = jnp.concatenate(
            [stacked, jnp.concatenate([number] * count, axis=0)], axis=1
        )
    for column in range(plane_experts):
        choice = jnp.concatenate(
            [
                choice_of(
                    slot_ref,
                    None if with_ids else gate_ref,
                    column,
                    2 * step + half,
                    out_refs[column].shape[0],
                )
                for step in range(count)
            ],
            axis=1,
        )
        out_refs[column][...] = jnp.dot(choice, stacked, preferred_element_type=f32).astype(bf16)


def combine_kernel(half, scaled, slot_ref, gate_ref, *refs):
    plane_experts, planes, _ = slot_ref.shape
    block_refs, out_refs = refs[:plane_experts], refs[plane_experts:]
    rows = block_refs[0].shape[0]
    stacked = jnp.concatenate([block[...] for block in block_refs], axis=0)
    for step in range(planes // 2):
        choice = jnp.concatenate(
            [
                choice_of(
                    slot_ref, gate_ref if scaled else None, column, 2 * step + half, rows
                )
                for column in range(plane_experts)
            ],
            axis=0,
        )
        out_refs[step][...] = lax.dot_general(
            choice, stacked, contract_first, preferred_element_type=f32
        ).astype(out_refs[step].dtype)


def assemble(weight_ref, piece_refs, place_ref, seq_count):
    _, half_width, width = piece_refs[0].shape
    for index, piece in enumerate(piece_refs):
        part = lax.rem(place_ref[1] + index % seq_count, seq_count)
        column = pl.multiple_of(part * width, width)
        row = index // seq_count * half_width
        for kind in range(3):
            weight_ref[kind, row : row + half_width, pl.ds(column, width)] = piece[kind]


def forward_kernel(seq_count, plane_experts, planes, capacity, place_ref, key_ref, *refs):
    blocks = 2 * plane_experts
    row_refs, refs = refs[:blocks], refs[blocks:]
    piece_refs, refs = refs[: 2 * seq_count], refs[2 * seq_count :]
    out_refs, (gate_ref, up_ref, hidden_ref, weight_ref) = refs[:blocks], refs[blocks:]
    assemble(weight_ref, piece_refs, place_ref, seq_count)
    _, hidden_width, model_width = weight_ref.shape
    half_width = hidden_width // 2
    rows = row_refs[0].shape[0]
    unit = lax.broadcasted_iota(jnp.int32, (1, hidden_width), 1)
    columns = place_ref[2] + jnp.where(
        unit < half_width, unit + place_ref[3], unit - half_width + place_ref[4]
    )
    spread_columns = columns * 40503
    base_hash = scramble(key_ref[0] ^ scramble(key_ref[1]))
    inputs = jnp.concatenate([row[:, :model_width] for row in row_refs], axis=0)
    gate_pre = lax.dot_general(inputs, weight_ref[0], contract_last, preferred_element_type=f32)
    up_pre = lax.dot_general(inputs, weight_ref[1], contract_last, preferred_element_type=f32)
    shift = capacity.bit_length() - 1
    mixed = []
    for index, row in enumerate(row_refs):
        column, half = index // 2, index % 2
        within = row[:, model_width : model_width + id_lanes].astype(f32).astype(jnp.int32)
        step = lax.broadcasted_iota(jnp.int32, within.shape, 0) >> shift
        source = place_ref[5] ^ ((2 * step + half) * (2 * plane_experts) + 2 * column)
        ids = (place_ref[6] + source) * place_ref[7] + within
        mixed.append(scramble(ids ^ base_hash))
    mixed = jnp.concatenate(mixed, axis=0)[:, 0:1]
    hashed = scramble(mixed ^ spread_columns)
    keep = jnp.where((hashed & 1023) >= 128, f32(8.0 / 7.0), f32(0.0))
    sigmoid_gate = jax.nn.sigmoid(gate_pre)
    silu_gate = gate_pre * sigmoid_gate
    hidden = (silu_gate * up_pre * keep).astype(bf16)
    gate_ref[...] = up_pre * sigmoid_gate * (1.0 + gate_pre * (1.0 - sigmoid_gate)) * keep
    up_ref[...] = silu_gate * keep
    hidden_ref[...] = hidden
    expert_out = jnp.dot(hidden, weight_ref[2], preferred_element_type=f32).astype(bf16)
    for index, out in enumerate(out_refs):
        out[...] = expert_out[index * rows : (index + 1) * rows]


def backward_kernel(seq_count, plane_experts, place_ref, *refs):
    blocks = 2 * plane_experts
    cot_refs, refs = refs[:blocks], refs[blocks:]
    piece_refs, refs = refs[: 2 * seq_count], refs[2 * seq_count :]
    (gate_ref, up_ref), refs = refs[:2], refs[2:]
    out_refs, (gate_grad_ref, up_grad_ref, weight_ref) = refs[:blocks], refs[blocks:]
    assemble(weight_ref, piece_refs, place_ref, seq_count)
    rows = cot_refs[0].shape[0]
    cot = jnp.concatenate([block[...] for block in cot_refs], axis=0)
    hidden_grad = lax.dot_general(cot, weight_ref[2], contract_last, preferred_element_type=f32)
    gate_grad = (hidden_grad * gate_ref[...]).astype(bf16)
    up_grad = (hidden_grad * up_ref[...]).astype(bf16)
    gate_grad_ref[...] = gate_grad
    up_grad_ref[...] = up_grad
    input_grad = (
        jnp.dot(gate_grad, weight_ref[0], preferred_element_type=f32)
        + jnp.dot(up_grad, weight_ref[1], preferred_element_type=f32)
    ).astype(bf16)
    for index, out in enumerate(out_refs):
        out[...] = input_grad[index * rows : (index + 1) * rows]


def weight_grad_kernel(plane_experts, seq_count, shift, place_ref, *refs):
    blocks = 2 * plane_experts
    row_refs, cot_refs, refs = refs[:blocks], refs[blocks : 2 * blocks], refs[2 * blocks :]
    (hidden_ref, gate_grad_ref, up_grad_ref), refs = refs[:3], refs[3:]
    added = refs[: seq_count - 1] if shift == 0 else ()
    out_refs = refs[len(added) :]
    width = out_refs[0].shape[2]
    part = lax.rem(place_ref[1] + shift, seq_count)
    lanes = pl.ds(pl.multiple_of(part * width, width), width)
    inputs = jnp.concatenate([row[:, lanes] for row in row_refs], axis=0)
    cot = jnp.concatenate([row[:, lanes] for row in cot_refs], axis=0)
    for kind, (left, right) in enumerate(
        ((gate_grad_ref, inputs), (up_grad_ref, inputs), (hidden_ref, cot))
    ):
        total = lax.dot_general(left[...], right, contract_first, preferred_element_type=f32)
        for part_ref in added:
            total = total + part_ref[kind].astype(f32)
        if shift:
            out_refs[0][kind] = total.astype(bf16)
        else:
            half_width = total.shape[0] // 2
            out_refs[0][kind] = total[:half_width]
            out_refs[1][kind] = total[half_width:].astype(bf16)


def local(tokens, cotangent, routes, gate_codes, dropout_key, w_gate, w_up, w_down):
    seq_count = lax.axis_size("seq")
    block_count = lax.axis_size("blk")
    seq_index = lax.axis_index("seq")
    blk_index = lax.axis_index("blk")
    tok_rows, model_width = tokens.shape
    top_count = routes.shape[1]
    expert_count = block_count // 2
    capacity = 2 * tok_rows * top_count // expert_count
    half_width = w_gate.shape[2]
    part_width = w_gate.shape[1]
    hidden_width = 2 * half_width
    planes = 1 << (block_count.bit_length() // 2)
    plane_experts = expert_count // planes
    plane_stride = 2 * plane_experts
    parity = blk_index % 2
    expert_here = blk_index // 2
    rows = planes // 2 * capacity
    slot_rows = 2 * plane_experts * rows
    blocks = 2 * plane_experts
    place = jnp.stack(
        [
            expert_here,
            seq_index,
            expert_here * hidden_width,
            parity * half_width,
            (1 - parity) * half_width,
            blk_index,
            seq_index * block_count,
            jnp.int32(tok_rows),
        ]
    ).astype(jnp.int32)

    table = jnp.concatenate([routes.T, gate_codes.T], axis=0)
    tables = jnp.stack(
        [table]
        + [flipped(table, "blk", step * plane_stride) for step in range(1, planes)],
        axis=1,
    )

    own_weights = jnp.stack([w_gate[0].T, w_up[0].T, w_down[0]])
    pair_weights = flipped(own_weights, "blk", 1)

    def shifted(values, shift):
        return lax.ppermute(
            values, "seq", [(i, (i + shift) % seq_count) for i in range(seq_count)]
        )

    pieces = [
        shifted(part, -shift) if shift else part
        for part in (own_weights, pair_weights)
        for shift in range(seq_count)
    ]

    def spread(part, starts):
        chunks = {0: part}
        step = planes // 2
        while step:
            for origin in sorted(chunks):
                sent = chunks[origin]
                if origin == 0 and step in starts:
                    sent = after(sent, starts[step])
                chunks[origin ^ step] = flipped(sent, "blk", step * plane_stride)
            step //= 2
        return [chunks[origin] for origin in range(planes)]

    token_chunks = spread(tokens, {})
    cot_chunks = spread(
        cotangent, {planes // 2: token_chunks[1], 1: token_chunks[planes // 2]}
    )

    slots, gates = called(
        functools.partial(prepare_kernel, top_count, plane_experts, capacity),
        (
            shape((plane_experts, planes, tok_rows), jnp.int32),
            shape((plane_experts, planes, tok_rows), f32),
        ),
        [smem, vmem],
        10**6,
        10**5,
    )(place, tables)

    def gathered(chunks, with_ids):
        width = model_width + (id_lanes if with_ids else 0)
        found = {}
        for half in (0, 1):
            picked = chunks[half::2]
            compact = called(
                functools.partial(compact_kernel, half, with_ids),
                [shape((rows, width), bf16)] * plane_experts,
                [vmem] * (2 + len(picked)),
                2 * plane_experts * rows * len(picked) * tok_rows * width,
                4 * rows * width,
            )(slots, gates, *picked)
            for column in range(plane_experts):
                found[column, half] = (
                    flipped(compact[column], "blk", 2 * column) if column else compact[0]
                )
        return [found[column, half] for column in range(plane_experts) for half in (0, 1)]

    row_blocks = gathered(token_chunks, True)
    cot_blocks = gathered(cot_chunks, False)

    weight_scratch = pltpu.VMEM((3, hidden_width, model_width), bf16)
    flops = 2 * slot_rows * hidden_width * model_width
    *out_blocks, gate_factor, up_factor, hidden = called(
        functools.partial(forward_kernel, seq_count, plane_experts, planes, capacity),
        [shape((rows, model_width), bf16)] * blocks
        + [shape((slot_rows, hidden_width), f32)] * 2
        + [shape((slot_rows, hidden_width), bf16)],
        [smem, smem] + [vmem] * (blocks + len(pieces)),
        3 * flops,
        10**7,
        [weight_scratch],
    )(place, dropout_key, *row_blocks, *pieces)
    *grad_blocks, gate_pre_grad, up_pre_grad = called(
        functools.partial(backward_kernel, seq_count, plane_experts),
        [shape((rows, model_width), bf16)] * blocks
        + [shape((slot_rows, hidden_width), bf16)] * 2,
        [smem] + [vmem] * (blocks + len(pieces) + 2),
        3 * flops,
        10**7,
        [weight_scratch],
    )(place, *cot_blocks, *pieces, gate_factor, up_factor)

    def brought_back(slot_blocks, scaled):
        sums = {}
        for half in (1, 0):
            held = [slot_blocks[half]] + [
                flipped(slot_blocks[2 * column + half], "blk", 2 * column)
                for column in range(1, plane_experts)
            ]
            combined = called(
                functools.partial(combine_kernel, half, scaled),
                [shape((tok_rows, model_width), bf16 if half else f32)] * (planes // 2),
                [vmem] * (2 + plane_experts),
                2 * plane_experts * rows * planes // 2 * tok_rows * model_width,
                4 * rows * model_width,
            )(slots, gates, *held)
            for step in range(planes // 2):
                sums[2 * step + half] = combined[step]
        step = 1
        while step < planes:
            for origin in sorted(sums, reverse=True):
                if origin & step:
                    sums[origin ^ step] = sums[origin ^ step] + flipped(
                        sums[origin].astype(bf16), "blk", step * plane_stride
                    ).astype(f32)
                    del sums[origin]
            step *= 2
        return sums[0].astype(bf16)

    layer_out = brought_back(out_blocks, True)
    tokens_grad = brought_back(grad_blocks, False)

    def weight_grads(shift, out_shape, added):
        return called(
            functools.partial(weight_grad_kernel, plane_experts, seq_count, shift),
            out_shape,
            [smem] + [vmem] * (2 * blocks + 3 + len(added)),
            3 * flops // seq_count,
            10**7,
        )(place, *row_blocks, *cot_blocks, hidden, gate_pre_grad, up_pre_grad, *added)

    arrived = [
        shifted(
            weight_grads(shift, [shape((3, hidden_width, part_width), bf16)], [])[0], shift
        )
        for shift in range(1, seq_count)
    ]
    own_sum, pair_sum = weight_grads(
        0,
        [shape((3, half_width, part_width), f32), shape((3, half_width, part_width), bf16)],
        arrived,
    )
    grads = (own_sum + flipped(pair_sum, "blk", 1).astype(f32)).astype(bf16)
    return (layer_out, tokens_grad, grads[0].T[None], grads[1].T[None], grads[2][None])


def solution(mesh):
    placed = (
        P(("seq", "blk"), None),
        P(("seq", "blk"), None),
        P(("seq", "blk"), None),
        P(("seq", "blk"), None),
        P(),
        P("blk", "seq", None),
        P("blk", "seq", None),
        P("blk", None, "seq"),
    )
    return jax.shard_map(
        local,
        mesh=mesh,
        in_specs=placed,
        out_specs=(
            P(("seq", "blk"), None),
            P(("seq", "blk"), None),
            P("blk", "seq", None),
            P("blk", "seq", None),
            P("blk", None, "seq"),
        ),
        check_vma=False,
    )
```

time: 186 us -> 156 us (0.84)
  blocking collectives: 56.4 us -> 0 us
  waiting for transfers between devices: 42.5 us -> 95.6 us
  matrix products: 32.4 us -> 0 us
  Pallas kernels: 0 us -> 21.1 us
  between operations: 16.7 us -> 0.86 us
  starting transfers between devices: 19 us -> 30.7 us
  local copies, waits for them, and re-layouts: 9.66 us -> 3.71 us
  other arithmetic: 9.01 us -> 3.51 us
    all_gather x1 -> x0, blocking collectives: 56.4 us -> none  [local(): tables = lax.all_gather(table, 'blk')]
    ppermute x18 -> x25, waiting for transfers between devices: 42.5 us -> 95.6 us  [flipped(): lax.ppermute(values, axis, [(i, i ^ mask) for i in range(lax.axis_size(ax...]
    dot_general x39 -> x0, matrix products: 32.4 us -> none  [the longest x16 14.6 us: compact(): jnp.dot(choice[place], chunks[place], preferred_element_type=jnp.float32)]
    pallas_call x0 -> x13, Pallas kernels: none -> 21.1 us  [the longest x1 5.48 us: local(): called(functools.partial(backward_kernel, seq_count, plane_experts), [sha...]
    ppermute x18 -> x25, starting transfers between devices: 18.9 us -> 30.6 us  [flipped(): lax.ppermute(values, axis, [(i, i ^ mask) for i in range(lax.axis_size(ax...]
    slice x6 -> x0, local copies, waits for them, and re-layouts: 3.5 us -> none  [the longest x1 2.71 us: local(): gate_mat, up_mat, down_mat = (weights[0], weights[1], weights[2])]
    another operation x4 -> x2, other arithmetic: 4.47 us -> 1.39 us  [the longest x1 1.37 us: local(): own_weights = jnp.stack([w_gate[0].T, w_up[0].T, w_down[0]])]
    squeeze x6 -> x0, local copies, waits for them, and re-layouts: 2.59 us -> none  [the longest x2 1.28 us: brought_back(): choices[column][place]]
  transfers between devices with their start and end apart: 20 -> 28, of which waited for: 8 -> 16; matrix products, arithmetic and copies ran while one was open for 19% -> 1% of each run, Pallas kernels for 0% -> 9%
where the time goes in v3:
time: 156 us
  waiting for transfers between devices  95.6 us (61%)
  starting transfers between devices  30.7 us (20%)
  Pallas kernels  21.1 us (14%)
  local copies, waits for them, and re-layouts  3.71 us (2%)
  other arithmetic  3.51 us (2%)
    ppermute x25, waiting for transfers between devices, flipped(): lax.ppermute(values, axis, [(i, i ^ mask) for i in range(lax.axis_size(ax...  95.6 us
    ppermute x25, starting transfers between devices, flipped(): lax.ppermute(values, axis, [(i, i ^ mask) for i in range(lax.axis_size(ax...  30.6 us
    pallas_call x1, Pallas kernels, local(): called(functools.partial(backward_kernel, seq_count, plane_experts), [sha...  5.48 us
    pallas_call x4, Pallas kernels, gathered(): called(functools.partial(compact_kernel, half, with_ids), [shape((rows, w...  5.11 us
    pallas_call x1, Pallas kernels, local(): called(functools.partial(forward_kernel, seq_count, plane_experts, planes...  4.84 us
    pallas_call x2, Pallas kernels, weight_grads(): called(functools.partial(weight_grad_kernel, plane_experts, seq_count, sh...  3.71 us
  transfers between devices with their start and end apart: 28, of which 16 were waited for; matrix products, arithmetic and copies ran while one was open for 1% of the time, Pallas kernels for 9%

profile of v3, /device:TPU:0, one launch (start us, length us, event | category | flops | bytes accessed | tf_op | source)
XLA Modules:
  0.0 155.5 jit_solution(8971409316963750608)
XLA Ops:
  0.7 1.4 pad_maximum_fusion.refs_4_
  2.1 3.0 %collective-permute-start.9 = (bf16[3,352,512]{2,1,0:T(8,128)(2,1)S(1)}, bf16[3,352,512]{2,1,0:T(8,128)(2,1)S(1)}, u32[]{:S(2)}, u32[]{:S(2)}) collective-permute-start(bf16[3,352,512]{2,1,0:T(8,128)(2,1)S(1)} %pad_maximum_fusion.refs_4_), channel_id=1, source_target_pairs={{0,1},{1,0},{2,3},{3,2},{4,5},{5,4},{6,7},{7,6},{8,9},{9,8},{10,11... | collective-permute-start | bytes 3244040 | tf_op jit(solution)/shard_map/ppermute | solution.py:29
  5.1 23.9 %collective-permute-done.9.refs_6_ = bf16[3,352,512]{2,1,0:T(8,128)(2,1)S(1)} collective-permute-done((bf16[3,352,512]{2,1,0:T(8,128)(2,1)S(1)}, bf16[3,352,512]{2,1,0:T(8,128)(2,1)S(1)}, u32[]{:S(2)}, u32[]{:S(2)}) %collective-permute-start.9) | collective-permute-done | bytes 1081376 | tf_op jit(solution)/shard_map/ppermute | solution.py:29
  28.9 1.8 %collective-permute-start.4 = (bf16[128,1024]{1,0:T(8,128)(2,1)S(1)}, bf16[128,1024]{1,0:T(8,128)(2,1)S(1)}, u32[]{:S(2)}, u32[]{:S(2)}) collective-permute-start(bf16[128,1024]{1,0:T(8,128)(2,1)S(1)} %copy-done.1), channel_id=1, source_target_pairs={{0,4},{1,5},{2,6},{3,7},{4,0},{5,1},{6,2},{7,3},{8,12},{9,13},{10,... | collective-permute-start | bytes 786440 | tf_op jit(solution)/shard_map/ppermute | solution.py:29
  30.7 2.6 %collective-permute-start.3 = (bf16[128,1024]{1,0:T(8,128)(2,1)S(1)}, bf16[128,1024]{1,0:T(8,128)(2,1)}, u32[]{:S(2)}, u32[]{:S(2)}) collective-permute-start(bf16[128,1024]{1,0:T(8,128)(2,1)S(1)} %copy-done.1), channel_id=1, source_target_pairs={{0,8},{1,9},{2,10},{3,11},{4,12},{5,13},{6,14},{7,15},{8,0},{9,1},... | collective-permute-start | bytes 786440 | tf_op jit(solution)/shard_map/ppermute | solution.py:29
  33.3 9.9 %collective-permute-done.4.refs_0_ = bf16[128,1024]{1,0:T(8,128)(2,1)S(1)} collective-permute-done((bf16[128,1024]{1,0:T(8,128)(2,1)S(1)}, bf16[128,1024]{1,0:T(8,128)(2,1)S(1)}, u32[]{:S(2)}, u32[]{:S(2)}) %collective-permute-start.4) | collective-permute-done | bytes 262176 | tf_op jit(solution)/shard_map/ppermute | solution.py:29
  43.2 0.7 copy-done.3
  43.9 0.7 collective-permute-start.16
  44.7 1.2 collective-permute-done.3.refs_1_
  45.9 1.3 collective-permute-start.5
  47.2 1.3 collective-permute-start.2
  48.4 10.2 %collective-permute-done.2 = s32[4,128]{1,0:T(4,128)S(1)} collective-permute-done((s32[4,128]{1,0:T(4,128)S(1)}, s32[4,128]{1,0:T(4,128)S(1)}, u32[]{:S(2)}, u32[]{:S(2)}) %collective-permute-start.2) | collective-permute-done | bytes 2080 | tf_op jit(solution)/shard_map/ppermute | solution.py:29
  58.7 0.6 collective-permute-start.1
  59.2 3.9 %collective-permute-done.1 = s32[4,128]{1,0:T(4,128)S(1)} collective-permute-done((s32[4,128]{1,0:T(4,128)S(1)}, s32[4,128]{1,0:T(4,128)S(1)}, u32[]{:S(2)}, u32[]{:S(2)}) %collective-permute-start.1) | collective-permute-done | bytes 2080 | tf_op jit(solution)/shard_map/ppermute | solution.py:29
  63.1 0.5 collective-permute-start
  63.7 3.1 %collective-permute-done = s32[4,128]{1,0:T(4,128)S(1)} collective-permute-done((s32[4,128]{1,0:T(4,128)S(1)}, s32[4,128]{1,0:T(4,128)S(1)}, u32[]{:S(2)}, u32[]{:S(2)}) %collective-permute-start) | collective-permute-done | bytes 2080 | tf_op jit(solution)/shard_map/ppermute | solution.py:29
  66.7 0.5 collective-permute-start.17
  67.3 0.1 stack.55.place_ref
  67.4 0.7 shard_map.119
  68.0 1.0 copy-done.2
  69.0 1.3 shard_map.120
  70.3 1.6 %collective-permute-start.6 = (bf16[128,1152]{1,0:T(8,128)(2,1)S(1)}, bf16[128,1152]{1,0:T(8,128)(2,1)S(1)}, u32[]{:S(2)}, u32[]{:S(2)}) collective-permute-start(bf16[128,1152]{1,0:T(8,128)(2,1)S(1)} %get-tuple-element.44), channel_id=1, source_target_pairs={{0,2},{1,3},{2,0},{3,1},{4,6},{5,7},{6,4},{7,5},{8,10},{9,11},{10,... | collective-permute-start | bytes 884744 | tf_op jit(solution)/shard_map/ppermute | solution.py:29
  71.9 1.5 collective-permute-start.18
  73.4 0.9 copy-done.4
  74.4 1.3 shard_map.121
  75.7 1.6 %collective-permute-start.7 = (bf16[128,1152]{1,0:T(8,128)(2,1)S(1)}, bf16[128,1152]{1,0:T(8,128)(2,1)S(1)}, u32[]{:S(2)}, u32[]{:S(2)}) collective-permute-start(bf16[128,1152]{1,0:T(8,128)(2,1)S(1)} %get-tuple-element.45), channel_id=1, source_target_pairs={{0,2},{1,3},{2,0},{3,1},{4,6},{5,7},{6,4},{7,5},{8,10},{9,11},{10,... | collective-permute-start | bytes 884744 | tf_op jit(solution)/shard_map/ppermute | solution.py:29
  77.3 1.3 shard_map.125
  78.5 0.2 collective-permute-done.18.refs_1_
  78.7 1.5 collective-permute-start.19
  80.2 1.3 shard_map.126
  81.5 0.6 collective-permute-start.20
  82.1 4.3 %collective-permute-done.7.refs_3_ = bf16[128,1152]{1,0:T(8,128)(2,1)S(1)} collective-permute-done((bf16[128,1152]{1,0:T(8,128)(2,1)S(1)}, bf16[128,1152]{1,0:T(8,128)(2,1)S(1)}, u32[]{:S(2)}, u32[]{:S(2)}) %collective-permute-start.7) | collective-permute-done | bytes 294944 | tf_op jit(solution)/shard_map/ppermute | solution.py:29
  86.4 4.8 %shard_map.122 = (bf16[128,1024]{1,0:T(8,128)(2,1)S(1)}, bf16[128,1024]{1,0:T(8,128)(2,1)S(1)}, bf16[128,1024]{1,0:T(8,128)(2,1)S(1)}, bf16[128,1024]{1,0:T(8,12...) custom-call(s32[8]{0:T(128)S(1)} %stack.55.place_ref, s32[2]{0:T(128)S(1)} %copy-done.5, ...), custom_call_target="tpu_custom_call" | custom-call | flops 2214592512 | bytes 10000000 | tf_op jit(solution)/shard_map/pallas_call | solution.py:329
  91.2 0.6 collective-permute-done.19.refs_2_.refs_6_
  91.9 2.8 %collective-permute-done.20.refs_3_.refs_7_ = bf16[128,1024]{1,0:T(8,128)(2,1)S(1)} collective-permute-done((bf16[128,1024]{1,0:T(8,128)(2,1)S(1)}, bf16[128,1024]{1,0:T(8,128)(2,1)S(1)}, u32[]{:S(2)}, u32[]{:S(2)}) %collective-permute-start.20) | collective-permute-done | bytes 262176 | tf_op jit(solution)/shard_map/ppermute | solution.py:29
  94.7 5.5 %shard_map.127 = (bf16[128,1024]{1,0:T(8,128)(2,1)S(1)}, bf16[128,1024]{1,0:T(8,128)(2,1)S(1)}, bf16[128,1024]{1,0:T(8,128)(2,1)S(1)}, bf16[128,1024]{1,0:T(8,12...) custom-call(s32[8]{0:T(128)S(1)} %stack.55.place_ref, ...), custom_call_target="tpu_custom_call" | custom-call | flops 2214592512 | bytes 10000000 | tf_op jit(solution)/shard_map/pallas_call | solution.py:339
  100.2 1.9 %shard_map.130 = bf16[3,704,512]{2,1,0:T(8,128)(2,1)S(1)} custom-call(s32[8]{0:T(128)S(1)} %stack.55.place_ref, bf16[128,1152]{1,0:T(8,128)(2,1)S(1)} %get-tuple-element.42.refs_0_, bf16[128,1152]{1,0:T(8,128)(2,1)S(1)} %get-tuple-element.43.refs_1_, bf16[128,1152]{1,0:T(8,128)(2,1)S(1)} %collective-permute-done.6.refs_2_, ...), custom_call_target="tpu_custom_call" | custom-call | flops 1107296256 | bytes 10000000 | tf_op jit(solution)/shard_map/pallas_call | solution.py:380
  102.0 0.1 collective-permute-start.26
  102.1 0.9 collective-permute-start.12
  103.0 1.2 collective-permute-start.22
  104.2 0.8 collective-permute-start.11
  105.0 6.2 %collective-permute-done.12.refs_1_ = bf16[128,1024]{1,0:T(8,128)(2,1)S(1)} collective-permute-done((bf16[128,1024]{1,0:T(8,128)(2,1)S(1)}, bf16[128,1024]{1,0:T(8,128)(2,1)S(1)}, u32[]{:S(2)}, u32[]{:S(2)}) %collective-permute-start.12) | collective-permute-done | bytes 262176 | tf_op jit(solution)/shard_map/ppermute | solution.py:29
  111.3 0.3 shard_map.124
  111.6 1.6 collective-permute-start.14
  113.2 1.9 %shard_map.131 = (f32[3,352,512]{2,1,0:T(8,128)S(1)}, bf16[3,352,512]{2,1,0:T(8,128)(2,1)S(1)}) custom-call(s32[8]{0:T(128)S(1)} %stack.55.place_ref, bf16[128,1152]{1,0:T(8,128)(2,1)S(1)} %get-tuple-element.42.refs_0_, bf16[128,1152]{1,0:T(8,128)(2,1)S(1)} %get-tuple-element.43.refs_1_, bf16[128,1152]{1,0:T(8,128)(2,1)S(1)} %collective-permute-done.6.refs_2_, ...), custom_call_target="tpu_custom_call" | custom-call | flops 1107296256 | bytes 10000000 | tf_op jit(solution)/shard_map/pallas_call | solution.py:380
  115.0 1.6 %collective-permute-start.27 = (bf16[3,352,512]{2,1,0:T(8,128)(2,1)S(1)}, bf16[3,352,512]{2,1,0:T(8,128)(2,1)S(1)}, u32[]{:S(2)}, u32[]{:S(2)}) collective-permute-start(bf16[3,352,512]{2,1,0:T(8,128)(2,1)S(1)} %get-tuple-element.74), channel_id=1, source_target_pairs={{0,1},{1,0},{2,3},{3,2},{4,5},{5,4},{6,7},{7,6},{8,9},{9,8},{10,11... | collective-permute-start | bytes 3244040 | tf_op jit(solution)/shard_map/ppermute | solution.py:29
  116.6 0.5 collective-permute-start.21
  117.1 1.3 collective-permute-start.13
  118.4 0.3 shard_map.129
  118.7 3.8 %collective-permute-done.11.refs_1_ = bf16[128,1024]{1,0:T(8,128)(2,1)S(1)} collective-permute-done((bf16[128,1024]{1,0:T(8,128)(2,1)S(1)}, bf16[128,1024]{1,0:T(8,128)(2,1)S(1)}, u32[]{:S(2)}, u32[]{:S(2)}) %collective-permute-start.11) | collective-permute-done | bytes 262176 | tf_op jit(solution)/shard_map/ppermute | solution.py:29
  122.5 1.5 collective-permute-start.24
  124.0 0.3 shard_map.123
  124.3 0.6 collective-permute-start.23
  125.0 2.7 %collective-permute-done.21.refs_1_ = bf16[128,1024]{1,0:T(8,128)(2,1)S(1)} collective-permute-done((bf16[128,1024]{1,0:T(8,128)(2,1)S(1)}, bf16[128,1024]{1,0:T(8,128)(2,1)S(1)}, u32[]{:S(2)}, u32[]{:S(2)}) %collective-permute-start.21) | collective-permute-done | bytes 262176 | tf_op jit(solution)/shard_map/ppermute | solution.py:29
  127.7 1.6 %collective-permute-start.15 = (bf16[128,1024]{1,0:T(8,128)(2,1)S(1)}, bf16[128,1024]{1,0:T(8,128)(2,1)S(1)}, u32[]{:S(2)}, u32[]{:S(2)}) collective-permute-start(bf16[128,1024]{1,0:T(8,128)(2,1)S(1)} %add_convert_fusion.4), channel_id=1, source_target_pairs={{0,8},{1,9},{2,10},{3,11},{4,12},{5,13},{6,14},{7,15},{8,0},{9,1},... | collective-permute-start | bytes 786440 | tf_op jit(solution)/shard_map/ppermute | solution.py:29
  129.2 0.3 shard_map.128
  129.6 7.7 %collective-permute-done.24 = bf16[128,1024]{1,0:T(8,128)(2,1)S(1)} collective-permute-done((bf16[128,1024]{1,0:T(8,128)(2,1)S(1)}, bf16[128,1024]{1,0:T(8,128)(2,1)S(1)}, u32[]{:S(2)}, u32[]{:S(2)}) %collective-permute-start.24) | collective-permute-done | bytes 262176 | tf_op jit(solution)/shard_map/ppermute | solution.py:29
  137.3 0.1 collective-permute-start.25
  137.4 11.6 %collective-permute-done.15 = bf16[128,1024]{1,0:T(8,128)(2,1)S(1)} collective-permute-done((bf16[128,1024]{1,0:T(8,128)(2,1)S(1)}, bf16[128,1024]{1,0:T(8,128)(2,1)S(1)}, u32[]{:S(2)}, u32[]{:S(2)}) %collective-permute-start.15) | collective-permute-done | bytes 262176 | tf_op jit(solution)/shard_map/ppermute | solution.py:29
  149.0 0.8 add_convert_fusion.3
  149.8 3.5 %collective-permute-done.25 = bf16[128,1024]{1,0:T(8,128)(2,1)S(1)} collective-permute-done((bf16[128,1024]{1,0:T(8,128)(2,1)S(1)}, bf16[128,1024]{1,0:T(8,128)(2,1)S(1)}, u32[]{:S(2)}, u32[]{:S(2)}) %collective-permute-start.25) | collective-permute-done | bytes 262176 | tf_op jit(solution)/shard_map/ppermute | solution.py:29
  153.3 0.8 add_convert_fusion.1
  154.2 0.4 add_convert_fusion
  154.5 1.0 fusion
  (31 shorter events, 0.2 us)
Async XLA Ops:
  0.6 28.3 %copy-start.1 = (bf16[128,1024]{1,0:T(8,128)(2,1)S(1)}, bf16[128,1024]{1,0:T(8,128)(2,1)}, u32[]{:S(2)}) copy-start(bf16[128,1024]{1,0:T(8,128)(2,1)} %refs_0_.2) | copy-start | bytes 786436
  0.6 43.3 %copy-start = (bf16[128,1024]{1,0:T(8,128)(2,1)S(1)}, bf16[128,1024]{1,0:T(8,128)(2,1)}, u32[]{:S(2)}) copy-start(bf16[128,1024]{1,0:T(8,128)(2,1)} %refs_0_.3) | copy-start | bytes 786436
  0.7 46.5 %copy-start.6 = (s32[128,2]{0,1:T(2,128)S(1)}, s32[128,2]{0,1:T(2,128)}, u32[]{:S(2)}) copy-start(s32[128,2]{0,1:T(2,128)} %param.11) | copy-start | bytes 3076
  0.7 46.5 %copy-start.7 = (s32[128,2]{0,1:T(2,128)S(1)}, s32[128,2]{0,1:T(2,128)}, u32[]{:S(2)}) copy-start(s32[128,2]{0,1:T(2,128)} %param.10) | copy-start | bytes 3076
  2.1 26.9 %collective-permute-start.9 = (bf16[3,352,512]{2,1,0:T(8,128)(2,1)S(1)}, bf16[3,352,512]{2,1,0:T(8,128)(2,1)S(1)}, u32[]{:S(2)}, u32[]{:S(2)}) collective-permute-start(bf16[3,352,512]{2,1,0:T(8,128)(2,1)S(1)} %pad_maximum_fusion.refs_4_), channel_id=1, source_target_pairs={{0,1},{1,0},{2,3},{3,2},{4,5},{5,4},{6,7},{7,6},{8,9},{9,8},{10,11... | collective-permute-start | bytes 3244040 | tf_op jit(solution)/shard_map/ppermute | solution.py:29
  5.1 81.3 %collective-permute-start.8 = (bf16[3,352,512]{2,1,0:T(8,128)(2,1)S(1)}, bf16[3,352,512]{2,1,0:T(8,128)(2,1)S(1)}, u32[]{:S(2)}, u32[]{:S(2)}) collective-permute-start(bf16[3,352,512]{2,1,0:T(8,128)(2,1)S(1)} %pad_maximum_fusion.refs_4_), channel_id=1, source_target_pairs={{0,16},{16,0},{1,17},{17,1},{2,18},{18,2},{3,19},{19,3},{4,20},{20... | collective-permute-start | bytes 3244040 | tf_op jit(solution)/shard_map/ppermute | solution.py:268
  28.9 57.5 %collective-permute-start.10 = (bf16[3,352,512]{2,1,0:T(8,128)(2,1)S(1)}, bf16[3,352,512]{2,1,0:T(8,128)(2,1)}, u32[]{:S(2)}, u32[]{:S(2)}) collective-permute-start(bf16[3,352,512]{2,1,0:T(8,128)(2,1)S(1)} %collective-permute-done.9.refs_6_), channel_id=1, source_target_pairs={{0,16},{16,0},{1,17},{17,1},{2,18},{18,2},{3,19},{19,3},{4,20},{20... | collective-permute-start | bytes 3244040 | tf_op jit(solution)/shard_map/ppermute | solution.py:268
  28.9 14.3 %collective-permute-start.4 = (bf16[128,1024]{1,0:T(8,128)(2,1)S(1)}, bf16[128,1024]{1,0:T(8,128)(2,1)S(1)}, u32[]{:S(2)}, u32[]{:S(2)}) collective-permute-start(bf16[128,1024]{1,0:T(8,128)(2,1)S(1)} %copy-done.1), channel_id=1, source_target_pairs={{0,4},{1,5},{2,6},{3,7},{4,0},{5,1},{6,2},{7,3},{8,12},{9,13},{10,... | collective-permute-start | bytes 786440 | tf_op jit(solution)/shard_map/ppermute | solution.py:29
  30.7 15.1 %collective-permute-start.3 = (bf16[128,1024]{1,0:T(8,128)(2,1)S(1)}, bf16[128,1024]{1,0:T(8,128)(2,1)}, u32[]{:S(2)}, u32[]{:S(2)}) collective-permute-start(bf16[128,1024]{1,0:T(8,128)(2,1)S(1)} %copy-done.1), channel_id=1, source_target_pairs={{0,8},{1,9},{2,10},{3,11},{4,12},{5,13},{6,14},{7,15},{8,0},{9,1},... | collective-permute-start | bytes 786440 | tf_op jit(solution)/shard_map/ppermute | solution.py:29
  43.2 0.7 copy-start.3
  43.9 28.0 %collective-permute-start.16 = (bf16[128,1024]{1,0:T(8,128)(2,1)S(1)}, bf16[128,1024]{1,0:T(8,128)(2,1)}, u32[]{:S(2)}, u32[]{:S(2)}) collective-permute-start(bf16[128,1024]{1,0:T(8,128)(2,1)S(1)} %copy-done), channel_id=1, source_target_pairs={{0,8},{1,9},{2,10},{3,11},{4,12},{5,13},{6,14},{7,15},{8,0},{9,1},... | collective-permute-start | bytes 786440 | tf_op jit(solution)/shard_map/ppermute | solution.py:29
  45.9 24.5 %collective-permute-start.5 = (bf16[128,1024]{1,0:T(8,128)(2,1)}, bf16[128,1024]{1,0:T(8,128)(2,1)}, u32[]{:S(2)}, u32[]{:S(2)}) collective-permute-start(bf16[128,1024]{1,0:T(8,128)(2,1)} %collective-permute-done.3.refs_1_), channel_id=1, source_target_pairs={{0,4},{1,5},{2,6},{3,7},{4,0},{5,1},{6,2},{7,3},{8,12},{9,13},{10,... | collective-permute-start | bytes 786440 | tf_op jit(solution)/shard_map/ppermute | solution.py:29
  47.2 11.5 %collective-permute-start.2 = (s32[4,128]{1,0:T(4,128)S(1)}, s32[4,128]{1,0:T(4,128)S(1)}, u32[]{:S(2)}, u32[]{:S(2)}) collective-permute-start(s32[4,128]{1,0:T(4,128)S(1)} %pad_add_fusion.1), channel_id=1, source_target_pairs={{0,12},{1,13},{2,14},{3,15},{4,8},{5,9},{6,10},{7,11},{8,4},{9,5},... | collective-permute-start | bytes 6152 | tf_op jit(solution)/shard_map/ppermute | solution.py:29
  58.7 4.5 %collective-permute-start.1 = (s32[4,128]{1,0:T(4,128)S(1)}, s32[4,128]{1,0:T(4,128)S(1)}, u32[]{:S(2)}, u32[]{:S(2)}) collective-permute-start(s32[4,128]{1,0:T(4,128)S(1)} %pad_add_fusion.1), channel_id=1, source_target_pairs={{0,8},{1,9},{2,10},{3,11},{4,12},{5,13},{6,14},{7,15},{8,0},{9,1},... | collective-permute-start | bytes 6152 | tf_op jit(solution)/shard_map/ppermute | solution.py:29
  63.1 3.6 %collective-permute-start = (s32[4,128]{1,0:T(4,128)S(1)}, s32[4,128]{1,0:T(4,128)S(1)}, u32[]{:S(2)}, u32[]{:S(2)}) collective-permute-start(s32[4,128]{1,0:T(4,128)S(1)} %pad_add_fusion.1), channel_id=1, source_target_pairs={{0,4},{1,5},{2,6},{3,7},{4,0},{5,1},{6,2},{7,3},{8,12},{9,13},{10,... | collective-permute-start | bytes 6152 | tf_op jit(solution)/shard_map/ppermute | solution.py:29
  66.7 8.9 %collective-permute-start.17 = (bf16[128,1024]{1,0:T(8,128)(2,1)S(1)}, bf16[128,1024]{1,0:T(8,128)(2,1)}, u32[]{:S(2)}, u32[]{:S(2)}) collective-permute-start(bf16[128,1024]{1,0:T(8,128)(2,1)S(1)} %copy-done), channel_id=1, source_target_pairs={{0,4},{1,5},{2,6},{3,7},{4,0},{5,1},{6,2},{7,3},{8,12},{9,13},{10,... | collective-permute-start | bytes 786440 | tf_op jit(solution)/shard_map/ppermute | solution.py:29
  68.0 1.0 copy-start.2
  69.0 17.4 %copy-start.5 = (s32[2]{0:T(128)S(1)}, s32[2]{0:T(128)}, u32[]{:S(2)}) copy-start(s32[2]{0:T(128)} %key_ref.1) | copy-start | bytes 28
  70.3 11.2 %collective-permute-start.6 = (bf16[128,1152]{1,0:T(8,128)(2,1)S(1)}, bf16[128,1152]{1,0:T(8,128)(2,1)S(1)}, u32[]{:S(2)}, u32[]{:S(2)}) collective-permute-start(bf16[128,1152]{1,0:T(8,128)(2,1)S(1)} %get-tuple-element.44), channel_id=1, source_target_pairs={{0,2},{1,3},{2,0},{3,1},{4,6},{5,7},{6,4},{7,5},{8,10},{9,11},{10,... | collective-permute-start | bytes 884744 | tf_op jit(solution)/shard_map/ppermute | solution.py:29
  71.9 6.8 %collective-permute-start.18 = (bf16[128,1024]{1,0:T(8,128)(2,1)}, bf16[128,1024]{1,0:T(8,128)(2,1)S(1)}, u32[]{:S(2)}, u32[]{:S(2)}) collective-permute-start(bf16[128,1024]{1,0:T(8,128)(2,1)} %collective-permute-done.16.refs_1_), channel_id=1, source_target_pairs={{0,4},{1,5},{2,6},{3,7},{4,0},{5,1},{6,2},{7,3},{8,12},{9,13},{10,... | collective-permute-start | bytes 786440 | tf_op jit(solution)/shard_map/ppermute | solution.py:29
  73.4 0.9 copy-start.4
  75.7 10.7 %collective-permute-start.7 = (bf16[128,1152]{1,0:T(8,128)(2,1)S(1)}, bf16[128,1152]{1,0:T(8,128)(2,1)S(1)}, u32[]{:S(2)}, u32[]{:S(2)}) collective-permute-start(bf16[128,1152]{1,0:T(8,128)(2,1)S(1)} %get-tuple-element.45), channel_id=1, source_target_pairs={{0,2},{1,3},{2,0},{3,1},{4,6},{5,7},{6,4},{7,5},{8,10},{9,11},{10,... | collective-permute-start | bytes 884744 | tf_op jit(solution)/shard_map/ppermute | solution.py:29
  78.7 13.1 %collective-permute-start.19 = (bf16[128,1024]{1,0:T(8,128)(2,1)S(1)}, bf16[128,1024]{1,0:T(8,128)(2,1)S(1)}, u32[]{:S(2)}, u32[]{:S(2)}) collective-permute-start(bf16[128,1024]{1,0:T(8,128)(2,1)S(1)} %get-tuple-element.58), channel_id=1, source_target_pairs={{0,2},{1,3},{2,0},{3,1},{4,6},{5,7},{6,4},{7,5},{8,10},{9,11},{10,... | collective-permute-start | bytes 786440 | tf_op jit(solution)/shard_map/ppermute | solution.py:29
  81.5 13.2 %collective-permute-start.20 = (bf16[128,1024]{1,0:T(8,128)(2,1)S(1)}, bf16[128,1024]{1,0:T(8,128)(2,1)S(1)}, u32[]{:S(2)}, u32[]{:S(2)}) collective-permute-start(bf16[128,1024]{1,0:T(8,128)(2,1)S(1)} %get-tuple-element.59), channel_id=1, source_target_pairs={{0,2},{1,3},{2,0},{3,1},{4,6},{5,7},{6,4},{7,5},{8,10},{9,11},{10,... | collective-permute-start | bytes 786440 | tf_op jit(solution)/shard_map/ppermute | solution.py:29
  102.0 11.1 %collective-permute-start.26 = (bf16[3,704,512]{2,1,0:T(8,128)(2,1)S(1)}, bf16[3,704,512]{2,1,0:T(8,128)(2,1)S(1)}, u32[]{:S(2)}, u32[]{:S(2)}) collective-permute-start(bf16[3,704,512]{2,1,0:T(8,128)(2,1)S(1)} %shard_map.130), channel_id=1, source_target_pairs={{0,16},{16,0},{1,17},{17,1},{2,18},{18,2},{3,19},{19,3},{4,20},{20... | collective-permute-start | bytes 6488072 | tf_op jit(solution)/shard_map/ppermute | solution.py:268
  102.1 9.2 %collective-permute-start.12 = (bf16[128,1024]{1,0:T(8,128)(2,1)S(1)}, bf16[128,1024]{1,0:T(8,128)(2,1)S(1)}, u32[]{:S(2)}, u32[]{:S(2)}) collective-permute-start(bf16[128,1024]{1,0:T(8,128)(2,1)S(1)} %get-tuple-element.50), channel_id=1, source_target_pairs={{0,2},{1,3},{2,0},{3,1},{4,6},{5,7},{6,4},{7,5},{8,10},{9,11},{10,... | collective-permute-start | bytes 786440 | tf_op jit(solution)/shard_map/ppermute | solution.py:29
  103.0 14.1 %collective-permute-start.22 = (bf16[128,1024]{1,0:T(8,128)(2,1)S(1)}, bf16[128,1024]{1,0:T(8,128)(2,1)S(1)}, u32[]{:S(2)}, u32[]{:S(2)}) collective-permute-start(bf16[128,1024]{1,0:T(8,128)(2,1)S(1)} %get-tuple-element.66), channel_id=1, source_target_pairs={{0,2},{1,3},{2,0},{3,1},{4,6},{5,7},{6,4},{7,5},{8,10},{9,11},{10,... | collective-permute-start | bytes 786440 | tf_op jit(solution)/shard_map/ppermute | solution.py:29
  104.2 18.3 %collective-permute-start.11 = (bf16[128,1024]{1,0:T(8,128)(2,1)S(1)}, bf16[128,1024]{1,0:T(8,128)(2,1)S(1)}, u32[]{:S(2)}, u32[]{:S(2)}) collective-permute-start(bf16[128,1024]{1,0:T(8,128)(2,1)S(1)} %get-tuple-element.47), channel_id=1, source_target_pairs={{0,2},{1,3},{2,0},{3,1},{4,6},{5,7},{6,4},{7,5},{8,10},{9,11},{10,... | collective-permute-start | bytes 786440 | tf_op jit(solution)/shard_map/ppermute | solution.py:29
  111.6 12.7 %collective-permute-start.14 = (bf16[128,1024]{1,0:T(8,128)(2,1)S(1)}, bf16[128,1024]{1,0:T(8,128)(2,1)S(1)}, u32[]{:S(2)}, u32[]{:S(2)}) collective-permute-start(bf16[128,1024]{1,0:T(8,128)(2,1)S(1)} %get-tuple-element.53), channel_id=1, source_target_pairs={{0,4},{1,5},{2,6},{3,7},{4,0},{5,1},{6,2},{7,3},{8,12},{9,13},{10,... | collective-permute-start | bytes 786440 | tf_op jit(solution)/shard_map/ppermute | solution.py:29
  115.0 39.1 %collective-permute-start.27 = (bf16[3,352,512]{2,1,0:T(8,128)(2,1)S(1)}, bf16[3,352,512]{2,1,0:T(8,128)(2,1)S(1)}, u32[]{:S(2)}, u32[]{:S(2)}) collective-permute-start(bf16[3,352,512]{2,1,0:T(8,128)(2,1)S(1)} %get-tuple-element.74), channel_id=1, source_target_pairs={{0,1},{1,0},{2,3},{3,2},{4,5},{5,4},{6,7},{7,6},{8,9},{9,8},{10,11... | collective-permute-start | bytes 3244040 | tf_op jit(solution)/shard_map/ppermute | solution.py:29
  116.6 11.1 %collective-permute-start.21 = (bf16[128,1024]{1,0:T(8,128)(2,1)S(1)}, bf16[128,1024]{1,0:T(8,128)(2,1)S(1)}, u32[]{:S(2)}, u32[]{:S(2)}) collective-permute-start(bf16[128,1024]{1,0:T(8,128)(2,1)S(1)} %get-tuple-element.63), channel_id=1, source_target_pairs={{0,2},{1,3},{2,0},{3,1},{4,6},{5,7},{6,4},{7,5},{8,10},{9,11},{10,... | collective-permute-start | bytes 786440 | tf_op jit(solution)/shard_map/ppermute | solution.py:29
  117.1 20.3 %collective-permute-start.13 = (bf16[128,1024]{1,0:T(8,128)(2,1)S(1)}, bf16[128,1024]{1,0:T(8,128)(2,1)S(1)}, u32[]{:S(2)}, u32[]{:S(2)}) collective-permute-start(bf16[128,1024]{1,0:T(8,128)(2,1)S(1)} %get-tuple-element.51), channel_id=1, source_target_pairs={{0,4},{1,5},{2,6},{3,7},{4,0},{5,1},{6,2},{7,3},{8,12},{9,13},{10,... | collective-permute-start | bytes 786440 | tf_op jit(solution)/shard_map/ppermute | solution.py:29
  122.5 14.8 %collective-permute-start.24 = (bf16[128,1024]{1,0:T(8,128)(2,1)S(1)}, bf16[128,1024]{1,0:T(8,128)(2,1)S(1)}, u32[]{:S(2)}, u32[]{:S(2)}) collective-permute-start(bf16[128,1024]{1,0:T(8,128)(2,1)S(1)} %get-tuple-element.69), channel_id=1, source_target_pairs={{0,4},{1,5},{2,6},{3,7},{4,0},{5,1},{6,2},{7,3},{8,12},{9,13},{10,... | collective-permute-start | bytes 786440 | tf_op jit(solution)/shard_map/ppermute | solution.py:29
  124.3 25.5 %collective-permute-start.23 = (bf16[128,1024]{1,0:T(8,128)(2,1)S(1)}, bf16[128,1024]{1,0:T(8,128)(2,1)S(1)}, u32[]{:S(2)}, u32[]{:S(2)}) collective-permute-start(bf16[128,1024]{1,0:T(8,128)(2,1)S(1)} %get-tuple-element.67), channel_id=1, source_target_pairs={{0,4},{1,5},{2,6},{3,7},{4,0},{5,1},{6,2},{7,3},{8,12},{9,13},{10,... | collective-permute-start | bytes 786440 | tf_op jit(solution)/shard_map/ppermute | solution.py:29
  127.7 21.4 %collective-permute-start.15 = (bf16[128,1024]{1,0:T(8,128)(2,1)S(1)}, bf16[128,1024]{1,0:T(8,128)(2,1)S(1)}, u32[]{:S(2)}, u32[]{:S(2)}) collective-permute-start(bf16[128,1024]{1,0:T(8,128)(2,1)S(1)} %add_convert_fusion.4), channel_id=1, source_target_pairs={{0,8},{1,9},{2,10},{3,11},{4,12},{5,13},{6,14},{7,15},{8,0},{9,1},... | collective-permute-start | bytes 786440 | tf_op jit(solution)/shard_map/ppermute | solution.py:29
  137.3 16.0 %collective-permute-start.25 = (bf16[128,1024]{1,0:T(8,128)(2,1)S(1)}, bf16[128,1024]{1,0:T(8,128)(2,1)S(1)}, u32[]{:S(2)}, u32[]{:S(2)}) collective-permute-start(bf16[128,1024]{1,0:T(8,128)(2,1)S(1)} %add_convert_fusion.2), channel_id=1, source_target_pairs={{0,8},{1,9},{2,10},{3,11},{4,12},{5,13},{6,14},{7,15},{8,0},{9,1},... | collective-permute-start | bytes 786440 | tf_op jit(solution)/shard_map/ppermute | solution.py:29

commit v4 on v3

--- a/solution.py
+++ b/solution.py
@@ -15,6 +15,20 @@
 vmem = pl.BlockSpec(memory_space=pltpu.VMEM)
 smem = pl.BlockSpec(memory_space=pltpu.SMEM)
 id_lanes = 128
+costs = {
+    "prepare": 10,
+    ("inputs", 0): 20,
+    ("inputs", 1): 20,
+    ("cot", 0): 20,
+    ("cot", 1): 20,
+    "forward": 20,
+    "backward": 20,
+    ("out", 0): 20,
+    ("out", 1): 20,
+    ("grad", 0): 1,
+    ("grad", 1): 1,
+    "weights": 5,
+}
 
 
 def scramble(values):
@@ -33,7 +47,7 @@
     return lax.optimization_barrier((values,) + earlier)[0]
 
 
-def called(kernel, out_shape, in_specs, flops, moved, scratch=()):
+def called(kernel, out_shape, in_specs, cost, scratch=()):
     return pl.pallas_call(
         kernel,
         out_shape=out_shape,
@@ -41,7 +55,9 @@
         out_specs=jax.tree.map(lambda _: vmem, out_shape),
         scratch_shapes=list(scratch),
         compiler_params=pltpu.CompilerParams(vmem_limit_bytes=40 * 1024 * 1024),
-        cost_estimate=pl.CostEstimate(flops=flops, bytes_accessed=moved, transcendentals=0),
+        cost_estimate=pl.CostEstimate(
+            flops=cost * 10**9, bytes_accessed=cost * 3 * 10**6, transcendentals=0
+        ),
     )
 
 
@@ -299,8 +315,7 @@
             shape((plane_experts, planes, tok_rows), f32),
         ),
         [smem, vmem],
-        10**6,
-        10**5,
+        costs["prepare"],
     )(place, tables)
 
     def gathered(chunks, with_ids):
@@ -312,8 +327,7 @@
                 functools.partial(compact_kernel, half, with_ids),
                 [shape((rows, width), bf16)] * plane_experts,
                 [vmem] * (2 + len(picked)),
-                2 * plane_experts * rows * len(picked) * tok_rows * width,
-                4 * rows * width,
+                costs["inputs" if with_ids else "cot", half],
             )(slots, gates, *picked)
             for column in range(plane_experts):
                 found[column, half] = (
@@ -325,15 +339,13 @@
     cot_blocks = gathered(cot_chunks, False)
 
     weight_scratch = pltpu.VMEM((3, hidden_width, model_width), bf16)
-    flops = 2 * slot_rows * hidden_width * model_width
     *out_blocks, gate_factor, up_factor, hidden = called(
         functools.partial(forward_kernel, seq_count, plane_experts, planes, capacity),
         [shape((rows, model_width), bf16)] * blocks
         + [shape((slot_rows, hidden_width), f32)] * 2
         + [shape((slot_rows, hidden_width), bf16)],
         [smem, smem] + [vmem] * (blocks + len(pieces)),
-        3 * flops,
-        10**7,
+        costs["forward"],
         [weight_scratch],
     )(place, dropout_key, *row_blocks, *pieces)
     *grad_blocks, gate_pre_grad, up_pre_grad = called(
@@ -341,8 +353,7 @@
         [shape((rows, model_width), bf16)] * blocks
         + [shape((slot_rows, hidden_width), bf16)] * 2,
         [smem] + [vmem] * (blocks + len(pieces) + 2),
-        3 * flops,
-        10**7,
+        costs["backward"],
         [weight_scratch],
     )(place, *cot_blocks, *pieces, gate_factor, up_factor)
 
@@ -357,8 +368,7 @@
                 functools.partial(combine_kernel, half, scaled),
                 [shape((tok_rows, model_width), bf16 if half else f32)] * (planes // 2),
                 [vmem] * (2 + plane_experts),
-                2 * plane_experts * rows * planes // 2 * tok_rows * model_width,
-                4 * rows * model_width,
+                costs["out" if scaled else "grad", half],
             )(slots, gates, *held)
             for step in range(planes // 2):
                 sums[2 * step + half] = combined[step]
@@ -381,8 +391,7 @@
             functools.partial(weight_grad_kernel, plane_experts, seq_count, shift),
             out_shape,
             [smem] + [vmem] * (2 * blocks + 3 + len(added)),
-            3 * flops // seq_count,
-            10**7,
+            costs["weights"],
         )(place, *row_blocks, *cot_blocks, hidden, gate_pre_grad, up_pre_grad, *added)
 
     arrived = [

time: 156 us -> 121 us (0.78)
  waiting for transfers between devices: 95.6 us -> 62.6 us
  starting transfers between devices: 30.7 us -> 35.9 us
  Pallas kernels: 21.1 us -> 16 us
  local copies, waits for them, and re-layouts: 3.71 us -> 1.1 us
    ppermute x25, waiting for transfers between devices: 95.6 us -> 62.1 us  [flipped(): lax.ppermute(values, axis, [(i, i ^ mask) for i in range(lax.axis_size(ax...]
    ppermute x25, starting transfers between devices: 30.6 us -> 35.8 us  [flipped(): lax.ppermute(values, axis, [(i, i ^ mask) for i in range(lax.axis_size(ax...]
    pallas_call x4, Pallas kernels: 5.11 us -> 1.31 us  [gathered(): called(functools.partial(compact_kernel, half, with_ids), [shape((rows, w...]
    unnamed x16 -> x6, local copies, waits for them, and re-layouts: 2.63 us -> 0.02 us
  transfers between devices with their start and end apart: 28 -> 28, of which waited for: 16 -> 13; matrix products, arithmetic and copies ran while one was open for 1% -> 3% of each run, Pallas kernels for 9% -> 13%
where the time goes in v4:
time: 121 us
  waiting for transfers between devices  62.6 us (52%)
  starting transfers between devices  35.9 us (30%)
  Pallas kernels  16 us (13%)
  other arithmetic  4.13 us (3%)
    ppermute x25, waiting for transfers between devices, flipped(): lax.ppermute(values, axis, [(i, i ^ mask) for i in range(lax.axis_size(ax...  62.1 us
    ppermute x25, starting transfers between devices, flipped(): lax.ppermute(values, axis, [(i, i ^ mask) for i in range(lax.axis_size(ax...  35.8 us
    pallas_call x1, Pallas kernels, local(): called(functools.partial(backward_kernel, seq_count, plane_experts), [sha...  4.77 us
    pallas_call x1, Pallas kernels, local(): called(functools.partial(forward_kernel, seq_count, plane_experts, planes...  4.18 us
    pallas_call x2, Pallas kernels, weight_grads(): called(functools.partial(weight_grad_kernel, plane_experts, seq_count, sh...  3.71 us
  transfers between devices with their start and end apart: 28, of which 13 were waited for; matrix products, arithmetic and copies ran while one was open for 3% of the time, Pallas kernels for 13%

profile of v4, /device:TPU:0, one launch (start us, length us, event | category | flops | bytes accessed | tf_op | source)
XLA Modules:
  0.0 120.6 jit_solution(15984066469654298429)
XLA Ops:
  0.6 0.7 pad_add_fusion.1
  1.3 5.0 %collective-permute-start.2 = (s32[4,128]{1,0:T(4,128)S(1)}, s32[4,128]{1,0:T(4,128)S(1)}, u32[]{:S(2)}, u32[]{:S(2)}) collective-permute-start(s32[4,128]{1,0:T(4,128)S(1)} %pad_add_fusion.1), channel_id=1, source_target_pairs={{0,12},{1,13},{2,14},{3,15},{4,8},{5,9},{6,10},{7,11},{8,4},{9,5},... | collective-permute-start | bytes 6152 | tf_op jit(solution)/shard_map/ppermute | solution.py:43
  6.4 0.0 collective-permute-start.1
  6.4 0.6 collective-permute-start
  7.0 2.3 %collective-permute-start.3 = (bf16[128,1024]{1,0:T(8,128)(2,1)}, bf16[128,1024]{1,0:T(8,128)(2,1)S(1)}, u32[]{:S(2)}, u32[]{:S(2)}) collective-permute-start(bf16[128,1024]{1,0:T(8,128)(2,1)} %refs_0_.2), channel_id=1, source_target_pairs={{0,8},{1,9},{2,10},{3,11},{4,12},{5,13},{6,14},{7,15},{8,0},{9,1},... | collective-permute-start | bytes 786440 | tf_op jit(solution)/shard_map/ppermute | solution.py:43
  9.3 2.0 %collective-permute-start.4 = (bf16[128,1024]{1,0:T(8,128)(2,1)}, bf16[128,1024]{1,0:T(8,128)(2,1)S(1)}, u32[]{:S(2)}, u32[]{:S(2)}) collective-permute-start(bf16[128,1024]{1,0:T(8,128)(2,1)} %refs_0_.2), channel_id=1, source_target_pairs={{0,4},{1,5},{2,6},{3,7},{4,0},{5,1},{6,2},{7,3},{8,12},{9,13},{10,... | collective-permute-start | bytes 786440 | tf_op jit(solution)/shard_map/ppermute | solution.py:43
  11.3 1.3 %pad_maximum_fusion.refs_4_ = bf16[3,352,512]{2,1,0:T(8,128)(2,1)S(1)} fusion(bf16[1,352,512]{2,1,0:T(8,128)(2,1)} %param.15, bf16[1,352,512]{2,1,0:T(8,128)(2,1)} %bitcast.41, bf16[1,352,512]{2,1,0:T(8,128)(2,1)} %bitcast.42), kind=kLoop, calls=%fused_computation.1 | loop fusion | flops 1081344 | bytes 2162688 | tf_op jit(solution)/shard_map/stack | solution.py:280
  12.7 0.1 stack.55.place_ref
  12.8 0.1 collective-permute-start.8
  12.9 1.6 %collective-permute-start.9 = (bf16[3,352,512]{2,1,0:T(8,128)(2,1)S(1)}, bf16[3,352,512]{2,1,0:T(8,128)(2,1)S(1)}, u32[]{:S(2)}, u32[]{:S(2)}) collective-permute-start(bf16[3,352,512]{2,1,0:T(8,128)(2,1)S(1)} %pad_maximum_fusion.refs_4_), channel_id=1, source_target_pairs={{0,1},{1,0},{2,3},{3,2},{4,5},{5,4},{6,7},{7,6},{8,9},{9,8},{10,11... | collective-permute-start | bytes 3244040 | tf_op jit(solution)/shard_map/ppermute | solution.py:43
  14.4 0.0 collective-permute-done
  14.4 0.0 copy-start.1
  14.5 0.0 copy-start
  14.5 0.7 shard_map.119
  15.1 6.3 %collective-permute-done.4.refs_0_ = bf16[128,1024]{1,0:T(8,128)(2,1)S(1)} collective-permute-done((bf16[128,1024]{1,0:T(8,128)(2,1)}, bf16[128,1024]{1,0:T(8,128)(2,1)S(1)}, u32[]{:S(2)}, u32[]{:S(2)}) %collective-permute-start.4) | collective-permute-done | bytes 262176 | tf_op jit(solution)/shard_map/ppermute | solution.py:43
  21.5 1.2 %collective-permute-start.16 = (bf16[128,1024]{1,0:T(8,128)(2,1)S(1)}, bf16[128,1024]{1,0:T(8,128)(2,1)S(1)}, u32[]{:S(2)}, u32[]{:S(2)}) collective-permute-start(bf16[128,1024]{1,0:T(8,128)(2,1)S(1)} %copy-done.1), channel_id=1, source_target_pairs={{0,8},{1,9},{2,10},{3,11},{4,12},{5,13},{6,14},{7,15},{8,0},{9,1},... | collective-permute-start | bytes 786440 | tf_op jit(solution)/shard_map/ppermute | solution.py:43
  22.7 0.0 collective-permute-done.3.refs_1_
  22.7 0.3 shard_map.120
  23.1 1.6 %collective-permute-start.6 = (bf16[128,1152]{1,0:T(8,128)(2,1)S(1)}, bf16[128,1152]{1,0:T(8,128)(2,1)S(1)}, u32[]{:S(2)}, u32[]{:S(2)}) collective-permute-start(bf16[128,1152]{1,0:T(8,128)(2,1)S(1)} %get-tuple-element.44), channel_id=1, source_target_pairs={{0,2},{1,3},{2,0},{3,1},{4,6},{5,7},{6,4},{7,5},{8,10},{9,11},{10,... | collective-permute-start | bytes 884744 | tf_op jit(solution)/shard_map/ppermute | solution.py:43
  24.6 8.8 %collective-permute-done.16.refs_1_ = bf16[128,1024]{1,0:T(8,128)(2,1)S(1)} collective-permute-done((bf16[128,1024]{1,0:T(8,128)(2,1)S(1)}, bf16[128,1024]{1,0:T(8,128)(2,1)S(1)}, u32[]{:S(2)}, u32[]{:S(2)}) %collective-permute-start.16) | collective-permute-done | bytes 262176 | tf_op jit(solution)/shard_map/ppermute | solution.py:43
  33.5 0.3 shard_map.125
  33.8 6.2 %collective-permute-done.5.refs_1_ = bf16[128,1024]{1,0:T(8,128)(2,1)S(1)} collective-permute-done((bf16[128,1024]{1,0:T(8,128)(2,1)S(1)}, bf16[128,1024]{1,0:T(8,128)(2,1)S(1)}, u32[]{:S(2)}, u32[]{:S(2)}) %collective-permute-start.5) | collective-permute-done | bytes 262176 | tf_op jit(solution)/shard_map/ppermute | solution.py:43
  40.0 0.6 collective-permute-start.18
  40.6 0.3 shard_map.121
  41.0 1.6 %collective-permute-start.7 = (bf16[128,1152]{1,0:T(8,128)(2,1)S(1)}, bf16[128,1152]{1,0:T(8,128)(2,1)S(1)}, u32[]{:S(2)}, u32[]{:S(2)}) collective-permute-start(bf16[128,1152]{1,0:T(8,128)(2,1)S(1)} %get-tuple-element.45), channel_id=1, source_target_pairs={{0,2},{1,3},{2,0},{3,1},{4,6},{5,7},{6,4},{7,5},{8,10},{9,11},{10,... | collective-permute-start | bytes 884744 | tf_op jit(solution)/shard_map/ppermute | solution.py:43
  42.6 3.8 %collective-permute-done.18.refs_1_ = bf16[128,1024]{1,0:T(8,128)(2,1)S(1)} collective-permute-done((bf16[128,1024]{1,0:T(8,128)(2,1)S(1)}, bf16[128,1024]{1,0:T(8,128)(2,1)S(1)}, u32[]{:S(2)}, u32[]{:S(2)}) %collective-permute-start.18) | collective-permute-done | bytes 262176 | tf_op jit(solution)/shard_map/ppermute | solution.py:43
  46.4 1.7 %collective-permute-start.19 = (bf16[128,1024]{1,0:T(8,128)(2,1)S(1)}, bf16[128,1024]{1,0:T(8,128)(2,1)S(1)}, u32[]{:S(2)}, u32[]{:S(2)}) collective-permute-start(bf16[128,1024]{1,0:T(8,128)(2,1)S(1)} %get-tuple-element.58), channel_id=1, source_target_pairs={{0,2},{1,3},{2,0},{3,1},{4,6},{5,7},{6,4},{7,5},{8,10},{9,11},{10,... | collective-permute-start | bytes 786440 | tf_op jit(solution)/shard_map/ppermute | solution.py:43
  48.1 0.3 shard_map.126
  48.4 0.4 collective-permute-start.20
  48.8 1.5 %collective-permute-done.7.refs_3_ = bf16[128,1152]{1,0:T(8,128)(2,1)S(1)} collective-permute-done((bf16[128,1152]{1,0:T(8,128)(2,1)S(1)}, bf16[128,1152]{1,0:T(8,128)(2,1)S(1)}, u32[]{:S(2)}, u32[]{:S(2)}) %collective-permute-start.7) | collective-permute-done | bytes 294944 | tf_op jit(solution)/shard_map/ppermute | solution.py:43
  50.3 0.5 collective-permute-done.10.refs_7_
  50.8 4.2 %shard_map.122 = (bf16[128,1024]{1,0:T(8,128)(2,1)S(1)}, bf16[128,1024]{1,0:T(8,128)(2,1)S(1)}, bf16[128,1024]{1,0:T(8,128)(2,1)S(1)}, bf16[128,1024]{1,0:T(8,12...) custom-call(s32[8]{0:T(128)S(1)} %stack.55.place_ref, s32[2]{0:T(128)S(1)} %copy-done.2, ...), custom_call_target="tpu_custom_call" | custom-call | flops 20000000000 | bytes 60000000 | tf_op jit(solution)/shard_map/pallas_call | solution.py:342
  55.0 1.3 %collective-permute-start.11 = (bf16[128,1024]{1,0:T(8,128)(2,1)S(1)}, bf16[128,1024]{1,0:T(8,128)(2,1)S(1)}, u32[]{:S(2)}, u32[]{:S(2)}) collective-permute-start(bf16[128,1024]{1,0:T(8,128)(2,1)S(1)} %get-tuple-element.47), channel_id=1, source_target_pairs={{0,2},{1,3},{2,0},{3,1},{4,6},{5,7},{6,4},{7,5},{8,10},{9,11},{10,... | collective-permute-start | bytes 786440 | tf_op jit(solution)/shard_map/ppermute | solution.py:43
  56.3 0.8 collective-permute-start.12
  57.1 3.2 %collective-permute-done.20.refs_3_.refs_7_ = bf16[128,1024]{1,0:T(8,128)(2,1)S(1)} collective-permute-done((bf16[128,1024]{1,0:T(8,128)(2,1)S(1)}, bf16[128,1024]{1,0:T(8,128)(2,1)S(1)}, u32[]{:S(2)}, u32[]{:S(2)}) %collective-permute-start.20) | collective-permute-done | bytes 262176 | tf_op jit(solution)/shard_map/ppermute | solution.py:43
  60.3 4.8 %shard_map.127 = (bf16[128,1024]{1,0:T(8,128)(2,1)S(1)}, bf16[128,1024]{1,0:T(8,128)(2,1)S(1)}, bf16[128,1024]{1,0:T(8,128)(2,1)S(1)}, bf16[128,1024]{1,0:T(8,12...) custom-call(s32[8]{0:T(128)S(1)} %stack.55.place_ref, ...), custom_call_target="tpu_custom_call" | custom-call | flops 20000000000 | bytes 60000000 | tf_op jit(solution)/shard_map/pallas_call | solution.py:351
  65.1 2.6 %collective-permute-start.21 = (bf16[128,1024]{1,0:T(8,128)(2,1)S(1)}, bf16[128,1024]{1,0:T(8,128)(2,1)S(1)}, u32[]{:S(2)}, u32[]{:S(2)}) collective-permute-start(bf16[128,1024]{1,0:T(8,128)(2,1)S(1)} %get-tuple-element.63), channel_id=1, source_target_pairs={{0,2},{1,3},{2,0},{3,1},{4,6},{5,7},{6,4},{7,5},{8,10},{9,11},{10,... | collective-permute-start | bytes 786440 | tf_op jit(solution)/shard_map/ppermute | solution.py:43
  67.7 0.1 collective-permute-start.22
  67.7 1.9 %shard_map.130 = bf16[3,704,512]{2,1,0:T(8,128)(2,1)S(1)} custom-call(s32[8]{0:T(128)S(1)} %stack.55.place_ref, bf16[128,1152]{1,0:T(8,128)(2,1)S(1)} %get-tuple-element.42.refs_0_, bf16[128,1152]{1,0:T(8,128)(2,1)S(1)} %get-tuple-element.43.refs_1_, bf16[128,1152]{1,0:T(8,128)(2,1)S(1)} %collective-permute-done.6.refs_2_, ...), custom_call_target="tpu_custom_call" | custom-call | flops 5000000000 | bytes 15000000 | tf_op jit(solution)/shard_map/pallas_call | solution.py:390
  69.6 0.1 collective-permute-start.26
  69.7 1.9 %collective-permute-done.12.refs_1_ = bf16[128,1024]{1,0:T(8,128)(2,1)S(1)} collective-permute-done((bf16[128,1024]{1,0:T(8,128)(2,1)S(1)}, bf16[128,1024]{1,0:T(8,128)(2,1)S(1)}, u32[]{:S(2)}, u32[]{:S(2)}) %collective-permute-start.12) | collective-permute-done | bytes 262176 | tf_op jit(solution)/shard_map/ppermute | solution.py:43
  71.6 0.3 shard_map.124
  71.9 2.3 %collective-permute-start.14 = (bf16[128,1024]{1,0:T(8,128)(2,1)S(1)}, bf16[128,1024]{1,0:T(8,128)(2,1)S(1)}, u32[]{:S(2)}, u32[]{:S(2)}) collective-permute-start(bf16[128,1024]{1,0:T(8,128)(2,1)S(1)} %get-tuple-element.53), channel_id=1, source_target_pairs={{0,4},{1,5},{2,6},{3,7},{4,0},{5,1},{6,2},{7,3},{8,12},{9,13},{10,... | collective-permute-start | bytes 786440 | tf_op jit(solution)/shard_map/ppermute | solution.py:43
  74.2 7.2 %collective-permute-done.22.refs_1_ = bf16[128,1024]{1,0:T(8,128)(2,1)S(1)} collective-permute-done((bf16[128,1024]{1,0:T(8,128)(2,1)S(1)}, bf16[128,1024]{1,0:T(8,128)(2,1)S(1)}, u32[]{:S(2)}, u32[]{:S(2)}) %collective-permute-start.22) | collective-permute-done | bytes 262176 | tf_op jit(solution)/shard_map/ppermute | solution.py:43
  81.5 1.4 %collective-permute-start.13 = (bf16[128,1024]{1,0:T(8,128)(2,1)S(1)}, bf16[128,1024]{1,0:T(8,128)(2,1)S(1)}, u32[]{:S(2)}, u32[]{:S(2)}) collective-permute-start(bf16[128,1024]{1,0:T(8,128)(2,1)S(1)} %get-tuple-element.51), channel_id=1, source_target_pairs={{0,4},{1,5},{2,6},{3,7},{4,0},{5,1},{6,2},{7,3},{8,12},{9,13},{10,... | collective-permute-start | bytes 786440 | tf_op jit(solution)/shard_map/ppermute | solution.py:43
  82.9 0.3 shard_map.129
  83.3 0.6 collective-permute-start.24
  83.9 0.3 shard_map.123
  84.2 1.5 %collective-permute-start.23 = (bf16[128,1024]{1,0:T(8,128)(2,1)S(1)}, bf16[128,1024]{1,0:T(8,128)(2,1)S(1)}, u32[]{:S(2)}, u32[]{:S(2)}) collective-permute-start(bf16[128,1024]{1,0:T(8,128)(2,1)S(1)} %get-tuple-element.67), channel_id=1, source_target_pairs={{0,4},{1,5},{2,6},{3,7},{4,0},{5,1},{6,2},{7,3},{8,12},{9,13},{10,... | collective-permute-start | bytes 786440 | tf_op jit(solution)/shard_map/ppermute | solution.py:43
  85.8 1.9 %shard_map.131 = (f32[3,352,512]{2,1,0:T(8,128)S(1)}, bf16[3,352,512]{2,1,0:T(8,128)(2,1)S(1)}) custom-call(s32[8]{0:T(128)S(1)} %stack.55.place_ref, bf16[128,1152]{1,0:T(8,128)(2,1)S(1)} %get-tuple-element.42.refs_0_, bf16[128,1152]{1,0:T(8,128)(2,1)S(1)} %get-tuple-element.43.refs_1_, bf16[128,1152]{1,0:T(8,128)(2,1)S(1)} %collective-permute-done.6.refs_2_, ...), custom_call_target="tpu_custom_call" | custom-call | flops 5000000000 | bytes 15000000 | tf_op jit(solution)/shard_map/pallas_call | solution.py:390
  87.6 1.5 %collective-permute-start.27 = (bf16[3,352,512]{2,1,0:T(8,128)(2,1)S(1)}, bf16[3,352,512]{2,1,0:T(8,128)(2,1)S(1)}, u32[]{:S(2)}, u32[]{:S(2)}) collective-permute-start(bf16[3,352,512]{2,1,0:T(8,128)(2,1)S(1)} %get-tuple-element.74), channel_id=1, source_target_pairs={{0,1},{1,0},{2,3},{3,2},{4,5},{5,4},{6,7},{7,6},{8,9},{9,8},{10,11... | collective-permute-start | bytes 3244040 | tf_op jit(solution)/shard_map/ppermute | solution.py:43
  89.2 0.1 add_convert_fusion.4
  89.2 4.2 %collective-permute-start.15 = (bf16[128,1024]{1,0:T(8,128)(2,1)S(1)}, bf16[128,1024]{1,0:T(8,128)(2,1)S(1)}, u32[]{:S(2)}, u32[]{:S(2)}) collective-permute-start(bf16[128,1024]{1,0:T(8,128)(2,1)S(1)} %add_convert_fusion.4), channel_id=1, source_target_pairs={{0,8},{1,9},{2,10},{3,11},{4,12},{5,13},{6,14},{7,15},{8,0},{9,1},... | collective-permute-start | bytes 786440 | tf_op jit(solution)/shard_map/ppermute | solution.py:43
  93.5 0.3 shard_map.128
  93.8 10.9 %collective-permute-done.24 = bf16[128,1024]{1,0:T(8,128)(2,1)S(1)} collective-permute-done((bf16[128,1024]{1,0:T(8,128)(2,1)S(1)}, bf16[128,1024]{1,0:T(8,128)(2,1)S(1)}, u32[]{:S(2)}, u32[]{:S(2)}) %collective-permute-start.24) | collective-permute-done | bytes 262176 | tf_op jit(solution)/shard_map/ppermute | solution.py:43
  104.8 0.1 add_convert_fusion.2
  104.8 0.7 collective-permute-start.25
  105.5 0.8 collective-permute-done.15
  106.3 0.8 add_convert_fusion.3
  107.1 1.2 %collective-permute-done.23 = bf16[128,1024]{1,0:T(8,128)(2,1)S(1)} collective-permute-done((bf16[128,1024]{1,0:T(8,128)(2,1)S(1)}, bf16[128,1024]{1,0:T(8,128)(2,1)S(1)}, u32[]{:S(2)}, u32[]{:S(2)}) %collective-permute-start.23) | collective-permute-done | bytes 262176 | tf_op jit(solution)/shard_map/ppermute | solution.py:43
  108.3 10.0 %collective-permute-done.25 = bf16[128,1024]{1,0:T(8,128)(2,1)S(1)} collective-permute-done((bf16[128,1024]{1,0:T(8,128)(2,1)S(1)}, bf16[128,1024]{1,0:T(8,128)(2,1)S(1)}, u32[]{:S(2)}, u32[]{:S(2)}) %collective-permute-start.25) | collective-permute-done | bytes 262176 | tf_op jit(solution)/shard_map/ppermute | solution.py:43
  118.4 0.8 add_convert_fusion.1
  119.2 0.4 add_convert_fusion
  119.6 1.0 fusion
  (21 shorter events, 0.1 us)
Async XLA Ops:
  1.3 11.4 %collective-permute-start.2 = (s32[4,128]{1,0:T(4,128)S(1)}, s32[4,128]{1,0:T(4,128)S(1)}, u32[]{:S(2)}, u32[]{:S(2)}) collective-permute-start(s32[4,128]{1,0:T(4,128)S(1)} %pad_add_fusion.1), channel_id=1, source_target_pairs={{0,12},{1,13},{2,14},{3,15},{4,8},{5,9},{6,10},{7,11},{8,4},{9,5},... | collective-permute-start | bytes 6152 | tf_op jit(solution)/shard_map/ppermute | solution.py:43
  6.4 6.5 %collective-permute-start.1 = (s32[4,128]{1,0:T(4,128)S(1)}, s32[4,128]{1,0:T(4,128)S(1)}, u32[]{:S(2)}, u32[]{:S(2)}) collective-permute-start(s32[4,128]{1,0:T(4,128)S(1)} %pad_add_fusion.1), channel_id=1, source_target_pairs={{0,8},{1,9},{2,10},{3,11},{4,12},{5,13},{6,14},{7,15},{8,0},{9,1},... | collective-permute-start | bytes 6152 | tf_op jit(solution)/shard_map/ppermute | solution.py:43
  6.4 8.0 %collective-permute-start = (s32[4,128]{1,0:T(4,128)S(1)}, s32[4,128]{1,0:T(4,128)S(1)}, u32[]{:S(2)}, u32[]{:S(2)}) collective-permute-start(s32[4,128]{1,0:T(4,128)S(1)} %pad_add_fusion.1), channel_id=1, source_target_pairs={{0,4},{1,5},{2,6},{3,7},{4,0},{5,1},{6,2},{7,3},{8,12},{9,13},{10,... | collective-permute-start | bytes 6152 | tf_op jit(solution)/shard_map/ppermute | solution.py:43
  7.0 15.7 %collective-permute-start.3 = (bf16[128,1024]{1,0:T(8,128)(2,1)}, bf16[128,1024]{1,0:T(8,128)(2,1)S(1)}, u32[]{:S(2)}, u32[]{:S(2)}) collective-permute-start(bf16[128,1024]{1,0:T(8,128)(2,1)} %refs_0_.2), channel_id=1, source_target_pairs={{0,8},{1,9},{2,10},{3,11},{4,12},{5,13},{6,14},{7,15},{8,0},{9,1},... | collective-permute-start | bytes 786440 | tf_op jit(solution)/shard_map/ppermute | solution.py:43
  9.3 12.2 %collective-permute-start.4 = (bf16[128,1024]{1,0:T(8,128)(2,1)}, bf16[128,1024]{1,0:T(8,128)(2,1)S(1)}, u32[]{:S(2)}, u32[]{:S(2)}) collective-permute-start(bf16[128,1024]{1,0:T(8,128)(2,1)} %refs_0_.2), channel_id=1, source_target_pairs={{0,4},{1,5},{2,6},{3,7},{4,0},{5,1},{6,2},{7,3},{8,12},{9,13},{10,... | collective-permute-start | bytes 786440 | tf_op jit(solution)/shard_map/ppermute | solution.py:43
  12.8 37.5 %collective-permute-start.8 = (bf16[3,352,512]{2,1,0:T(8,128)(2,1)S(1)}, bf16[3,352,512]{2,1,0:T(8,128)(2,1)S(1)}, u32[]{:S(2)}, u32[]{:S(2)}) collective-permute-start(bf16[3,352,512]{2,1,0:T(8,128)(2,1)S(1)} %pad_maximum_fusion.refs_4_), channel_id=1, source_target_pairs={{0,16},{16,0},{1,17},{17,1},{2,18},{18,2},{3,19},{19,3},{4,20},{20... | collective-permute-start | bytes 3244040 | tf_op jit(solution)/shard_map/ppermute | solution.py:284
  12.9 35.2 %collective-permute-start.9 = (bf16[3,352,512]{2,1,0:T(8,128)(2,1)S(1)}, bf16[3,352,512]{2,1,0:T(8,128)(2,1)S(1)}, u32[]{:S(2)}, u32[]{:S(2)}) collective-permute-start(bf16[3,352,512]{2,1,0:T(8,128)(2,1)S(1)} %pad_maximum_fusion.refs_4_), channel_id=1, source_target_pairs={{0,1},{1,0},{2,3},{3,2},{4,5},{5,4},{6,7},{7,6},{8,9},{9,8},{10,11... | collective-permute-start | bytes 3244040 | tf_op jit(solution)/shard_map/ppermute | solution.py:43
  14.4 7.0 %copy-start.1 = (bf16[128,1024]{1,0:T(8,128)(2,1)S(1)}, bf16[128,1024]{1,0:T(8,128)(2,1)}, u32[]{:S(2)}) copy-start(bf16[128,1024]{1,0:T(8,128)(2,1)} %refs_0_.3) | copy-start | bytes 786436
  14.5 8.2 %copy-start = (bf16[128,1024]{1,0:T(8,128)(2,1)S(1)}, bf16[128,1024]{1,0:T(8,128)(2,1)}, u32[]{:S(2)}) copy-start(bf16[128,1024]{1,0:T(8,128)(2,1)} %refs_0_.2) | copy-start | bytes 786436
  21.5 12.0 %collective-permute-start.16 = (bf16[128,1024]{1,0:T(8,128)(2,1)S(1)}, bf16[128,1024]{1,0:T(8,128)(2,1)S(1)}, u32[]{:S(2)}, u32[]{:S(2)}) collective-permute-start(bf16[128,1024]{1,0:T(8,128)(2,1)S(1)} %copy-done.1), channel_id=1, source_target_pairs={{0,8},{1,9},{2,10},{3,11},{4,12},{5,13},{6,14},{7,15},{8,0},{9,1},... | collective-permute-start | bytes 786440 | tf_op jit(solution)/shard_map/ppermute | solution.py:43
  23.1 25.4 %collective-permute-start.6 = (bf16[128,1152]{1,0:T(8,128)(2,1)S(1)}, bf16[128,1152]{1,0:T(8,128)(2,1)S(1)}, u32[]{:S(2)}, u32[]{:S(2)}) collective-permute-start(bf16[128,1152]{1,0:T(8,128)(2,1)S(1)} %get-tuple-element.44), channel_id=1, source_target_pairs={{0,2},{1,3},{2,0},{3,1},{4,6},{5,7},{6,4},{7,5},{8,10},{9,11},{10,... | collective-permute-start | bytes 884744 | tf_op jit(solution)/shard_map/ppermute | solution.py:43
  24.6 16.3 %collective-permute-start.17 = (bf16[128,1024]{1,0:T(8,128)(2,1)S(1)}, bf16[128,1024]{1,0:T(8,128)(2,1)S(1)}, u32[]{:S(2)}, u32[]{:S(2)}) collective-permute-start(bf16[128,1024]{1,0:T(8,128)(2,1)S(1)} %copy-done.1), channel_id=1, source_target_pairs={{0,4},{1,5},{2,6},{3,7},{4,0},{5,1},{6,2},{7,3},{8,12},{9,13},{10,... | collective-permute-start | bytes 786440 | tf_op jit(solution)/shard_map/ppermute | solution.py:43
  33.5 6.5 %collective-permute-start.5 = (bf16[128,1024]{1,0:T(8,128)(2,1)S(1)}, bf16[128,1024]{1,0:T(8,128)(2,1)S(1)}, u32[]{:S(2)}, u32[]{:S(2)}) collective-permute-start(bf16[128,1024]{1,0:T(8,128)(2,1)S(1)} %collective-permute-done.3.refs_1_), channel_id=1, source_target_pairs={{0,4},{1,5},{2,6},{3,7},{4,0},{5,1},{6,2},{7,3},{8,12},{9,13},{10,... | collective-permute-start | bytes 786440 | tf_op jit(solution)/shard_map/ppermute | solution.py:43
  40.0 6.4 %collective-permute-start.18 = (bf16[128,1024]{1,0:T(8,128)(2,1)S(1)}, bf16[128,1024]{1,0:T(8,128)(2,1)S(1)}, u32[]{:S(2)}, u32[]{:S(2)}) collective-permute-start(bf16[128,1024]{1,0:T(8,128)(2,1)S(1)} %collective-permute-done.16.refs_1_), channel_id=1, source_target_pairs={{0,4},{1,5},{2,6},{3,7},{4,0},{5,1},{6,2},{7,3},{8,12},{9,13},{10,... | collective-permute-start | bytes 786440 | tf_op jit(solution)/shard_map/ppermute | solution.py:43
  41.0 9.3 %collective-permute-start.7 = (bf16[128,1152]{1,0:T(8,128)(2,1)S(1)}, bf16[128,1152]{1,0:T(8,128)(2,1)S(1)}, u32[]{:S(2)}, u32[]{:S(2)}) collective-permute-start(bf16[128,1152]{1,0:T(8,128)(2,1)S(1)} %get-tuple-element.45), channel_id=1, source_target_pairs={{0,2},{1,3},{2,0},{3,1},{4,6},{5,7},{6,4},{7,5},{8,10},{9,11},{10,... | collective-permute-start | bytes 884744 | tf_op jit(solution)/shard_map/ppermute | solution.py:43
  46.4 4.4 %copy-start.2 = (s32[2]{0:T(128)S(1)}, s32[2]{0:T(128)}, u32[]{:S(2)}) copy-start(s32[2]{0:T(128)} %key_ref.1) | copy-start | bytes 28
  46.4 10.7 %collective-permute-start.19 = (bf16[128,1024]{1,0:T(8,128)(2,1)S(1)}, bf16[128,1024]{1,0:T(8,128)(2,1)S(1)}, u32[]{:S(2)}, u32[]{:S(2)}) collective-permute-start(bf16[128,1024]{1,0:T(8,128)(2,1)S(1)} %get-tuple-element.58), channel_id=1, source_target_pairs={{0,2},{1,3},{2,0},{3,1},{4,6},{5,7},{6,4},{7,5},{8,10},{9,11},{10,... | collective-permute-start | bytes 786440 | tf_op jit(solution)/shard_map/ppermute | solution.py:43
  48.1 2.7 %collective-permute-start.10 = (bf16[3,352,512]{2,1,0:T(8,128)(2,1)S(1)}, bf16[3,352,512]{2,1,0:T(8,128)(2,1)S(1)}, u32[]{:S(2)}, u32[]{:S(2)}) collective-permute-start(bf16[3,352,512]{2,1,0:T(8,128)(2,1)S(1)} %collective-permute-done.9.refs_6_), channel_id=1, source_target_pairs={{0,16},{16,0},{1,17},{17,1},{2,18},{18,2},{3,19},{19,3},{4,20},{20... | collective-permute-start | bytes 3244040 | tf_op jit(solution)/shard_map/ppermute | solution.py:284
  48.4 11.9 %collective-permute-start.20 = (bf16[128,1024]{1,0:T(8,128)(2,1)S(1)}, bf16[128,1024]{1,0:T(8,128)(2,1)S(1)}, u32[]{:S(2)}, u32[]{:S(2)}) collective-permute-start(bf16[128,1024]{1,0:T(8,128)(2,1)S(1)} %get-tuple-element.59), channel_id=1, source_target_pairs={{0,2},{1,3},{2,0},{3,1},{4,6},{5,7},{6,4},{7,5},{8,10},{9,11},{10,... | collective-permute-start | bytes 786440 | tf_op jit(solution)/shard_map/ppermute | solution.py:43
  55.0 28.3 %collective-permute-start.11 = (bf16[128,1024]{1,0:T(8,128)(2,1)S(1)}, bf16[128,1024]{1,0:T(8,128)(2,1)S(1)}, u32[]{:S(2)}, u32[]{:S(2)}) collective-permute-start(bf16[128,1024]{1,0:T(8,128)(2,1)S(1)} %get-tuple-element.47), channel_id=1, source_target_pairs={{0,2},{1,3},{2,0},{3,1},{4,6},{5,7},{6,4},{7,5},{8,10},{9,11},{10,... | collective-permute-start | bytes 786440 | tf_op jit(solution)/shard_map/ppermute | solution.py:43
  56.3 15.3 %collective-permute-start.12 = (bf16[128,1024]{1,0:T(8,128)(2,1)S(1)}, bf16[128,1024]{1,0:T(8,128)(2,1)S(1)}, u32[]{:S(2)}, u32[]{:S(2)}) collective-permute-start(bf16[128,1024]{1,0:T(8,128)(2,1)S(1)} %get-tuple-element.50), channel_id=1, source_target_pairs={{0,2},{1,3},{2,0},{3,1},{4,6},{5,7},{6,4},{7,5},{8,10},{9,11},{10,... | collective-permute-start | bytes 786440 | tf_op jit(solution)/shard_map/ppermute | solution.py:43
  65.1 24.1 %collective-permute-start.21 = (bf16[128,1024]{1,0:T(8,128)(2,1)S(1)}, bf16[128,1024]{1,0:T(8,128)(2,1)S(1)}, u32[]{:S(2)}, u32[]{:S(2)}) collective-permute-start(bf16[128,1024]{1,0:T(8,128)(2,1)S(1)} %get-tuple-element.63), channel_id=1, source_target_pairs={{0,2},{1,3},{2,0},{3,1},{4,6},{5,7},{6,4},{7,5},{8,10},{9,11},{10,... | collective-permute-start | bytes 786440 | tf_op jit(solution)/shard_map/ppermute | solution.py:43
  67.7 13.8 %collective-permute-start.22 = (bf16[128,1024]{1,0:T(8,128)(2,1)S(1)}, bf16[128,1024]{1,0:T(8,128)(2,1)S(1)}, u32[]{:S(2)}, u32[]{:S(2)}) collective-permute-start(bf16[128,1024]{1,0:T(8,128)(2,1)S(1)} %get-tuple-element.66), channel_id=1, source_target_pairs={{0,2},{1,3},{2,0},{3,1},{4,6},{5,7},{6,4},{7,5},{8,10},{9,11},{10,... | collective-permute-start | bytes 786440 | tf_op jit(solution)/shard_map/ppermute | solution.py:43
  69.6 14.6 %collective-permute-start.26 = (bf16[3,704,512]{2,1,0:T(8,128)(2,1)S(1)}, bf16[3,704,512]{2,1,0:T(8,128)(2,1)S(1)}, u32[]{:S(2)}, u32[]{:S(2)}) collective-permute-start(bf16[3,704,512]{2,1,0:T(8,128)(2,1)S(1)} %shard_map.130), channel_id=1, source_target_pairs={{0,16},{16,0},{1,17},{17,1},{2,18},{18,2},{3,19},{19,3},{4,20},{20... | collective-permute-start | bytes 6488072 | tf_op jit(solution)/shard_map/ppermute | solution.py:284
  71.9 15.7 %collective-permute-start.14 = (bf16[128,1024]{1,0:T(8,128)(2,1)S(1)}, bf16[128,1024]{1,0:T(8,128)(2,1)S(1)}, u32[]{:S(2)}, u32[]{:S(2)}) collective-permute-start(bf16[128,1024]{1,0:T(8,128)(2,1)S(1)} %get-tuple-element.53), channel_id=1, source_target_pairs={{0,4},{1,5},{2,6},{3,7},{4,0},{5,1},{6,2},{7,3},{8,12},{9,13},{10,... | collective-permute-start | bytes 786440 | tf_op jit(solution)/shard_map/ppermute | solution.py:43
  81.5 24.1 %collective-permute-start.13 = (bf16[128,1024]{1,0:T(8,128)(2,1)S(1)}, bf16[128,1024]{1,0:T(8,128)(2,1)S(1)}, u32[]{:S(2)}, u32[]{:S(2)}) collective-permute-start(bf16[128,1024]{1,0:T(8,128)(2,1)S(1)} %get-tuple-element.51), channel_id=1, source_target_pairs={{0,4},{1,5},{2,6},{3,7},{4,0},{5,1},{6,2},{7,3},{8,12},{9,13},{10,... | collective-permute-start | bytes 786440 | tf_op jit(solution)/shard_map/ppermute | solution.py:43
  83.3 21.5 %collective-permute-start.24 = (bf16[128,1024]{1,0:T(8,128)(2,1)S(1)}, bf16[128,1024]{1,0:T(8,128)(2,1)S(1)}, u32[]{:S(2)}, u32[]{:S(2)}) collective-permute-start(bf16[128,1024]{1,0:T(8,128)(2,1)S(1)} %get-tuple-element.69), channel_id=1, source_target_pairs={{0,4},{1,5},{2,6},{3,7},{4,0},{5,1},{6,2},{7,3},{8,12},{9,13},{10,... | collective-permute-start | bytes 786440 | tf_op jit(solution)/shard_map/ppermute | solution.py:43
  84.2 24.1 %collective-permute-start.23 = (bf16[128,1024]{1,0:T(8,128)(2,1)S(1)}, bf16[128,1024]{1,0:T(8,128)(2,1)S(1)}, u32[]{:S(2)}, u32[]{:S(2)}) collective-permute-start(bf16[128,1024]{1,0:T(8,128)(2,1)S(1)} %get-tuple-element.67), channel_id=1, source_target_pairs={{0,4},{1,5},{2,6},{3,7},{4,0},{5,1},{6,2},{7,3},{8,12},{9,13},{10,... | collective-permute-start | bytes 786440 | tf_op jit(solution)/shard_map/ppermute | solution.py:43
  87.6 31.6 %collective-permute-start.27 = (bf16[3,352,512]{2,1,0:T(8,128)(2,1)S(1)}, bf16[3,352,512]{2,1,0:T(8,128)(2,1)S(1)}, u32[]{:S(2)}, u32[]{:S(2)}) collective-permute-start(bf16[3,352,512]{2,1,0:T(8,128)(2,1)S(1)} %get-tuple-element.74), channel_id=1, source_target_pairs={{0,1},{1,0},{2,3},{3,2},{4,5},{5,4},{6,7},{7,6},{8,9},{9,8},{10,11... | collective-permute-start | bytes 3244040 | tf_op jit(solution)/shard_map/ppermute | solution.py:43
  89.2 17.1 %collective-permute-start.15 = (bf16[128,1024]{1,0:T(8,128)(2,1)S(1)}, bf16[128,1024]{1,0:T(8,128)(2,1)S(1)}, u32[]{:S(2)}, u32[]{:S(2)}) collective-permute-start(bf16[128,1024]{1,0:T(8,128)(2,1)S(1)} %add_convert_fusion.4), channel_id=1, source_target_pairs={{0,8},{1,9},{2,10},{3,11},{4,12},{5,13},{6,14},{7,15},{8,0},{9,1},... | collective-permute-start | bytes 786440 | tf_op jit(solution)/shard_map/ppermute | solution.py:43
  104.8 13.6 %collective-permute-start.25 = (bf16[128,1024]{1,0:T(8,128)(2,1)S(1)}, bf16[128,1024]{1,0:T(8,128)(2,1)S(1)}, u32[]{:S(2)}, u32[]{:S(2)}) collective-permute-start(bf16[128,1024]{1,0:T(8,128)(2,1)S(1)} %add_convert_fusion.2), channel_id=1, source_target_pairs={{0,8},{1,9},{2,10},{3,11},{4,12},{5,13},{6,14},{7,15},{8,0},{9,1},... | collective-permute-start | bytes 786440 | tf_op jit(solution)/shard_map/ppermute | solution.py:43

commit v5 on v4

--- a/solution.py
+++ b/solution.py
@@ -16,18 +16,33 @@
 smem = pl.BlockSpec(memory_space=pltpu.SMEM)
 id_lanes = 128
 costs = {
-    "prepare": 10,
-    ("inputs", 0): 20,
-    ("inputs", 1): 20,
-    ("cot", 0): 20,
-    ("cot", 1): 20,
-    "forward": 20,
-    "backward": 20,
-    ("out", 0): 20,
-    ("out", 1): 20,
-    ("grad", 0): 1,
-    ("grad", 1): 1,
-    "weights": 5,
+    "prep": 10,
+    "pt0": 20,
+    "pt1": 20,
+    "pc0": 20,
+    "pc1": 20,
+    "fwd": 20,
+    "bwd": 20,
+    "co0": 20,
+    "co1": 20,
+    "cg0": 1,
+    "cg1": 1,
+    "ddk1": 5,
+    "ddk0": 5,
+    "dik1": 5,
+    "dik0": 5,
+}
+order = {
+    "t3": ("t1",),
+    "c2": ("t1", "t2",),
+    "c3": ("t3", "yt0", "wx",),
+    "c1": ("t3", "c2", "yt0",),
+    "pc0": ("yt0", "pt1",),
+    "wp1": ("c2", "t3",),
+    "pc1": ("yt1", "yc0", "wp1",),
+    "bwd": ("yo1",),
+    "o": ("cg0",),
+    "ws1": ("T2",),
 }
 
 
@@ -212,20 +227,16 @@
         out[...] = input_grad[index * rows : (index + 1) * rows]
 
 
-def weight_grad_kernel(plane_experts, seq_count, shift, place_ref, *refs):
-    blocks = 2 * plane_experts
-    row_refs, cot_refs, refs = refs[:blocks], refs[blocks : 2 * blocks], refs[2 * blocks :]
-    (hidden_ref, gate_grad_ref, up_grad_ref), refs = refs[:3], refs[3:]
+def weight_grad_kernel(blocks, seq_count, shift, kinds, place_ref, *refs):
+    row_refs, refs = refs[:blocks], refs[blocks:]
+    left_refs, refs = refs[:kinds], refs[kinds:]
     added = refs[: seq_count - 1] if shift == 0 else ()
     out_refs = refs[len(added) :]
     width = out_refs[0].shape[2]
     part = lax.rem(place_ref[1] + shift, seq_count)
     lanes = pl.ds(pl.multiple_of(part * width, width), width)
-    inputs = jnp.concatenate([row[:, lanes] for row in row_refs], axis=0)
-    cot = jnp.concatenate([row[:, lanes] for row in cot_refs], axis=0)
-    for kind, (left, right) in enumerate(
-        ((gate_grad_ref, inputs), (up_grad_ref, inputs), (hidden_ref, cot))
-    ):
+    right = jnp.concatenate([row[:, lanes] for row in row_refs], axis=0)
+    for kind, left in enumerate(left_refs):
         total = lax.dot_general(left[...], right, contract_first, preferred_element_type=f32)
         for part_ref in added:
             total = total + part_ref[kind].astype(f32)
@@ -270,143 +281,225 @@
         ]
     ).astype(jnp.int32)
 
-    table = jnp.concatenate([routes.T, gate_codes.T], axis=0)
-    tables = jnp.stack(
-        [table]
-        + [flipped(table, "blk", step * plane_stride) for step in range(1, planes)],
-        axis=1,
-    )
-
-    own_weights = jnp.stack([w_gate[0].T, w_up[0].T, w_down[0]])
-    pair_weights = flipped(own_weights, "blk", 1)
+    steps = {}
+    made = {}
+
+    def step(name, build):
+        steps[name] = build
+
+    def get(name):
+        if name not in made:
+            waits = [jax.tree.leaves(get(other))[-1] for other in order.get(name, ())]
+            made[name] = steps[name](lambda value: after(value, *waits) if waits else value)
+        return made[name]
+
+    def across(mask):
+        return lambda value: flipped(value, "blk", mask)
+
+    def low_bit(origin):
+        return origin & -origin
 
     def shifted(values, shift):
         return lax.ppermute(
             values, "seq", [(i, (i + shift) % seq_count) for i in range(seq_count)]
         )
 
-    pieces = [
-        shifted(part, -shift) if shift else part
-        for part in (own_weights, pair_weights)
-        for shift in range(seq_count)
-    ]
-
-    def spread(part, starts):
-        chunks = {0: part}
-        step = planes // 2
-        while step:
-            for origin in sorted(chunks):
-                sent = chunks[origin]
-                if origin == 0 and step in starts:
-                    sent = after(sent, starts[step])
-                chunks[origin ^ step] = flipped(sent, "blk", step * plane_stride)
-            step //= 2
-        return [chunks[origin] for origin in range(planes)]
-
-    token_chunks = spread(tokens, {})
-    cot_chunks = spread(
-        cotangent, {planes // 2: token_chunks[1], 1: token_chunks[planes // 2]}
+    table = jnp.concatenate([routes.T, gate_codes.T], axis=0)
+    for origin in range(1, planes):
+        step(
+            f"T{origin}",
+            lambda wait, origin=origin: flipped(wait(table), "blk", origin * plane_stride),
+        )
+
+    for kind, part in (("t", tokens), ("c", cotangent)):
+        step(f"{kind}0", lambda wait, part=part: part)
+        for origin in range(1, planes):
+            step(
+                f"{kind}{origin}",
+                lambda wait, kind=kind, origin=origin: flipped(
+                    wait(get(f"{kind}{origin - low_bit(origin)}")),
+                    "blk",
+                    low_bit(origin) * plane_stride,
+                ),
+            )
+
+    own_weights = jnp.stack([w_gate[0].T, w_up[0].T, w_down[0]])
+    step("wx", lambda wait: flipped(wait(own_weights), "blk", 1))
+    for shift in range(1, seq_count):
+        step(f"ws{shift}", lambda wait, shift=shift: shifted(wait(own_weights), -shift))
+        step(f"wp{shift}", lambda wait, shift=shift: shifted(wait(get("wx")), -shift))
+
+    def pieces():
+        others = range(1, seq_count)
+        return [own_weights, *(get(f"ws{k}") for k in others)] + [
+            get("wx"),
+            *(get(f"wp{k}") for k in others),
+        ]
+
+    step(
+        "prep",
+        lambda wait: called(
+            functools.partial(prepare_kernel, top_count, plane_experts, capacity),
+            (
+                shape((plane_experts, planes, tok_rows), jnp.int32),
+                shape((plane_experts, planes, tok_rows), f32),
+            ),
+            [smem, vmem],
+            costs["prep"],
+        )(
+            place,
+            wait(jnp.stack([table] + [get(f"T{k}") for k in range(1, planes)], axis=1)),
+        ),
     )
 
-    slots, gates = called(
-        functools.partial(prepare_kernel, top_count, plane_experts, capacity),
-        (
-            shape((plane_experts, planes, tok_rows), jnp.int32),
-            shape((plane_experts, planes, tok_rows), f32),
-        ),
-        [smem, vmem],
-        costs["prepare"],
-    )(place, tables)
-
-    def gathered(chunks, with_ids):
-        width = model_width + (id_lanes if with_ids else 0)
-        found = {}
+    def packed(kind, half, wait):
+        width = model_width + (id_lanes if kind == "t" else 0)
+        chunks = [get(f"{kind}{origin}") for origin in range(half, planes, 2)]
+        chunks[0] = wait(chunks[0])
+        return called(
+            functools.partial(compact_kernel, half, kind == "t"),
+            [shape((rows, width), bf16)] * plane_experts,
+            [vmem] * (2 + len(chunks)),
+            costs[f"p{kind}{half}"],
+        )(*get("prep"), *chunks)
+
+    def exchanged(blocks_out, wait):
+        return [
+            flipped(wait(blocks_out[column]), "blk", 2 * column)
+            for column in range(1, plane_experts)
+        ]
+
+    for kind in "tc":
         for half in (0, 1):
-            picked = chunks[half::2]
-            compact = called(
-                functools.partial(compact_kernel, half, with_ids),
-                [shape((rows, width), bf16)] * plane_experts,
-                [vmem] * (2 + len(picked)),
-                costs["inputs" if with_ids else "cot", half],
-            )(slots, gates, *picked)
-            for column in range(plane_experts):
-                found[column, half] = (
-                    flipped(compact[column], "blk", 2 * column) if column else compact[0]
-                )
-        return [found[column, half] for column in range(plane_experts) for half in (0, 1)]
-
-    row_blocks = gathered(token_chunks, True)
-    cot_blocks = gathered(cot_chunks, False)
+            step(f"p{kind}{half}", lambda wait, kind=kind, half=half: packed(kind, half, wait))
+            step(
+                f"y{kind}{half}",
+                lambda wait, kind=kind, half=half: exchanged(get(f"p{kind}{half}"), wait),
+            )
+
+    def row_blocks(kind):
+        halves = [[get(f"p{kind}{half}")[0], *get(f"y{kind}{half}")] for half in (0, 1)]
+        return [block for pair in zip(*halves) for block in pair]
 
     weight_scratch = pltpu.VMEM((3, hidden_width, model_width), bf16)
-    *out_blocks, gate_factor, up_factor, hidden = called(
-        functools.partial(forward_kernel, seq_count, plane_experts, planes, capacity),
-        [shape((rows, model_width), bf16)] * blocks
-        + [shape((slot_rows, hidden_width), f32)] * 2
-        + [shape((slot_rows, hidden_width), bf16)],
-        [smem, smem] + [vmem] * (blocks + len(pieces)),
-        costs["forward"],
-        [weight_scratch],
-    )(place, dropout_key, *row_blocks, *pieces)
-    *grad_blocks, gate_pre_grad, up_pre_grad = called(
-        functools.partial(backward_kernel, seq_count, plane_experts),
-        [shape((rows, model_width), bf16)] * blocks
-        + [shape((slot_rows, hidden_width), bf16)] * 2,
-        [smem] + [vmem] * (blocks + len(pieces) + 2),
-        costs["backward"],
-        [weight_scratch],
-    )(place, *cot_blocks, *pieces, gate_factor, up_factor)
-
-    def brought_back(slot_blocks, scaled):
-        sums = {}
-        for half in (1, 0):
-            held = [slot_blocks[half]] + [
-                flipped(slot_blocks[2 * column + half], "blk", 2 * column)
-                for column in range(1, plane_experts)
+
+    def forward(wait):
+        row_parts, piece_parts = row_blocks("t"), pieces()
+        row_parts[0] = wait(row_parts[0])
+        return called(
+            functools.partial(forward_kernel, seq_count, plane_experts, planes, capacity),
+            [shape((rows, model_width), bf16)] * blocks
+            + [shape((slot_rows, hidden_width), f32)] * 2
+            + [shape((slot_rows, hidden_width), bf16)],
+            [smem, smem] + [vmem] * (blocks + len(piece_parts)),
+            costs["fwd"],
+            [weight_scratch],
+        )(place, dropout_key, *row_parts, *piece_parts)
+
+    def backward(wait):
+        cot_parts, piece_parts = row_blocks("c"), pieces()
+        cot_parts[0] = wait(cot_parts[0])
+        return called(
+            functools.partial(backward_kernel, seq_count, plane_experts),
+            [shape((rows, model_width), bf16)] * blocks
+            + [shape((slot_rows, hidden_width), bf16)] * 2,
+            [smem] + [vmem] * (blocks + len(piece_parts) + 2),
+            costs["bwd"],
+            [weight_scratch],
+        )(place, *cot_parts, *piece_parts, *get("fwd")[blocks : blocks + 2])
+
+    step("fwd", forward)
+    step("bwd", backward)
+
+    def combined(kind, half, wait):
+        source = get("fwd" if kind == "o" else "bwd")
+        held = [wait(source[half]), *get(f"y{kind}{half}")]
+        return called(
+            functools.partial(combine_kernel, half, kind == "o"),
+            [shape((tok_rows, model_width), bf16 if half else f32)] * (planes // 2),
+            [vmem] * (2 + plane_experts),
+            costs[f"c{kind}{half}"],
+        )(*get("prep"), *held)
+
+    def total(kind, origin):
+        value = get(f"c{kind}{origin % 2}")[origin // 2]
+        for other in range(origin + 1, planes):
+            if other - low_bit(other) == origin:
+                value = value.astype(f32) + get(f"z{kind}{other}").astype(f32)
+        return value.astype(bf16)
+
+    for kind in "og":
+        for half in (0, 1):
+            step(
+                f"y{kind}{half}",
+                lambda wait, kind=kind, half=half: exchanged(
+                    [
+                        get("fwd" if kind == "o" else "bwd")[2 * column + half]
+                        for column in range(plane_experts)
+                    ],
+                    wait,
+                ),
+            )
+            step(f"c{kind}{half}", lambda wait, kind=kind, half=half: combined(kind, half, wait))
+        for origin in range(1, planes):
+            step(
+                f"z{kind}{origin}",
+                lambda wait, kind=kind, origin=origin: flipped(
+                    wait(total(kind, origin)), "blk", low_bit(origin) * plane_stride
+                ),
+            )
+        step(f"{kind}", lambda wait, kind=kind: wait(total(kind, 0)))
+
+    def weight_kernel(name, wait, shift):
+        if name == "dd":
+            row_parts, lefts = row_blocks("c"), [get("fwd")[blocks + 2]]
+        else:
+            row_parts, lefts = row_blocks("t"), get("bwd")[blocks:]
+        kinds = len(lefts)
+        arrived = [] if shift else [get(f"{name}s{k}") for k in range(1, seq_count)]
+        lefts = [wait(lefts[0]), *lefts[1:]]
+        if shift:
+            result = [shape((kinds, hidden_width, part_width), bf16)]
+        else:
+            result = [
+                shape((kinds, half_width, part_width), f32),
+                shape((kinds, half_width, part_width), bf16),
             ]
-            combined = called(
-                functools.partial(combine_kernel, half, scaled),
-                [shape((tok_rows, model_width), bf16 if half else f32)] * (planes // 2),
-                [vmem] * (2 + plane_experts),
-                costs["out" if scaled else "grad", half],
-            )(slots, gates, *held)
-            for step in range(planes // 2):
-                sums[2 * step + half] = combined[step]
-        step = 1
-        while step < planes:
-            for origin in sorted(sums, reverse=True):
-                if origin & step:
-                    sums[origin ^ step] = sums[origin ^ step] + flipped(
-                        sums[origin].astype(bf16), "blk", step * plane_stride
-                    ).astype(f32)
-                    del sums[origin]
-            step *= 2
-        return sums[0].astype(bf16)
-
-    layer_out = brought_back(out_blocks, True)
-    tokens_grad = brought_back(grad_blocks, False)
-
-    def weight_grads(shift, out_shape, added):
         return called(
-            functools.partial(weight_grad_kernel, plane_experts, seq_count, shift),
-            out_shape,
-            [smem] + [vmem] * (2 * blocks + 3 + len(added)),
-            costs["weights"],
-        )(place, *row_blocks, *cot_blocks, hidden, gate_pre_grad, up_pre_grad, *added)
-
-    arrived = [
-        shifted(
-            weight_grads(shift, [shape((3, hidden_width, part_width), bf16)], [])[0], shift
+            functools.partial(weight_grad_kernel, blocks, seq_count, shift, kinds),
+            result,
+            [smem] + [vmem] * (blocks + kinds + len(arrived)),
+            costs[f"{name}k{min(shift, 1)}"],
+        )(place, *row_parts, *lefts, *arrived)
+
+    for name in ("dd", "di"):
+        for shift in range(seq_count):
+            step(
+                f"{name}k{shift}",
+                lambda wait, name=name, shift=shift: weight_kernel(name, wait, shift),
+            )
+            step(
+                f"{name}s{shift}",
+                lambda wait, name=name, shift=shift: shifted(
+                    wait(get(f"{name}k{shift}")[0]), shift
+                ),
+            )
+        step(f"{name}x", lambda wait, name=name: across(1)(wait(get(f"{name}k0")[1])))
+        step(
+            name,
+            lambda wait, name=name: (
+                wait(get(f"{name}k0")[0]) + get(f"{name}x").astype(f32)
+            ).astype(bf16),
         )
-        for shift in range(1, seq_count)
-    ]
-    own_sum, pair_sum = weight_grads(
-        0,
-        [shape((3, half_width, part_width), f32), shape((3, half_width, part_width), bf16)],
-        arrived,
+
+    down_grad, input_grads = get("dd"), get("di")
+    return (
+        get("o"),
+        get("g"),
+        input_grads[0].T[None],
+        input_grads[1].T[None],
+        down_grad,
     )
-    grads = (own_sum + flipped(pair_sum, "blk", 1).astype(f32)).astype(bf16)
-    return (layer_out, tokens_grad, grads[0].T[None], grads[1].T[None], grads[2][None])
 
 
 def solution(mesh):

time: 121 us -> 115 us (0.950)
  waiting for transfers between devices: 62.6 us -> 52.7 us
  starting transfers between devices: 35.9 us -> 37.7 us
  Pallas kernels: 16 us -> 17.4 us
    ppermute x25 -> x26, waiting for transfers between devices: 62.1 us -> 52.7 us  [flipped(): lax.ppermute(values, axis, [(i, i ^ mask) for i in range(lax.axis_size(ax...]
    pallas_call x12 -> x14, Pallas kernels: 15.3 us -> 16.7 us  [the longest x4 5.17 us: weight_kernel(): called(functools.partial(weight_grad_kernel, blocks, seq_count, shift, ki...]
    ppermute x25 -> x26, starting transfers between devices: 35.8 us -> 37.1 us  [flipped(): lax.ppermute(values, axis, [(i, i ^ mask) for i in range(lax.axis_size(ax...]
    convert_element_type x5 -> x6, other arithmetic: 2.09 us -> 2.82 us  [the longest x4 1.73 us: total(): return value.astype(bf16)]
  transfers between devices with their start and end apart: 28 -> 30, of which waited for: 13 -> 13; matrix products, arithmetic and copies ran while one was open for 3% -> 3% of each run, Pallas kernels for 13% -> 15%
where the time goes in v5:
time: 115 us
  waiting for transfers between devices  52.7 us (46%)
  starting transfers between devices  37.7 us (33%)
  Pallas kernels  17.4 us (15%)
  other arithmetic  4.86 us (4%)
    ppermute x26, waiting for transfers between devices, flipped(): lax.ppermute(values, axis, [(i, i ^ mask) for i in range(lax.axis_size(ax...  52.7 us
    ppermute x26, starting transfers between devices, flipped(): lax.ppermute(values, axis, [(i, i ^ mask) for i in range(lax.axis_size(ax...  37.1 us
    pallas_call x4, Pallas kernels, weight_kernel(): called(functools.partial(weight_grad_kernel, blocks, seq_count, shift, ki...  5.17 us
    pallas_call x1, Pallas kernels, backward(): called(functools.partial(backward_kernel, seq_count, plane_experts), [sha...  4.77 us
    pallas_call x1, Pallas kernels, forward(): called(functools.partial(forward_kernel, seq_count, plane_experts, planes...  4.19 us
  transfers between devices with their start and end apart: 30, of which 13 were waited for; matrix products, arithmetic and copies ran while one was open for 3% of the time, Pallas kernels for 15%

profile of v5, /device:TPU:0, one launch (start us, length us, event | category | flops | bytes accessed | tf_op | source)
XLA Modules:
  0.0 114.6 jit_solution(9888512282034327420)
XLA Ops:
  0.6 0.7 pad_add_fusion.1
  1.3 5.0 %collective-permute-start.2 = (s32[4,128]{1,0:T(4,128)S(1)}, s32[4,128]{1,0:T(4,128)S(1)}, u32[]{:S(2)}, u32[]{:S(2)}) collective-permute-start(s32[4,128]{1,0:T(4,128)S(1)} %pad_add_fusion.1), channel_id=1, source_target_pairs={{0,12},{1,13},{2,14},{3,15},{4,8},{5,9},{6,10},{7,11},{8,4},{9,5},... | collective-permute-start | bytes 6152 | tf_op jit(solution)/shard_map/ppermute | solution.py:58
  6.4 0.6 collective-permute-start
  7.0 2.3 %collective-permute-start.3 = (bf16[128,1024]{1,0:T(8,128)(2,1)}, bf16[128,1024]{1,0:T(8,128)(2,1)S(1)}, u32[]{:S(2)}, u32[]{:S(2)}) collective-permute-start(bf16[128,1024]{1,0:T(8,128)(2,1)} %refs_0_.1), channel_id=1, source_target_pairs={{0,8},{1,9},{2,10},{3,11},{4,12},{5,13},{6,14},{7,15},{8,0},{9,1},... | collective-permute-start | bytes 786440 | tf_op jit(solution)/shard_map/ppermute | solution.py:58
  9.3 2.0 %collective-permute-start.4 = (bf16[128,1024]{1,0:T(8,128)(2,1)}, bf16[128,1024]{1,0:T(8,128)(2,1)S(1)}, u32[]{:S(2)}, u32[]{:S(2)}) collective-permute-start(bf16[128,1024]{1,0:T(8,128)(2,1)} %refs_0_.1), channel_id=1, source_target_pairs={{0,4},{1,5},{2,6},{3,7},{4,0},{5,1},{6,2},{7,3},{8,12},{9,13},{10,... | collective-permute-start | bytes 786440 | tf_op jit(solution)/shard_map/ppermute | solution.py:58
  11.3 1.3 %pad_maximum_fusion.refs_4_ = bf16[3,352,512]{2,1,0:T(8,128)(2,1)S(1)} fusion(bf16[1,352,512]{2,1,0:T(8,128)(2,1)} %param.15, bf16[1,352,512]{2,1,0:T(8,128)(2,1)} %bitcast.41, bf16[1,352,512]{2,1,0:T(8,128)(2,1)} %bitcast.42), kind=kLoop, calls=%fused_computation.1 | loop fusion | flops 1081344 | bytes 2162688 | tf_op jit(solution)/shard_map/stack | solution.py:326
  12.7 0.1 stack.55.place_ref
  12.8 1.6 %collective-permute-start.9 = (bf16[3,352,512]{2,1,0:T(8,128)(2,1)S(1)}, bf16[3,352,512]{2,1,0:T(8,128)(2,1)S(1)}, u32[]{:S(2)}, u32[]{:S(2)}) collective-permute-start(bf16[3,352,512]{2,1,0:T(8,128)(2,1)S(1)} %pad_maximum_fusion.refs_4_), channel_id=1, source_target_pairs={{0,1},{1,0},{2,3},{3,2},{4,5},{5,4},{6,7},{7,6},{8,9},{9,8},{10,11... | collective-permute-start | bytes 3244040 | tf_op jit(solution)/shard_map/ppermute | solution.py:58
  14.4 0.7 shard_map.119
  15.1 6.3 %collective-permute-done.3.refs_1_ = bf16[128,1024]{1,0:T(8,128)(2,1)S(1)} collective-permute-done((bf16[128,1024]{1,0:T(8,128)(2,1)}, bf16[128,1024]{1,0:T(8,128)(2,1)S(1)}, u32[]{:S(2)}, u32[]{:S(2)}) %collective-permute-start.3) | collective-permute-done | bytes 262176 | tf_op jit(solution)/shard_map/ppermute | solution.py:58
  21.4 0.1 collective-permute-done.4.refs_0_
  21.5 1.2 %collective-permute-start.5 = (bf16[128,1024]{1,0:T(8,128)(2,1)S(1)}, bf16[128,1024]{1,0:T(8,128)(2,1)S(1)}, u32[]{:S(2)}, u32[]{:S(2)}) collective-permute-start(bf16[128,1024]{1,0:T(8,128)(2,1)S(1)} %collective-permute-done.3.refs_1_), channel_id=1, source_target_pairs={{0,4},{1,5},{2,6},{3,7},{4,0},{5,1},{6,2},{7,3},{8,12},{9,13},{10,... | collective-permute-start | bytes 786440 | tf_op jit(solution)/shard_map/ppermute | solution.py:58
  22.7 0.3 shard_map.120
  23.0 1.6 %collective-permute-start.6 = (bf16[128,1152]{1,0:T(8,128)(2,1)S(1)}, bf16[128,1152]{1,0:T(8,128)(2,1)S(1)}, u32[]{:S(2)}, u32[]{:S(2)}) collective-permute-start(bf16[128,1152]{1,0:T(8,128)(2,1)S(1)} %get-tuple-element.55), channel_id=1, source_target_pairs={{0,2},{1,3},{2,0},{3,1},{4,6},{5,7},{6,4},{7,5},{8,10},{9,11},{10,... | collective-permute-start | bytes 884744 | tf_op jit(solution)/shard_map/ppermute | solution.py:58
  24.6 2.3 %collective-permute-start.10 = (bf16[128,1024]{1,0:T(8,128)(2,1)S(1)}, bf16[128,1024]{1,0:T(8,128)(2,1)S(1)}, u32[]{:S(2)}, u32[]{:S(2)}) collective-permute-start(bf16[128,1024]{1,0:T(8,128)(2,1)S(1)} %copy-done.1), channel_id=1, source_target_pairs={{0,8},{1,9},{2,10},{3,11},{4,12},{5,13},{6,14},{7,15},{8,0},{9,1},... | collective-permute-start | bytes 786440 | tf_op jit(solution)/shard_map/ppermute | solution.py:58
  26.9 5.5 %collective-permute-done.5.refs_1_ = bf16[128,1024]{1,0:T(8,128)(2,1)S(1)} collective-permute-done((bf16[128,1024]{1,0:T(8,128)(2,1)S(1)}, bf16[128,1024]{1,0:T(8,128)(2,1)S(1)}, u32[]{:S(2)}, u32[]{:S(2)}) %collective-permute-start.5) | collective-permute-done | bytes 262176 | tf_op jit(solution)/shard_map/ppermute | solution.py:58
  32.4 0.3 shard_map.121
  32.8 2.3 %collective-permute-start.7 = (bf16[128,1152]{1,0:T(8,128)(2,1)S(1)}, bf16[128,1152]{1,0:T(8,128)(2,1)S(1)}, u32[]{:S(2)}, u32[]{:S(2)}) collective-permute-start(bf16[128,1152]{1,0:T(8,128)(2,1)S(1)} %get-tuple-element.56), channel_id=1, source_target_pairs={{0,2},{1,3},{2,0},{3,1},{4,6},{5,7},{6,4},{7,5},{8,10},{9,11},{10,... | collective-permute-start | bytes 884744 | tf_op jit(solution)/shard_map/ppermute | solution.py:58
  35.0 3.5 %collective-permute-done.10.refs_1_ = bf16[128,1024]{1,0:T(8,128)(2,1)S(1)} collective-permute-done((bf16[128,1024]{1,0:T(8,128)(2,1)S(1)}, bf16[128,1024]{1,0:T(8,128)(2,1)S(1)}, u32[]{:S(2)}, u32[]{:S(2)}) %collective-permute-start.10) | collective-permute-done | bytes 262176 | tf_op jit(solution)/shard_map/ppermute | solution.py:58
  38.5 0.3 shard_map.125
  38.9 0.9 collective-permute-start.18
  39.8 2.0 %collective-permute-start.19 = (bf16[128,1024]{1,0:T(8,128)(2,1)S(1)}, bf16[128,1024]{1,0:T(8,128)(2,1)S(1)}, u32[]{:S(2)}, u32[]{:S(2)}) collective-permute-start(bf16[128,1024]{1,0:T(8,128)(2,1)S(1)} %collective-permute-done.10.refs_1_), channel_id=1, source_target_pairs={{0,4},{1,5},{2,6},{3,7},{4,0},{5,1},{6,2},{7,3},{8,12},{9,13},{10,... | collective-permute-start | bytes 786440 | tf_op jit(solution)/shard_map/ppermute | solution.py:58
  41.8 4.2 %shard_map.122 = (bf16[128,1024]{1,0:T(8,128)(2,1)S(1)}, bf16[128,1024]{1,0:T(8,128)(2,1)S(1)}, bf16[128,1024]{1,0:T(8,128)(2,1)S(1)}, bf16[128,1024]{1,0:T(8,12...) custom-call(s32[8]{0:T(128)S(1)} %stack.55.place_ref, s32[2]{0:T(128)S(1)} %copy-done.2, ...), custom_call_target="tpu_custom_call" | custom-call | flops 20000000000 | bytes 60000000 | tf_op jit(solution)/shard_map/pallas_call | solution.py:389
  46.0 1.2 %collective-permute-start.12 = (bf16[128,1024]{1,0:T(8,128)(2,1)S(1)}, bf16[128,1024]{1,0:T(8,128)(2,1)S(1)}, u32[]{:S(2)}, u32[]{:S(2)}) collective-permute-start(bf16[128,1024]{1,0:T(8,128)(2,1)S(1)} %get-tuple-element.61), channel_id=1, source_target_pairs={{0,2},{1,3},{2,0},{3,1},{4,6},{5,7},{6,4},{7,5},{8,10},{9,11},{10,... | collective-permute-start | bytes 786440 | tf_op jit(solution)/shard_map/ppermute | solution.py:58
  47.2 0.8 collective-permute-start.13
  48.1 2.5 %collective-permute-done.19.refs_1_ = bf16[128,1024]{1,0:T(8,128)(2,1)S(1)} collective-permute-done((bf16[128,1024]{1,0:T(8,128)(2,1)S(1)}, bf16[128,1024]{1,0:T(8,128)(2,1)S(1)}, u32[]{:S(2)}, u32[]{:S(2)}) %collective-permute-start.19) | collective-permute-done | bytes 262176 | tf_op jit(solution)/shard_map/ppermute | solution.py:58
  50.6 0.3 shard_map.126
  50.9 0.8 collective-permute-start.20
  51.7 9.1 %collective-permute-done.13.refs_1_ = bf16[128,1024]{1,0:T(8,128)(2,1)S(1)} collective-permute-done((bf16[128,1024]{1,0:T(8,128)(2,1)S(1)}, bf16[128,1024]{1,0:T(8,128)(2,1)S(1)}, u32[]{:S(2)}, u32[]{:S(2)}) %collective-permute-start.13) | collective-permute-done | bytes 262176 | tf_op jit(solution)/shard_map/ppermute | solution.py:58
  60.9 0.3 shard_map.124
  61.2 1.5 %collective-permute-start.15 = (bf16[128,1024]{1,0:T(8,128)(2,1)S(1)}, bf16[128,1024]{1,0:T(8,128)(2,1)S(1)}, u32[]{:S(2)}, u32[]{:S(2)}) collective-permute-start(bf16[128,1024]{1,0:T(8,128)(2,1)S(1)} %get-tuple-element.67), channel_id=1, source_target_pairs={{0,4},{1,5},{2,6},{3,7},{4,0},{5,1},{6,2},{7,3},{8,12},{9,13},{10,... | collective-permute-start | bytes 786440 | tf_op jit(solution)/shard_map/ppermute | solution.py:58
  62.7 0.6 collective-permute-start.14
  63.3 2.2 %collective-permute-done.20.refs_3_ = bf16[128,1024]{1,0:T(8,128)(2,1)S(1)} collective-permute-done((bf16[128,1024]{1,0:T(8,128)(2,1)S(1)}, bf16[128,1024]{1,0:T(8,128)(2,1)S(1)}, u32[]{:S(2)}, u32[]{:S(2)}) %collective-permute-start.20) | collective-permute-done | bytes 262176 | tf_op jit(solution)/shard_map/ppermute | solution.py:58
  65.5 4.8 %shard_map.127 = (bf16[128,1024]{1,0:T(8,128)(2,1)S(1)}, bf16[128,1024]{1,0:T(8,128)(2,1)S(1)}, bf16[128,1024]{1,0:T(8,128)(2,1)S(1)}, bf16[128,1024]{1,0:T(8,12...) custom-call(s32[8]{0:T(128)S(1)} %stack.55.place_ref, ...), custom_call_target="tpu_custom_call" | custom-call | flops 20000000000 | bytes 60000000 | tf_op jit(solution)/shard_map/pallas_call | solution.py:402
  70.3 1.2 %collective-permute-start.22 = (bf16[128,1024]{1,0:T(8,128)(2,1)S(1)}, bf16[128,1024]{1,0:T(8,128)(2,1)S(1)}, u32[]{:S(2)}, u32[]{:S(2)}) collective-permute-start(bf16[128,1024]{1,0:T(8,128)(2,1)S(1)} %get-tuple-element.85), channel_id=1, source_target_pairs={{0,2},{1,3},{2,0},{3,1},{4,6},{5,7},{6,4},{7,5},{8,10},{9,11},{10,... | collective-permute-start | bytes 786440 | tf_op jit(solution)/shard_map/ppermute | solution.py:58
  71.5 1.5 %shard_map.130 = bf16[2,704,512]{2,1,0:T(8,128)(2,1)S(1)} custom-call(s32[8]{0:T(128)S(1)} %stack.55.place_ref, bf16[128,1152]{1,0:T(8,128)(2,1)S(1)} %get-tuple-element.52.refs_0_, bf16[128,1152]{1,0:T(8,128)(2,1)S(1)} %get-tuple-element.54.refs_1_, bf16[128,1152]{1,0:T(8,128)(2,1)S(1)} %collective-permute-done.6.refs_2_, ...), custom_call_target="tpu_custom_call" | custom-call | flops 5000000000 | bytes 15000000 | tf_op jit(solution)/shard_map/pallas_call | solution.py:468
  73.0 0.1 collective-permute-start.26
  73.1 1.1 shard_map.132
  74.2 0.6 collective-permute-start.28
  74.8 0.3 shard_map.123
  75.1 2.6 %collective-permute-done.22.refs_1_ = bf16[128,1024]{1,0:T(8,128)(2,1)S(1)} collective-permute-done((bf16[128,1024]{1,0:T(8,128)(2,1)S(1)}, bf16[128,1024]{1,0:T(8,128)(2,1)S(1)}, u32[]{:S(2)}, u32[]{:S(2)}) %collective-permute-start.22) | collective-permute-done | bytes 262176 | tf_op jit(solution)/shard_map/ppermute | solution.py:58
  77.7 1.2 %collective-permute-start.21 = (bf16[128,1024]{1,0:T(8,128)(2,1)S(1)}, bf16[128,1024]{1,0:T(8,128)(2,1)S(1)}, u32[]{:S(2)}, u32[]{:S(2)}) collective-permute-start(bf16[128,1024]{1,0:T(8,128)(2,1)S(1)} %get-tuple-element.80), channel_id=1, source_target_pairs={{0,2},{1,3},{2,0},{3,1},{4,6},{5,7},{6,4},{7,5},{8,10},{9,11},{10,... | collective-permute-start | bytes 786440 | tf_op jit(solution)/shard_map/ppermute | solution.py:58
  78.9 0.3 shard_map.129
  79.2 1.6 %collective-permute-start.24 = (bf16[128,1024]{1,0:T(8,128)(2,1)S(1)}, bf16[128,1024]{1,0:T(8,128)(2,1)S(1)}, u32[]{:S(2)}, u32[]{:S(2)}) collective-permute-start(bf16[128,1024]{1,0:T(8,128)(2,1)S(1)} %get-tuple-element.87), channel_id=1, source_target_pairs={{0,4},{1,5},{2,6},{3,7},{4,0},{5,1},{6,2},{7,3},{8,12},{9,13},{10,... | collective-permute-start | bytes 786440 | tf_op jit(solution)/shard_map/ppermute | solution.py:58
  80.8 0.1 add_convert_fusion.5
  80.9 3.3 %collective-permute-done.21.refs_1_ = bf16[128,1024]{1,0:T(8,128)(2,1)S(1)} collective-permute-done((bf16[128,1024]{1,0:T(8,128)(2,1)S(1)}, bf16[128,1024]{1,0:T(8,128)(2,1)S(1)}, u32[]{:S(2)}, u32[]{:S(2)}) %collective-permute-start.21) | collective-permute-done | bytes 262176 | tf_op jit(solution)/shard_map/ppermute | solution.py:58
  84.2 2.3 %collective-permute-start.16 = (bf16[128,1024]{1,0:T(8,128)(2,1)S(1)}, bf16[128,1024]{1,0:T(8,128)(2,1)S(1)}, u32[]{:S(2)}, u32[]{:S(2)}) collective-permute-start(bf16[128,1024]{1,0:T(8,128)(2,1)S(1)} %add_convert_fusion.5), channel_id=1, source_target_pairs={{0,8},{1,9},{2,10},{3,11},{4,12},{5,13},{6,14},{7,15},{8,0},{9,1},... | collective-permute-start | bytes 786440 | tf_op jit(solution)/shard_map/ppermute | solution.py:58
  86.5 0.3 shard_map.128
  86.8 1.2 %collective-permute-done.24 = bf16[128,1024]{1,0:T(8,128)(2,1)S(1)} collective-permute-done((bf16[128,1024]{1,0:T(8,128)(2,1)S(1)}, bf16[128,1024]{1,0:T(8,128)(2,1)S(1)}, u32[]{:S(2)}, u32[]{:S(2)}) %collective-permute-start.24) | collective-permute-done | bytes 262176 | tf_op jit(solution)/shard_map/ppermute | solution.py:58
  88.0 0.4 collective-permute-start.23
  88.4 0.1 add_convert_fusion.3
  88.4 1.3 %collective-permute-start.25 = (bf16[128,1024]{1,0:T(8,128)(2,1)S(1)}, bf16[128,1024]{1,0:T(8,128)(2,1)S(1)}, u32[]{:S(2)}, u32[]{:S(2)}) collective-permute-start(bf16[128,1024]{1,0:T(8,128)(2,1)S(1)} %add_convert_fusion.3), channel_id=1, source_target_pairs={{0,8},{1,9},{2,10},{3,11},{4,12},{5,13},{6,14},{7,15},{8,0},{9,1},... | collective-permute-start | bytes 786440 | tf_op jit(solution)/shard_map/ppermute | solution.py:58
  89.8 1.1 shard_map.133
  90.9 1.6 %collective-permute-start.29 = (bf16[1,352,512]{2,1,0:T(8,128)(2,1)S(1)}, bf16[1,352,512]{2,1,0:T(8,128)(2,1)S(1)}, u32[]{:S(2)}, u32[]{:S(2)}) collective-permute-start(bf16[1,352,512]{2,1,0:T(8,128)(2,1)S(1)} %get-tuple-element.94), channel_id=1, source_target_pairs={{0,1},{1,0},{2,3},{3,2},{4,5},{5,4},{6,7},{7,6},{8,9},{9,8},{10,11... | collective-permute-start | bytes 1081352 | tf_op jit(solution)/shard_map/ppermute | solution.py:58
  92.4 1.5 %shard_map.131 = (f32[2,352,512]{2,1,0:T(8,128)S(1)}, bf16[2,352,512]{2,1,0:T(8,128)(2,1)S(1)}) custom-call(s32[8]{0:T(128)S(1)} %stack.55.place_ref, bf16[128,1152]{1,0:T(8,128)(2,1)S(1)} %get-tuple-element.52.refs_0_, bf16[128,1152]{1,0:T(8,128)(2,1)S(1)} %get-tuple-element.54.refs_1_, bf16[128,1152]{1,0:T(8,128)(2,1)S(1)} %collective-permute-done.6.refs_2_, ...), custom_call_target="tpu_custom_call" | custom-call | flops 5000000000 | bytes 15000000 | tf_op jit(solution)/shard_map/pallas_call | solution.py:468
  93.9 0.6 collective-permute-start.27
  94.5 6.5 %collective-permute-done.16 = bf16[128,1024]{1,0:T(8,128)(2,1)S(1)} collective-permute-done((bf16[128,1024]{1,0:T(8,128)(2,1)S(1)}, bf16[128,1024]{1,0:T(8,128)(2,1)S(1)}, u32[]{:S(2)}, u32[]{:S(2)}) %collective-permute-start.16) | collective-permute-done | bytes 262176 | tf_op jit(solution)/shard_map/ppermute | solution.py:58
  101.0 0.8 add_convert_fusion.4
  101.8 5.7 %collective-permute-done.25 = bf16[128,1024]{1,0:T(8,128)(2,1)S(1)} collective-permute-done((bf16[128,1024]{1,0:T(8,128)(2,1)S(1)}, bf16[128,1024]{1,0:T(8,128)(2,1)S(1)}, u32[]{:S(2)}, u32[]{:S(2)}) %collective-permute-start.25) | collective-permute-done | bytes 262176 | tf_op jit(solution)/shard_map/ppermute | solution.py:58
  107.5 0.8 add_convert_fusion.2
  108.3 0.8 add_convert_fusion.1
  109.2 4.3 %collective-permute-done.27 = bf16[2,352,512]{2,1,0:T(8,128)(2,1)S(1)} collective-permute-done((bf16[2,352,512]{2,1,0:T(8,128)(2,1)S(1)}, bf16[2,352,512]{2,1,0:T(8,128)(2,1)S(1)}, u32[]{:S(2)}, u32[]{:S(2)}) %collective-permute-start.27) | collective-permute-done | bytes 720928 | tf_op jit(solution)/shard_map/ppermute | solution.py:58
  113.4 0.2 add_convert_fusion
  113.7 0.9 slice_bitcast_fusion
  (28 shorter events, 0.1 us)
Async XLA Ops:
  1.3 13.0 %collective-permute-start.2 = (s32[4,128]{1,0:T(4,128)S(1)}, s32[4,128]{1,0:T(4,128)S(1)}, u32[]{:S(2)}, u32[]{:S(2)}) collective-permute-start(s32[4,128]{1,0:T(4,128)S(1)} %pad_add_fusion.1), channel_id=1, source_target_pairs={{0,12},{1,13},{2,14},{3,15},{4,8},{5,9},{6,10},{7,11},{8,4},{9,5},... | collective-permute-start | bytes 6152 | tf_op jit(solution)/shard_map/ppermute | solution.py:58
  6.4 6.4 %collective-permute-start.1 = (s32[4,128]{1,0:T(4,128)S(1)}, s32[4,128]{1,0:T(4,128)S(1)}, u32[]{:S(2)}, u32[]{:S(2)}) collective-permute-start(s32[4,128]{1,0:T(4,128)S(1)} %pad_add_fusion.1), channel_id=1, source_target_pairs={{0,8},{1,9},{2,10},{3,11},{4,12},{5,13},{6,14},{7,15},{8,0},{9,1},... | collective-permute-start | bytes 6152 | tf_op jit(solution)/shard_map/ppermute | solution.py:58
  6.4 8.0 %collective-permute-start = (s32[4,128]{1,0:T(4,128)S(1)}, s32[4,128]{1,0:T(4,128)S(1)}, u32[]{:S(2)}, u32[]{:S(2)}) collective-permute-start(s32[4,128]{1,0:T(4,128)S(1)} %pad_add_fusion.1), channel_id=1, source_target_pairs={{0,4},{1,5},{2,6},{3,7},{4,0},{5,1},{6,2},{7,3},{8,12},{9,13},{10,... | collective-permute-start | bytes 6152 | tf_op jit(solution)/shard_map/ppermute | solution.py:58
  7.0 14.3 %collective-permute-start.3 = (bf16[128,1024]{1,0:T(8,128)(2,1)}, bf16[128,1024]{1,0:T(8,128)(2,1)S(1)}, u32[]{:S(2)}, u32[]{:S(2)}) collective-permute-start(bf16[128,1024]{1,0:T(8,128)(2,1)} %refs_0_.1), channel_id=1, source_target_pairs={{0,8},{1,9},{2,10},{3,11},{4,12},{5,13},{6,14},{7,15},{8,0},{9,1},... | collective-permute-start | bytes 786440 | tf_op jit(solution)/shard_map/ppermute | solution.py:58
  9.3 12.2 %collective-permute-start.4 = (bf16[128,1024]{1,0:T(8,128)(2,1)}, bf16[128,1024]{1,0:T(8,128)(2,1)S(1)}, u32[]{:S(2)}, u32[]{:S(2)}) collective-permute-start(bf16[128,1024]{1,0:T(8,128)(2,1)} %refs_0_.1), channel_id=1, source_target_pairs={{0,4},{1,5},{2,6},{3,7},{4,0},{5,1},{6,2},{7,3},{8,12},{9,13},{10,... | collective-permute-start | bytes 786440 | tf_op jit(solution)/shard_map/ppermute | solution.py:58
  12.8 25.8 %collective-permute-start.9 = (bf16[3,352,512]{2,1,0:T(8,128)(2,1)S(1)}, bf16[3,352,512]{2,1,0:T(8,128)(2,1)S(1)}, u32[]{:S(2)}, u32[]{:S(2)}) collective-permute-start(bf16[3,352,512]{2,1,0:T(8,128)(2,1)S(1)} %pad_maximum_fusion.refs_4_), channel_id=1, source_target_pairs={{0,1},{1,0},{2,3},{3,2},{4,5},{5,4},{6,7},{7,6},{8,9},{9,8},{10,11... | collective-permute-start | bytes 3244040 | tf_op jit(solution)/shard_map/ppermute | solution.py:58
  14.3 27.5 %collective-permute-start.8 = (bf16[3,352,512]{2,1,0:T(8,128)(2,1)S(1)}, bf16[3,352,512]{2,1,0:T(8,128)(2,1)S(1)}, u32[]{:S(2)}, u32[]{:S(2)}) collective-permute-start(bf16[3,352,512]{2,1,0:T(8,128)(2,1)S(1)} %pad_maximum_fusion.refs_4_), channel_id=1, source_target_pairs={{0,16},{16,0},{1,17},{17,1},{2,18},{18,2},{3,19},{19,3},{4,20},{20... | collective-permute-start | bytes 3244040 | tf_op jit(solution)/shard_map/ppermute | solution.py:303
  14.4 8.3 %copy-start = (bf16[128,1024]{1,0:T(8,128)(2,1)S(1)}, bf16[128,1024]{1,0:T(8,128)(2,1)}, u32[]{:S(2)}) copy-start(bf16[128,1024]{1,0:T(8,128)(2,1)} %refs_0_.1) | copy-start | bytes 786436
  21.5 10.9 %collective-permute-start.5 = (bf16[128,1024]{1,0:T(8,128)(2,1)S(1)}, bf16[128,1024]{1,0:T(8,128)(2,1)S(1)}, u32[]{:S(2)}, u32[]{:S(2)}) collective-permute-start(bf16[128,1024]{1,0:T(8,128)(2,1)S(1)} %collective-permute-done.3.refs_1_), channel_id=1, source_target_pairs={{0,4},{1,5},{2,6},{3,7},{4,0},{5,1},{6,2},{7,3},{8,12},{9,13},{10,... | collective-permute-start | bytes 786440 | tf_op jit(solution)/shard_map/ppermute | solution.py:58
  22.7 1.9 %copy-start.1 = (bf16[128,1024]{1,0:T(8,128)(2,1)S(1)}, bf16[128,1024]{1,0:T(8,128)(2,1)}, u32[]{:S(2)}) copy-start(bf16[128,1024]{1,0:T(8,128)(2,1)} %refs_0_.2) | copy-start | bytes 786436
  23.0 12.0 %collective-permute-start.6 = (bf16[128,1152]{1,0:T(8,128)(2,1)S(1)}, bf16[128,1152]{1,0:T(8,128)(2,1)S(1)}, u32[]{:S(2)}, u32[]{:S(2)}) collective-permute-start(bf16[128,1152]{1,0:T(8,128)(2,1)S(1)} %get-tuple-element.55), channel_id=1, source_target_pairs={{0,2},{1,3},{2,0},{3,1},{4,6},{5,7},{6,4},{7,5},{8,10},{9,11},{10,... | collective-permute-start | bytes 884744 | tf_op jit(solution)/shard_map/ppermute | solution.py:58
  24.6 13.9 %collective-permute-start.10 = (bf16[128,1024]{1,0:T(8,128)(2,1)S(1)}, bf16[128,1024]{1,0:T(8,128)(2,1)S(1)}, u32[]{:S(2)}, u32[]{:S(2)}) collective-permute-start(bf16[128,1024]{1,0:T(8,128)(2,1)S(1)} %copy-done.1), channel_id=1, source_target_pairs={{0,8},{1,9},{2,10},{3,11},{4,12},{5,13},{6,14},{7,15},{8,0},{9,1},... | collective-permute-start | bytes 786440 | tf_op jit(solution)/shard_map/ppermute | solution.py:58
  32.7 9.1 %copy-start.2 = (s32[2]{0:T(128)S(1)}, s32[2]{0:T(128)}, u32[]{:S(2)}) copy-start(s32[2]{0:T(128)} %key_ref.1) | copy-start | bytes 28
  32.8 7.0 %collective-permute-start.7 = (bf16[128,1152]{1,0:T(8,128)(2,1)S(1)}, bf16[128,1152]{1,0:T(8,128)(2,1)S(1)}, u32[]{:S(2)}, u32[]{:S(2)}) collective-permute-start(bf16[128,1152]{1,0:T(8,128)(2,1)S(1)} %get-tuple-element.56), channel_id=1, source_target_pairs={{0,2},{1,3},{2,0},{3,1},{4,6},{5,7},{6,4},{7,5},{8,10},{9,11},{10,... | collective-permute-start | bytes 884744 | tf_op jit(solution)/shard_map/ppermute | solution.py:58
  38.5 9.6 %collective-permute-start.17 = (bf16[128,1024]{1,0:T(8,128)(2,1)S(1)}, bf16[128,1024]{1,0:T(8,128)(2,1)S(1)}, u32[]{:S(2)}, u32[]{:S(2)}) collective-permute-start(bf16[128,1024]{1,0:T(8,128)(2,1)S(1)} %copy-done.1), channel_id=1, source_target_pairs={{0,4},{1,5},{2,6},{3,7},{4,0},{5,1},{6,2},{7,3},{8,12},{9,13},{10,... | collective-permute-start | bytes 786440 | tf_op jit(solution)/shard_map/ppermute | solution.py:58
  38.5 3.3 %collective-permute-start.11 = (bf16[3,352,512]{2,1,0:T(8,128)(2,1)S(1)}, bf16[3,352,512]{2,1,0:T(8,128)(2,1)S(1)}, u32[]{:S(2)}, u32[]{:S(2)}) collective-permute-start(bf16[3,352,512]{2,1,0:T(8,128)(2,1)S(1)} %collective-permute-done.9.refs_6_), channel_id=1, source_target_pairs={{0,16},{16,0},{1,17},{17,1},{2,18},{18,2},{3,19},{19,3},{4,20},{20... | collective-permute-start | bytes 3244040 | tf_op jit(solution)/shard_map/ppermute | solution.py:303
  38.9 9.2 %collective-permute-start.18 = (bf16[128,1024]{1,0:T(8,128)(2,1)S(1)}, bf16[128,1024]{1,0:T(8,128)(2,1)S(1)}, u32[]{:S(2)}, u32[]{:S(2)}) collective-permute-start(bf16[128,1024]{1,0:T(8,128)(2,1)S(1)} %get-tuple-element.72), channel_id=1, source_target_pairs={{0,2},{1,3},{2,0},{3,1},{4,6},{5,7},{6,4},{7,5},{8,10},{9,11},{10,... | collective-permute-start | bytes 786440 | tf_op jit(solution)/shard_map/ppermute | solution.py:58
  39.8 10.8 %collective-permute-start.19 = (bf16[128,1024]{1,0:T(8,128)(2,1)S(1)}, bf16[128,1024]{1,0:T(8,128)(2,1)S(1)}, u32[]{:S(2)}, u32[]{:S(2)}) collective-permute-start(bf16[128,1024]{1,0:T(8,128)(2,1)S(1)} %collective-permute-done.10.refs_1_), channel_id=1, source_target_pairs={{0,4},{1,5},{2,6},{3,7},{4,0},{5,1},{6,2},{7,3},{8,12},{9,13},{10,... | collective-permute-start | bytes 786440 | tf_op jit(solution)/shard_map/ppermute | solution.py:58
  46.0 28.2 %collective-permute-start.12 = (bf16[128,1024]{1,0:T(8,128)(2,1)S(1)}, bf16[128,1024]{1,0:T(8,128)(2,1)S(1)}, u32[]{:S(2)}, u32[]{:S(2)}) collective-permute-start(bf16[128,1024]{1,0:T(8,128)(2,1)S(1)} %get-tuple-element.61), channel_id=1, source_target_pairs={{0,2},{1,3},{2,0},{3,1},{4,6},{5,7},{6,4},{7,5},{8,10},{9,11},{10,... | collective-permute-start | bytes 786440 | tf_op jit(solution)/shard_map/ppermute | solution.py:58
  47.2 13.6 %collective-permute-start.13 = (bf16[128,1024]{1,0:T(8,128)(2,1)S(1)}, bf16[128,1024]{1,0:T(8,128)(2,1)S(1)}, u32[]{:S(2)}, u32[]{:S(2)}) collective-permute-start(bf16[128,1024]{1,0:T(8,128)(2,1)S(1)} %get-tuple-element.64), channel_id=1, source_target_pairs={{0,2},{1,3},{2,0},{3,1},{4,6},{5,7},{6,4},{7,5},{8,10},{9,11},{10,... | collective-permute-start | bytes 786440 | tf_op jit(solution)/shard_map/ppermute | solution.py:58
  50.9 14.6 %collective-permute-start.20 = (bf16[128,1024]{1,0:T(8,128)(2,1)S(1)}, bf16[128,1024]{1,0:T(8,128)(2,1)S(1)}, u32[]{:S(2)}, u32[]{:S(2)}) collective-permute-start(bf16[128,1024]{1,0:T(8,128)(2,1)S(1)} %get-tuple-element.76), channel_id=1, source_target_pairs={{0,2},{1,3},{2,0},{3,1},{4,6},{5,7},{6,4},{7,5},{8,10},{9,11},{10,... | collective-permute-start | bytes 786440 | tf_op jit(solution)/shard_map/ppermute | solution.py:58
  61.2 18.0 %collective-permute-start.15 = (bf16[128,1024]{1,0:T(8,128)(2,1)S(1)}, bf16[128,1024]{1,0:T(8,128)(2,1)S(1)}, u32[]{:S(2)}, u32[]{:S(2)}) collective-permute-start(bf16[128,1024]{1,0:T(8,128)(2,1)S(1)} %get-tuple-element.67), channel_id=1, source_target_pairs={{0,4},{1,5},{2,6},{3,7},{4,0},{5,1},{6,2},{7,3},{8,12},{9,13},{10,... | collective-permute-start | bytes 786440 | tf_op jit(solution)/shard_map/ppermute | solution.py:58
  62.7 31.2 %collective-permute-start.14 = (bf16[128,1024]{1,0:T(8,128)(2,1)S(1)}, bf16[128,1024]{1,0:T(8,128)(2,1)S(1)}, u32[]{:S(2)}, u32[]{:S(2)}) collective-permute-start(bf16[128,1024]{1,0:T(8,128)(2,1)S(1)} %get-tuple-element.65), channel_id=1, source_target_pairs={{0,4},{1,5},{2,6},{3,7},{4,0},{5,1},{6,2},{7,3},{8,12},{9,13},{10,... | collective-permute-start | bytes 786440 | tf_op jit(solution)/shard_map/ppermute | solution.py:58
  70.3 7.5 %collective-permute-start.22 = (bf16[128,1024]{1,0:T(8,128)(2,1)S(1)}, bf16[128,1024]{1,0:T(8,128)(2,1)S(1)}, u32[]{:S(2)}, u32[]{:S(2)}) collective-permute-start(bf16[128,1024]{1,0:T(8,128)(2,1)S(1)} %get-tuple-element.85), channel_id=1, source_target_pairs={{0,2},{1,3},{2,0},{3,1},{4,6},{5,7},{6,4},{7,5},{8,10},{9,11},{10,... | collective-permute-start | bytes 786440 | tf_op jit(solution)/shard_map/ppermute | solution.py:58
  73.0 17.9 %collective-permute-start.26 = (bf16[2,704,512]{2,1,0:T(8,128)(2,1)S(1)}, bf16[2,704,512]{2,1,0:T(8,128)(2,1)S(1)}, u32[]{:S(2)}, u32[]{:S(2)}) collective-permute-start(bf16[2,704,512]{2,1,0:T(8,128)(2,1)S(1)} %shard_map.130), channel_id=1, source_target_pairs={{0,16},{16,0},{1,17},{17,1},{2,18},{18,2},{3,19},{19,3},{4,20},{20... | collective-permute-start | bytes 4325384 | tf_op jit(solution)/shard_map/ppermute | solution.py:303
  74.2 14.2 %collective-permute-start.28 = (bf16[1,704,512]{2,1,0:T(8,128)(2,1)S(1)}, bf16[1,704,512]{2,1,0:T(8,128)(2,1)S(1)}, u32[]{:S(2)}, u32[]{:S(2)}) collective-permute-start(bf16[1,704,512]{2,1,0:T(8,128)(2,1)S(1)} %shard_map.132), channel_id=1, source_target_pairs={{0,16},{16,0},{1,17},{17,1},{2,18},{18,2},{3,19},{19,3},{4,20},{20... | collective-permute-start | bytes 2162696 | tf_op jit(solution)/shard_map/ppermute | solution.py:303
  77.7 6.5 %collective-permute-start.21 = (bf16[128,1024]{1,0:T(8,128)(2,1)S(1)}, bf16[128,1024]{1,0:T(8,128)(2,1)S(1)}, u32[]{:S(2)}, u32[]{:S(2)}) collective-permute-start(bf16[128,1024]{1,0:T(8,128)(2,1)S(1)} %get-tuple-element.80), channel_id=1, source_target_pairs={{0,2},{1,3},{2,0},{3,1},{4,6},{5,7},{6,4},{7,5},{8,10},{9,11},{10,... | collective-permute-start | bytes 786440 | tf_op jit(solution)/shard_map/ppermute | solution.py:58
  79.2 8.8 %collective-permute-start.24 = (bf16[128,1024]{1,0:T(8,128)(2,1)S(1)}, bf16[128,1024]{1,0:T(8,128)(2,1)S(1)}, u32[]{:S(2)}, u32[]{:S(2)}) collective-permute-start(bf16[128,1024]{1,0:T(8,128)(2,1)S(1)} %get-tuple-element.87), channel_id=1, source_target_pairs={{0,4},{1,5},{2,6},{3,7},{4,0},{5,1},{6,2},{7,3},{8,12},{9,13},{10,... | collective-permute-start | bytes 786440 | tf_op jit(solution)/shard_map/ppermute | solution.py:58
  84.2 16.8 %collective-permute-start.16 = (bf16[128,1024]{1,0:T(8,128)(2,1)S(1)}, bf16[128,1024]{1,0:T(8,128)(2,1)S(1)}, u32[]{:S(2)}, u32[]{:S(2)}) collective-permute-start(bf16[128,1024]{1,0:T(8,128)(2,1)S(1)} %add_convert_fusion.5), channel_id=1, source_target_pairs={{0,8},{1,9},{2,10},{3,11},{4,12},{5,13},{6,14},{7,15},{8,0},{9,1},... | collective-permute-start | bytes 786440 | tf_op jit(solution)/shard_map/ppermute | solution.py:58
  88.0 13.8 %collective-permute-start.23 = (bf16[128,1024]{1,0:T(8,128)(2,1)S(1)}, bf16[128,1024]{1,0:T(8,128)(2,1)S(1)}, u32[]{:S(2)}, u32[]{:S(2)}) collective-permute-start(bf16[128,1024]{1,0:T(8,128)(2,1)S(1)} %get-tuple-element.86), channel_id=1, source_target_pairs={{0,4},{1,5},{2,6},{3,7},{4,0},{5,1},{6,2},{7,3},{8,12},{9,13},{10,... | collective-permute-start | bytes 786440 | tf_op jit(solution)/shard_map/ppermute | solution.py:58
  88.4 19.1 %collective-permute-start.25 = (bf16[128,1024]{1,0:T(8,128)(2,1)S(1)}, bf16[128,1024]{1,0:T(8,128)(2,1)S(1)}, u32[]{:S(2)}, u32[]{:S(2)}) collective-permute-start(bf16[128,1024]{1,0:T(8,128)(2,1)S(1)} %add_convert_fusion.3), channel_id=1, source_target_pairs={{0,8},{1,9},{2,10},{3,11},{4,12},{5,13},{6,14},{7,15},{8,0},{9,1},... | collective-permute-start | bytes 786440 | tf_op jit(solution)/shard_map/ppermute | solution.py:58
  90.9 17.5 %collective-permute-start.29 = (bf16[1,352,512]{2,1,0:T(8,128)(2,1)S(1)}, bf16[1,352,512]{2,1,0:T(8,128)(2,1)S(1)}, u32[]{:S(2)}, u32[]{:S(2)}) collective-permute-start(bf16[1,352,512]{2,1,0:T(8,128)(2,1)S(1)} %get-tuple-element.94), channel_id=1, source_target_pairs={{0,1},{1,0},{2,3},{3,2},{4,5},{5,4},{6,7},{7,6},{8,9},{9,8},{10,11... | collective-permute-start | bytes 1081352 | tf_op jit(solution)/shard_map/ppermute | solution.py:58
  93.9 19.5 %collective-permute-start.27 = (bf16[2,352,512]{2,1,0:T(8,128)(2,1)S(1)}, bf16[2,352,512]{2,1,0:T(8,128)(2,1)S(1)}, u32[]{:S(2)}, u32[]{:S(2)}) collective-permute-start(bf16[2,352,512]{2,1,0:T(8,128)(2,1)S(1)} %get-tuple-element.91), channel_id=1, source_target_pairs={{0,1},{1,0},{2,3},{3,2},{4,5},{5,4},{6,7},{7,6},{8,9},{9,8},{10,11... | collective-permute-start | bytes 2162696 | tf_op jit(solution)/shard_map/ppermute | solution.py:58

commit v6 on v5

--- a/solution.py
+++ b/solution.py
@@ -21,12 +21,16 @@
     "pt1": 20,
     "pc0": 20,
     "pc1": 20,
+    "pc2": 20,
     "fwd": 20,
-    "bwd": 20,
+    "bwd0": 20,
+    "bwd1": 20,
     "co0": 20,
     "co1": 20,
+    "co2": 20,
     "cg0": 1,
     "cg1": 1,
+    "cg2": 1,
     "ddk1": 5,
     "ddk0": 5,
     "dik1": 5,
@@ -39,10 +43,15 @@
     "c1": ("t3", "c2", "yt0",),
     "pc0": ("yt0", "pt1",),
     "wp1": ("c2", "t3",),
-    "pc1": ("yt1", "yc0", "wp1",),
-    "bwd": ("yo1",),
-    "o": ("cg0",),
-    "ws1": ("T2",),
+    "pc2": ("yt1", "yc0", "wp1", "fwd",),
+    "yo0": ("yc2",),
+    "co2": ("bwd1",),
+    "yg1": ("yg2",),
+    "yg0": ("yg2", "yo0",),
+    "yo1": ("yo2",),
+    "g": ("dd", "di",),
+    "cg1": ("ddk0",),
+    "cg0": ("dik0",),
 }
 
 
@@ -99,59 +108,51 @@
         gate_ref[column] = gates * (1.0 / 64.0)
 
 
-def choice_of(slot_ref, gate_ref, column, place, rows):
-    row = lax.broadcasted_iota(jnp.int32, (rows, slot_ref.shape[2]), 0)
+def choice_of(slot_ref, gate_ref, column, place, first, rows):
+    row = lax.broadcasted_iota(jnp.int32, (rows, slot_ref.shape[2]), 0) + first
     hit = row == slot_ref[column, place : place + 1, :]
     if gate_ref is None:
         return jnp.where(hit, 1.0, 0.0).astype(bf16)
     return jnp.where(hit, gate_ref[column, place : place + 1, :], 0.0).astype(bf16)
 
 
-def compact_kernel(half, with_ids, slot_ref, gate_ref, *refs):
-    plane_experts, planes, tok_rows = slot_ref.shape
-    count = planes // 2
-    chunk_refs, out_refs = refs[:count], refs[count:]
+def compact_kernel(places, first, with_ids, slot_ref, gate_ref, *refs):
+    plane_experts, _, tok_rows = slot_ref.shape
+    chunk_refs, out_refs = refs[: len(places)], refs[len(places) :]
     stacked = jnp.concatenate([chunk[...] for chunk in chunk_refs], axis=0)
     if with_ids:
         number = lax.broadcasted_iota(jnp.int32, (tok_rows, id_lanes), 0).astype(f32).astype(bf16)
         stacked = jnp.concatenate(
-            [stacked, jnp.concatenate([number] * count, axis=0)], axis=1
+            [stacked, jnp.concatenate([number] * len(places), axis=0)], axis=1
         )
     for column in range(plane_experts):
+        rows = out_refs[column].shape[0]
         choice = jnp.concatenate(
             [
-                choice_of(
-                    slot_ref,
-                    None if with_ids else gate_ref,
-                    column,
-                    2 * step + half,
-                    out_refs[column].shape[0],
-                )
-                for step in range(count)
+                choice_of(slot_ref, None if with_ids else gate_ref, column, place, first, rows)
+                for place in places
             ],
             axis=1,
         )
         out_refs[column][...] = jnp.dot(choice, stacked, preferred_element_type=f32).astype(bf16)
 
 
-def combine_kernel(half, scaled, slot_ref, gate_ref, *refs):
-    plane_experts, planes, _ = slot_ref.shape
+def combine_kernel(places, first, scaled, slot_ref, gate_ref, *refs):
+    plane_experts = slot_ref.shape[0]
     block_refs, out_refs = refs[:plane_experts], refs[plane_experts:]
     rows = block_refs[0].shape[0]
     stacked = jnp.concatenate([block[...] for block in block_refs], axis=0)
-    for step in range(planes // 2):
+    for place, out_ref in zip(places, out_refs):
         choice = jnp.concatenate(
             [
-                choice_of(
-                    slot_ref, gate_ref if scaled else None, column, 2 * step + half, rows
-                )
+                choice_of(slot_ref, gate_ref if scaled else None, column, place, first, rows)
                 for column in range(plane_experts)
             ],
             axis=0,
         )
-        out_refs[step][...] = lax.dot_general(
+        out_ref[...] = lax.dot_general(
             choice, stacked, contract_first, preferred_element_type=f32
-        ).astype(out_refs[step].dtype)
+        ).astype(out_ref.dtype)
 
 
 def assemble(weight_ref, piece_refs, place_ref, seq_count):
@@ -164,15 +165,21 @@
             weight_ref[kind, row : row + half_width, pl.ds(column, width)] = piece[kind]
 
 
-def forward_kernel(seq_count, plane_experts, planes, capacity, place_ref, key_ref, *refs):
-    blocks = 2 * plane_experts
-    row_refs, refs = refs[:blocks], refs[blocks:]
+def stored(values, out_refs):
+    start = 0
+    for out in out_refs:
+        out[...] = values[start : start + out.shape[0]]
+        start += out.shape[0]
+
+
+def forward_kernel(seq_count, plane_experts, capacity, layout, outs, place_ref, key_ref, *refs):
+    row_refs, refs = refs[: len(layout)], refs[len(layout) :]
     piece_refs, refs = refs[: 2 * seq_count], refs[2 * seq_count :]
-    out_refs, (gate_ref, up_ref, hidden_ref, weight_ref) = refs[:blocks], refs[blocks:]
+    out_refs, refs = refs[:outs], refs[outs:]
+    gate_refs, up_refs, hidden_refs, weight_ref = refs[:2], refs[2:4], refs[4:6], refs[6]
     assemble(weight_ref, piece_refs, place_ref, seq_count)
     _, hidden_width, model_width = weight_ref.shape
     half_width = hidden_width // 2
-    rows = row_refs[0].shape[0]
     unit = lax.broadcasted_iota(jnp.int32, (1, hidden_width), 1)
     columns = place_ref[2] + jnp.where(
         unit < half_width, unit + place_ref[3], unit - half_width + place_ref[4]
@@ -184,10 +191,9 @@
     up_pre = lax.dot_general(inputs, weight_ref[1], contract_last, preferred_element_type=f32)
     shift = capacity.bit_length() - 1
     mixed = []
-    for index, row in enumerate(row_refs):
-        column, half = index // 2, index % 2
+    for (half, column, first), row in zip(layout, row_refs):
         within = row[:, model_width : model_width + id_lanes].astype(f32).astype(jnp.int32)
-        step = lax.broadcasted_iota(jnp.int32, within.shape, 0) >> shift
+        step = (lax.broadcasted_iota(jnp.int32, within.shape, 0) + first) >> shift
         source = place_ref[5] ^ ((2 * step + half) * (2 * plane_experts) + 2 * column)
         ids = (place_ref[6] + source) * place_ref[7] + within
         mixed.append(scramble(ids ^ base_hash))
@@ -197,22 +203,18 @@
     sigmoid_gate = jax.nn.sigmoid(gate_pre)
     silu_gate = gate_pre * sigmoid_gate
     hidden = (silu_gate * up_pre * keep).astype(bf16)
-    gate_ref[...] = up_pre * sigmoid_gate * (1.0 + gate_pre * (1.0 - sigmoid_gate)) * keep
-    up_ref[...] = silu_gate * keep
-    hidden_ref[...] = hidden
-    expert_out = jnp.dot(hidden, weight_ref[2], preferred_element_type=f32).astype(bf16)
-    for index, out in enumerate(out_refs):
-        out[...] = expert_out[index * rows : (index + 1) * rows]
-
-
-def backward_kernel(seq_count, plane_experts, place_ref, *refs):
-    blocks = 2 * plane_experts
+    stored(up_pre * sigmoid_gate * (1.0 + gate_pre * (1.0 - sigmoid_gate)) * keep, gate_refs)
+    stored(silu_gate * keep, up_refs)
+    stored(hidden, hidden_refs)
+    stored(jnp.dot(hidden, weight_ref[2], preferred_element_type=f32).astype(bf16), out_refs)
+
+
+def backward_kernel(seq_count, blocks, outs, place_ref, *refs):
     cot_refs, refs = refs[:blocks], refs[blocks:]
     piece_refs, refs = refs[: 2 * seq_count], refs[2 * seq_count :]
     (gate_ref, up_ref), refs = refs[:2], refs[2:]
-    out_refs, (gate_grad_ref, up_grad_ref, weight_ref) = refs[:blocks], refs[blocks:]
+    out_refs, (gate_grad_ref, up_grad_ref, weight_ref) = refs[:outs], refs[outs:]
     assemble(weight_ref, piece_refs, place_ref, seq_count)
-    rows = cot_refs[0].shape[0]
     cot = jnp.concatenate([block[...] for block in cot_refs], axis=0)
     hidden_grad = lax.dot_general(cot, weight_ref[2], contract_last, preferred_element_type=f32)
     gate_grad = (hidden_grad * gate_ref[...]).astype(bf16)
@@ -223,21 +225,21 @@
         jnp.dot(gate_grad, weight_ref[0], preferred_element_type=f32)
         + jnp.dot(up_grad, weight_ref[1], preferred_element_type=f32)
     ).astype(bf16)
-    for index, out in enumerate(out_refs):
-        out[...] = input_grad[index * rows : (index + 1) * rows]
+    stored(input_grad, out_refs)
 
 
 def weight_grad_kernel(blocks, seq_count, shift, kinds, place_ref, *refs):
     row_refs, refs = refs[:blocks], refs[blocks:]
-    left_refs, refs = refs[:kinds], refs[kinds:]
+    left_refs, refs = refs[: 2 * kinds], refs[2 * kinds :]
     added = refs[: seq_count - 1] if shift == 0 else ()
     out_refs = refs[len(added) :]
     width = out_refs[0].shape[2]
     part = lax.rem(place_ref[1] + shift, seq_count)
     lanes = pl.ds(pl.multiple_of(part * width, width), width)
     right = jnp.concatenate([row[:, lanes] for row in row_refs], axis=0)
-    for kind, left in enumerate(left_refs):
-        total = lax.dot_general(left[...], right, contract_first, preferred_element_type=f32)
+    for kind in range(kinds):
+        left = jnp.concatenate([ref[...] for ref in left_refs[2 * kind : 2 * kind + 2]], axis=0)
+        total = lax.dot_general(left, right, contract_first, preferred_element_type=f32)
         for part_ref in added:
             total = total + part_ref[kind].astype(f32)
         if shift:
@@ -265,9 +267,27 @@
     plane_stride = 2 * plane_experts
     parity = blk_index % 2
     expert_here = blk_index // 2
-    rows = planes // 2 * capacity
-    slot_rows = 2 * plane_experts * rows
-    blocks = 2 * plane_experts
+    half_rows = plane_experts * (planes // 2) * capacity
+    even, odd = list(range(0, planes, 2)), list(range(1, planes, 2))
+    cut = len(odd) // 2
+    whole_halves, cut_halves = [even, odd], [even, odd[:cut], odd[cut:]]
+    groups = {"t": whole_halves, "c": cut_halves, "o": cut_halves, "g": cut_halves}
+
+    def group_rows(group):
+        return len(group) * capacity
+
+    def first_slot(group):
+        return group[0] // 2 * capacity
+
+    def layout(kind, halves=(0, 1)):
+        return [
+            (half, column, index)
+            for half in halves
+            for column in range(plane_experts)
+            for index, group in enumerate(groups[kind])
+            if group[0] % 2 == half
+        ]
+
     place = jnp.stack(
         [
             expert_here,
@@ -289,8 +309,9 @@
 
     def get(name):
         if name not in made:
-            waits = [jax.tree.leaves(get(other))[-1] for other in order.get(name, ())]
-            made[name] = steps[name](lambda value: after(value, *waits) if waits else value)
+            waits = [jax.tree.leaves(get(other))[0] for other in order.get(name, ())]
+            with jax.named_scope(name):
+                made[name] = steps[name](lambda value: after(value, *waits) if waits else value)
         return made[name]
 
     def across(mask):
@@ -324,6 +345,7 @@
             )
 
     own_weights = jnp.stack([w_gate[0].T, w_up[0].T, w_down[0]])
+    step("ow", lambda wait: own_weights)
     step("wx", lambda wait: flipped(wait(own_weights), "blk", 1))
     for shift in range(1, seq_count):
         step(f"ws{shift}", lambda wait, shift=shift: shifted(wait(own_weights), -shift))
@@ -352,95 +374,124 @@
         ),
     )
 
-    def packed(kind, half, wait):
+    def packed(kind, index, wait):
+        group = groups[kind][index]
         width = model_width + (id_lanes if kind == "t" else 0)
-        chunks = [get(f"{kind}{origin}") for origin in range(half, planes, 2)]
+        chunks = [get(f"{kind}{origin}") for origin in group]
         chunks[0] = wait(chunks[0])
         return called(
-            functools.partial(compact_kernel, half, kind == "t"),
-            [shape((rows, width), bf16)] * plane_experts,
+            functools.partial(compact_kernel, group, first_slot(group), kind == "t"),
+            [shape((group_rows(group), width), bf16)] * plane_experts,
             [vmem] * (2 + len(chunks)),
-            costs[f"p{kind}{half}"],
+            costs[f"p{kind}{index}"],
         )(*get("prep"), *chunks)
 
-    def exchanged(blocks_out, wait):
+    def exchanged(by_column, wait):
+        return [None] + [
+            flipped(wait(by_column(column)), "blk", 2 * column)
+            for column in range(1, plane_experts)
+        ]
+
+    for kind in "tc":
+        for index in range(len(groups[kind])):
+            step(
+                f"p{kind}{index}",
+                lambda wait, kind=kind, index=index: packed(kind, index, wait),
+            )
+            step(
+                f"y{kind}{index}",
+                lambda wait, kind=kind, index=index: exchanged(
+                    lambda column: get(f"p{kind}{index}")[column], wait
+                ),
+            )
+
+    def row_blocks(kind, halves=(0, 1)):
         return [
-            flipped(wait(blocks_out[column]), "blk", 2 * column)
-            for column in range(1, plane_experts)
-        ]
-
-    for kind in "tc":
-        for half in (0, 1):
-            step(f"p{kind}{half}", lambda wait, kind=kind, half=half: packed(kind, half, wait))
-            step(
-                f"y{kind}{half}",
-                lambda wait, kind=kind, half=half: exchanged(get(f"p{kind}{half}"), wait),
-            )
-
-    def row_blocks(kind):
-        halves = [[get(f"p{kind}{half}")[0], *get(f"y{kind}{half}")] for half in (0, 1)]
-        return [block for pair in zip(*halves) for block in pair]
+            get(f"{'y' if column else 'p'}{kind}{index}")[column]
+            for half, column, index in layout(kind, halves)
+        ]
 
     weight_scratch = pltpu.VMEM((3, hidden_width, model_width), bf16)
+
+    def out_shapes(kind, halves=(0, 1)):
+        return [
+            shape((group_rows(groups[kind][index]), model_width), bf16)
+            for half, column, index in layout(kind, halves)
+        ]
 
     def forward(wait):
         row_parts, piece_parts = row_blocks("t"), pieces()
         row_parts[0] = wait(row_parts[0])
-        return called(
-            functools.partial(forward_kernel, seq_count, plane_experts, planes, capacity),
-            [shape((rows, model_width), bf16)] * blocks
-            + [shape((slot_rows, hidden_width), f32)] * 2
-            + [shape((slot_rows, hidden_width), bf16)],
-            [smem, smem] + [vmem] * (blocks + len(piece_parts)),
+        described = [
+            (half, column, first_slot(groups["t"][index])) for half, column, index in layout("t")
+        ]
+        outs = out_shapes("o")
+        results = called(
+            functools.partial(
+                forward_kernel, seq_count, plane_experts, capacity, described, len(outs)
+            ),
+            outs
+            + [shape((half_rows, hidden_width), f32)] * 4
+            + [shape((half_rows, hidden_width), bf16)] * 2,
+            [smem, smem] + [vmem] * (len(row_parts) + len(piece_parts)),
             costs["fwd"],
             [weight_scratch],
         )(place, dropout_key, *row_parts, *piece_parts)
-
-    def backward(wait):
-        cot_parts, piece_parts = row_blocks("c"), pieces()
+        return results[len(outs) :] + results[: len(outs)]
+
+    def backward(half, wait):
+        cot_parts, piece_parts = row_blocks("c", (half,)), pieces()
         cot_parts[0] = wait(cot_parts[0])
+        outs = out_shapes("g", (half,))
+        results = called(
+            functools.partial(backward_kernel, seq_count, len(cot_parts), len(outs)),
+            outs + [shape((half_rows, hidden_width), bf16)] * 2,
+            [smem] + [vmem] * (len(cot_parts) + len(piece_parts) + 2),
+            costs[f"bwd{half}"],
+            [weight_scratch],
+        )(place, *cot_parts, *piece_parts, get("fwd")[half], get("fwd")[2 + half])
+        return results[len(outs) :] + results[: len(outs)]
+
+    step("fwd", forward)
+    for half in (0, 1):
+        step(f"bwd{half}", lambda wait, half=half: backward(half, wait))
+
+    def slot_block(kind, column, index):
+        half = groups[kind][index][0] % 2
+        if kind == "o":
+            return get("fwd")[6 + layout("o").index((half, column, index))]
+        return get(f"bwd{half}")[2 + layout("g", (half,)).index((half, column, index))]
+
+    def combined(kind, index, wait):
+        group = groups[kind][index]
+        held = [wait(slot_block(kind, 0, index)), *get(f"y{kind}{index}")[1:]]
         return called(
-            functools.partial(backward_kernel, seq_count, plane_experts),
-            [shape((rows, model_width), bf16)] * blocks
-            + [shape((slot_rows, hidden_width), bf16)] * 2,
-            [smem] + [vmem] * (blocks + len(piece_parts) + 2),
-            costs["bwd"],
-            [weight_scratch],
-        )(place, *cot_parts, *piece_parts, *get("fwd")[blocks : blocks + 2])
-
-    step("fwd", forward)
-    step("bwd", backward)
-
-    def combined(kind, half, wait):
-        source = get("fwd" if kind == "o" else "bwd")
-        held = [wait(source[half]), *get(f"y{kind}{half}")]
-        return called(
-            functools.partial(combine_kernel, half, kind == "o"),
-            [shape((tok_rows, model_width), bf16 if half else f32)] * (planes // 2),
+            functools.partial(combine_kernel, group, first_slot(group), kind == "o"),
+            [shape((tok_rows, model_width), bf16 if group[0] % 2 else f32)] * len(group),
             [vmem] * (2 + plane_experts),
-            costs[f"c{kind}{half}"],
+            costs[f"c{kind}{index}"],
         )(*get("prep"), *held)
 
     def total(kind, origin):
-        value = get(f"c{kind}{origin % 2}")[origin // 2]
+        index = [origin in group for group in groups[kind]].index(True)
+        value = get(f"c{kind}{index}")[groups[kind][index].index(origin)]
         for other in range(origin + 1, planes):
             if other - low_bit(other) == origin:
                 value = value.astype(f32) + get(f"z{kind}{other}").astype(f32)
         return value.astype(bf16)
 
     for kind in "og":
-        for half in (0, 1):
-            step(
-                f"y{kind}{half}",
-                lambda wait, kind=kind, half=half: exchanged(
-                    [
-                        get("fwd" if kind == "o" else "bwd")[2 * column + half]
-                        for column in range(plane_experts)
-                    ],
-                    wait,
+        for index in range(len(groups[kind])):
+            step(
+                f"y{kind}{index}",
+                lambda wait, kind=kind, index=index: exchanged(
+                    lambda column: slot_block(kind, column, index), wait
                 ),
             )
-            step(f"c{kind}{half}", lambda wait, kind=kind, half=half: combined(kind, half, wait))
+            step(
+                f"c{kind}{index}",
+                lambda wait, kind=kind, index=index: combined(kind, index, wait),
+            )
         for origin in range(1, planes):
             step(
                 f"z{kind}{origin}",
@@ -452,10 +503,11 @@
 
     def weight_kernel(name, wait, shift):
         if name == "dd":
-            row_parts, lefts = row_blocks("c"), [get("fwd")[blocks + 2]]
+            row_parts, lefts = row_blocks("c"), list(get("fwd")[4:6])
         else:
-            row_parts, lefts = row_blocks("t"), get("bwd")[blocks:]
-        kinds = len(lefts)
+            row_parts = row_blocks("t")
+            lefts = [get(f"bwd{half}")[kind] for kind in (0, 1) for half in (0, 1)]
+        kinds = len(lefts) // 2
         arrived = [] if shift else [get(f"{name}s{k}") for k in range(1, seq_count)]
         lefts = [wait(lefts[0]), *lefts[1:]]
         if shift:
@@ -466,9 +518,9 @@
                 shape((kinds, half_width, part_width), bf16),
             ]
         return called(
-            functools.partial(weight_grad_kernel, blocks, seq_count, shift, kinds),
+            functools.partial(weight_grad_kernel, len(row_parts), seq_count, shift, kinds),
             result,
-            [smem] + [vmem] * (blocks + kinds + len(arrived)),
+            [smem] + [vmem] * (len(row_parts) + len(lefts) + len(arrived)),
             costs[f"{name}k{min(shift, 1)}"],
         )(place, *row_parts, *lefts, *arrived)
 
@@ -487,9 +539,10 @@
         step(f"{name}x", lambda wait, name=name: across(1)(wait(get(f"{name}k0")[1])))
         step(
             name,
-            lambda wait, name=name: (
-                wait(get(f"{name}k0")[0]) + get(f"{name}x").astype(f32)
-            ).astype(bf16),
+            lambda wait, name=name: [
+                (wait(own) + other.astype(f32)).astype(bf16)
+                for own, other in zip(get(f"{name}k0")[0], get(f"{name}x"))
+            ],
         )
 
     down_grad, input_grads = get("dd"), get("di")
@@ -498,7 +551,7 @@
         get("g"),
         input_grads[0].T[None],
         input_grads[1].T[None],
-        down_grad,
+        down_grad[0][None],
     )
 
 

time: 115 us -> 107 us (0.930)
  waiting for transfers between devices: 52.7 us -> 38.9 us
  starting transfers between devices: 37.7 us -> 41.5 us
  Pallas kernels: 17.4 us -> 19.3 us
    ppermute x26 -> x29, waiting for transfers between devices: 52.7 us -> 38.9 us  [flipped(): lax.ppermute(values, axis, [(i, i ^ mask) for i in range(lax.axis_size(ax...]
    ppermute x26 -> x29, starting transfers between devices: 37.1 us -> 40.9 us  [flipped(): lax.ppermute(values, axis, [(i, i ^ mask) for i in range(lax.axis_size(ax...]
    pallas_call x14 -> x18, Pallas kernels: 16.7 us -> 18.6 us  [the longest x2 6.13 us: backward(): called(functools.partial(backward_kernel, seq_count, len(cot_parts), len(...]
  transfers between devices with their start and end apart: 30 -> 33, of which waited for: 13 -> 11; matrix products, arithmetic and copies ran while one was open for 3% -> 4% of each run, Pallas kernels for 15% -> 18%
where the time goes in v6:
time: 107 us
  starting transfers between devices  41.5 us (39%)
  waiting for transfers between devices  38.9 us (36%)
  Pallas kernels  19.3 us (18%)
  other arithmetic  5.71 us (5%)
    ppermute x29, starting transfers between devices, flipped(): lax.ppermute(values, axis, [(i, i ^ mask) for i in range(lax.axis_size(ax...  40.9 us
    ppermute x29, waiting for transfers between devices, flipped(): lax.ppermute(values, axis, [(i, i ^ mask) for i in range(lax.axis_size(ax...  38.9 us
    pallas_call x2, Pallas kernels, backward(): called(functools.partial(backward_kernel, seq_count, len(cot_parts), len(...  6.13 us
    pallas_call x4, Pallas kernels, weight_kernel(): called(functools.partial(weight_grad_kernel, len(row_parts), seq_count, s...  5.19 us
    pallas_call x1, Pallas kernels, forward(): called(functools.partial(forward_kernel, seq_count, plane_experts, capaci...  4.25 us
  transfers between devices with their start and end apart: 33, of which 11 were waited for; matrix products, arithmetic and copies ran while one was open for 4% of the time, Pallas kernels for 18%

profile of v6, /device:TPU:0, one launch (start us, length us, event | category | flops | bytes accessed | tf_op | source)
XLA Modules:
  0.0 106.5 jit_solution(3105378296062191475)
XLA Ops:
  0.6 0.7 pad_add_fusion.1
  1.3 5.0 %collective-permute-start.2 = (s32[4,128]{1,0:T(4,128)S(1)}, s32[4,128]{1,0:T(4,128)S(1)}, u32[]{:S(2)}, u32[]{:S(2)}) collective-permute-start(s32[4,128]{1,0:T(4,128)S(1)} %pad_add_fusion.1), channel_id=1, source_target_pairs={{0,12},{1,13},{2,14},{3,15},{4,8},{5,9},{6,10},{7,11},{8,4},{9,5},... | collective-permute-start | bytes 6152 | tf_op jit(solution)/shard_map/dd/ddk0/yt0/pt0/prep/T3/ppermute | solution.py:67
  6.4 0.6 collective-permute-start
  7.0 2.3 %collective-permute-start.3 = (bf16[128,1024]{1,0:T(8,128)(2,1)}, bf16[128,1024]{1,0:T(8,128)(2,1)S(1)}, u32[]{:S(2)}, u32[]{:S(2)}) collective-permute-start(bf16[128,1024]{1,0:T(8,128)(2,1)} %refs_0_.1), channel_id=1, source_target_pairs={{0,8},{1,9},{2,10},{3,11},{4,12},{5,13},{6,14},{7,15},{8,0},{9,1},... | collective-permute-start | bytes 786440 | tf_op jit(solution)/shard_map/dd/ddk0/yt0/pt0/t2/ppermute | solution.py:67
  9.3 2.0 %collective-permute-start.5 = (bf16[128,1024]{1,0:T(8,128)(2,1)}, bf16[128,1024]{1,0:T(8,128)(2,1)S(1)}, u32[]{:S(2)}, u32[]{:S(2)}) collective-permute-start(bf16[128,1024]{1,0:T(8,128)(2,1)} %refs_0_.1), channel_id=1, source_target_pairs={{0,4},{1,5},{2,6},{3,7},{4,0},{5,1},{6,2},{7,3},{8,12},{9,13},{10,... | collective-permute-start | bytes 786440 | tf_op jit(solution)/shard_map/dd/ddk0/pt1/t1/ppermute | solution.py:67
  11.3 1.3 %pad_maximum_fusion.refs_4_.refs_2_ = bf16[3,352,512]{2,1,0:T(8,128)(2,1)S(1)} fusion(bf16[1,352,512]{2,1,0:T(8,128)(2,1)} %param.15, bf16[1,352,512]{2,1,0:T(8,128)(2,1)} %bitcast.41, bf16[1,352,512]{2,1,0:T(8,128)(2,1)} %bitcast.42), kind=kLoop, calls=%fused_computation | loop fusion | flops 1081344 | bytes 2162688 | tf_op jit(solution)/shard_map/stack | solution.py:347
  12.8 1.6 %collective-permute-start.9 = (bf16[3,352,512]{2,1,0:T(8,128)(2,1)S(1)}, bf16[3,352,512]{2,1,0:T(8,128)(2,1)S(1)}, u32[]{:S(2)}, u32[]{:S(2)}) collective-permute-start(bf16[3,352,512]{2,1,0:T(8,128)(2,1)S(1)} %pad_maximum_fusion.refs_4_.refs_2_), channel_id=1, source_target_pairs={{0,1},{1,0},{2,3},{3,2},{4,5},{5,4},{6,7},{7,6},{8,9},{9,8},{10,11... | collective-permute-start | bytes 3244040 | tf_op jit(solution)/shard_map/dd/ddk0/wp1/wx/ppermute | solution.py:67
  14.4 0.7 prep.1
  15.1 6.3 %collective-permute-done.3.refs_1_ = bf16[128,1024]{1,0:T(8,128)(2,1)S(1)} collective-permute-done((bf16[128,1024]{1,0:T(8,128)(2,1)}, bf16[128,1024]{1,0:T(8,128)(2,1)S(1)}, u32[]{:S(2)}, u32[]{:S(2)}) %collective-permute-start.3) | collective-permute-done | bytes 262176 | tf_op jit(solution)/shard_map/dd/ddk0/yt0/pt0/t2/ppermute | solution.py:67
  21.5 1.2 %collective-permute-start.6 = (bf16[128,1024]{1,0:T(8,128)(2,1)S(1)}, bf16[128,1024]{1,0:T(8,128)(2,1)S(1)}, u32[]{:S(2)}, u32[]{:S(2)}) collective-permute-start(bf16[128,1024]{1,0:T(8,128)(2,1)S(1)} %collective-permute-done.3.refs_1_), channel_id=1, source_target_pairs={{0,4},{1,5},{2,6},{3,7},{4,0},{5,1},{6,2},{7,3},{8,12},{9,13},{10,... | collective-permute-start | bytes 786440 | tf_op jit(solution)/shard_map/dd/ddk0/pt1/t3/ppermute | solution.py:67
  22.7 2.3 %collective-permute-start.10 = (bf16[128,1024]{1,0:T(8,128)(2,1)S(1)}, bf16[128,1024]{1,0:T(8,128)(2,1)S(1)}, u32[]{:S(2)}, u32[]{:S(2)}) collective-permute-start(bf16[128,1024]{1,0:T(8,128)(2,1)S(1)} %copy-done.1), channel_id=1, source_target_pairs={{0,8},{1,9},{2,10},{3,11},{4,12},{5,13},{6,14},{7,15},{8,0},{9,1},... | collective-permute-start | bytes 786440 | tf_op jit(solution)/shard_map/dd/ddk0/pc0/c2/ppermute | solution.py:67
  25.0 0.3 pt0.1
  25.3 1.6 %collective-permute-start.4 = (bf16[128,1152]{1,0:T(8,128)(2,1)S(1)}, bf16[128,1152]{1,0:T(8,128)(2,1)S(1)}, u32[]{:S(2)}, u32[]{:S(2)}) collective-permute-start(bf16[128,1152]{1,0:T(8,128)(2,1)S(1)} %get-tuple-element.65), channel_id=1, source_target_pairs={{0,2},{1,3},{2,0},{3,1},{4,6},{5,7},{6,4},{7,5},{8,10},{9,11},{10,... | collective-permute-start | bytes 884744 | tf_op jit(solution)/shard_map/dd/ddk0/yt0/ppermute | solution.py:67
  26.9 7.1 %collective-permute-done.6.refs_1_ = bf16[128,1024]{1,0:T(8,128)(2,1)S(1)} collective-permute-done((bf16[128,1024]{1,0:T(8,128)(2,1)S(1)}, bf16[128,1024]{1,0:T(8,128)(2,1)S(1)}, u32[]{:S(2)}, u32[]{:S(2)}) %collective-permute-start.6) | collective-permute-done | bytes 262176 | tf_op jit(solution)/shard_map/dd/ddk0/pt1/t3/ppermute | solution.py:67
  34.0 0.3 pt1.1
  34.4 1.6 %collective-permute-start.7 = (bf16[128,1152]{1,0:T(8,128)(2,1)S(1)}, bf16[128,1152]{1,0:T(8,128)(2,1)S(1)}, u32[]{:S(2)}, u32[]{:S(2)}) collective-permute-start(bf16[128,1152]{1,0:T(8,128)(2,1)S(1)} %get-tuple-element.68), channel_id=1, source_target_pairs={{0,2},{1,3},{2,0},{3,1},{4,6},{5,7},{6,4},{7,5},{8,10},{9,11},{10,... | collective-permute-start | bytes 884744 | tf_op jit(solution)/shard_map/dd/ddk0/yt1/ppermute | solution.py:67
  36.0 0.9 collective-permute-done.10.refs_1_
  36.9 0.3 collective-permute-start.19
  37.2 0.3 pc0.1
  37.5 1.6 %collective-permute-start.13 = (bf16[128,1024]{1,0:T(8,128)(2,1)S(1)}, bf16[128,1024]{1,0:T(8,128)(2,1)S(1)}, u32[]{:S(2)}, u32[]{:S(2)}) collective-permute-start(bf16[128,1024]{1,0:T(8,128)(2,1)S(1)} %get-tuple-element.75), channel_id=1, source_target_pairs={{0,2},{1,3},{2,0},{3,1},{4,6},{5,7},{6,4},{7,5},{8,10},{9,11},{10,... | collective-permute-start | bytes 786440 | tf_op jit(solution)/shard_map/dd/ddk0/yc0/ppermute | solution.py:67
  39.1 4.1 %collective-permute-done.19.refs_0_ = bf16[128,1024]{1,0:T(8,128)(2,1)S(1)} collective-permute-done((bf16[128,1024]{1,0:T(8,128)(2,1)S(1)}, bf16[128,1024]{1,0:T(8,128)(2,1)S(1)}, u32[]{:S(2)}, u32[]{:S(2)}) %collective-permute-start.19) | collective-permute-done | bytes 262176 | tf_op jit(solution)/shard_map/dd/ddk0/pc1/c1/ppermute | solution.py:67
  43.2 0.2 pc1.1
  43.5 1.6 %collective-permute-start.20 = (bf16[64,1024]{1,0:T(8,128)(2,1)S(1)}, bf16[64,1024]{1,0:T(8,128)(2,1)S(1)}, u32[]{:S(2)}, u32[]{:S(2)}) collective-permute-start(bf16[64,1024]{1,0:T(8,128)(2,1)S(1)} %get-tuple-element.90), channel_id=1, source_target_pairs={{0,2},{1,3},{2,0},{3,1},{4,6},{5,7},{6,4},{7,5},{8,10},{9,11},{10,... | collective-permute-start | bytes 393224 | tf_op jit(solution)/shard_map/dd/ddk0/yc1/ppermute | solution.py:67
  45.1 1.6 %collective-permute-start.12 = (bf16[128,1024]{1,0:T(8,128)(2,1)S(1)}, bf16[128,1024]{1,0:T(8,128)(2,1)S(1)}, u32[]{:S(2)}, u32[]{:S(2)}) collective-permute-start(bf16[128,1024]{1,0:T(8,128)(2,1)S(1)} %collective-permute-done.10.refs_1_), channel_id=1, source_target_pairs={{0,4},{1,5},{2,6},{3,7},{4,0},{5,1},{6,2},{7,3},{8,12},{9,13},{10,... | collective-permute-start | bytes 786440 | tf_op jit(solution)/shard_map/dd/ddk0/pc2/c3/ppermute | solution.py:67
  46.7 4.2 %fwd.1 = (bf16[128,1024]{1,0:T(8,128)(2,1)S(1)}, bf16[128,1024]{1,0:T(8,128)(2,1)S(1)}, bf16[64,1024]{1,0:T(8,128)(2,1)S(1)}, bf16[64,1024]{1,0:T(8,128)(2,1)S(1...) custom-call(s32[8]{0:T(128)S(1)} %stack.55.place_ref, ...), custom_call_target="tpu_custom_call" | custom-call | flops 20000000000 | bytes 60000000 | tf_op jit(solution)/shard_map/dd/ddk0/fwd/pallas_call | solution.py:429
  50.9 0.5 collective-permute-done.12.refs_0_
  51.4 0.2 pc2.1
  51.6 0.6 collective-permute-start.14
  52.2 1.5 %collective-permute-start.16 = (bf16[64,1024]{1,0:T(8,128)(2,1)S(1)}, bf16[64,1024]{1,0:T(8,128)(2,1)S(1)}, u32[]{:S(2)}, u32[]{:S(2)}) collective-permute-start(bf16[64,1024]{1,0:T(8,128)(2,1)S(1)} %get-tuple-element.83), channel_id=1, source_target_pairs={{0,2},{1,3},{2,0},{3,1},{4,6},{5,7},{6,4},{7,5},{8,10},{9,11},{10,... | collective-permute-start | bytes 393224 | tf_op jit(solution)/shard_map/o/zo1/co1/yo2/ppermute | solution.py:67
  53.7 3.1 %bwd0.1 = (bf16[128,1024]{1,0:T(8,128)(2,1)S(1)}, bf16[128,1024]{1,0:T(8,128)(2,1)S(1)}, bf16[256,704]{1,0:T(8,128)(2,1)S(1)}, bf16[256,704]{1,0:T(8,128)(2,1)S(1)}) custom-call(s32[8]{0:T(128)S(1)} %stack.55.place_ref, bf16[128,1024]{1,0:T(8,128)(2,1)S(1)} %get-tuple-element.95.refs_0_, bf16[128,1024]{1,0:T(8,128)(2,1)S(1)} %collective-permute-done.13.refs_1_, ...), custom_call_target="tpu_custom_call" | custom-call | flops 20000000000 | bytes 60000000 | tf_op jit(solution)/shard_map/di/dik0/bwd0/pallas_call | solution.py:446
  56.8 3.1 %bwd1.1 = (bf16[64,1024]{1,0:T(8,128)(2,1)S(1)}, bf16[64,1024]{1,0:T(8,128)(2,1)S(1)}, bf16[64,1024]{1,0:T(8,128)(2,1)S(1)}, bf16[64,1024]{1,0:T(8,128)(2,1)S(1)...) custom-call(s32[8]{0:T(128)S(1)} %stack.55.place_ref, ...), custom_call_target="tpu_custom_call" | custom-call | flops 20000000000 | bytes 60000000 | tf_op jit(solution)/shard_map/di/dik0/bwd1/pallas_call | solution.py:446
  59.9 0.6 collective-permute-start.24
  60.5 1.5 %collective-permute-start.17 = (bf16[64,1024]{1,0:T(8,128)(2,1)S(1)}, bf16[64,1024]{1,0:T(8,128)(2,1)S(1)}, u32[]{:S(2)}, u32[]{:S(2)}) collective-permute-start(bf16[64,1024]{1,0:T(8,128)(2,1)S(1)} %get-tuple-element.84), channel_id=1, source_target_pairs={{0,2},{1,3},{2,0},{3,1},{4,6},{5,7},{6,4},{7,5},{8,10},{9,11},{10,... | collective-permute-start | bytes 393224 | tf_op jit(solution)/shard_map/o/zo1/co1/yo1/ppermute | solution.py:67
  62.0 0.2 co2.1
  62.3 1.7 %collective-permute-start.21 = (bf16[128,1024]{1,0:T(8,128)(2,1)S(1)}, bf16[128,1024]{1,0:T(8,128)(2,1)S(1)}, u32[]{:S(2)}, u32[]{:S(2)}) collective-permute-start(bf16[128,1024]{1,0:T(8,128)(2,1)S(1)} %co2.1), channel_id=1, source_target_pairs={{0,4},{1,5},{2,6},{3,7},{4,0},{5,1},{6,2},{7,3},{8,12},{9,13},{10,... | collective-permute-start | bytes 786440 | tf_op jit(solution)/shard_map/o/zo2/zo3/ppermute | solution.py:67
  64.0 0.5 collective-permute-start.15
  64.5 1.1 %ddk1.1 = bf16[1,704,512]{2,1,0:T(8,128)(2,1)S(1)} custom-call(s32[8]{0:T(128)S(1)} %stack.55.place_ref, bf16[128,1024]{1,0:T(8,128)(2,1)S(1)} %get-tuple-element.95.refs_0_, bf16[128,1024]{1,0:T(8,128)(2,1)S(1)} %collective-permute-done.13.refs_1_, bf16[64,1024]{1,0:T(8,128)(2,1)S(1)} %get-tuple-element.88.refs_0_.refs_2_, ...), custom_call_target="tpu_custom_call" | custom-call | flops 5000000000 | bytes 15000000 | tf_op jit(solution)/shard_map/dd/ddk0/dds1/ddk1/pallas_call | solution.py:520
  65.7 1.5 %dik1.1 = bf16[2,704,512]{2,1,0:T(8,128)(2,1)S(1)} custom-call(s32[8]{0:T(128)S(1)} %stack.55.place_ref, bf16[128,1152]{1,0:T(8,128)(2,1)S(1)} %get-tuple-element.64.refs_0_, bf16[128,1152]{1,0:T(8,128)(2,1)S(1)} %collective-permute-done.4.refs_1_, bf16[128,1152]{1,0:T(8,128)(2,1)S(1)} %get-tuple-element.67.refs_2_, ...), custom_call_target="tpu_custom_call" | custom-call | flops 5000000000 | bytes 15000000 | tf_op jit(solution)/shard_map/di/dik0/dis1/dik1/pallas_call | solution.py:520
  67.2 0.6 collective-permute-start.23
  67.8 0.4 collective-permute-done.17.refs_1_
  68.2 1.1 %collective-permute-start.27 = (bf16[64,1024]{1,0:T(8,128)(2,1)S(1)}, bf16[64,1024]{1,0:T(8,128)(2,1)S(1)}, u32[]{:S(2)}, u32[]{:S(2)}) collective-permute-start(bf16[64,1024]{1,0:T(8,128)(2,1)S(1)} %get-tuple-element.113), channel_id=1, source_target_pairs={{0,2},{1,3},{2,0},{3,1},{4,6},{5,7},{6,4},{7,5},{8,10},{9,11},{10,... | collective-permute-start | bytes 393224 | tf_op jit(solution)/shard_map/g/zg1/cg1/yg1/ppermute | solution.py:67
  69.3 0.3 co1.1
  69.5 0.3 cg2.1
  69.8 1.6 %collective-permute-done.15.refs_1_ = bf16[128,1024]{1,0:T(8,128)(2,1)S(1)} collective-permute-done((bf16[128,1024]{1,0:T(8,128)(2,1)S(1)}, bf16[128,1024]{1,0:T(8,128)(2,1)S(1)}, u32[]{:S(2)}, u32[]{:S(2)}) %collective-permute-start.15) | collective-permute-done | bytes 262176 | tf_op jit(solution)/shard_map/o/co0/yo0/ppermute | solution.py:67
  71.4 1.9 %collective-permute-start.18 = (bf16[128,1024]{1,0:T(8,128)(2,1)S(1)}, bf16[128,1024]{1,0:T(8,128)(2,1)S(1)}, u32[]{:S(2)}, u32[]{:S(2)}) collective-permute-start(bf16[128,1024]{1,0:T(8,128)(2,1)S(1)} %co1.1), channel_id=1, source_target_pairs={{0,4},{1,5},{2,6},{3,7},{4,0},{5,1},{6,2},{7,3},{8,12},{9,13},{10,... | collective-permute-start | bytes 786440 | tf_op jit(solution)/shard_map/o/zo1/ppermute | solution.py:67
  73.3 0.3 co0.1
  73.6 0.2 collective-permute-start.29
  73.9 0.1 collective-permute-start.25
  74.0 1.1 %ddk0.1 = (f32[1,352,512]{2,1,0:T(8,128)S(1)}, bf16[1,352,512]{2,1,0:T(8,128)(2,1)S(1)}) custom-call(s32[8]{0:T(128)S(1)} %stack.55.place_ref, bf16[128,1024]{1,0:T(8,128)(2,1)S(1)} %get-tuple-element.95.refs_0_, bf16[128,1024]{1,0:T(8,128)(2,1)S(1)} %collective-permute-done.13.refs_1_, bf16[64,1024]{1,0:T(8,128)(2,1)S(1)} %get-tuple-element.88.refs_0_.refs_2_, ...), custom_call_target="tpu_custom_call" | custom-call | flops 5000000000 | bytes 15000000 | tf_op jit(solution)/shard_map/dd/ddk0/pallas_call | solution.py:520
  75.2 2.2 %collective-permute-start.22 = (bf16[128,1024]{1,0:T(8,128)(2,1)S(1)}, bf16[128,1024]{1,0:T(8,128)(2,1)S(1)}, u32[]{:S(2)}, u32[]{:S(2)}) collective-permute-start(bf16[128,1024]{1,0:T(8,128)(2,1)S(1)} %add_convert_fusion.6), channel_id=1, source_target_pairs={{0,8},{1,9},{2,10},{3,11},{4,12},{5,13},{6,14},{7,15},{8,0},{9,1},... | collective-permute-start | bytes 786440 | tf_op jit(solution)/shard_map/o/zo2/ppermute | solution.py:67
  77.4 0.2 cg1.1
  77.6 1.9 %collective-permute-start.28 = (bf16[128,1024]{1,0:T(8,128)(2,1)S(1)}, bf16[128,1024]{1,0:T(8,128)(2,1)S(1)}, u32[]{:S(2)}, u32[]{:S(2)}) collective-permute-start(bf16[128,1024]{1,0:T(8,128)(2,1)S(1)} %cg1.1), channel_id=1, source_target_pairs={{0,4},{1,5},{2,6},{3,7},{4,0},{5,1},{6,2},{7,3},{8,12},{9,13},{10,... | collective-permute-start | bytes 786440 | tf_op jit(solution)/shard_map/g/zg1/ppermute | solution.py:67
  79.5 1.5 %dik0.1 = (f32[2,352,512]{2,1,0:T(8,128)S(1)}, bf16[2,352,512]{2,1,0:T(8,128)(2,1)S(1)}) custom-call(s32[8]{0:T(128)S(1)} %stack.55.place_ref, bf16[128,1152]{1,0:T(8,128)(2,1)S(1)} %get-tuple-element.64.refs_0_, bf16[128,1152]{1,0:T(8,128)(2,1)S(1)} %collective-permute-done.4.refs_1_, bf16[128,1152]{1,0:T(8,128)(2,1)S(1)} %get-tuple-element.67.refs_2_, ...), custom_call_target="tpu_custom_call" | custom-call | flops 5000000000 | bytes 15000000 | tf_op jit(solution)/shard_map/di/dik0/pallas_call | solution.py:520
  81.0 1.6 %collective-permute-start.32 = (bf16[1,352,512]{2,1,0:T(8,128)(2,1)S(1)}, bf16[1,352,512]{2,1,0:T(8,128)(2,1)S(1)}, u32[]{:S(2)}, u32[]{:S(2)}) collective-permute-start(bf16[1,352,512]{2,1,0:T(8,128)(2,1)S(1)} %get-tuple-element.118), channel_id=1, source_target_pairs={{0,1},{1,0},{2,3},{3,2},{4,5},{5,4},{6,7},{7,6},{8,9},{9,8},{10,11... | collective-permute-start | bytes 1081352 | tf_op jit(solution)/shard_map/dd/ddx/ppermute | solution.py:67
  82.6 0.3 cg0.1
  82.9 10.4 %collective-permute-done.29 = bf16[128,1024]{1,0:T(8,128)(2,1)S(1)} collective-permute-done((bf16[128,1024]{1,0:T(8,128)(2,1)S(1)}, bf16[128,1024]{1,0:T(8,128)(2,1)S(1)}, u32[]{:S(2)}, u32[]{:S(2)}) %collective-permute-start.29) | collective-permute-done | bytes 262176 | tf_op jit(solution)/shard_map/g/zg2/zg3/ppermute | solution.py:67
  93.4 0.6 collective-permute-start.30
  94.0 1.5 %collective-permute-start.31 = (bf16[2,352,512]{2,1,0:T(8,128)(2,1)S(1)}, bf16[2,352,512]{2,1,0:T(8,128)(2,1)S(1)}, u32[]{:S(2)}, u32[]{:S(2)}) collective-permute-start(bf16[2,352,512]{2,1,0:T(8,128)(2,1)S(1)} %get-tuple-element.116), channel_id=1, source_target_pairs={{0,1},{1,0},{2,3},{3,2},{4,5},{5,4},{6,7},{7,6},{8,9},{9,8},{10,11... | collective-permute-start | bytes 2162696 | tf_op jit(solution)/shard_map/di/dix/ppermute | solution.py:67
  95.5 0.8 add_convert_fusion.5
  96.3 0.8 add_convert_fusion
  97.2 0.5 collective-permute-done.28
  97.7 6.9 %collective-permute-done.30 = bf16[128,1024]{1,0:T(8,128)(2,1)S(1)} collective-permute-done((bf16[128,1024]{1,0:T(8,128)(2,1)S(1)}, bf16[128,1024]{1,0:T(8,128)(2,1)S(1)}, u32[]{:S(2)}, u32[]{:S(2)}) %collective-permute-start.30) | collective-permute-done | bytes 262176 | tf_op jit(solution)/shard_map/g/zg2/ppermute | solution.py:67
  104.6 0.8 add_convert_fusion.3
  105.4 1.1 %fusion.1 = (bf16[1,512,352]{1,2,0:T(8,128)(2,1)}, bf16[1,512,352]{1,2,0:T(8,128)(2,1)}) fusion(f32[2,352,512]{2,1,0:T(8,128)S(1)} %get-tuple-element.101, bf16[2,352,512]{2,1,0:T(8,128)(2,1)S(1)} %collective-permute-done.31), kind=kLoop, calls=%fused_computation.9 | loop fusion | flops 1081344 | bytes 2883584 | tf_op jit(solution)/shard_map/broadcast_in_dim | solution.py:553
  (37 shorter events, 0.5 us)
Async XLA Ops:
  1.3 11.4 %collective-permute-start.2 = (s32[4,128]{1,0:T(4,128)S(1)}, s32[4,128]{1,0:T(4,128)S(1)}, u32[]{:S(2)}, u32[]{:S(2)}) collective-permute-start(s32[4,128]{1,0:T(4,128)S(1)} %pad_add_fusion.1), channel_id=1, source_target_pairs={{0,12},{1,13},{2,14},{3,15},{4,8},{5,9},{6,10},{7,11},{8,4},{9,5},... | collective-permute-start | bytes 6152 | tf_op jit(solution)/shard_map/dd/ddk0/yt0/pt0/prep/T3/ppermute | solution.py:67
  6.4 7.9 %collective-permute-start.1 = (s32[4,128]{1,0:T(4,128)S(1)}, s32[4,128]{1,0:T(4,128)S(1)}, u32[]{:S(2)}, u32[]{:S(2)}) collective-permute-start(s32[4,128]{1,0:T(4,128)S(1)} %pad_add_fusion.1), channel_id=1, source_target_pairs={{0,8},{1,9},{2,10},{3,11},{4,12},{5,13},{6,14},{7,15},{8,0},{9,1},... | collective-permute-start | bytes 6152 | tf_op jit(solution)/shard_map/dd/ddk0/yt0/pt0/prep/T2/ppermute | solution.py:67
  6.4 8.0 %collective-permute-start = (s32[4,128]{1,0:T(4,128)S(1)}, s32[4,128]{1,0:T(4,128)S(1)}, u32[]{:S(2)}, u32[]{:S(2)}) collective-permute-start(s32[4,128]{1,0:T(4,128)S(1)} %pad_add_fusion.1), channel_id=1, source_target_pairs={{0,4},{1,5},{2,6},{3,7},{4,0},{5,1},{6,2},{7,3},{8,12},{9,13},{10,... | collective-permute-start | bytes 6152 | tf_op jit(solution)/shard_map/dd/ddk0/yt0/pt0/prep/T1/ppermute | solution.py:67
  7.0 14.3 %collective-permute-start.3 = (bf16[128,1024]{1,0:T(8,128)(2,1)}, bf16[128,1024]{1,0:T(8,128)(2,1)S(1)}, u32[]{:S(2)}, u32[]{:S(2)}) collective-permute-start(bf16[128,1024]{1,0:T(8,128)(2,1)} %refs_0_.1), channel_id=1, source_target_pairs={{0,8},{1,9},{2,10},{3,11},{4,12},{5,13},{6,14},{7,15},{8,0},{9,1},... | collective-permute-start | bytes 786440 | tf_op jit(solution)/shard_map/dd/ddk0/yt0/pt0/t2/ppermute | solution.py:67
  9.3 12.2 %collective-permute-start.5 = (bf16[128,1024]{1,0:T(8,128)(2,1)}, bf16[128,1024]{1,0:T(8,128)(2,1)S(1)}, u32[]{:S(2)}, u32[]{:S(2)}) collective-permute-start(bf16[128,1024]{1,0:T(8,128)(2,1)} %refs_0_.1), channel_id=1, source_target_pairs={{0,4},{1,5},{2,6},{3,7},{4,0},{5,1},{6,2},{7,3},{8,12},{9,13},{10,... | collective-permute-start | bytes 786440 | tf_op jit(solution)/shard_map/dd/ddk0/pt1/t1/ppermute | solution.py:67
  12.8 26.3 %collective-permute-start.9 = (bf16[3,352,512]{2,1,0:T(8,128)(2,1)S(1)}, bf16[3,352,512]{2,1,0:T(8,128)(2,1)S(1)}, u32[]{:S(2)}, u32[]{:S(2)}) collective-permute-start(bf16[3,352,512]{2,1,0:T(8,128)(2,1)S(1)} %pad_maximum_fusion.refs_4_.refs_2_), channel_id=1, source_target_pairs={{0,1},{1,0},{2,3},{3,2},{4,5},{5,4},{6,7},{7,6},{8,9},{9,8},{10,11... | collective-permute-start | bytes 3244040 | tf_op jit(solution)/shard_map/dd/ddk0/wp1/wx/ppermute | solution.py:67
  14.3 32.3 %collective-permute-start.8 = (bf16[3,352,512]{2,1,0:T(8,128)(2,1)S(1)}, bf16[3,352,512]{2,1,0:T(8,128)(2,1)S(1)}, u32[]{:S(2)}, u32[]{:S(2)}) collective-permute-start(bf16[3,352,512]{2,1,0:T(8,128)(2,1)S(1)} %pad_maximum_fusion.refs_4_.refs_2_), channel_id=1, source_target_pairs={{0,16},{16,0},{1,17},{17,1},{2,18},{18,2},{3,19},{19,3},{4,20},{20... | collective-permute-start | bytes 3244040 | tf_op jit(solution)/shard_map/dd/ddk0/fwd/ws1/ppermute | solution.py:324
  14.4 8.3 %copy-start.1 = (bf16[128,1024]{1,0:T(8,128)(2,1)S(1)}, bf16[128,1024]{1,0:T(8,128)(2,1)}, u32[]{:S(2)}) copy-start(bf16[128,1024]{1,0:T(8,128)(2,1)} %refs_0_.2) | copy-start | bytes 786436
  14.4 10.6 %copy-start = (bf16[128,1024]{1,0:T(8,128)(2,1)S(1)}, bf16[128,1024]{1,0:T(8,128)(2,1)}, u32[]{:S(2)}) copy-start(bf16[128,1024]{1,0:T(8,128)(2,1)} %refs_0_.1) | copy-start | bytes 786436
  21.5 12.6 %collective-permute-start.6 = (bf16[128,1024]{1,0:T(8,128)(2,1)S(1)}, bf16[128,1024]{1,0:T(8,128)(2,1)S(1)}, u32[]{:S(2)}, u32[]{:S(2)}) collective-permute-start(bf16[128,1024]{1,0:T(8,128)(2,1)S(1)} %collective-permute-done.3.refs_1_), channel_id=1, source_target_pairs={{0,4},{1,5},{2,6},{3,7},{4,0},{5,1},{6,2},{7,3},{8,12},{9,13},{10,... | collective-permute-start | bytes 786440 | tf_op jit(solution)/shard_map/dd/ddk0/pt1/t3/ppermute | solution.py:67
  22.7 14.2 %collective-permute-start.10 = (bf16[128,1024]{1,0:T(8,128)(2,1)S(1)}, bf16[128,1024]{1,0:T(8,128)(2,1)S(1)}, u32[]{:S(2)}, u32[]{:S(2)}) collective-permute-start(bf16[128,1024]{1,0:T(8,128)(2,1)S(1)} %copy-done.1), channel_id=1, source_target_pairs={{0,8},{1,9},{2,10},{3,11},{4,12},{5,13},{6,14},{7,15},{8,0},{9,1},... | collective-permute-start | bytes 786440 | tf_op jit(solution)/shard_map/dd/ddk0/pc0/c2/ppermute | solution.py:67
  25.3 11.5 %collective-permute-start.4 = (bf16[128,1152]{1,0:T(8,128)(2,1)S(1)}, bf16[128,1152]{1,0:T(8,128)(2,1)S(1)}, u32[]{:S(2)}, u32[]{:S(2)}) collective-permute-start(bf16[128,1152]{1,0:T(8,128)(2,1)S(1)} %get-tuple-element.65), channel_id=1, source_target_pairs={{0,2},{1,3},{2,0},{3,1},{4,6},{5,7},{6,4},{7,5},{8,10},{9,11},{10,... | collective-permute-start | bytes 884744 | tf_op jit(solution)/shard_map/dd/ddk0/yt0/ppermute | solution.py:67
  34.4 10.7 %collective-permute-start.7 = (bf16[128,1152]{1,0:T(8,128)(2,1)S(1)}, bf16[128,1152]{1,0:T(8,128)(2,1)S(1)}, u32[]{:S(2)}, u32[]{:S(2)}) collective-permute-start(bf16[128,1152]{1,0:T(8,128)(2,1)S(1)} %get-tuple-element.68), channel_id=1, source_target_pairs={{0,2},{1,3},{2,0},{3,1},{4,6},{5,7},{6,4},{7,5},{8,10},{9,11},{10,... | collective-permute-start | bytes 884744 | tf_op jit(solution)/shard_map/dd/ddk0/yt1/ppermute | solution.py:67
  36.9 6.4 %collective-permute-start.19 = (bf16[128,1024]{1,0:T(8,128)(2,1)S(1)}, bf16[128,1024]{1,0:T(8,128)(2,1)S(1)}, u32[]{:S(2)}, u32[]{:S(2)}) collective-permute-start(bf16[128,1024]{1,0:T(8,128)(2,1)S(1)} %copy-done.1), channel_id=1, source_target_pairs={{0,4},{1,5},{2,6},{3,7},{4,0},{5,1},{6,2},{7,3},{8,12},{9,13},{10,... | collective-permute-start | bytes 786440 | tf_op jit(solution)/shard_map/dd/ddk0/pc1/c1/ppermute | solution.py:67
  37.5 9.1 %copy-start.2 = (s32[2]{0:T(128)S(1)}, s32[2]{0:T(128)}, u32[]{:S(2)}) copy-start(s32[2]{0:T(128)} %key_ref.1) | copy-start | bytes 28
  37.5 13.4 %collective-permute-start.13 = (bf16[128,1024]{1,0:T(8,128)(2,1)S(1)}, bf16[128,1024]{1,0:T(8,128)(2,1)S(1)}, u32[]{:S(2)}, u32[]{:S(2)}) collective-permute-start(bf16[128,1024]{1,0:T(8,128)(2,1)S(1)} %get-tuple-element.75), channel_id=1, source_target_pairs={{0,2},{1,3},{2,0},{3,1},{4,6},{5,7},{6,4},{7,5},{8,10},{9,11},{10,... | collective-permute-start | bytes 786440 | tf_op jit(solution)/shard_map/dd/ddk0/yc0/ppermute | solution.py:67
  39.1 7.5 %collective-permute-start.11 = (bf16[3,352,512]{2,1,0:T(8,128)(2,1)S(1)}, bf16[3,352,512]{2,1,0:T(8,128)(2,1)S(1)}, u32[]{:S(2)}, u32[]{:S(2)}) collective-permute-start(bf16[3,352,512]{2,1,0:T(8,128)(2,1)S(1)} %collective-permute-done.9.refs_6_.refs_4_), channel_id=1, source_target_pairs={{0,16},{16,0},{1,17},{17,1},{2,18},{18,2},{3,19},{19,3},{4,20},{20... | collective-permute-start | bytes 3244040 | tf_op jit(solution)/shard_map/dd/ddk0/wp1/ppermute | solution.py:324
  43.5 13.3 %collective-permute-start.20 = (bf16[64,1024]{1,0:T(8,128)(2,1)S(1)}, bf16[64,1024]{1,0:T(8,128)(2,1)S(1)}, u32[]{:S(2)}, u32[]{:S(2)}) collective-permute-start(bf16[64,1024]{1,0:T(8,128)(2,1)S(1)} %get-tuple-element.90), channel_id=1, source_target_pairs={{0,2},{1,3},{2,0},{3,1},{4,6},{5,7},{6,4},{7,5},{8,10},{9,11},{10,... | collective-permute-start | bytes 393224 | tf_op jit(solution)/shard_map/dd/ddk0/yc1/ppermute | solution.py:67
  45.1 6.4 %collective-permute-start.12 = (bf16[128,1024]{1,0:T(8,128)(2,1)S(1)}, bf16[128,1024]{1,0:T(8,128)(2,1)S(1)}, u32[]{:S(2)}, u32[]{:S(2)}) collective-permute-start(bf16[128,1024]{1,0:T(8,128)(2,1)S(1)} %collective-permute-done.10.refs_1_), channel_id=1, source_target_pairs={{0,4},{1,5},{2,6},{3,7},{4,0},{5,1},{6,2},{7,3},{8,12},{9,13},{10,... | collective-permute-start | bytes 786440 | tf_op jit(solution)/shard_map/dd/ddk0/pc2/c3/ppermute | solution.py:67
  51.6 5.2 %collective-permute-start.14 = (bf16[64,1024]{1,0:T(8,128)(2,1)S(1)}, bf16[64,1024]{1,0:T(8,128)(2,1)S(1)}, u32[]{:S(2)}, u32[]{:S(2)}) collective-permute-start(bf16[64,1024]{1,0:T(8,128)(2,1)S(1)} %get-tuple-element.78), channel_id=1, source_target_pairs={{0,2},{1,3},{2,0},{3,1},{4,6},{5,7},{6,4},{7,5},{8,10},{9,11},{10,... | collective-permute-start | bytes 393224 | tf_op jit(solution)/shard_map/dd/ddk0/yc2/ppermute | solution.py:67
  52.2 8.3 %collective-permute-start.16 = (bf16[64,1024]{1,0:T(8,128)(2,1)S(1)}, bf16[64,1024]{1,0:T(8,128)(2,1)S(1)}, u32[]{:S(2)}, u32[]{:S(2)}) collective-permute-start(bf16[64,1024]{1,0:T(8,128)(2,1)S(1)} %get-tuple-element.83), channel_id=1, source_target_pairs={{0,2},{1,3},{2,0},{3,1},{4,6},{5,7},{6,4},{7,5},{8,10},{9,11},{10,... | collective-permute-start | bytes 393224 | tf_op jit(solution)/shard_map/o/zo1/co1/yo2/ppermute | solution.py:67
  59.9 7.3 %collective-permute-start.24 = (bf16[64,1024]{1,0:T(8,128)(2,1)S(1)}, bf16[64,1024]{1,0:T(8,128)(2,1)S(1)}, u32[]{:S(2)}, u32[]{:S(2)}) collective-permute-start(bf16[64,1024]{1,0:T(8,128)(2,1)S(1)} %get-tuple-element.104), channel_id=1, source_target_pairs={{0,2},{1,3},{2,0},{3,1},{4,6},{5,7},{6,4},{7,5},{8,10},{9,11},{10,... | collective-permute-start | bytes 393224 | tf_op jit(solution)/shard_map/g/cg0/yg2/ppermute | solution.py:67
  60.5 7.7 %collective-permute-start.17 = (bf16[64,1024]{1,0:T(8,128)(2,1)S(1)}, bf16[64,1024]{1,0:T(8,128)(2,1)S(1)}, u32[]{:S(2)}, u32[]{:S(2)}) collective-permute-start(bf16[64,1024]{1,0:T(8,128)(2,1)S(1)} %get-tuple-element.84), channel_id=1, source_target_pairs={{0,2},{1,3},{2,0},{3,1},{4,6},{5,7},{6,4},{7,5},{8,10},{9,11},{10,... | collective-permute-start | bytes 393224 | tf_op jit(solution)/shard_map/o/zo1/co1/yo1/ppermute | solution.py:67
  62.3 11.4 %collective-permute-start.21 = (bf16[128,1024]{1,0:T(8,128)(2,1)S(1)}, bf16[128,1024]{1,0:T(8,128)(2,1)S(1)}, u32[]{:S(2)}, u32[]{:S(2)}) collective-permute-start(bf16[128,1024]{1,0:T(8,128)(2,1)S(1)} %co2.1), channel_id=1, source_target_pairs={{0,4},{1,5},{2,6},{3,7},{4,0},{5,1},{6,2},{7,3},{8,12},{9,13},{10,... | collective-permute-start | bytes 786440 | tf_op jit(solution)/shard_map/o/zo2/zo3/ppermute | solution.py:67
  64.0 7.4 %collective-permute-start.15 = (bf16[128,1024]{1,0:T(8,128)(2,1)S(1)}, bf16[128,1024]{1,0:T(8,128)(2,1)S(1)}, u32[]{:S(2)}, u32[]{:S(2)}) collective-permute-start(bf16[128,1024]{1,0:T(8,128)(2,1)S(1)} %get-tuple-element.79), channel_id=1, source_target_pairs={{0,2},{1,3},{2,0},{3,1},{4,6},{5,7},{6,4},{7,5},{8,10},{9,11},{10,... | collective-permute-start | bytes 786440 | tf_op jit(solution)/shard_map/o/co0/yo0/ppermute | solution.py:67
  65.6 8.3 %collective-permute-start.26 = (bf16[1,704,512]{2,1,0:T(8,128)(2,1)S(1)}, bf16[1,704,512]{2,1,0:T(8,128)(2,1)S(1)}, u32[]{:S(2)}, u32[]{:S(2)}) collective-permute-start(bf16[1,704,512]{2,1,0:T(8,128)(2,1)S(1)} %ddk1.1), channel_id=1, source_target_pairs={{0,16},{16,0},{1,17},{17,1},{2,18},{18,2},{3,19},{19,3},{4,20},{20... | collective-permute-start | bytes 2162696 | tf_op jit(solution)/shard_map/dd/ddk0/dds1/ppermute | solution.py:324
  67.2 10.4 %collective-permute-start.23 = (bf16[2,704,512]{2,1,0:T(8,128)(2,1)S(1)}, bf16[2,704,512]{2,1,0:T(8,128)(2,1)S(1)}, u32[]{:S(2)}, u32[]{:S(2)}) collective-permute-start(bf16[2,704,512]{2,1,0:T(8,128)(2,1)S(1)} %dik1.1), channel_id=1, source_target_pairs={{0,16},{16,0},{1,17},{17,1},{2,18},{18,2},{3,19},{19,3},{4,20},{20... | collective-permute-start | bytes 4325384 | tf_op jit(solution)/shard_map/di/dik0/dis1/ppermute | solution.py:324
  68.2 7.0 %collective-permute-start.27 = (bf16[64,1024]{1,0:T(8,128)(2,1)S(1)}, bf16[64,1024]{1,0:T(8,128)(2,1)S(1)}, u32[]{:S(2)}, u32[]{:S(2)}) collective-permute-start(bf16[64,1024]{1,0:T(8,128)(2,1)S(1)} %get-tuple-element.113), channel_id=1, source_target_pairs={{0,2},{1,3},{2,0},{3,1},{4,6},{5,7},{6,4},{7,5},{8,10},{9,11},{10,... | collective-permute-start | bytes 393224 | tf_op jit(solution)/shard_map/g/zg1/cg1/yg1/ppermute | solution.py:67
  71.4 22.6 %collective-permute-start.18 = (bf16[128,1024]{1,0:T(8,128)(2,1)S(1)}, bf16[128,1024]{1,0:T(8,128)(2,1)S(1)}, u32[]{:S(2)}, u32[]{:S(2)}) collective-permute-start(bf16[128,1024]{1,0:T(8,128)(2,1)S(1)} %co1.1), channel_id=1, source_target_pairs={{0,4},{1,5},{2,6},{3,7},{4,0},{5,1},{6,2},{7,3},{8,12},{9,13},{10,... | collective-permute-start | bytes 786440 | tf_op jit(solution)/shard_map/o/zo1/ppermute | solution.py:67
  73.6 19.7 %collective-permute-start.29 = (bf16[128,1024]{1,0:T(8,128)(2,1)S(1)}, bf16[128,1024]{1,0:T(8,128)(2,1)S(1)}, u32[]{:S(2)}, u32[]{:S(2)}) collective-permute-start(bf16[128,1024]{1,0:T(8,128)(2,1)S(1)} %cg2.1), channel_id=1, source_target_pairs={{0,4},{1,5},{2,6},{3,7},{4,0},{5,1},{6,2},{7,3},{8,12},{9,13},{10,... | collective-permute-start | bytes 786440 | tf_op jit(solution)/shard_map/g/zg2/zg3/ppermute | solution.py:67
  73.9 7.1 %collective-permute-start.25 = (bf16[128,1024]{1,0:T(8,128)(2,1)S(1)}, bf16[128,1024]{1,0:T(8,128)(2,1)S(1)}, u32[]{:S(2)}, u32[]{:S(2)}) collective-permute-start(bf16[128,1024]{1,0:T(8,128)(2,1)S(1)} %get-tuple-element.105), channel_id=1, source_target_pairs={{0,2},{1,3},{2,0},{3,1},{4,6},{5,7},{6,4},{7,5},{8,10},{9,11},{10,... | collective-permute-start | bytes 786440 | tf_op jit(solution)/shard_map/g/cg0/yg0/ppermute | solution.py:67
  75.2 20.3 %collective-permute-start.22 = (bf16[128,1024]{1,0:T(8,128)(2,1)S(1)}, bf16[128,1024]{1,0:T(8,128)(2,1)S(1)}, u32[]{:S(2)}, u32[]{:S(2)}) collective-permute-start(bf16[128,1024]{1,0:T(8,128)(2,1)S(1)} %add_convert_fusion.6), channel_id=1, source_target_pairs={{0,8},{1,9},{2,10},{3,11},{4,12},{5,13},{6,14},{7,15},{8,0},{9,1},... | collective-permute-start | bytes 786440 | tf_op jit(solution)/shard_map/o/zo2/ppermute | solution.py:67
  77.6 20.1 %collective-permute-start.28 = (bf16[128,1024]{1,0:T(8,128)(2,1)S(1)}, bf16[128,1024]{1,0:T(8,128)(2,1)S(1)}, u32[]{:S(2)}, u32[]{:S(2)}) collective-permute-start(bf16[128,1024]{1,0:T(8,128)(2,1)S(1)} %cg1.1), channel_id=1, source_target_pairs={{0,4},{1,5},{2,6},{3,7},{4,0},{5,1},{6,2},{7,3},{8,12},{9,13},{10,... | collective-permute-start | bytes 786440 | tf_op jit(solution)/shard_map/g/zg1/ppermute | solution.py:67
  81.0 15.3 %collective-permute-start.32 = (bf16[1,352,512]{2,1,0:T(8,128)(2,1)S(1)}, bf16[1,352,512]{2,1,0:T(8,128)(2,1)S(1)}, u32[]{:S(2)}, u32[]{:S(2)}) collective-permute-start(bf16[1,352,512]{2,1,0:T(8,128)(2,1)S(1)} %get-tuple-element.118), channel_id=1, source_target_pairs={{0,1},{1,0},{2,3},{3,2},{4,5},{5,4},{6,7},{7,6},{8,9},{9,8},{10,11... | collective-permute-start | bytes 1081352 | tf_op jit(solution)/shard_map/dd/ddx/ppermute | solution.py:67
  93.4 11.2 %collective-permute-start.30 = (bf16[128,1024]{1,0:T(8,128)(2,1)S(1)}, bf16[128,1024]{1,0:T(8,128)(2,1)S(1)}, u32[]{:S(2)}, u32[]{:S(2)}) collective-permute-start(bf16[128,1024]{1,0:T(8,128)(2,1)S(1)} %add_convert_fusion.4), channel_id=1, source_target_pairs={{0,8},{1,9},{2,10},{3,11},{4,12},{5,13},{6,14},{7,15},{8,0},{9,1},... | collective-permute-start | bytes 786440 | tf_op jit(solution)/shard_map/g/zg2/ppermute | solution.py:67
  94.0 11.4 %collective-permute-start.31 = (bf16[2,352,512]{2,1,0:T(8,128)(2,1)S(1)}, bf16[2,352,512]{2,1,0:T(8,128)(2,1)S(1)}, u32[]{:S(2)}, u32[]{:S(2)}) collective-permute-start(bf16[2,352,512]{2,1,0:T(8,128)(2,1)S(1)} %get-tuple-element.116), channel_id=1, source_target_pairs={{0,1},{1,0},{2,3},{3,2},{4,5},{5,4},{6,7},{7,6},{8,9},{9,8},{10,11... | collective-permute-start | bytes 2162696 | tf_op jit(solution)/shard_map/di/dix/ppermute | solution.py:67

commit v7 on v6

--- a/solution.py
+++ b/solution.py
@@ -28,7 +28,7 @@
     "co0": 20,
     "co1": 20,
     "co2": 20,
-    "cg0": 1,
+    "cg0": 20,
     "cg1": 1,
     "cg2": 1,
     "ddk1": 5,
@@ -42,16 +42,20 @@
     "c3": ("t3", "yt0", "wx",),
     "c1": ("t3", "c2", "yt0",),
     "pc0": ("yt0", "pt1",),
-    "wp1": ("c2", "t3",),
+    "wp1": ("t3",),
     "pc2": ("yt1", "yc0", "wp1", "fwd",),
     "yo0": ("yc2",),
     "co2": ("bwd1",),
     "yg1": ("yg2",),
     "yg0": ("yg2", "yo0",),
-    "yo1": ("yo2",),
-    "g": ("dd", "di",),
-    "cg1": ("ddk0",),
+    "g": ("dd", "dix",),
+    "cg1": ("ddk0", "co0",),
     "cg0": ("dik0",),
+    "dd": ("di",),
+    "dik1": ("ddk1", "yo1",),
+    "zg2": ("dik0",),
+    "pt0": ("prep",),
+    "dis1": ("ddk1",),
 }
 
 

time: 107 us -> 102 us (0.953)
  starting transfers between devices: 41.5 us -> 36 us
    ppermute x29, starting transfers between devices: 40.9 us -> 35.4 us  [flipped(): lax.ppermute(values, axis, [(i, i ^ mask) for i in range(lax.axis_size(ax...]
  transfers between devices with their start and end apart: 33 -> 33, of which waited for: 11 -> 12; matrix products, arithmetic and copies ran while one was open for 4% -> 4% of each run, Pallas kernels for 18% -> 19%
where the time goes in v7:
time: 102 us
  waiting for transfers between devices  39.5 us (39%)
  starting transfers between devices  36 us (35%)
  Pallas kernels  19.3 us (19%)
  other arithmetic  5.73 us (6%)
    ppermute x29, waiting for transfers between devices, flipped(): lax.ppermute(values, axis, [(i, i ^ mask) for i in range(lax.axis_size(ax...  39.5 us
    ppermute x29, starting transfers between devices, flipped(): lax.ppermute(values, axis, [(i, i ^ mask) for i in range(lax.axis_size(ax...  35.4 us
    pallas_call x2, Pallas kernels, backward(): called(functools.partial(backward_kernel, seq_count, len(cot_parts), len(...  6.13 us
    pallas_call x4, Pallas kernels, weight_kernel(): called(functools.partial(weight_grad_kernel, len(row_parts), seq_count, s...  5.19 us
    pallas_call x1, Pallas kernels, forward(): called(functools.partial(forward_kernel, seq_count, plane_experts, capaci...  4.24 us
  transfers between devices with their start and end apart: 33, of which 12 were waited for; matrix products, arithmetic and copies ran while one was open for 4% of the time, Pallas kernels for 19%

profile of v7, /device:TPU:0, one launch (start us, length us, event | category | flops | bytes accessed | tf_op | source)
XLA Modules:
  0.0 101.7 jit_solution(10297669423155634376)
XLA Ops:
  0.6 0.7 pad_add_fusion.1
  1.3 5.0 %collective-permute-start.2 = (s32[4,128]{1,0:T(4,128)S(1)}, s32[4,128]{1,0:T(4,128)S(1)}, u32[]{:S(2)}, u32[]{:S(2)}) collective-permute-start(s32[4,128]{1,0:T(4,128)S(1)} %pad_add_fusion.1), channel_id=1, source_target_pairs={{0,12},{1,13},{2,14},{3,15},{4,8},{5,9},{6,10},{7,11},{8,4},{9,5},... | collective-permute-start | bytes 6152 | tf_op jit(solution)/shard_map/di/dik0/prep/T3/ppermute | solution.py:71
  6.4 0.6 collective-permute-start
  7.0 1.4 %collective-permute-start.5 = (bf16[128,1024]{1,0:T(8,128)(2,1)}, bf16[128,1024]{1,0:T(8,128)(2,1)S(1)}, u32[]{:S(2)}, u32[]{:S(2)}) collective-permute-start(bf16[128,1024]{1,0:T(8,128)(2,1)} %refs_0_), channel_id=1, source_target_pairs={{0,4},{1,5},{2,6},{3,7},{4,0},{5,1},{6,2},{7,3},{8,12},{9,13},{10,... | collective-permute-start | bytes 786440 | tf_op jit(solution)/shard_map/di/dik0/pt1/t1/ppermute | solution.py:71
  8.4 2.9 %collective-permute-start.3 = (bf16[128,1024]{1,0:T(8,128)(2,1)}, bf16[128,1024]{1,0:T(8,128)(2,1)S(1)}, u32[]{:S(2)}, u32[]{:S(2)}) collective-permute-start(bf16[128,1024]{1,0:T(8,128)(2,1)} %refs_0_), channel_id=1, source_target_pairs={{0,8},{1,9},{2,10},{3,11},{4,12},{5,13},{6,14},{7,15},{8,0},{9,1},... | collective-permute-start | bytes 786440 | tf_op jit(solution)/shard_map/di/dik0/pt0/t2/ppermute | solution.py:71
  11.3 1.3 %pad_maximum_fusion.refs_4_.refs_2_ = bf16[3,352,512]{2,1,0:T(8,128)(2,1)S(1)} fusion(bf16[1,352,512]{2,1,0:T(8,128)(2,1)} %param.15, bf16[1,352,512]{2,1,0:T(8,128)(2,1)} %bitcast.47, bf16[1,352,512]{2,1,0:T(8,128)(2,1)} %bitcast.48), kind=kLoop, calls=%fused_computation | loop fusion | flops 1081344 | bytes 2162688 | tf_op jit(solution)/shard_map/stack | solution.py:351
  12.7 0.1 stack.55.place_ref
  12.8 1.6 %collective-permute-start.9 = (bf16[3,352,512]{2,1,0:T(8,128)(2,1)S(1)}, bf16[3,352,512]{2,1,0:T(8,128)(2,1)S(1)}, u32[]{:S(2)}, u32[]{:S(2)}) collective-permute-start(bf16[3,352,512]{2,1,0:T(8,128)(2,1)S(1)} %pad_maximum_fusion.refs_4_.refs_2_), channel_id=1, source_target_pairs={{0,1},{1,0},{2,3},{3,2},{4,5},{5,4},{6,7},{7,6},{8,9},{9,8},{10,11... | collective-permute-start | bytes 3244040 | tf_op jit(solution)/shard_map/di/dik0/bwd0/wx/ppermute | solution.py:71
  14.4 0.7 prep.1
  15.1 5.2 %collective-permute-done.5.refs_0_ = bf16[128,1024]{1,0:T(8,128)(2,1)S(1)} collective-permute-done((bf16[128,1024]{1,0:T(8,128)(2,1)}, bf16[128,1024]{1,0:T(8,128)(2,1)S(1)}, u32[]{:S(2)}, u32[]{:S(2)}) %collective-permute-start.5) | collective-permute-done | bytes 262176 | tf_op jit(solution)/shard_map/di/dik0/pt1/t1/ppermute | solution.py:71
  20.2 2.3 %collective-permute-done.3.refs_1_ = bf16[128,1024]{1,0:T(8,128)(2,1)S(1)} collective-permute-done((bf16[128,1024]{1,0:T(8,128)(2,1)}, bf16[128,1024]{1,0:T(8,128)(2,1)S(1)}, u32[]{:S(2)}, u32[]{:S(2)}) %collective-permute-start.3) | collective-permute-done | bytes 262176 | tf_op jit(solution)/shard_map/di/dik0/pt0/t2/ppermute | solution.py:71
  22.5 0.3 collective-permute-start.6
  22.8 2.6 %collective-permute-start.11 = (bf16[128,1024]{1,0:T(8,128)(2,1)S(1)}, bf16[128,1024]{1,0:T(8,128)(2,1)S(1)}, u32[]{:S(2)}, u32[]{:S(2)}) collective-permute-start(bf16[128,1024]{1,0:T(8,128)(2,1)S(1)} %copy-done.1), channel_id=1, source_target_pairs={{0,8},{1,9},{2,10},{3,11},{4,12},{5,13},{6,14},{7,15},{8,0},{9,1},... | collective-permute-start | bytes 786440 | tf_op jit(solution)/shard_map/di/dik0/bwd0/pc0/c2/ppermute | solution.py:71
  25.4 0.3 pt0.1
  25.8 1.6 %collective-permute-start.4 = (bf16[128,1152]{1,0:T(8,128)(2,1)S(1)}, bf16[128,1152]{1,0:T(8,128)(2,1)S(1)}, u32[]{:S(2)}, u32[]{:S(2)}) collective-permute-start(bf16[128,1152]{1,0:T(8,128)(2,1)S(1)} %get-tuple-element.70), channel_id=1, source_target_pairs={{0,2},{1,3},{2,0},{3,1},{4,6},{5,7},{6,4},{7,5},{8,10},{9,11},{10,... | collective-permute-start | bytes 884744 | tf_op jit(solution)/shard_map/di/dik0/yt0/ppermute | solution.py:71
  27.3 4.8 %collective-permute-done.6.refs_1_ = bf16[128,1024]{1,0:T(8,128)(2,1)S(1)} collective-permute-done((bf16[128,1024]{1,0:T(8,128)(2,1)S(1)}, bf16[128,1024]{1,0:T(8,128)(2,1)S(1)}, u32[]{:S(2)}, u32[]{:S(2)}) %collective-permute-start.6) | collective-permute-done | bytes 262176 | tf_op jit(solution)/shard_map/di/dik0/pt1/t3/ppermute | solution.py:71
  32.2 0.3 pt1.1
  32.5 1.6 %collective-permute-start.7 = (bf16[128,1152]{1,0:T(8,128)(2,1)S(1)}, bf16[128,1152]{1,0:T(8,128)(2,1)S(1)}, u32[]{:S(2)}, u32[]{:S(2)}) collective-permute-start(bf16[128,1152]{1,0:T(8,128)(2,1)S(1)} %get-tuple-element.73), channel_id=1, source_target_pairs={{0,2},{1,3},{2,0},{3,1},{4,6},{5,7},{6,4},{7,5},{8,10},{9,11},{10,... | collective-permute-start | bytes 884744 | tf_op jit(solution)/shard_map/di/dik0/yt1/ppermute | solution.py:71
  34.1 1.6 %collective-permute-done.11.refs_1_ = bf16[128,1024]{1,0:T(8,128)(2,1)S(1)} collective-permute-done((bf16[128,1024]{1,0:T(8,128)(2,1)S(1)}, bf16[128,1024]{1,0:T(8,128)(2,1)S(1)}, u32[]{:S(2)}, u32[]{:S(2)}) %collective-permute-start.11) | collective-permute-done | bytes 262176 | tf_op jit(solution)/shard_map/di/dik0/bwd0/pc0/c2/ppermute | solution.py:71
  35.7 0.3 pc0.1
  36.0 1.6 %collective-permute-start.13 = (bf16[128,1024]{1,0:T(8,128)(2,1)S(1)}, bf16[128,1024]{1,0:T(8,128)(2,1)S(1)}, u32[]{:S(2)}, u32[]{:S(2)}) collective-permute-start(bf16[128,1024]{1,0:T(8,128)(2,1)S(1)} %get-tuple-element.80), channel_id=1, source_target_pairs={{0,2},{1,3},{2,0},{3,1},{4,6},{5,7},{6,4},{7,5},{8,10},{9,11},{10,... | collective-permute-start | bytes 786440 | tf_op jit(solution)/shard_map/di/dik0/bwd0/yc0/ppermute | solution.py:71
  37.6 4.8 %collective-permute-done.18.refs_0_ = bf16[128,1024]{1,0:T(8,128)(2,1)S(1)} collective-permute-done((bf16[128,1024]{1,0:T(8,128)(2,1)S(1)}, bf16[128,1024]{1,0:T(8,128)(2,1)S(1)}, u32[]{:S(2)}, u32[]{:S(2)}) %collective-permute-start.18) | collective-permute-done | bytes 262176 | tf_op jit(solution)/shard_map/di/dik0/bwd1/pc1/c1/ppermute | solution.py:71
  42.4 0.2 pc1.1
  42.6 1.7 %collective-permute-start.19 = (bf16[64,1024]{1,0:T(8,128)(2,1)S(1)}, bf16[64,1024]{1,0:T(8,128)(2,1)S(1)}, u32[]{:S(2)}, u32[]{:S(2)}) collective-permute-start(bf16[64,1024]{1,0:T(8,128)(2,1)S(1)} %get-tuple-element.93), channel_id=1, source_target_pairs={{0,2},{1,3},{2,0},{3,1},{4,6},{5,7},{6,4},{7,5},{8,10},{9,11},{10,... | collective-permute-start | bytes 393224 | tf_op jit(solution)/shard_map/di/dik0/bwd1/yc1/ppermute | solution.py:71
  44.4 4.2 %fwd.1 = (bf16[128,1024]{1,0:T(8,128)(2,1)S(1)}, bf16[128,1024]{1,0:T(8,128)(2,1)S(1)}, bf16[64,1024]{1,0:T(8,128)(2,1)S(1)}, bf16[64,1024]{1,0:T(8,128)(2,1)S(1...) custom-call(s32[8]{0:T(128)S(1)} %stack.55.place_ref, ...), custom_call_target="tpu_custom_call" | custom-call | flops 20000000000 | bytes 60000000 | tf_op jit(solution)/shard_map/di/dik0/bwd0/fwd/pallas_call | solution.py:433
  48.7 2.1 %collective-permute-done.12.refs_0_ = bf16[128,1024]{1,0:T(8,128)(2,1)S(1)} collective-permute-done((bf16[128,1024]{1,0:T(8,128)(2,1)S(1)}, bf16[128,1024]{1,0:T(8,128)(2,1)S(1)}, u32[]{:S(2)}, u32[]{:S(2)}) %collective-permute-start.12) | collective-permute-done | bytes 262176 | tf_op jit(solution)/shard_map/di/dik0/bwd1/pc2/c3/ppermute | solution.py:71
  50.7 0.2 pc2.1
  51.0 0.4 collective-permute-start.14
  51.4 1.7 %collective-permute-start.16 = (bf16[64,1024]{1,0:T(8,128)(2,1)S(1)}, bf16[64,1024]{1,0:T(8,128)(2,1)S(1)}, u32[]{:S(2)}, u32[]{:S(2)}) collective-permute-start(bf16[64,1024]{1,0:T(8,128)(2,1)S(1)} %get-tuple-element.87), channel_id=1, source_target_pairs={{0,2},{1,3},{2,0},{3,1},{4,6},{5,7},{6,4},{7,5},{8,10},{9,11},{10,... | collective-permute-start | bytes 393224 | tf_op jit(solution)/shard_map/di/dik0/dis1/yo1/ppermute | solution.py:71
  53.1 0.4 collective-permute-start.20
  53.4 3.1 %bwd0.1 = (bf16[128,1024]{1,0:T(8,128)(2,1)S(1)}, bf16[128,1024]{1,0:T(8,128)(2,1)S(1)}, bf16[256,704]{1,0:T(8,128)(2,1)S(1)}, bf16[256,704]{1,0:T(8,128)(2,1)S(1)}) custom-call(s32[8]{0:T(128)S(1)} %stack.55.place_ref, bf16[128,1024]{1,0:T(8,128)(2,1)S(1)} %get-tuple-element.99.refs_0_, bf16[128,1024]{1,0:T(8,128)(2,1)S(1)} %collective-permute-done.13.refs_1_, ...), custom_call_target="tpu_custom_call" | custom-call | flops 20000000000 | bytes 60000000 | tf_op jit(solution)/shard_map/di/dik0/bwd0/pallas_call | solution.py:450
  56.5 3.1 %bwd1.1 = (bf16[64,1024]{1,0:T(8,128)(2,1)S(1)}, bf16[64,1024]{1,0:T(8,128)(2,1)S(1)}, bf16[64,1024]{1,0:T(8,128)(2,1)S(1)}, bf16[64,1024]{1,0:T(8,128)(2,1)S(1)...) custom-call(s32[8]{0:T(128)S(1)} %stack.55.place_ref, ...), custom_call_target="tpu_custom_call" | custom-call | flops 20000000000 | bytes 60000000 | tf_op jit(solution)/shard_map/di/dik0/bwd1/pallas_call | solution.py:450
  59.6 1.7 %collective-permute-start.24 = (bf16[64,1024]{1,0:T(8,128)(2,1)S(1)}, bf16[64,1024]{1,0:T(8,128)(2,1)S(1)}, u32[]{:S(2)}, u32[]{:S(2)}) collective-permute-start(bf16[64,1024]{1,0:T(8,128)(2,1)S(1)} %get-tuple-element.112), channel_id=1, source_target_pairs={{0,2},{1,3},{2,0},{3,1},{4,6},{5,7},{6,4},{7,5},{8,10},{9,11},{10,... | collective-permute-start | bytes 393224 | tf_op jit(solution)/shard_map/g/cg0/yg2/ppermute | solution.py:71
  61.3 0.2 co2.1
  61.7 0.2 co1.1
  61.9 2.1 %collective-permute-start.17 = (bf16[128,1024]{1,0:T(8,128)(2,1)S(1)}, bf16[128,1024]{1,0:T(8,128)(2,1)S(1)}, u32[]{:S(2)}, u32[]{:S(2)}) collective-permute-start(bf16[128,1024]{1,0:T(8,128)(2,1)S(1)} %co1.1), channel_id=1, source_target_pairs={{0,4},{1,5},{2,6},{3,7},{4,0},{5,1},{6,2},{7,3},{8,12},{9,13},{10,... | collective-permute-start | bytes 786440 | tf_op jit(solution)/shard_map/o/zo1/ppermute | solution.py:71
  64.0 0.4 collective-permute-start.15
  64.4 1.1 %ddk1.1 = bf16[1,704,512]{2,1,0:T(8,128)(2,1)S(1)} custom-call(s32[8]{0:T(128)S(1)} %stack.55.place_ref, bf16[128,1024]{1,0:T(8,128)(2,1)S(1)} %get-tuple-element.99.refs_0_, bf16[128,1024]{1,0:T(8,128)(2,1)S(1)} %collective-permute-done.13.refs_1_, bf16[64,1024]{1,0:T(8,128)(2,1)S(1)} %get-tuple-element.91.refs_0_.refs_2_, ...), custom_call_target="tpu_custom_call" | custom-call | flops 5000000000 | bytes 15000000 | tf_op jit(solution)/shard_map/di/dik0/ddk1/pallas_call | solution.py:524
  65.5 1.5 %dik1.1 = bf16[2,704,512]{2,1,0:T(8,128)(2,1)S(1)} custom-call(s32[8]{0:T(128)S(1)} %stack.55.place_ref, bf16[128,1152]{1,0:T(8,128)(2,1)S(1)} %get-tuple-element.69.refs_0_, bf16[128,1152]{1,0:T(8,128)(2,1)S(1)} %collective-permute-done.4.refs_1_, bf16[128,1152]{1,0:T(8,128)(2,1)S(1)} %get-tuple-element.72.refs_2_, ...), custom_call_target="tpu_custom_call" | custom-call | flops 5000000000 | bytes 15000000 | tf_op jit(solution)/shard_map/di/dik0/dis1/dik1/pallas_call | solution.py:524
  67.0 0.6 collective-permute-start.23
  67.6 0.2 cg2.1
  67.9 2.5 %collective-permute-done.15.refs_1_ = bf16[128,1024]{1,0:T(8,128)(2,1)S(1)} collective-permute-done((bf16[128,1024]{1,0:T(8,128)(2,1)S(1)}, bf16[128,1024]{1,0:T(8,128)(2,1)S(1)}, u32[]{:S(2)}, u32[]{:S(2)}) %collective-permute-start.15) | collective-permute-done | bytes 262176 | tf_op jit(solution)/shard_map/o/co0/yo0/ppermute | solution.py:71
  70.4 0.4 collective-permute-start.27
  70.7 0.3 co0.1
  71.1 0.1 collective-permute-start.29
  71.3 1.7 %collective-permute-start.25 = (bf16[128,1024]{1,0:T(8,128)(2,1)S(1)}, bf16[128,1024]{1,0:T(8,128)(2,1)S(1)}, u32[]{:S(2)}, u32[]{:S(2)}) collective-permute-start(bf16[128,1024]{1,0:T(8,128)(2,1)S(1)} %get-tuple-element.113), channel_id=1, source_target_pairs={{0,2},{1,3},{2,0},{3,1},{4,6},{5,7},{6,4},{7,5},{8,10},{9,11},{10,... | collective-permute-start | bytes 786440 | tf_op jit(solution)/shard_map/g/cg0/yg0/ppermute | solution.py:71
  73.0 1.1 %ddk0.1 = (f32[1,352,512]{2,1,0:T(8,128)S(1)}, bf16[1,352,512]{2,1,0:T(8,128)(2,1)S(1)}) custom-call(s32[8]{0:T(128)S(1)} %stack.55.place_ref, bf16[128,1024]{1,0:T(8,128)(2,1)S(1)} %get-tuple-element.99.refs_0_, bf16[128,1024]{1,0:T(8,128)(2,1)S(1)} %collective-permute-done.13.refs_1_, bf16[64,1024]{1,0:T(8,128)(2,1)S(1)} %get-tuple-element.91.refs_0_.refs_2_, ...), custom_call_target="tpu_custom_call" | custom-call | flops 5000000000 | bytes 15000000 | tf_op jit(solution)/shard_map/dd/ddk0/pallas_call | solution.py:524
  74.1 2.6 %collective-permute-done.27.refs_1_ = bf16[64,1024]{1,0:T(8,128)(2,1)S(1)} collective-permute-done((bf16[64,1024]{1,0:T(8,128)(2,1)S(1)}, bf16[64,1024]{1,0:T(8,128)(2,1)S(1)}, u32[]{:S(2)}, u32[]{:S(2)}) %collective-permute-start.27) | collective-permute-done | bytes 131104 | tf_op jit(solution)/shard_map/g/zg1/cg1/yg1/ppermute | solution.py:71
  76.8 0.6 collective-permute-start.22
  77.3 0.2 cg1.1
  77.6 1.6 %collective-permute-start.32 = (bf16[1,352,512]{2,1,0:T(8,128)(2,1)S(1)}, bf16[1,352,512]{2,1,0:T(8,128)(2,1)S(1)}, u32[]{:S(2)}, u32[]{:S(2)}) collective-permute-start(bf16[1,352,512]{2,1,0:T(8,128)(2,1)S(1)} %get-tuple-element.125), channel_id=1, source_target_pairs={{0,1},{1,0},{2,3},{3,2},{4,5},{5,4},{6,7},{7,6},{8,9},{9,8},{10,11... | collective-permute-start | bytes 1081352 | tf_op jit(solution)/shard_map/dd/ddx/ppermute | solution.py:71
  79.2 1.5 %dik0.1 = (f32[2,352,512]{2,1,0:T(8,128)S(1)}, bf16[2,352,512]{2,1,0:T(8,128)(2,1)S(1)}) custom-call(s32[8]{0:T(128)S(1)} %stack.55.place_ref, bf16[128,1152]{1,0:T(8,128)(2,1)S(1)} %get-tuple-element.69.refs_0_, bf16[128,1152]{1,0:T(8,128)(2,1)S(1)} %collective-permute-done.4.refs_1_, bf16[128,1152]{1,0:T(8,128)(2,1)S(1)} %get-tuple-element.72.refs_2_, ...), custom_call_target="tpu_custom_call" | custom-call | flops 5000000000 | bytes 15000000 | tf_op jit(solution)/shard_map/di/dik0/pallas_call | solution.py:524
  80.7 1.7 %collective-permute-start.28 = (bf16[128,1024]{1,0:T(8,128)(2,1)S(1)}, bf16[128,1024]{1,0:T(8,128)(2,1)S(1)}, u32[]{:S(2)}, u32[]{:S(2)}) collective-permute-start(bf16[128,1024]{1,0:T(8,128)(2,1)S(1)} %cg1.1), channel_id=1, source_target_pairs={{0,4},{1,5},{2,6},{3,7},{4,0},{5,1},{6,2},{7,3},{8,12},{9,13},{10,... | collective-permute-start | bytes 786440 | tf_op jit(solution)/shard_map/g/zg1/ppermute | solution.py:71
  82.3 0.3 cg0.1
  82.8 0.8 collective-permute-start.30
  83.6 0.8 collective-permute-start.31
  84.4 5.6 %collective-permute-done.22 = bf16[128,1024]{1,0:T(8,128)(2,1)S(1)} collective-permute-done((bf16[128,1024]{1,0:T(8,128)(2,1)S(1)}, bf16[128,1024]{1,0:T(8,128)(2,1)S(1)}, u32[]{:S(2)}, u32[]{:S(2)}) %collective-permute-start.22) | collective-permute-done | bytes 262176 | tf_op jit(solution)/shard_map/o/zo2/ppermute | solution.py:71
  90.0 0.8 add_convert_fusion.4
  90.8 0.8 fusion
  91.7 0.5 collective-permute-done.28
  92.2 5.8 %collective-permute-done.30 = bf16[128,1024]{1,0:T(8,128)(2,1)S(1)} collective-permute-done((bf16[128,1024]{1,0:T(8,128)(2,1)S(1)}, bf16[128,1024]{1,0:T(8,128)(2,1)S(1)}, u32[]{:S(2)}, u32[]{:S(2)}) %collective-permute-start.30) | collective-permute-done | bytes 262176 | tf_op jit(solution)/shard_map/g/zg2/ppermute | solution.py:71
  98.0 0.8 add_convert_fusion.2
  98.8 1.8 %collective-permute-done.31 = bf16[2,352,512]{2,1,0:T(8,128)(2,1)S(1)} collective-permute-done((bf16[2,352,512]{2,1,0:T(8,128)(2,1)S(1)}, bf16[2,352,512]{2,1,0:T(8,128)(2,1)S(1)}, u32[]{:S(2)}, u32[]{:S(2)}) %collective-permute-start.31) | collective-permute-done | bytes 720928 | tf_op jit(solution)/shard_map/di/dix/ppermute | solution.py:71
  100.6 1.1 %fusion.2 = (bf16[1,512,352]{1,2,0:T(8,128)(2,1)}, bf16[1,512,352]{1,2,0:T(8,128)(2,1)}) fusion(f32[2,352,512]{2,1,0:T(8,128)S(1)} %get-tuple-element.109, bf16[2,352,512]{2,1,0:T(8,128)(2,1)S(1)} %collective-permute-done.31), kind=kLoop, calls=%fused_computation.10 | loop fusion | flops 1081344 | bytes 2883584 | tf_op jit(solution)/shard_map/broadcast_in_dim | solution.py:557
  (37 shorter events, 0.4 us)
Async XLA Ops:
  1.3 11.4 %collective-permute-start.2 = (s32[4,128]{1,0:T(4,128)S(1)}, s32[4,128]{1,0:T(4,128)S(1)}, u32[]{:S(2)}, u32[]{:S(2)}) collective-permute-start(s32[4,128]{1,0:T(4,128)S(1)} %pad_add_fusion.1), channel_id=1, source_target_pairs={{0,12},{1,13},{2,14},{3,15},{4,8},{5,9},{6,10},{7,11},{8,4},{9,5},... | collective-permute-start | bytes 6152 | tf_op jit(solution)/shard_map/di/dik0/prep/T3/ppermute | solution.py:71
  6.4 7.9 %collective-permute-start.1 = (s32[4,128]{1,0:T(4,128)S(1)}, s32[4,128]{1,0:T(4,128)S(1)}, u32[]{:S(2)}, u32[]{:S(2)}) collective-permute-start(s32[4,128]{1,0:T(4,128)S(1)} %pad_add_fusion.1), channel_id=1, source_target_pairs={{0,8},{1,9},{2,10},{3,11},{4,12},{5,13},{6,14},{7,15},{8,0},{9,1},... | collective-permute-start | bytes 6152 | tf_op jit(solution)/shard_map/di/dik0/prep/T2/ppermute | solution.py:71
  6.4 8.0 %collective-permute-start = (s32[4,128]{1,0:T(4,128)S(1)}, s32[4,128]{1,0:T(4,128)S(1)}, u32[]{:S(2)}, u32[]{:S(2)}) collective-permute-start(s32[4,128]{1,0:T(4,128)S(1)} %pad_add_fusion.1), channel_id=1, source_target_pairs={{0,4},{1,5},{2,6},{3,7},{4,0},{5,1},{6,2},{7,3},{8,12},{9,13},{10,... | collective-permute-start | bytes 6152 | tf_op jit(solution)/shard_map/di/dik0/prep/T1/ppermute | solution.py:71
  7.0 13.2 %collective-permute-start.5 = (bf16[128,1024]{1,0:T(8,128)(2,1)}, bf16[128,1024]{1,0:T(8,128)(2,1)S(1)}, u32[]{:S(2)}, u32[]{:S(2)}) collective-permute-start(bf16[128,1024]{1,0:T(8,128)(2,1)} %refs_0_), channel_id=1, source_target_pairs={{0,4},{1,5},{2,6},{3,7},{4,0},{5,1},{6,2},{7,3},{8,12},{9,13},{10,... | collective-permute-start | bytes 786440 | tf_op jit(solution)/shard_map/di/dik0/pt1/t1/ppermute | solution.py:71
  8.4 14.1 %collective-permute-start.3 = (bf16[128,1024]{1,0:T(8,128)(2,1)}, bf16[128,1024]{1,0:T(8,128)(2,1)S(1)}, u32[]{:S(2)}, u32[]{:S(2)}) collective-permute-start(bf16[128,1024]{1,0:T(8,128)(2,1)} %refs_0_), channel_id=1, source_target_pairs={{0,8},{1,9},{2,10},{3,11},{4,12},{5,13},{6,14},{7,15},{8,0},{9,1},... | collective-permute-start | bytes 786440 | tf_op jit(solution)/shard_map/di/dik0/pt0/t2/ppermute | solution.py:71
  12.8 24.9 %collective-permute-start.9 = (bf16[3,352,512]{2,1,0:T(8,128)(2,1)S(1)}, bf16[3,352,512]{2,1,0:T(8,128)(2,1)S(1)}, u32[]{:S(2)}, u32[]{:S(2)}) collective-permute-start(bf16[3,352,512]{2,1,0:T(8,128)(2,1)S(1)} %pad_maximum_fusion.refs_4_.refs_2_), channel_id=1, source_target_pairs={{0,1},{1,0},{2,3},{3,2},{4,5},{5,4},{6,7},{7,6},{8,9},{9,8},{10,11... | collective-permute-start | bytes 3244040 | tf_op jit(solution)/shard_map/di/dik0/bwd0/wx/ppermute | solution.py:71
  14.3 30.0 %collective-permute-start.8 = (bf16[3,352,512]{2,1,0:T(8,128)(2,1)S(1)}, bf16[3,352,512]{2,1,0:T(8,128)(2,1)S(1)}, u32[]{:S(2)}, u32[]{:S(2)}) collective-permute-start(bf16[3,352,512]{2,1,0:T(8,128)(2,1)S(1)} %pad_maximum_fusion.refs_4_.refs_2_), channel_id=1, source_target_pairs={{0,16},{16,0},{1,17},{17,1},{2,18},{18,2},{3,19},{19,3},{4,20},{20... | collective-permute-start | bytes 3244040 | tf_op jit(solution)/shard_map/di/dik0/bwd0/ws1/ppermute | solution.py:328
  14.4 8.4 %copy-start.1 = (bf16[128,1024]{1,0:T(8,128)(2,1)S(1)}, bf16[128,1024]{1,0:T(8,128)(2,1)}, u32[]{:S(2)}) copy-start(bf16[128,1024]{1,0:T(8,128)(2,1)} %refs_0_.1) | copy-start | bytes 786436
  14.4 11.0 %copy-start = (bf16[128,1024]{1,0:T(8,128)(2,1)S(1)}, bf16[128,1024]{1,0:T(8,128)(2,1)}, u32[]{:S(2)}) copy-start(bf16[128,1024]{1,0:T(8,128)(2,1)} %refs_0_) | copy-start | bytes 786436
  22.5 9.7 %collective-permute-start.6 = (bf16[128,1024]{1,0:T(8,128)(2,1)S(1)}, bf16[128,1024]{1,0:T(8,128)(2,1)S(1)}, u32[]{:S(2)}, u32[]{:S(2)}) collective-permute-start(bf16[128,1024]{1,0:T(8,128)(2,1)S(1)} %collective-permute-done.3.refs_1_), channel_id=1, source_target_pairs={{0,4},{1,5},{2,6},{3,7},{4,0},{5,1},{6,2},{7,3},{8,12},{9,13},{10,... | collective-permute-start | bytes 786440 | tf_op jit(solution)/shard_map/di/dik0/pt1/t3/ppermute | solution.py:71
  22.8 12.9 %collective-permute-start.11 = (bf16[128,1024]{1,0:T(8,128)(2,1)S(1)}, bf16[128,1024]{1,0:T(8,128)(2,1)S(1)}, u32[]{:S(2)}, u32[]{:S(2)}) collective-permute-start(bf16[128,1024]{1,0:T(8,128)(2,1)S(1)} %copy-done.1), channel_id=1, source_target_pairs={{0,8},{1,9},{2,10},{3,11},{4,12},{5,13},{6,14},{7,15},{8,0},{9,1},... | collective-permute-start | bytes 786440 | tf_op jit(solution)/shard_map/di/dik0/bwd0/pc0/c2/ppermute | solution.py:71
  25.8 9.9 %collective-permute-start.4 = (bf16[128,1152]{1,0:T(8,128)(2,1)S(1)}, bf16[128,1152]{1,0:T(8,128)(2,1)S(1)}, u32[]{:S(2)}, u32[]{:S(2)}) collective-permute-start(bf16[128,1152]{1,0:T(8,128)(2,1)S(1)} %get-tuple-element.70), channel_id=1, source_target_pairs={{0,2},{1,3},{2,0},{3,1},{4,6},{5,7},{6,4},{7,5},{8,10},{9,11},{10,... | collective-permute-start | bytes 884744 | tf_op jit(solution)/shard_map/di/dik0/yt0/ppermute | solution.py:71
  32.5 11.8 %collective-permute-start.7 = (bf16[128,1152]{1,0:T(8,128)(2,1)S(1)}, bf16[128,1152]{1,0:T(8,128)(2,1)S(1)}, u32[]{:S(2)}, u32[]{:S(2)}) collective-permute-start(bf16[128,1152]{1,0:T(8,128)(2,1)S(1)} %get-tuple-element.73), channel_id=1, source_target_pairs={{0,2},{1,3},{2,0},{3,1},{4,6},{5,7},{6,4},{7,5},{8,10},{9,11},{10,... | collective-permute-start | bytes 884744 | tf_op jit(solution)/shard_map/di/dik0/yt1/ppermute | solution.py:71
  35.7 6.7 %collective-permute-start.18 = (bf16[128,1024]{1,0:T(8,128)(2,1)S(1)}, bf16[128,1024]{1,0:T(8,128)(2,1)S(1)}, u32[]{:S(2)}, u32[]{:S(2)}) collective-permute-start(bf16[128,1024]{1,0:T(8,128)(2,1)S(1)} %copy-done.1), channel_id=1, source_target_pairs={{0,4},{1,5},{2,6},{3,7},{4,0},{5,1},{6,2},{7,3},{8,12},{9,13},{10,... | collective-permute-start | bytes 786440 | tf_op jit(solution)/shard_map/di/dik0/bwd1/pc1/c1/ppermute | solution.py:71
  36.0 8.4 %copy-start.2 = (s32[2]{0:T(128)S(1)}, s32[2]{0:T(128)}, u32[]{:S(2)}) copy-start(s32[2]{0:T(128)} %key_ref.1) | copy-start | bytes 28
  36.0 12.6 %collective-permute-start.13 = (bf16[128,1024]{1,0:T(8,128)(2,1)S(1)}, bf16[128,1024]{1,0:T(8,128)(2,1)S(1)}, u32[]{:S(2)}, u32[]{:S(2)}) collective-permute-start(bf16[128,1024]{1,0:T(8,128)(2,1)S(1)} %get-tuple-element.80), channel_id=1, source_target_pairs={{0,2},{1,3},{2,0},{3,1},{4,6},{5,7},{6,4},{7,5},{8,10},{9,11},{10,... | collective-permute-start | bytes 786440 | tf_op jit(solution)/shard_map/di/dik0/bwd0/yc0/ppermute | solution.py:71
  37.6 6.8 %collective-permute-start.10 = (bf16[3,352,512]{2,1,0:T(8,128)(2,1)S(1)}, bf16[3,352,512]{2,1,0:T(8,128)(2,1)S(1)}, u32[]{:S(2)}, u32[]{:S(2)}) collective-permute-start(bf16[3,352,512]{2,1,0:T(8,128)(2,1)S(1)} %collective-permute-done.9.refs_6_.refs_4_), channel_id=1, source_target_pairs={{0,16},{16,0},{1,17},{17,1},{2,18},{18,2},{3,19},{19,3},{4,20},{20... | collective-permute-start | bytes 3244040 | tf_op jit(solution)/shard_map/di/dik0/bwd0/wp1/ppermute | solution.py:328
  42.6 13.9 %collective-permute-start.19 = (bf16[64,1024]{1,0:T(8,128)(2,1)S(1)}, bf16[64,1024]{1,0:T(8,128)(2,1)S(1)}, u32[]{:S(2)}, u32[]{:S(2)}) collective-permute-start(bf16[64,1024]{1,0:T(8,128)(2,1)S(1)} %get-tuple-element.93), channel_id=1, source_target_pairs={{0,2},{1,3},{2,0},{3,1},{4,6},{5,7},{6,4},{7,5},{8,10},{9,11},{10,... | collective-permute-start | bytes 393224 | tf_op jit(solution)/shard_map/di/dik0/bwd1/yc1/ppermute | solution.py:71
  44.4 6.4 %collective-permute-start.12 = (bf16[128,1024]{1,0:T(8,128)(2,1)S(1)}, bf16[128,1024]{1,0:T(8,128)(2,1)S(1)}, u32[]{:S(2)}, u32[]{:S(2)}) collective-permute-start(bf16[128,1024]{1,0:T(8,128)(2,1)S(1)} %collective-permute-done.11.refs_1_), channel_id=1, source_target_pairs={{0,4},{1,5},{2,6},{3,7},{4,0},{5,1},{6,2},{7,3},{8,12},{9,13},{10,... | collective-permute-start | bytes 786440 | tf_op jit(solution)/shard_map/di/dik0/bwd1/pc2/c3/ppermute | solution.py:71
  51.0 5.5 %collective-permute-start.14 = (bf16[64,1024]{1,0:T(8,128)(2,1)S(1)}, bf16[64,1024]{1,0:T(8,128)(2,1)S(1)}, u32[]{:S(2)}, u32[]{:S(2)}) collective-permute-start(bf16[64,1024]{1,0:T(8,128)(2,1)S(1)} %get-tuple-element.83), channel_id=1, source_target_pairs={{0,2},{1,3},{2,0},{3,1},{4,6},{5,7},{6,4},{7,5},{8,10},{9,11},{10,... | collective-permute-start | bytes 393224 | tf_op jit(solution)/shard_map/di/dik0/bwd1/yc2/ppermute | solution.py:71
  51.4 10.3 %collective-permute-start.16 = (bf16[64,1024]{1,0:T(8,128)(2,1)S(1)}, bf16[64,1024]{1,0:T(8,128)(2,1)S(1)}, u32[]{:S(2)}, u32[]{:S(2)}) collective-permute-start(bf16[64,1024]{1,0:T(8,128)(2,1)S(1)} %get-tuple-element.87), channel_id=1, source_target_pairs={{0,2},{1,3},{2,0},{3,1},{4,6},{5,7},{6,4},{7,5},{8,10},{9,11},{10,... | collective-permute-start | bytes 393224 | tf_op jit(solution)/shard_map/di/dik0/dis1/yo1/ppermute | solution.py:71
  53.1 8.3 %collective-permute-start.20 = (bf16[64,1024]{1,0:T(8,128)(2,1)S(1)}, bf16[64,1024]{1,0:T(8,128)(2,1)S(1)}, u32[]{:S(2)}, u32[]{:S(2)}) collective-permute-start(bf16[64,1024]{1,0:T(8,128)(2,1)S(1)} %get-tuple-element.98), channel_id=1, source_target_pairs={{0,2},{1,3},{2,0},{3,1},{4,6},{5,7},{6,4},{7,5},{8,10},{9,11},{10,... | collective-permute-start | bytes 393224 | tf_op jit(solution)/shard_map/o/zo2/zo3/co2/yo2/ppermute | solution.py:71
  59.6 7.5 %collective-permute-start.24 = (bf16[64,1024]{1,0:T(8,128)(2,1)S(1)}, bf16[64,1024]{1,0:T(8,128)(2,1)S(1)}, u32[]{:S(2)}, u32[]{:S(2)}) collective-permute-start(bf16[64,1024]{1,0:T(8,128)(2,1)S(1)} %get-tuple-element.112), channel_id=1, source_target_pairs={{0,2},{1,3},{2,0},{3,1},{4,6},{5,7},{6,4},{7,5},{8,10},{9,11},{10,... | collective-permute-start | bytes 393224 | tf_op jit(solution)/shard_map/g/cg0/yg2/ppermute | solution.py:71
  61.6 9.5 %collective-permute-start.21 = (bf16[128,1024]{1,0:T(8,128)(2,1)S(1)}, bf16[128,1024]{1,0:T(8,128)(2,1)S(1)}, u32[]{:S(2)}, u32[]{:S(2)}) collective-permute-start(bf16[128,1024]{1,0:T(8,128)(2,1)S(1)} %co2.1), channel_id=1, source_target_pairs={{0,4},{1,5},{2,6},{3,7},{4,0},{5,1},{6,2},{7,3},{8,12},{9,13},{10,... | collective-permute-start | bytes 786440 | tf_op jit(solution)/shard_map/o/zo2/zo3/ppermute | solution.py:71
  61.9 21.7 %collective-permute-start.17 = (bf16[128,1024]{1,0:T(8,128)(2,1)S(1)}, bf16[128,1024]{1,0:T(8,128)(2,1)S(1)}, u32[]{:S(2)}, u32[]{:S(2)}) collective-permute-start(bf16[128,1024]{1,0:T(8,128)(2,1)S(1)} %co1.1), channel_id=1, source_target_pairs={{0,4},{1,5},{2,6},{3,7},{4,0},{5,1},{6,2},{7,3},{8,12},{9,13},{10,... | collective-permute-start | bytes 786440 | tf_op jit(solution)/shard_map/o/zo1/ppermute | solution.py:71
  64.0 6.4 %collective-permute-start.15 = (bf16[128,1024]{1,0:T(8,128)(2,1)S(1)}, bf16[128,1024]{1,0:T(8,128)(2,1)S(1)}, u32[]{:S(2)}, u32[]{:S(2)}) collective-permute-start(bf16[128,1024]{1,0:T(8,128)(2,1)S(1)} %get-tuple-element.84), channel_id=1, source_target_pairs={{0,2},{1,3},{2,0},{3,1},{4,6},{5,7},{6,4},{7,5},{8,10},{9,11},{10,... | collective-permute-start | bytes 786440 | tf_op jit(solution)/shard_map/o/co0/yo0/ppermute | solution.py:71
  65.5 5.8 %collective-permute-start.26 = (bf16[1,704,512]{2,1,0:T(8,128)(2,1)S(1)}, bf16[1,704,512]{2,1,0:T(8,128)(2,1)S(1)}, u32[]{:S(2)}, u32[]{:S(2)}) collective-permute-start(bf16[1,704,512]{2,1,0:T(8,128)(2,1)S(1)} %ddk1.1), channel_id=1, source_target_pairs={{0,16},{16,0},{1,17},{17,1},{2,18},{18,2},{3,19},{19,3},{4,20},{20... | collective-permute-start | bytes 2162696 | tf_op jit(solution)/shard_map/dd/ddk0/dds1/ppermute | solution.py:328
  67.0 10.6 %collective-permute-start.23 = (bf16[2,704,512]{2,1,0:T(8,128)(2,1)S(1)}, bf16[2,704,512]{2,1,0:T(8,128)(2,1)S(1)}, u32[]{:S(2)}, u32[]{:S(2)}) collective-permute-start(bf16[2,704,512]{2,1,0:T(8,128)(2,1)S(1)} %dik1.1), channel_id=1, source_target_pairs={{0,16},{16,0},{1,17},{17,1},{2,18},{18,2},{3,19},{19,3},{4,20},{20... | collective-permute-start | bytes 4325384 | tf_op jit(solution)/shard_map/di/dik0/dis1/ppermute | solution.py:328
  70.4 6.4 %collective-permute-start.27 = (bf16[64,1024]{1,0:T(8,128)(2,1)S(1)}, bf16[64,1024]{1,0:T(8,128)(2,1)S(1)}, u32[]{:S(2)}, u32[]{:S(2)}) collective-permute-start(bf16[64,1024]{1,0:T(8,128)(2,1)S(1)} %get-tuple-element.119), channel_id=1, source_target_pairs={{0,2},{1,3},{2,0},{3,1},{4,6},{5,7},{6,4},{7,5},{8,10},{9,11},{10,... | collective-permute-start | bytes 393224 | tf_op jit(solution)/shard_map/g/zg1/cg1/yg1/ppermute | solution.py:71
  71.1 11.6 %collective-permute-start.29 = (bf16[128,1024]{1,0:T(8,128)(2,1)S(1)}, bf16[128,1024]{1,0:T(8,128)(2,1)S(1)}, u32[]{:S(2)}, u32[]{:S(2)}) collective-permute-start(bf16[128,1024]{1,0:T(8,128)(2,1)S(1)} %cg2.1), channel_id=1, source_target_pairs={{0,4},{1,5},{2,6},{3,7},{4,0},{5,1},{6,2},{7,3},{8,12},{9,13},{10,... | collective-permute-start | bytes 786440 | tf_op jit(solution)/shard_map/g/zg2/zg3/ppermute | solution.py:71
  71.3 9.4 %collective-permute-start.25 = (bf16[128,1024]{1,0:T(8,128)(2,1)S(1)}, bf16[128,1024]{1,0:T(8,128)(2,1)S(1)}, u32[]{:S(2)}, u32[]{:S(2)}) collective-permute-start(bf16[128,1024]{1,0:T(8,128)(2,1)S(1)} %get-tuple-element.113), channel_id=1, source_target_pairs={{0,2},{1,3},{2,0},{3,1},{4,6},{5,7},{6,4},{7,5},{8,10},{9,11},{10,... | collective-permute-start | bytes 786440 | tf_op jit(solution)/shard_map/g/cg0/yg0/ppermute | solution.py:71
  76.8 13.2 %collective-permute-start.22 = (bf16[128,1024]{1,0:T(8,128)(2,1)S(1)}, bf16[128,1024]{1,0:T(8,128)(2,1)S(1)}, u32[]{:S(2)}, u32[]{:S(2)}) collective-permute-start(bf16[128,1024]{1,0:T(8,128)(2,1)S(1)} %add_convert_fusion.5), channel_id=1, source_target_pairs={{0,8},{1,9},{2,10},{3,11},{4,12},{5,13},{6,14},{7,15},{8,0},{9,1},... | collective-permute-start | bytes 786440 | tf_op jit(solution)/shard_map/o/zo2/ppermute | solution.py:71
  77.6 13.2 %collective-permute-start.32 = (bf16[1,352,512]{2,1,0:T(8,128)(2,1)S(1)}, bf16[1,352,512]{2,1,0:T(8,128)(2,1)S(1)}, u32[]{:S(2)}, u32[]{:S(2)}) collective-permute-start(bf16[1,352,512]{2,1,0:T(8,128)(2,1)S(1)} %get-tuple-element.125), channel_id=1, source_target_pairs={{0,1},{1,0},{2,3},{3,2},{4,5},{5,4},{6,7},{7,6},{8,9},{9,8},{10,11... | collective-permute-start | bytes 1081352 | tf_op jit(solution)/shard_map/dd/ddx/ppermute | solution.py:71
  80.7 11.5 %collective-permute-start.28 = (bf16[128,1024]{1,0:T(8,128)(2,1)S(1)}, bf16[128,1024]{1,0:T(8,128)(2,1)S(1)}, u32[]{:S(2)}, u32[]{:S(2)}) collective-permute-start(bf16[128,1024]{1,0:T(8,128)(2,1)S(1)} %cg1.1), channel_id=1, source_target_pairs={{0,4},{1,5},{2,6},{3,7},{4,0},{5,1},{6,2},{7,3},{8,12},{9,13},{10,... | collective-permute-start | bytes 786440 | tf_op jit(solution)/shard_map/g/zg1/ppermute | solution.py:71
  82.8 15.2 %collective-permute-start.30 = (bf16[128,1024]{1,0:T(8,128)(2,1)S(1)}, bf16[128,1024]{1,0:T(8,128)(2,1)S(1)}, u32[]{:S(2)}, u32[]{:S(2)}) collective-permute-start(bf16[128,1024]{1,0:T(8,128)(2,1)S(1)} %add_convert_fusion.3), channel_id=1, source_target_pairs={{0,8},{1,9},{2,10},{3,11},{4,12},{5,13},{6,14},{7,15},{8,0},{9,1},... | collective-permute-start | bytes 786440 | tf_op jit(solution)/shard_map/g/zg2/ppermute | solution.py:71
  83.6 17.0 %collective-permute-start.31 = (bf16[2,352,512]{2,1,0:T(8,128)(2,1)S(1)}, bf16[2,352,512]{2,1,0:T(8,128)(2,1)S(1)}, u32[]{:S(2)}, u32[]{:S(2)}) collective-permute-start(bf16[2,352,512]{2,1,0:T(8,128)(2,1)S(1)} %get-tuple-element.123), channel_id=1, source_target_pairs={{0,1},{1,0},{2,3},{3,2},{4,5},{5,4},{6,7},{7,6},{8,9},{9,8},{10,11... | collective-permute-start | bytes 2162696 | tf_op jit(solution)/shard_map/di/dix/ppermute | solution.py:71

commit v8 on v7

--- a/solution.py
+++ b/solution.py
@@ -17,7 +17,7 @@
 id_lanes = 128
 costs = {
     "prep": 10,
-    "pt0": 20,
+    "pt0": 5,
     "pt1": 20,
     "pc0": 20,
     "pc1": 20,
@@ -47,8 +47,8 @@
     "yo0": ("yc2",),
     "co2": ("bwd1",),
     "yg1": ("yg2",),
-    "yg0": ("yg2", "yo0",),
-    "g": ("dd", "dix",),
+    "yg0": ("yg2", "yo0", "dis1",),
+    "g": ("dix",),
     "cg1": ("ddk0", "co0",),
     "cg0": ("dik0",),
     "dd": ("di",),
@@ -56,6 +56,7 @@
     "zg2": ("dik0",),
     "pt0": ("prep",),
     "dis1": ("ddk1",),
+    "pc1": ("wp1",),
 }
 
 

time: 102 us -> 99.6 us (0.976)
  waiting for transfers between devices: 39.5 us -> 32.7 us
  starting transfers between devices: 36 us -> 40.6 us
    ppermute x29, waiting for transfers between devices: 39.5 us -> 32.7 us  [flipped(): lax.ppermute(values, axis, [(i, i ^ mask) for i in range(lax.axis_size(ax...]
    ppermute x29, starting transfers between devices: 35.4 us -> 40 us  [flipped(): lax.ppermute(values, axis, [(i, i ^ mask) for i in range(lax.axis_size(ax...]
  transfers between devices with their start and end apart: 33 -> 33, of which waited for: 12 -> 11; matrix products, arithmetic and copies ran while one was open for 4% -> 4% of each run, Pallas kernels for 19% -> 19%
where the time goes in v8:
time: 99.6 us; the launch traced here: 99.4 us
  starting transfers between devices  40.6 us (41%)
  waiting for transfers between devices  32.7 us (33%)
  Pallas kernels  19.3 us (19%)
  other arithmetic  5.72 us (6%)
    ppermute x29, starting transfers between devices, flipped(): lax.ppermute(values, axis, [(i, i ^ mask) for i in range(lax.axis_size(ax...  40 us
    ppermute x29, waiting for transfers between devices, flipped(): lax.ppermute(values, axis, [(i, i ^ mask) for i in range(lax.axis_size(ax...  32.7 us
    pallas_call x2, Pallas kernels, backward(): called(functools.partial(backward_kernel, seq_count, len(cot_parts), len(...  6.13 us
    pallas_call x4, Pallas kernels, weight_kernel(): called(functools.partial(weight_grad_kernel, len(row_parts), seq_count, s...  5.18 us
    pallas_call x1, Pallas kernels, forward(): called(functools.partial(forward_kernel, seq_count, plane_experts, capaci...  4.25 us
  transfers between devices with their start and end apart: 33, of which 11 were waited for; matrix products, arithmetic and copies ran while one was open for 4% of the time, Pallas kernels for 19%

profile of v8, /device:TPU:0, one launch (start us, length us, event | category | flops | bytes accessed | tf_op | source)
XLA Modules:
  0.0 99.4 jit_solution(5171168701194052446)
XLA Ops:
  0.6 0.7 pad_add_fusion.1
  1.3 5.0 %collective-permute-start.2 = (s32[4,128]{1,0:T(4,128)S(1)}, s32[4,128]{1,0:T(4,128)S(1)}, u32[]{:S(2)}, u32[]{:S(2)}) collective-permute-start(s32[4,128]{1,0:T(4,128)S(1)} %pad_add_fusion.1), channel_id=1, source_target_pairs={{0,12},{1,13},{2,14},{3,15},{4,8},{5,9},{6,10},{7,11},{8,4},{9,5},... | collective-permute-start | bytes 6152 | tf_op jit(solution)/shard_map/di/dik0/prep/T3/ppermute | solution.py:72
  6.4 0.6 collective-permute-start
  7.0 1.4 %collective-permute-start.5 = (bf16[128,1024]{1,0:T(8,128)(2,1)}, bf16[128,1024]{1,0:T(8,128)(2,1)S(1)}, u32[]{:S(2)}, u32[]{:S(2)}) collective-permute-start(bf16[128,1024]{1,0:T(8,128)(2,1)} %refs_0_), channel_id=1, source_target_pairs={{0,4},{1,5},{2,6},{3,7},{4,0},{5,1},{6,2},{7,3},{8,12},{9,13},{10,... | collective-permute-start | bytes 786440 | tf_op jit(solution)/shard_map/di/dik0/pt1/t1/ppermute | solution.py:72
  8.4 2.9 %collective-permute-start.3 = (bf16[128,1024]{1,0:T(8,128)(2,1)}, bf16[128,1024]{1,0:T(8,128)(2,1)S(1)}, u32[]{:S(2)}, u32[]{:S(2)}) collective-permute-start(bf16[128,1024]{1,0:T(8,128)(2,1)} %refs_0_), channel_id=1, source_target_pairs={{0,8},{1,9},{2,10},{3,11},{4,12},{5,13},{6,14},{7,15},{8,0},{9,1},... | collective-permute-start | bytes 786440 | tf_op jit(solution)/shard_map/di/dik0/pt0/t2/ppermute | solution.py:72
  11.3 1.3 %pad_maximum_fusion.refs_4_.refs_2_ = bf16[3,352,512]{2,1,0:T(8,128)(2,1)S(1)} fusion(bf16[1,352,512]{2,1,0:T(8,128)(2,1)} %param.15, bf16[1,352,512]{2,1,0:T(8,128)(2,1)} %bitcast.48, bf16[1,352,512]{2,1,0:T(8,128)(2,1)} %bitcast.49), kind=kLoop, calls=%fused_computation | loop fusion | flops 1081344 | bytes 2162688 | tf_op jit(solution)/shard_map/stack | solution.py:352
  12.7 0.1 stack.55.place_ref
  12.8 1.6 %collective-permute-start.9 = (bf16[3,352,512]{2,1,0:T(8,128)(2,1)S(1)}, bf16[3,352,512]{2,1,0:T(8,128)(2,1)S(1)}, u32[]{:S(2)}, u32[]{:S(2)}) collective-permute-start(bf16[3,352,512]{2,1,0:T(8,128)(2,1)S(1)} %pad_maximum_fusion.refs_4_.refs_2_), channel_id=1, source_target_pairs={{0,1},{1,0},{2,3},{3,2},{4,5},{5,4},{6,7},{7,6},{8,9},{9,8},{10,11... | collective-permute-start | bytes 3244040 | tf_op jit(solution)/shard_map/di/dik0/bwd0/wx/ppermute | solution.py:72
  14.4 0.7 prep.1
  15.1 5.2 %collective-permute-done.5.refs_0_ = bf16[128,1024]{1,0:T(8,128)(2,1)S(1)} collective-permute-done((bf16[128,1024]{1,0:T(8,128)(2,1)}, bf16[128,1024]{1,0:T(8,128)(2,1)S(1)}, u32[]{:S(2)}, u32[]{:S(2)}) %collective-permute-start.5) | collective-permute-done | bytes 262176 | tf_op jit(solution)/shard_map/di/dik0/pt1/t1/ppermute | solution.py:72
  20.2 2.3 %collective-permute-done.3.refs_1_ = bf16[128,1024]{1,0:T(8,128)(2,1)S(1)} collective-permute-done((bf16[128,1024]{1,0:T(8,128)(2,1)}, bf16[128,1024]{1,0:T(8,128)(2,1)S(1)}, u32[]{:S(2)}, u32[]{:S(2)}) %collective-permute-start.3) | collective-permute-done | bytes 262176 | tf_op jit(solution)/shard_map/di/dik0/pt0/t2/ppermute | solution.py:72
  22.5 0.3 collective-permute-start.6
  22.8 2.6 %collective-permute-start.11 = (bf16[128,1024]{1,0:T(8,128)(2,1)S(1)}, bf16[128,1024]{1,0:T(8,128)(2,1)S(1)}, u32[]{:S(2)}, u32[]{:S(2)}) collective-permute-start(bf16[128,1024]{1,0:T(8,128)(2,1)S(1)} %copy-done.1), channel_id=1, source_target_pairs={{0,8},{1,9},{2,10},{3,11},{4,12},{5,13},{6,14},{7,15},{8,0},{9,1},... | collective-permute-start | bytes 786440 | tf_op jit(solution)/shard_map/di/dik0/bwd0/pc0/c2/ppermute | solution.py:72
  25.4 0.3 pt0.1
  25.8 1.6 %collective-permute-start.4 = (bf16[128,1152]{1,0:T(8,128)(2,1)S(1)}, bf16[128,1152]{1,0:T(8,128)(2,1)S(1)}, u32[]{:S(2)}, u32[]{:S(2)}) collective-permute-start(bf16[128,1152]{1,0:T(8,128)(2,1)S(1)} %get-tuple-element.71), channel_id=1, source_target_pairs={{0,2},{1,3},{2,0},{3,1},{4,6},{5,7},{6,4},{7,5},{8,10},{9,11},{10,... | collective-permute-start | bytes 884744 | tf_op jit(solution)/shard_map/di/dik0/yt0/ppermute | solution.py:72
  27.3 4.8 %collective-permute-done.6.refs_1_ = bf16[128,1024]{1,0:T(8,128)(2,1)S(1)} collective-permute-done((bf16[128,1024]{1,0:T(8,128)(2,1)S(1)}, bf16[128,1024]{1,0:T(8,128)(2,1)S(1)}, u32[]{:S(2)}, u32[]{:S(2)}) %collective-permute-start.6) | collective-permute-done | bytes 262176 | tf_op jit(solution)/shard_map/di/dik0/pt1/t3/ppermute | solution.py:72
  32.2 0.3 pt1.1
  32.5 1.6 %collective-permute-start.7 = (bf16[128,1152]{1,0:T(8,128)(2,1)S(1)}, bf16[128,1152]{1,0:T(8,128)(2,1)S(1)}, u32[]{:S(2)}, u32[]{:S(2)}) collective-permute-start(bf16[128,1152]{1,0:T(8,128)(2,1)S(1)} %get-tuple-element.74), channel_id=1, source_target_pairs={{0,2},{1,3},{2,0},{3,1},{4,6},{5,7},{6,4},{7,5},{8,10},{9,11},{10,... | collective-permute-start | bytes 884744 | tf_op jit(solution)/shard_map/di/dik0/yt1/ppermute | solution.py:72
  34.1 1.6 %collective-permute-done.11.refs_1_ = bf16[128,1024]{1,0:T(8,128)(2,1)S(1)} collective-permute-done((bf16[128,1024]{1,0:T(8,128)(2,1)S(1)}, bf16[128,1024]{1,0:T(8,128)(2,1)S(1)}, u32[]{:S(2)}, u32[]{:S(2)}) %collective-permute-start.11) | collective-permute-done | bytes 262176 | tf_op jit(solution)/shard_map/di/dik0/bwd0/pc0/c2/ppermute | solution.py:72
  35.7 1.3 %collective-permute-done.9.refs_6_.refs_4_ = bf16[3,352,512]{2,1,0:T(8,128)(2,1)S(1)} collective-permute-done((bf16[3,352,512]{2,1,0:T(8,128)(2,1)S(1)}, bf16[3,352,512]{2,1,0:T(8,128)(2,1)S(1)}, u32[]{:S(2)}, u32[]{:S(2)}) %collective-permute-start.9) | collective-permute-done | bytes 1081376 | tf_op jit(solution)/shard_map/di/dik0/bwd0/wx/ppermute | solution.py:72
  37.0 0.3 pc0.1
  37.4 1.6 %collective-permute-start.13 = (bf16[128,1024]{1,0:T(8,128)(2,1)S(1)}, bf16[128,1024]{1,0:T(8,128)(2,1)S(1)}, u32[]{:S(2)}, u32[]{:S(2)}) collective-permute-start(bf16[128,1024]{1,0:T(8,128)(2,1)S(1)} %get-tuple-element.81), channel_id=1, source_target_pairs={{0,2},{1,3},{2,0},{3,1},{4,6},{5,7},{6,4},{7,5},{8,10},{9,11},{10,... | collective-permute-start | bytes 786440 | tf_op jit(solution)/shard_map/di/dik0/bwd0/yc0/ppermute | solution.py:72
  39.0 3.4 %collective-permute-done.18.refs_0_ = bf16[128,1024]{1,0:T(8,128)(2,1)S(1)} collective-permute-done((bf16[128,1024]{1,0:T(8,128)(2,1)S(1)}, bf16[128,1024]{1,0:T(8,128)(2,1)S(1)}, u32[]{:S(2)}, u32[]{:S(2)}) %collective-permute-start.18) | collective-permute-done | bytes 262176 | tf_op jit(solution)/shard_map/di/dik0/bwd1/pc1/c1/ppermute | solution.py:72
  42.3 0.2 pc1.1
  42.5 2.6 %collective-permute-start.19 = (bf16[64,1024]{1,0:T(8,128)(2,1)S(1)}, bf16[64,1024]{1,0:T(8,128)(2,1)S(1)}, u32[]{:S(2)}, u32[]{:S(2)}) collective-permute-start(bf16[64,1024]{1,0:T(8,128)(2,1)S(1)} %get-tuple-element.95), channel_id=1, source_target_pairs={{0,2},{1,3},{2,0},{3,1},{4,6},{5,7},{6,4},{7,5},{8,10},{9,11},{10,... | collective-permute-start | bytes 393224 | tf_op jit(solution)/shard_map/di/dik0/bwd1/yc1/ppermute | solution.py:72
  45.1 4.2 %fwd.1 = (bf16[128,1024]{1,0:T(8,128)(2,1)S(1)}, bf16[128,1024]{1,0:T(8,128)(2,1)S(1)}, bf16[64,1024]{1,0:T(8,128)(2,1)S(1)}, bf16[64,1024]{1,0:T(8,128)(2,1)S(1...) custom-call(s32[8]{0:T(128)S(1)} %stack.55.place_ref, ...), custom_call_target="tpu_custom_call" | custom-call | flops 20000000000 | bytes 60000000 | tf_op jit(solution)/shard_map/di/dik0/bwd0/fwd/pallas_call | solution.py:434
  49.4 0.2 pc2.1
  49.6 1.9 %collective-permute-start.14 = (bf16[64,1024]{1,0:T(8,128)(2,1)S(1)}, bf16[64,1024]{1,0:T(8,128)(2,1)S(1)}, u32[]{:S(2)}, u32[]{:S(2)}) collective-permute-start(bf16[64,1024]{1,0:T(8,128)(2,1)S(1)} %get-tuple-element.84), channel_id=1, source_target_pairs={{0,2},{1,3},{2,0},{3,1},{4,6},{5,7},{6,4},{7,5},{8,10},{9,11},{10,... | collective-permute-start | bytes 393224 | tf_op jit(solution)/shard_map/di/dik0/bwd1/yc2/ppermute | solution.py:72
  51.5 0.2 collective-permute-start.16
  51.7 1.8 %collective-permute-start.20 = (bf16[64,1024]{1,0:T(8,128)(2,1)S(1)}, bf16[64,1024]{1,0:T(8,128)(2,1)S(1)}, u32[]{:S(2)}, u32[]{:S(2)}) collective-permute-start(bf16[64,1024]{1,0:T(8,128)(2,1)S(1)} %get-tuple-element.100), channel_id=1, source_target_pairs={{0,2},{1,3},{2,0},{3,1},{4,6},{5,7},{6,4},{7,5},{8,10},{9,11},{10,... | collective-permute-start | bytes 393224 | tf_op jit(solution)/shard_map/o/zo2/zo3/co2/yo2/ppermute | solution.py:72
  53.5 3.1 %bwd0.1 = (bf16[128,1024]{1,0:T(8,128)(2,1)S(1)}, bf16[128,1024]{1,0:T(8,128)(2,1)S(1)}, bf16[256,704]{1,0:T(8,128)(2,1)S(1)}, bf16[256,704]{1,0:T(8,128)(2,1)S(1)}) custom-call(s32[8]{0:T(128)S(1)} %stack.55.place_ref, bf16[128,1024]{1,0:T(8,128)(2,1)S(1)} %get-tuple-element.101.refs_0_, bf16[128,1024]{1,0:T(8,128)(2,1)S(1)} %collective-permute-done.13.refs_1_, ...), custom_call_target="tpu_custom_call" | custom-call | flops 20000000000 | bytes 60000000 | tf_op jit(solution)/shard_map/di/dik0/bwd0/pallas_call | solution.py:451
  56.6 3.1 %bwd1.1 = (bf16[64,1024]{1,0:T(8,128)(2,1)S(1)}, bf16[64,1024]{1,0:T(8,128)(2,1)S(1)}, bf16[64,1024]{1,0:T(8,128)(2,1)S(1)}, bf16[64,1024]{1,0:T(8,128)(2,1)S(1)...) custom-call(s32[8]{0:T(128)S(1)} %stack.55.place_ref, ...), custom_call_target="tpu_custom_call" | custom-call | flops 20000000000 | bytes 60000000 | tf_op jit(solution)/shard_map/di/dik0/bwd1/pallas_call | solution.py:451
  59.7 0.3 collective-permute-start.24
  60.0 0.3 co2.1
  60.3 2.1 %collective-permute-start.21 = (bf16[128,1024]{1,0:T(8,128)(2,1)S(1)}, bf16[128,1024]{1,0:T(8,128)(2,1)S(1)}, u32[]{:S(2)}, u32[]{:S(2)}) collective-permute-start(bf16[128,1024]{1,0:T(8,128)(2,1)S(1)} %co2.1), channel_id=1, source_target_pairs={{0,4},{1,5},{2,6},{3,7},{4,0},{5,1},{6,2},{7,3},{8,12},{9,13},{10,... | collective-permute-start | bytes 786440 | tf_op jit(solution)/shard_map/o/zo2/zo3/ppermute | solution.py:72
  62.3 0.2 co1.1
  62.6 0.1 collective-permute-start.17
  62.7 1.8 %collective-permute-start.15 = (bf16[128,1024]{1,0:T(8,128)(2,1)S(1)}, bf16[128,1024]{1,0:T(8,128)(2,1)S(1)}, u32[]{:S(2)}, u32[]{:S(2)}) collective-permute-start(bf16[128,1024]{1,0:T(8,128)(2,1)S(1)} %get-tuple-element.85), channel_id=1, source_target_pairs={{0,2},{1,3},{2,0},{3,1},{4,6},{5,7},{6,4},{7,5},{8,10},{9,11},{10,... | collective-permute-start | bytes 786440 | tf_op jit(solution)/shard_map/o/co0/yo0/ppermute | solution.py:72
  64.5 1.1 %ddk1.1 = bf16[1,704,512]{2,1,0:T(8,128)(2,1)S(1)} custom-call(s32[8]{0:T(128)S(1)} %stack.55.place_ref, bf16[128,1024]{1,0:T(8,128)(2,1)S(1)} %get-tuple-element.101.refs_0_, bf16[128,1024]{1,0:T(8,128)(2,1)S(1)} %collective-permute-done.13.refs_1_, bf16[64,1024]{1,0:T(8,128)(2,1)S(1)} %get-tuple-element.93.refs_0_.refs_2_, ...), custom_call_target="tpu_custom_call" | custom-call | flops 5000000000 | bytes 15000000 | tf_op jit(solution)/shard_map/di/dik0/ddk1/pallas_call | solution.py:525
  65.7 1.5 %dik1.1 = bf16[2,704,512]{2,1,0:T(8,128)(2,1)S(1)} custom-call(s32[8]{0:T(128)S(1)} %stack.55.place_ref, bf16[128,1152]{1,0:T(8,128)(2,1)S(1)} %get-tuple-element.70.refs_0_, bf16[128,1152]{1,0:T(8,128)(2,1)S(1)} %collective-permute-done.4.refs_1_, bf16[128,1152]{1,0:T(8,128)(2,1)S(1)} %get-tuple-element.73.refs_2_, ...), custom_call_target="tpu_custom_call" | custom-call | flops 5000000000 | bytes 15000000 | tf_op jit(solution)/shard_map/di/dik0/dis1/dik1/pallas_call | solution.py:525
  67.2 0.6 collective-permute-start.23
  67.7 0.2 cg2.1
  68.0 1.1 %collective-permute-done.15.refs_1_ = bf16[128,1024]{1,0:T(8,128)(2,1)S(1)} collective-permute-done((bf16[128,1024]{1,0:T(8,128)(2,1)S(1)}, bf16[128,1024]{1,0:T(8,128)(2,1)S(1)}, u32[]{:S(2)}, u32[]{:S(2)}) %collective-permute-start.15) | collective-permute-done | bytes 262176 | tf_op jit(solution)/shard_map/o/co0/yo0/ppermute | solution.py:72
  69.1 1.7 %collective-permute-start.27 = (bf16[64,1024]{1,0:T(8,128)(2,1)S(1)}, bf16[64,1024]{1,0:T(8,128)(2,1)S(1)}, u32[]{:S(2)}, u32[]{:S(2)}) collective-permute-start(bf16[64,1024]{1,0:T(8,128)(2,1)S(1)} %get-tuple-element.121), channel_id=1, source_target_pairs={{0,2},{1,3},{2,0},{3,1},{4,6},{5,7},{6,4},{7,5},{8,10},{9,11},{10,... | collective-permute-start | bytes 393224 | tf_op jit(solution)/shard_map/g/zg1/cg1/yg1/ppermute | solution.py:72
  70.8 0.3 co0.1
  71.2 0.4 collective-permute-start.29
  71.6 2.2 %collective-permute-start.22 = (bf16[128,1024]{1,0:T(8,128)(2,1)S(1)}, bf16[128,1024]{1,0:T(8,128)(2,1)S(1)}, u32[]{:S(2)}, u32[]{:S(2)}) collective-permute-start(bf16[128,1024]{1,0:T(8,128)(2,1)S(1)} %add_convert_fusion.5), channel_id=1, source_target_pairs={{0,8},{1,9},{2,10},{3,11},{4,12},{5,13},{6,14},{7,15},{8,0},{9,1},... | collective-permute-start | bytes 786440 | tf_op jit(solution)/shard_map/o/zo2/ppermute | solution.py:72
  73.8 1.1 %ddk0.1 = (f32[1,352,512]{2,1,0:T(8,128)S(1)}, bf16[1,352,512]{2,1,0:T(8,128)(2,1)S(1)}) custom-call(s32[8]{0:T(128)S(1)} %stack.55.place_ref, bf16[128,1024]{1,0:T(8,128)(2,1)S(1)} %get-tuple-element.101.refs_0_, bf16[128,1024]{1,0:T(8,128)(2,1)S(1)} %collective-permute-done.13.refs_1_, bf16[64,1024]{1,0:T(8,128)(2,1)S(1)} %get-tuple-element.93.refs_0_.refs_2_, ...), custom_call_target="tpu_custom_call" | custom-call | flops 5000000000 | bytes 15000000 | tf_op jit(solution)/shard_map/dd/ddk0/pallas_call | solution.py:525
  75.0 1.6 %collective-permute-start.32 = (bf16[1,352,512]{2,1,0:T(8,128)(2,1)S(1)}, bf16[1,352,512]{2,1,0:T(8,128)(2,1)S(1)}, u32[]{:S(2)}, u32[]{:S(2)}) collective-permute-start(bf16[1,352,512]{2,1,0:T(8,128)(2,1)S(1)} %get-tuple-element.128), channel_id=1, source_target_pairs={{0,1},{1,0},{2,3},{3,2},{4,5},{5,4},{6,7},{7,6},{8,9},{9,8},{10,11... | collective-permute-start | bytes 1081352 | tf_op jit(solution)/shard_map/dd/ddx/ppermute | solution.py:72
  76.5 0.2 cg1.1
  76.8 1.0 %collective-permute-start.25 = (bf16[128,1024]{1,0:T(8,128)(2,1)S(1)}, bf16[128,1024]{1,0:T(8,128)(2,1)S(1)}, u32[]{:S(2)}, u32[]{:S(2)}) collective-permute-start(bf16[128,1024]{1,0:T(8,128)(2,1)S(1)} %get-tuple-element.115), channel_id=1, source_target_pairs={{0,2},{1,3},{2,0},{3,1},{4,6},{5,7},{6,4},{7,5},{8,10},{9,11},{10,... | collective-permute-start | bytes 786440 | tf_op jit(solution)/shard_map/g/cg0/yg0/ppermute | solution.py:72
  77.8 1.5 %dik0.1 = (f32[2,352,512]{2,1,0:T(8,128)S(1)}, bf16[2,352,512]{2,1,0:T(8,128)(2,1)S(1)}) custom-call(s32[8]{0:T(128)S(1)} %stack.55.place_ref, bf16[128,1152]{1,0:T(8,128)(2,1)S(1)} %get-tuple-element.70.refs_0_, bf16[128,1152]{1,0:T(8,128)(2,1)S(1)} %collective-permute-done.4.refs_1_, bf16[128,1152]{1,0:T(8,128)(2,1)S(1)} %get-tuple-element.73.refs_2_, ...), custom_call_target="tpu_custom_call" | custom-call | flops 5000000000 | bytes 15000000 | tf_op jit(solution)/shard_map/di/dik0/pallas_call | solution.py:525
  79.3 3.9 %collective-permute-done.25.refs_1_ = bf16[128,1024]{1,0:T(8,128)(2,1)S(1)} collective-permute-done((bf16[128,1024]{1,0:T(8,128)(2,1)S(1)}, bf16[128,1024]{1,0:T(8,128)(2,1)S(1)}, u32[]{:S(2)}, u32[]{:S(2)}) %collective-permute-start.25) | collective-permute-done | bytes 262176 | tf_op jit(solution)/shard_map/g/cg0/yg0/ppermute | solution.py:72
  83.2 1.0 %collective-permute-start.28 = (bf16[128,1024]{1,0:T(8,128)(2,1)S(1)}, bf16[128,1024]{1,0:T(8,128)(2,1)S(1)}, u32[]{:S(2)}, u32[]{:S(2)}) collective-permute-start(bf16[128,1024]{1,0:T(8,128)(2,1)S(1)} %cg1.1), channel_id=1, source_target_pairs={{0,4},{1,5},{2,6},{3,7},{4,0},{5,1},{6,2},{7,3},{8,12},{9,13},{10,... | collective-permute-start | bytes 786440 | tf_op jit(solution)/shard_map/g/zg1/ppermute | solution.py:72
  84.2 0.3 cg0.1
  84.6 0.6 collective-permute-start.31
  85.2 1.6 %collective-permute-start.30 = (bf16[128,1024]{1,0:T(8,128)(2,1)S(1)}, bf16[128,1024]{1,0:T(8,128)(2,1)S(1)}, u32[]{:S(2)}, u32[]{:S(2)}) collective-permute-start(bf16[128,1024]{1,0:T(8,128)(2,1)S(1)} %add_convert_fusion.3), channel_id=1, source_target_pairs={{0,8},{1,9},{2,10},{3,11},{4,12},{5,13},{6,14},{7,15},{8,0},{9,1},... | collective-permute-start | bytes 786440 | tf_op jit(solution)/shard_map/g/zg2/ppermute | solution.py:72
  86.8 0.8 add_convert_fusion.4
  87.6 0.9 fusion.3
  88.5 5.2 %collective-permute-done.28 = bf16[128,1024]{1,0:T(8,128)(2,1)S(1)} collective-permute-done((bf16[128,1024]{1,0:T(8,128)(2,1)S(1)}, bf16[128,1024]{1,0:T(8,128)(2,1)S(1)}, u32[]{:S(2)}, u32[]{:S(2)}) %collective-permute-start.28) | collective-permute-done | bytes 262176 | tf_op jit(solution)/shard_map/g/zg1/ppermute | solution.py:72
  93.6 2.9 %collective-permute-done.30 = bf16[128,1024]{1,0:T(8,128)(2,1)S(1)} collective-permute-done((bf16[128,1024]{1,0:T(8,128)(2,1)S(1)}, bf16[128,1024]{1,0:T(8,128)(2,1)S(1)}, u32[]{:S(2)}, u32[]{:S(2)}) %collective-permute-start.30) | collective-permute-done | bytes 262176 | tf_op jit(solution)/shard_map/g/zg2/ppermute | solution.py:72
  96.5 0.8 add_convert_fusion.2
  97.3 1.0 %collective-permute-done.31 = bf16[2,352,512]{2,1,0:T(8,128)(2,1)S(1)} collective-permute-done((bf16[2,352,512]{2,1,0:T(8,128)(2,1)S(1)}, bf16[2,352,512]{2,1,0:T(8,128)(2,1)S(1)}, u32[]{:S(2)}, u32[]{:S(2)}) %collective-permute-start.31) | collective-permute-done | bytes 720928 | tf_op jit(solution)/shard_map/di/dix/ppermute | solution.py:72
  98.3 1.1 %fusion.2 = (bf16[1,512,352]{1,2,0:T(8,128)(2,1)}, bf16[1,512,352]{1,2,0:T(8,128)(2,1)}) fusion(f32[2,352,512]{2,1,0:T(8,128)S(1)} %get-tuple-element.111, bf16[2,352,512]{2,1,0:T(8,128)(2,1)S(1)} %collective-permute-done.31), kind=kLoop, calls=%fused_computation.10 | loop fusion | flops 1081344 | bytes 2883584 | tf_op jit(solution)/shard_map/broadcast_in_dim | solution.py:558
  (37 shorter events, 0.3 us)
Async XLA Ops:
  1.3 11.4 %collective-permute-start.2 = (s32[4,128]{1,0:T(4,128)S(1)}, s32[4,128]{1,0:T(4,128)S(1)}, u32[]{:S(2)}, u32[]{:S(2)}) collective-permute-start(s32[4,128]{1,0:T(4,128)S(1)} %pad_add_fusion.1), channel_id=1, source_target_pairs={{0,12},{1,13},{2,14},{3,15},{4,8},{5,9},{6,10},{7,11},{8,4},{9,5},... | collective-permute-start | bytes 6152 | tf_op jit(solution)/shard_map/di/dik0/prep/T3/ppermute | solution.py:72
  6.4 7.9 %collective-permute-start.1 = (s32[4,128]{1,0:T(4,128)S(1)}, s32[4,128]{1,0:T(4,128)S(1)}, u32[]{:S(2)}, u32[]{:S(2)}) collective-permute-start(s32[4,128]{1,0:T(4,128)S(1)} %pad_add_fusion.1), channel_id=1, source_target_pairs={{0,8},{1,9},{2,10},{3,11},{4,12},{5,13},{6,14},{7,15},{8,0},{9,1},... | collective-permute-start | bytes 6152 | tf_op jit(solution)/shard_map/di/dik0/prep/T2/ppermute | solution.py:72
  6.4 8.0 %collective-permute-start = (s32[4,128]{1,0:T(4,128)S(1)}, s32[4,128]{1,0:T(4,128)S(1)}, u32[]{:S(2)}, u32[]{:S(2)}) collective-permute-start(s32[4,128]{1,0:T(4,128)S(1)} %pad_add_fusion.1), channel_id=1, source_target_pairs={{0,4},{1,5},{2,6},{3,7},{4,0},{5,1},{6,2},{7,3},{8,12},{9,13},{10,... | collective-permute-start | bytes 6152 | tf_op jit(solution)/shard_map/di/dik0/prep/T1/ppermute | solution.py:72
  7.0 13.2 %collective-permute-start.5 = (bf16[128,1024]{1,0:T(8,128)(2,1)}, bf16[128,1024]{1,0:T(8,128)(2,1)S(1)}, u32[]{:S(2)}, u32[]{:S(2)}) collective-permute-start(bf16[128,1024]{1,0:T(8,128)(2,1)} %refs_0_), channel_id=1, source_target_pairs={{0,4},{1,5},{2,6},{3,7},{4,0},{5,1},{6,2},{7,3},{8,12},{9,13},{10,... | collective-permute-start | bytes 786440 | tf_op jit(solution)/shard_map/di/dik0/pt1/t1/ppermute | solution.py:72
  8.4 14.1 %collective-permute-start.3 = (bf16[128,1024]{1,0:T(8,128)(2,1)}, bf16[128,1024]{1,0:T(8,128)(2,1)S(1)}, u32[]{:S(2)}, u32[]{:S(2)}) collective-permute-start(bf16[128,1024]{1,0:T(8,128)(2,1)} %refs_0_), channel_id=1, source_target_pairs={{0,8},{1,9},{2,10},{3,11},{4,12},{5,13},{6,14},{7,15},{8,0},{9,1},... | collective-permute-start | bytes 786440 | tf_op jit(solution)/shard_map/di/dik0/pt0/t2/ppermute | solution.py:72
  12.8 24.3 %collective-permute-start.9 = (bf16[3,352,512]{2,1,0:T(8,128)(2,1)S(1)}, bf16[3,352,512]{2,1,0:T(8,128)(2,1)S(1)}, u32[]{:S(2)}, u32[]{:S(2)}) collective-permute-start(bf16[3,352,512]{2,1,0:T(8,128)(2,1)S(1)} %pad_maximum_fusion.refs_4_.refs_2_), channel_id=1, source_target_pairs={{0,1},{1,0},{2,3},{3,2},{4,5},{5,4},{6,7},{7,6},{8,9},{9,8},{10,11... | collective-permute-start | bytes 3244040 | tf_op jit(solution)/shard_map/di/dik0/bwd0/wx/ppermute | solution.py:72
  14.3 30.8 %collective-permute-start.8 = (bf16[3,352,512]{2,1,0:T(8,128)(2,1)S(1)}, bf16[3,352,512]{2,1,0:T(8,128)(2,1)S(1)}, u32[]{:S(2)}, u32[]{:S(2)}) collective-permute-start(bf16[3,352,512]{2,1,0:T(8,128)(2,1)S(1)} %pad_maximum_fusion.refs_4_.refs_2_), channel_id=1, source_target_pairs={{0,16},{16,0},{1,17},{17,1},{2,18},{18,2},{3,19},{19,3},{4,20},{20... | collective-permute-start | bytes 3244040 | tf_op jit(solution)/shard_map/di/dik0/bwd0/ws1/ppermute | solution.py:329
  14.4 8.4 %copy-start.1 = (bf16[128,1024]{1,0:T(8,128)(2,1)S(1)}, bf16[128,1024]{1,0:T(8,128)(2,1)}, u32[]{:S(2)}) copy-start(bf16[128,1024]{1,0:T(8,128)(2,1)} %refs_0_.1) | copy-start | bytes 786436
  14.4 11.0 %copy-start = (bf16[128,1024]{1,0:T(8,128)(2,1)S(1)}, bf16[128,1024]{1,0:T(8,128)(2,1)}, u32[]{:S(2)}) copy-start(bf16[128,1024]{1,0:T(8,128)(2,1)} %refs_0_) | copy-start | bytes 786436
  22.5 9.7 %collective-permute-start.6 = (bf16[128,1024]{1,0:T(8,128)(2,1)S(1)}, bf16[128,1024]{1,0:T(8,128)(2,1)S(1)}, u32[]{:S(2)}, u32[]{:S(2)}) collective-permute-start(bf16[128,1024]{1,0:T(8,128)(2,1)S(1)} %collective-permute-done.3.refs_1_), channel_id=1, source_target_pairs={{0,4},{1,5},{2,6},{3,7},{4,0},{5,1},{6,2},{7,3},{8,12},{9,13},{10,... | collective-permute-start | bytes 786440 | tf_op jit(solution)/shard_map/di/dik0/pt1/t3/ppermute | solution.py:72
  22.8 12.9 %collective-permute-start.11 = (bf16[128,1024]{1,0:T(8,128)(2,1)S(1)}, bf16[128,1024]{1,0:T(8,128)(2,1)S(1)}, u32[]{:S(2)}, u32[]{:S(2)}) collective-permute-start(bf16[128,1024]{1,0:T(8,128)(2,1)S(1)} %copy-done.1), channel_id=1, source_target_pairs={{0,8},{1,9},{2,10},{3,11},{4,12},{5,13},{6,14},{7,15},{8,0},{9,1},... | collective-permute-start | bytes 786440 | tf_op jit(solution)/shard_map/di/dik0/bwd0/pc0/c2/ppermute | solution.py:72
  25.8 9.9 %collective-permute-start.4 = (bf16[128,1152]{1,0:T(8,128)(2,1)S(1)}, bf16[128,1152]{1,0:T(8,128)(2,1)S(1)}, u32[]{:S(2)}, u32[]{:S(2)}) collective-permute-start(bf16[128,1152]{1,0:T(8,128)(2,1)S(1)} %get-tuple-element.71), channel_id=1, source_target_pairs={{0,2},{1,3},{2,0},{3,1},{4,6},{5,7},{6,4},{7,5},{8,10},{9,11},{10,... | collective-permute-start | bytes 884744 | tf_op jit(solution)/shard_map/di/dik0/yt0/ppermute | solution.py:72
  32.5 12.6 %collective-permute-start.7 = (bf16[128,1152]{1,0:T(8,128)(2,1)S(1)}, bf16[128,1152]{1,0:T(8,128)(2,1)S(1)}, u32[]{:S(2)}, u32[]{:S(2)}) collective-permute-start(bf16[128,1152]{1,0:T(8,128)(2,1)S(1)} %get-tuple-element.74), channel_id=1, source_target_pairs={{0,2},{1,3},{2,0},{3,1},{4,6},{5,7},{6,4},{7,5},{8,10},{9,11},{10,... | collective-permute-start | bytes 884744 | tf_op jit(solution)/shard_map/di/dik0/yt1/ppermute | solution.py:72
  35.7 6.6 %collective-permute-start.18 = (bf16[128,1024]{1,0:T(8,128)(2,1)S(1)}, bf16[128,1024]{1,0:T(8,128)(2,1)S(1)}, u32[]{:S(2)}, u32[]{:S(2)}) collective-permute-start(bf16[128,1024]{1,0:T(8,128)(2,1)S(1)} %copy-done.1), channel_id=1, source_target_pairs={{0,4},{1,5},{2,6},{3,7},{4,0},{5,1},{6,2},{7,3},{8,12},{9,13},{10,... | collective-permute-start | bytes 786440 | tf_op jit(solution)/shard_map/di/dik0/bwd1/pc1/c1/ppermute | solution.py:72
  37.0 5.3 %collective-permute-start.10 = (bf16[3,352,512]{2,1,0:T(8,128)(2,1)S(1)}, bf16[3,352,512]{2,1,0:T(8,128)(2,1)S(1)}, u32[]{:S(2)}, u32[]{:S(2)}) collective-permute-start(bf16[3,352,512]{2,1,0:T(8,128)(2,1)S(1)} %collective-permute-done.9.refs_6_.refs_4_), channel_id=1, source_target_pairs={{0,16},{16,0},{1,17},{17,1},{2,18},{18,2},{3,19},{19,3},{4,20},{20... | collective-permute-start | bytes 3244040 | tf_op jit(solution)/shard_map/di/dik0/bwd0/wp1/ppermute | solution.py:329
  37.4 7.8 %copy-start.2 = (s32[2]{0:T(128)S(1)}, s32[2]{0:T(128)}, u32[]{:S(2)}) copy-start(s32[2]{0:T(128)} %key_ref.1) | copy-start | bytes 28
  37.4 12.0 %collective-permute-start.13 = (bf16[128,1024]{1,0:T(8,128)(2,1)S(1)}, bf16[128,1024]{1,0:T(8,128)(2,1)S(1)}, u32[]{:S(2)}, u32[]{:S(2)}) collective-permute-start(bf16[128,1024]{1,0:T(8,128)(2,1)S(1)} %get-tuple-element.81), channel_id=1, source_target_pairs={{0,2},{1,3},{2,0},{3,1},{4,6},{5,7},{6,4},{7,5},{8,10},{9,11},{10,... | collective-permute-start | bytes 786440 | tf_op jit(solution)/shard_map/di/dik0/bwd0/yc0/ppermute | solution.py:72
  42.3 7.1 %collective-permute-start.12 = (bf16[128,1024]{1,0:T(8,128)(2,1)S(1)}, bf16[128,1024]{1,0:T(8,128)(2,1)S(1)}, u32[]{:S(2)}, u32[]{:S(2)}) collective-permute-start(bf16[128,1024]{1,0:T(8,128)(2,1)S(1)} %collective-permute-done.11.refs_1_), channel_id=1, source_target_pairs={{0,4},{1,5},{2,6},{3,7},{4,0},{5,1},{6,2},{7,3},{8,12},{9,13},{10,... | collective-permute-start | bytes 786440 | tf_op jit(solution)/shard_map/di/dik0/bwd1/pc2/c3/ppermute | solution.py:72
  42.5 14.1 %collective-permute-start.19 = (bf16[64,1024]{1,0:T(8,128)(2,1)S(1)}, bf16[64,1024]{1,0:T(8,128)(2,1)S(1)}, u32[]{:S(2)}, u32[]{:S(2)}) collective-permute-start(bf16[64,1024]{1,0:T(8,128)(2,1)S(1)} %get-tuple-element.95), channel_id=1, source_target_pairs={{0,2},{1,3},{2,0},{3,1},{4,6},{5,7},{6,4},{7,5},{8,10},{9,11},{10,... | collective-permute-start | bytes 393224 | tf_op jit(solution)/shard_map/di/dik0/bwd1/yc1/ppermute | solution.py:72
  49.6 7.0 %collective-permute-start.14 = (bf16[64,1024]{1,0:T(8,128)(2,1)S(1)}, bf16[64,1024]{1,0:T(8,128)(2,1)S(1)}, u32[]{:S(2)}, u32[]{:S(2)}) collective-permute-start(bf16[64,1024]{1,0:T(8,128)(2,1)S(1)} %get-tuple-element.84), channel_id=1, source_target_pairs={{0,2},{1,3},{2,0},{3,1},{4,6},{5,7},{6,4},{7,5},{8,10},{9,11},{10,... | collective-permute-start | bytes 393224 | tf_op jit(solution)/shard_map/di/dik0/bwd1/yc2/ppermute | solution.py:72
  51.5 10.8 %collective-permute-start.16 = (bf16[64,1024]{1,0:T(8,128)(2,1)S(1)}, bf16[64,1024]{1,0:T(8,128)(2,1)S(1)}, u32[]{:S(2)}, u32[]{:S(2)}) collective-permute-start(bf16[64,1024]{1,0:T(8,128)(2,1)S(1)} %get-tuple-element.88), channel_id=1, source_target_pairs={{0,2},{1,3},{2,0},{3,1},{4,6},{5,7},{6,4},{7,5},{8,10},{9,11},{10,... | collective-permute-start | bytes 393224 | tf_op jit(solution)/shard_map/di/dik0/dis1/yo1/ppermute | solution.py:72
  51.7 8.3 %collective-permute-start.20 = (bf16[64,1024]{1,0:T(8,128)(2,1)S(1)}, bf16[64,1024]{1,0:T(8,128)(2,1)S(1)}, u32[]{:S(2)}, u32[]{:S(2)}) collective-permute-start(bf16[64,1024]{1,0:T(8,128)(2,1)S(1)} %get-tuple-element.100), channel_id=1, source_target_pairs={{0,2},{1,3},{2,0},{3,1},{4,6},{5,7},{6,4},{7,5},{8,10},{9,11},{10,... | collective-permute-start | bytes 393224 | tf_op jit(solution)/shard_map/o/zo2/zo3/co2/yo2/ppermute | solution.py:72
  59.7 7.5 %collective-permute-start.24 = (bf16[64,1024]{1,0:T(8,128)(2,1)S(1)}, bf16[64,1024]{1,0:T(8,128)(2,1)S(1)}, u32[]{:S(2)}, u32[]{:S(2)}) collective-permute-start(bf16[64,1024]{1,0:T(8,128)(2,1)S(1)} %get-tuple-element.114), channel_id=1, source_target_pairs={{0,2},{1,3},{2,0},{3,1},{4,6},{5,7},{6,4},{7,5},{8,10},{9,11},{10,... | collective-permute-start | bytes 393224 | tf_op jit(solution)/shard_map/g/cg0/yg2/ppermute | solution.py:72
  60.3 10.9 %collective-permute-start.21 = (bf16[128,1024]{1,0:T(8,128)(2,1)S(1)}, bf16[128,1024]{1,0:T(8,128)(2,1)S(1)}, u32[]{:S(2)}, u32[]{:S(2)}) collective-permute-start(bf16[128,1024]{1,0:T(8,128)(2,1)S(1)} %co2.1), channel_id=1, source_target_pairs={{0,4},{1,5},{2,6},{3,7},{4,0},{5,1},{6,2},{7,3},{8,12},{9,13},{10,... | collective-permute-start | bytes 786440 | tf_op jit(solution)/shard_map/o/zo2/zo3/ppermute | solution.py:72
  62.6 22.6 %collective-permute-start.17 = (bf16[128,1024]{1,0:T(8,128)(2,1)S(1)}, bf16[128,1024]{1,0:T(8,128)(2,1)S(1)}, u32[]{:S(2)}, u32[]{:S(2)}) collective-permute-start(bf16[128,1024]{1,0:T(8,128)(2,1)S(1)} %co1.1), channel_id=1, source_target_pairs={{0,4},{1,5},{2,6},{3,7},{4,0},{5,1},{6,2},{7,3},{8,12},{9,13},{10,... | collective-permute-start | bytes 786440 | tf_op jit(solution)/shard_map/o/zo1/ppermute | solution.py:72
  62.7 6.4 %collective-permute-start.15 = (bf16[128,1024]{1,0:T(8,128)(2,1)S(1)}, bf16[128,1024]{1,0:T(8,128)(2,1)S(1)}, u32[]{:S(2)}, u32[]{:S(2)}) collective-permute-start(bf16[128,1024]{1,0:T(8,128)(2,1)S(1)} %get-tuple-element.85), channel_id=1, source_target_pairs={{0,2},{1,3},{2,0},{3,1},{4,6},{5,7},{6,4},{7,5},{8,10},{9,11},{10,... | collective-permute-start | bytes 786440 | tf_op jit(solution)/shard_map/o/co0/yo0/ppermute | solution.py:72
  65.6 6.0 %collective-permute-start.26 = (bf16[1,704,512]{2,1,0:T(8,128)(2,1)S(1)}, bf16[1,704,512]{2,1,0:T(8,128)(2,1)S(1)}, u32[]{:S(2)}, u32[]{:S(2)}) collective-permute-start(bf16[1,704,512]{2,1,0:T(8,128)(2,1)S(1)} %ddk1.1), channel_id=1, source_target_pairs={{0,16},{16,0},{1,17},{17,1},{2,18},{18,2},{3,19},{19,3},{4,20},{20... | collective-permute-start | bytes 2162696 | tf_op jit(solution)/shard_map/dd/ddk0/dds1/ppermute | solution.py:329
  67.2 9.6 %collective-permute-start.23 = (bf16[2,704,512]{2,1,0:T(8,128)(2,1)S(1)}, bf16[2,704,512]{2,1,0:T(8,128)(2,1)S(1)}, u32[]{:S(2)}, u32[]{:S(2)}) collective-permute-start(bf16[2,704,512]{2,1,0:T(8,128)(2,1)S(1)} %dik1.1), channel_id=1, source_target_pairs={{0,16},{16,0},{1,17},{17,1},{2,18},{18,2},{3,19},{19,3},{4,20},{20... | collective-permute-start | bytes 4325384 | tf_op jit(solution)/shard_map/di/dik0/dis1/ppermute | solution.py:329
  69.1 5.8 %collective-permute-start.27 = (bf16[64,1024]{1,0:T(8,128)(2,1)S(1)}, bf16[64,1024]{1,0:T(8,128)(2,1)S(1)}, u32[]{:S(2)}, u32[]{:S(2)}) collective-permute-start(bf16[64,1024]{1,0:T(8,128)(2,1)S(1)} %get-tuple-element.121), channel_id=1, source_target_pairs={{0,2},{1,3},{2,0},{3,1},{4,6},{5,7},{6,4},{7,5},{8,10},{9,11},{10,... | collective-permute-start | bytes 393224 | tf_op jit(solution)/shard_map/g/zg1/cg1/yg1/ppermute | solution.py:72
  71.2 13.4 %collective-permute-start.29 = (bf16[128,1024]{1,0:T(8,128)(2,1)S(1)}, bf16[128,1024]{1,0:T(8,128)(2,1)S(1)}, u32[]{:S(2)}, u32[]{:S(2)}) collective-permute-start(bf16[128,1024]{1,0:T(8,128)(2,1)S(1)} %cg2.1), channel_id=1, source_target_pairs={{0,4},{1,5},{2,6},{3,7},{4,0},{5,1},{6,2},{7,3},{8,12},{9,13},{10,... | collective-permute-start | bytes 786440 | tf_op jit(solution)/shard_map/g/zg2/zg3/ppermute | solution.py:72
  71.6 15.2 %collective-permute-start.22 = (bf16[128,1024]{1,0:T(8,128)(2,1)S(1)}, bf16[128,1024]{1,0:T(8,128)(2,1)S(1)}, u32[]{:S(2)}, u32[]{:S(2)}) collective-permute-start(bf16[128,1024]{1,0:T(8,128)(2,1)S(1)} %add_convert_fusion.5), channel_id=1, source_target_pairs={{0,8},{1,9},{2,10},{3,11},{4,12},{5,13},{6,14},{7,15},{8,0},{9,1},... | collective-permute-start | bytes 786440 | tf_op jit(solution)/shard_map/o/zo2/ppermute | solution.py:72
  75.0 12.7 %collective-permute-start.32 = (bf16[1,352,512]{2,1,0:T(8,128)(2,1)S(1)}, bf16[1,352,512]{2,1,0:T(8,128)(2,1)S(1)}, u32[]{:S(2)}, u32[]{:S(2)}) collective-permute-start(bf16[1,352,512]{2,1,0:T(8,128)(2,1)S(1)} %get-tuple-element.128), channel_id=1, source_target_pairs={{0,1},{1,0},{2,3},{3,2},{4,5},{5,4},{6,7},{7,6},{8,9},{9,8},{10,11... | collective-permute-start | bytes 1081352 | tf_op jit(solution)/shard_map/dd/ddx/ppermute | solution.py:72
  76.8 6.4 %collective-permute-start.25 = (bf16[128,1024]{1,0:T(8,128)(2,1)S(1)}, bf16[128,1024]{1,0:T(8,128)(2,1)S(1)}, u32[]{:S(2)}, u32[]{:S(2)}) collective-permute-start(bf16[128,1024]{1,0:T(8,128)(2,1)S(1)} %get-tuple-element.115), channel_id=1, source_target_pairs={{0,2},{1,3},{2,0},{3,1},{4,6},{5,7},{6,4},{7,5},{8,10},{9,11},{10,... | collective-permute-start | bytes 786440 | tf_op jit(solution)/shard_map/g/cg0/yg0/ppermute | solution.py:72
  83.2 10.4 %collective-permute-start.28 = (bf16[128,1024]{1,0:T(8,128)(2,1)S(1)}, bf16[128,1024]{1,0:T(8,128)(2,1)S(1)}, u32[]{:S(2)}, u32[]{:S(2)}) collective-permute-start(bf16[128,1024]{1,0:T(8,128)(2,1)S(1)} %cg1.1), channel_id=1, source_target_pairs={{0,4},{1,5},{2,6},{3,7},{4,0},{5,1},{6,2},{7,3},{8,12},{9,13},{10,... | collective-permute-start | bytes 786440 | tf_op jit(solution)/shard_map/g/zg1/ppermute | solution.py:72
  84.6 13.7 %collective-permute-start.31 = (bf16[2,352,512]{2,1,0:T(8,128)(2,1)S(1)}, bf16[2,352,512]{2,1,0:T(8,128)(2,1)S(1)}, u32[]{:S(2)}, u32[]{:S(2)}) collective-permute-start(bf16[2,352,512]{2,1,0:T(8,128)(2,1)S(1)} %get-tuple-element.125), channel_id=1, source_target_pairs={{0,1},{1,0},{2,3},{3,2},{4,5},{5,4},{6,7},{7,6},{8,9},{9,8},{10,11... | collective-permute-start | bytes 2162696 | tf_op jit(solution)/shard_map/di/dix/ppermute | solution.py:72
  85.2 11.2 %collective-permute-start.30 = (bf16[128,1024]{1,0:T(8,128)(2,1)S(1)}, bf16[128,1024]{1,0:T(8,128)(2,1)S(1)}, u32[]{:S(2)}, u32[]{:S(2)}) collective-permute-start(bf16[128,1024]{1,0:T(8,128)(2,1)S(1)} %add_convert_fusion.3), channel_id=1, source_target_pairs={{0,8},{1,9},{2,10},{3,11},{4,12},{5,13},{6,14},{7,15},{8,0},{9,1},... | collective-permute-start | bytes 786440 | tf_op jit(solution)/shard_map/g/zg2/ppermute | solution.py:72
